TPU v7x, 128 devices: a whole 4x4x4 slice. The times are simulated.
128 devices in a mesh: segment: 2 (over z_hi), ctx: 16 (over z_lo, y, core), mp: 4 (over x).
Axes of the slice: x: 4, y: 4, z: 4 (z_hi: 2, z_lo: 2; z = z_hi * 2 + z_lo), core: 2. Of those that a mesh axis runs over, the one named last changes fastest.
Arguments:
- targets: bfloat16 [8192, 4096], P('ctx'), may hold values from -6 to 6
- memory: bfloat16 [4096, 4096], P('ctx'), may hold values from -6 to 6
- pad_counts: int32 [16], P('ctx'), may hold values from 0 to 256, as said below
- norm_gains: float32 [2, 4096], P('segment'), may hold values from 0.5 to 4
- proj_weights: bfloat16 [2, 4096, 2, 4096], P('segment', None, None, 'mp'), may hold values from -0.09375 to 0.09375
Outputs:
- scored: bfloat16 [8192, 4096], P('ctx', ('segment', 'mp'))
Inputs may be any that keep to these rules, and one draw needn't show every extreme that they name: `pad_counts`: the live memory rows form one prefix: blocks before the one holding its end are full, later blocks are all padding. The first block is full and the last block is all padding in every draw.
All inputs are finite; a program needn't handle non-finite values.
Results may differ from a plain program's by a relative error of at most 0.02.
The roundings to bfloat16 on the way count: a program that leaves them out, or rounds other values in their place, can miss the bound.
Values may be sent and summed in bfloat16 or wider, within the bound.
No kernel may reach another device: no remote copies, remote signals or barrier semaphores. Data moves between devices by JAX's collectives and lax.ppermute only.
A program may use at most 256 MiB of HBM per device.

v0:
```python
import jax
import jax.numpy as jnp
from jax import lax
from jax.sharding import PartitionSpec as P

HEADS = 16


def passed_along(block, axis, distance):
    devices = range(lax.axis_size(axis))
    route = [(i - distance, i) for i in devices if i - distance in devices]
    return lax.ppermute(block, axis, route)


def norm_rows(hidden_rows, gain_row):
    widened = hidden_rows.astype(jnp.float32)
    inverse = lax.rsqrt(jnp.mean(widened * widened, axis=-1, keepdims=True) + 1e-06)
    return (widened * inverse * gain_row).astype(jnp.bfloat16)


def local(targets, memory, pad_counts, norm_gains, proj_weights):
    segment_index = lax.axis_index("segment")
    weights = proj_weights[0]
    norm_gain = norm_gains[0]
    model_width = weights.shape[0]
    local_width = weights.shape[2]
    local_heads = HEADS // lax.axis_size("mp")
    head_dim = local_width // local_heads
    target_rows = targets.shape[0]
    memory_rows = memory.shape[0]
    key_value = weights.reshape(model_width, 2 * local_width)

    def encode(hidden_rows):
        normed = norm_rows(hidden_rows, norm_gain)
        projected = jnp.dot(normed, key_value, preferred_element_type=jnp.float32).astype(
            jnp.bfloat16
        )
        return projected.reshape(hidden_rows.shape[0], 2, local_width)

    queries = lax.cond(
        segment_index == 1,
        lambda: jnp.dot(
            norm_rows(targets, norm_gain), weights[:, 0, :], preferred_element_type=jnp.float32
        ).astype(jnp.bfloat16),
        lambda: jnp.zeros((target_rows, local_width), jnp.bfloat16),
    )
    queries = queries.reshape(target_rows, local_heads, head_dim)
    live_keys = (jnp.arange(memory_rows) < memory_rows - pad_counts[0]).astype(jnp.bfloat16)
    initial = (
        jnp.full((local_heads, target_rows), -1e30, jnp.float32),
        jnp.zeros((local_heads, target_rows), jnp.float32),
        jnp.zeros((target_rows, local_heads, head_dim), jnp.float32),
    )
    arrived = passed_along(
        lax.cond(
            segment_index == 0,
            lambda: encode(memory),
            lambda: jnp.zeros((memory.shape[0], 2, local_width), jnp.bfloat16),
        ),
        "segment",
        1,
    )
    pieces = (
        lax.all_gather(arrived, "ctx", axis=0, tiled=True),
        lax.all_gather(live_keys, "ctx", axis=0, tiled=True),
    )

    def update(current):
        row_peaks, totals, weighted = current
        memory_block, live_marks = pieces
        key_rows = memory_block[:, 0, :].reshape(-1, local_heads, head_dim)
        value_rows = memory_block[:, 1, :].reshape(-1, local_heads, head_dim)
        scores = jnp.einsum("qhd,khd->hqk", queries, key_rows, preferred_element_type=jnp.float32)
        alive_mask = live_marks[None, None, :] > 0
        scores = jnp.where(alive_mask, scores, -1e30)
        new_peaks = jnp.maximum(row_peaks, jnp.max(scores, axis=2))
        soft_weights = jnp.where(alive_mask, jnp.exp(scores - new_peaks[:, :, None]), 0.0)
        rescale = jnp.exp(row_peaks - new_peaks)
        totals = jnp.sum(soft_weights, axis=2)
        mixed = jnp.einsum(
            "hqk,khd->qhd",
            soft_weights.astype(jnp.bfloat16),
            value_rows,
            preferred_element_type=jnp.float32,
        )
        weighted = weighted * rescale.T[:, :, None] + mixed
        return (new_peaks, totals, weighted)

    running = lax.cond(segment_index == 1, update, lambda current: current, initial)
    row_peaks, totals, weighted = running

    def finish():
        context = (
            (weighted / totals.T[:, :, None]).reshape(target_rows, local_width).astype(jnp.bfloat16)
        )
        return lax.dot_general(
            context, weights[:, 1, :], (((1,), (1,)), ((), ())), preferred_element_type=jnp.float32
        )

    partial_out = lax.cond(
        segment_index == 1, finish, lambda: jnp.zeros((target_rows, model_width), jnp.float32)
    )
    groups = lax.axis_size("mp")
    slice_width = model_width // (lax.axis_size("segment") * groups)
    summed = lax.psum_scatter(
        partial_out.astype(jnp.bfloat16), ("segment", "mp"), scatter_dimension=1, tiled=True
    ).astype(jnp.float32)
    own_slice = lax.dynamic_slice_in_dim(
        targets, lax.axis_index(("segment", "mp")) * slice_width, slice_width, 1
    )
    return (own_slice.astype(jnp.float32) + summed).astype(jnp.bfloat16)


def solution(mesh):
    placed = (
        P("ctx", None),
        P("ctx", None),
        P("ctx"),
        P("segment", None),
        P("segment", None, None, "mp"),
    )
    return jax.shard_map(
        local, mesh=mesh, in_specs=placed, out_specs=P("ctx", ("segment", "mp")), check_vma=False
    )
```

profile of v0, /device:TPU:38, one launch (start us, length us, event | category | flops | bytes accessed | tf_op | source)
XLA Modules:
  0.0 318.2 jit_solution(15851750304355277247)
XLA Ops:
  6.5 0.0 all-gather.3.cloned.1.call-start
  6.5 21.3 %conditional.4 = (bf16[256,2,1024]{2,1,0:T(2,128)(2,1)S(1)}) conditional(s32[]{:T(128)} %convert_element_type.53, () %tuple.35, (bf16[256,4096]{1,0:T(8,128)(2,1)}, f32[1,4096]{1,0:T(1,128)}, bf16[1,4096,2,1024]{3,2,1,0:T(2,128)(2,1)}) %tuple.36), branch_computations={%region_0.0_spmd, %region_1.0_spmd} | conditional | flops 4302831616 | bytes 66146368 | solution.py:55
  6.5 2.1 fusion
  8.6 0.0 copy-start
  8.6 0.0 copy-start.3
  8.7 11.9 %copy.26 = bf16[512,8,2,1024]{3,1,2,0:T(8,128)(2,1)S(1)} copy(bf16[512,8,2,1024]{3,2,1,0:T(2,128)(2,1)} %bitcast.32) | data formatting | bytes 33554432 | tf_op jit(solution)/shard_map/cond
  20.5 0.0 copy-done
  20.5 0.0 copy-done.3
  20.5 5.5 %convolution_convert_fusion = bf16[256,2048]{1,0:T(8,128)(2,1)} fusion(bf16[4096,2048]{1,0:T(8,128)(2,1)S(1)} %bitcast.36, bf16[256,4096]{1,0:T(8,128)(2,1)S(1)} %copy-done, f32[4096]{0:T(1024)S(1)} %bitcast.43, f32[256]{0:T(256)S(1)} %add_rsqrt_fusion), kind=kOutput, calls=%fused_computation.5 | convolution fusion | flops 4299685888 | bytes 19940352 | tf_op jit(solution)/shard_map/cond/branch_1_fun/dot_general | solution.py:35
  26.0 1.8 reshape.34
  27.9 1.1 copy.20
  28.9 1.4 collective-permute-start
  30.3 22.6 %collective-permute-done = bf16[256,2,1024]{0,2,1:T(8,128)(2,1)S(1)} collective-permute-done((bf16[256,2,1024]{0,2,1:T(8,128)(2,1)S(1)}, bf16[256,2,1024]{0,2,1:T(8,128)(2,1)S(1)}, u32[]{:S(2)}, u32[]{:S(2)}) %collective-permute-start) | collective-permute-done | bytes 1048608 | tf_op jit(solution)/shard_map/ppermute | solution.py:12
  52.9 0.0 copy-start.1
  52.9 1.0 copy-done.1
  53.9 0.0 all-gather.3.cloned.1.call-update
  53.9 0.0 reduce-scatter.2.cloned.1.call-start
  54.0 0.0 copy-start.2
  54.0 16.5 %copy.37 = bf16[1,4096,2,1024]{3,1,2,0:T(8,128)(2,1)} copy(bf16[1,4096,2,1024]{3,2,1,0:T(2,128)(2,1)} %param.17) | data formatting | bytes 33554432 | tf_op args[4]
  71.1 0.0 copy-done.2
  71.1 0.5 conditional.5
  71.2 0.3 reshape.35
  71.6 18.5 %all-gather = bf16[16,1,256]{2,1,0:T(2,128)(2,1)S(1)} all-gather(bf16[1,1,256]{2,1,0:T(2,128)(2,1)S(1)} %reshape.37), channel_id=1, replica_groups=mesh['segment'=2,'ctx'=16,'mp'=4] {'ctx'}, dimensions={0}, use_global_device_ids=true | all-gather | bytes 8704 | tf_op jit(solution)/shard_map/all_gather | solution.py:65
  90.1 65.5 %all-gather.3.cloned.1.call-done = bf16[4096,2,1024]{0,2,1:T(8,128)(2,1)} async-done(((bf16[256,2,1024]{0,2,1:T(8,128)(2,1)}), bf16[4096,2,1024]{0,2,1:T(8,128)(2,1)}) %all-gather.3.cloned.1.call-update) | async-done | bytes 16777232 | tf_op jit(solution)/shard_map/all_gather | solution.py:64
  155.6 1.5 conditional.6
  155.6 1.5 broadcast_in_dim.30
  157.2 2.4 conditional.7
  157.2 2.4 broadcast.61
  159.6 0.0 reduce-scatter.2.cloned.1.call-update
  159.6 149.6 %reduce-scatter.2.cloned.1.call-done = bf16[512,512]{1,0:T(8,128)(2,1)} async-done(((bf16[512,4096]{1,0:T(8,128)(2,1)}), bf16[512,512]{1,0:T(8,128)(2,1)}) %reduce-scatter.2.cloned.1.call-update) | async-done | bytes 524304 | tf_op jit(solution)/shard_map/reduce_scatter | solution.py:105
  309.2 2.1 add_convert_fusion
  (4 shorter events, 0.0 us)
Async XLA Ops:
  6.5 149.1 %all-gather.3.cloned.1.call-start = ((), (), s32[]{:S(2)}) async-start(), calls=%async_computation.1 | async-start | bytes 17825792 | tf_op jit(solution)/shard_map/all_gather | solution.py:64
  8.6 11.9 %copy-start = (bf16[256,4096]{1,0:T(8,128)(2,1)S(1)}, bf16[256,4096]{1,0:T(8,128)(2,1)}, u32[]{:S(2)}) copy-start(bf16[256,4096]{1,0:T(8,128)(2,1)} %get-tuple-element.57) | copy-start | bytes 6291460 | tf_op jit(solution)/shard_map/cond
  8.6 11.9 %copy-start.3 = (f32[1,4096]{1,0:T(1,128)S(1)}, f32[1,4096]{1,0:T(1,128)}, u32[]{:S(2)}) copy-start(f32[1,4096]{1,0:T(1,128)} %get-tuple-element.40) | copy-start | bytes 49156 | tf_op jit(solution)/shard_map/cond
  28.9 24.0 %collective-permute-start = (bf16[256,2,1024]{0,2,1:T(8,128)(2,1)S(1)}, bf16[256,2,1024]{0,2,1:T(8,128)(2,1)S(1)}, u32[]{:S(2)}, u32[]{:S(2)}) collective-permute-start(bf16[256,2,1024]{0,2,1:T(8,128)(2,1)S(1)} %copy.20), channel_id=1, source_target_pairs={{0,64},{1,65},{2,66},{3,67},{4,68},{5,69},{6,70},{7,71},{8,72},{9,... | collective-permute-start | bytes 3145736 | tf_op jit(solution)/shard_map/ppermute | solution.py:12
  52.9 1.0 copy-start.1
  53.9 255.3 %reduce-scatter.2.cloned.1.call-start = ((), (), s32[]{:S(2)}) async-start(), calls=%async_computation.2 | async-start | bytes 4718592 | tf_op jit(solution)/shard_map/reduce_scatter | solution.py:105
  54.0 17.2 %copy-start.2 = (f32[1,4096]{1,0:T(1,128)S(1)}, f32[1,4096]{1,0:T(1,128)}, u32[]{:S(2)}) copy-start(f32[1,4096]{1,0:T(1,128)} %param.16) | copy-start | bytes 49156
Sparse Core Ops, SparseCore 0:
  54.0 101.5 all-gather.2
  159.8 149.4 reduce-scatter.1
where the time goes:
time: 320 us; the launch traced here: 318 us
  waiting for transfers between devices  238 us (74%)
  local copies, waits for them, and re-layouts  36.4 us (11%)
  blocking collectives  18.5 us (6%)
  between operations  14.1 us (4%)
  matrix products  5.51 us (2%)
  other arithmetic  4.22 us (1%)
    reduce_scatter x1, waiting for transfers between devices, local(): lax.psum_scatter(partial_out.astype(jnp.bfloat16), ('segment', 'mp'), sca...  150 us
    all_gather x1, waiting for transfers between devices, local(): lax.all_gather(arrived, 'ctx', axis=0, tiled=True)  65.5 us
    ppermute x1, waiting for transfers between devices, passed_along(): return lax.ppermute(block, axis, route)  22.6 us
    all_gather x1, blocking collectives, local(): lax.all_gather(live_keys, 'ctx', axis=0, tiled=True)  18.5 us
    unnamed x6, local copies, waits for them, and re-layouts  17.5 us
    cond x5, local copies, waits for them, and re-layouts  11.9 us
  transfers between devices with their start and end apart: 3, of which 3 were waited for; matrix products, arithmetic and copies ran while one was open for 5% of the time, Pallas kernels for 0%

commit v1 on v0

v1 whole, which is shorter than its diff:
```python
import functools

import jax
import jax.numpy as jnp
from jax import lax
from jax.experimental import pallas as pl
from jax.experimental.pallas import tpu as pltpu
from jax.sharding import PartitionSpec as P

HEADS = 16
AXES = ("segment", "ctx", "mp")
MARK_ROWS = 16
DEAD = -1e30
VMEM = 56 * 2**20


def device_of(x, y, z, core):
    return (z // 2) * 64 + (z % 2) * 32 + y * 8 + core * 4 + x


def place_of(i):
    return i % 4, (i // 8) % 4, (i // 64) * 2 + (i // 32) % 2, (i // 4) % 2


def moved(block, step, senders=lambda x, y, z, core: True):
    route = []
    for i in range(128):
        place = place_of(i)
        if senders(*place):
            x, y, z, core = step(*place)
            route.append((i, device_of(x % 4, y % 4, z % 4, core % 2)))
    return lax.ppermute(block, AXES, route)


def along_x(block, d):
    return moved(block, lambda x, y, z, c: (x + d, y, z, c))


def along_y(block, d, senders=lambda x, y, z, core: True):
    return moved(block, lambda x, y, z, c: (x, y + d, z, c), senders)


def along_z(block, d):
    return moved(block, lambda x, y, z, c: (x, y, z + d, c))


def other_core(block, senders=lambda x, y, z, core: True):
    return moved(block, lambda x, y, z, c: (x, y, z, c + 1), senders)


def norm_rows(hidden_rows, gain_row):
    widened = hidden_rows.astype(jnp.float32)
    inverse = lax.rsqrt(jnp.mean(widened * widened, axis=-1, keepdims=True) + 1e-06)
    return (widened * inverse * gain_row).astype(jnp.bfloat16)


def normed_into(x_ref, gain_ref, normed, depth):
    rows = x_ref.shape[0]
    for top in range(0, rows, 128):
        part = norm_rows(x_ref[pl.ds(top, 128), :], gain_ref[...])
        for j in range(normed.shape[0]):
            normed[j, pl.ds(top, 128), :] = part[:, j * depth : (j + 1) * depth]


def encode_kernel(pad_ref, x_ref, gain_ref, w_ref, out_ref, normed, total):
    k, steps = pl.program_id(0), pl.num_programs(0)
    depth, width = w_ref.shape[1], w_ref.shape[3]
    rows = x_ref.shape[0]
    dim = out_ref.shape[2]

    @pl.when(k == 0)
    def _():
        normed_into(x_ref, gain_ref, normed, depth)
        total[...] = jnp.zeros_like(total)

    both = w_ref[0].reshape(depth, 2 * width)
    total[...] += jnp.dot(normed[k], both, preferred_element_type=jnp.float32)

    @pl.when(k == steps - 1)
    def _():
        position = lax.broadcasted_iota(jnp.int32, (MARK_ROWS, dim), 1)
        marks = jnp.where(position < rows - pad_ref[0], 0.0, DEAD).astype(jnp.bfloat16)
        for h in range(out_ref.shape[0]):
            out_ref[h, :rows, :] = total[:, h * dim : (h + 1) * dim].astype(jnp.bfloat16)
            out_ref[h, rows : 2 * rows, :] = total[
                :, width + h * dim : width + (h + 1) * dim
            ].astype(jnp.bfloat16)
            out_ref[h, 2 * rows :, :] = marks


def encode(memory, pad_counts, gains, weights, heads, dim):
    rows, model = memory.shape
    depth, width = 512, weights.shape[3]
    return pl.pallas_call(
        encode_kernel,
        grid=(model // depth,),
        in_specs=[
            pl.BlockSpec(memory_space=pltpu.SMEM),
            pl.BlockSpec((rows, model), lambda k: (0, 0)),
            pl.BlockSpec((1, model), lambda k: (0, 0)),
            pl.BlockSpec((1, depth, 2, width), lambda k: (0, k, 0, 0)),
        ],
        out_specs=pl.BlockSpec((heads, 2 * rows + MARK_ROWS, dim), lambda k: (0, 0, 0)),
        out_shape=jax.ShapeDtypeStruct((heads, 2 * rows + MARK_ROWS, dim), jnp.bfloat16),
        scratch_shapes=[
            pltpu.VMEM((model // depth, rows, depth), jnp.bfloat16),
            pltpu.VMEM((rows, 2 * width), jnp.float32),
        ],
        compiler_params=pltpu.CompilerParams(vmem_limit_bytes=VMEM),
    )(pad_counts, memory, gains, weights)


def query_kernel(x_ref, gain_ref, w_ref, out_ref, own_ref, normed, total):
    k, steps = pl.program_id(0), pl.num_programs(0)
    depth, width = w_ref.shape[1], w_ref.shape[3]
    rows = x_ref.shape[0]
    dim = out_ref.shape[2]

    @pl.when(k == 0)
    def _():
        normed_into(x_ref, gain_ref, normed, depth)
        total[...] = jnp.zeros_like(total)

    both = w_ref[0].reshape(depth, 2 * width)
    total[...] += jnp.dot(normed[k], both[:, :width], preferred_element_type=jnp.float32)

    @pl.when(k >= steps // 2)
    def _():
        own_ref[...] = both[:, width:]

    @pl.when(k == steps - 1)
    def _():
        for h in range(out_ref.shape[0]):
            out_ref[h, :rows, :] = total[:, h * dim : (h + 1) * dim].astype(jnp.bfloat16)
            out_ref[h, rows:, :] = jnp.zeros((MARK_ROWS, dim), jnp.bfloat16)


def query(targets, gains, weights, heads, dim):
    rows, model = targets.shape
    depth, width = 512, weights.shape[3]
    steps = model // depth
    return pl.pallas_call(
        query_kernel,
        grid=(steps,),
        in_specs=[
            pl.BlockSpec((rows, model), lambda k: (0, 0)),
            pl.BlockSpec((1, model), lambda k: (0, 0)),
            pl.BlockSpec((1, depth, 2, width), lambda k: (0, k, 0, 0)),
        ],
        out_specs=[
            pl.BlockSpec((heads, rows + MARK_ROWS, dim), lambda k: (0, 0, 0)),
            pl.BlockSpec((depth, width), lambda k: (jnp.maximum(k - steps // 2, 0), 0)),
        ],
        out_shape=[
            jax.ShapeDtypeStruct((heads, rows + MARK_ROWS, dim), jnp.bfloat16),
            jax.ShapeDtypeStruct((model // 2, width), jnp.bfloat16),
        ],
        scratch_shapes=[
            pltpu.VMEM((steps, rows, depth), jnp.bfloat16),
            pltpu.VMEM((rows, width), jnp.float32),
        ],
        compiler_params=pltpu.CompilerParams(vmem_limit_bytes=VMEM),
    )(targets, gains, weights)


def attend_kernel(place_ref, q_ref, *refs):
    blocks, out_ref, scores = refs[:-2], refs[-2], refs[-1]
    queries = q_ref[0]
    rows, keys = queries.shape[0], (blocks[0].shape[1] - MARK_ROWS) // 2
    pieces = [(ref, j) for ref in blocks for j in range(ref.shape[0])]
    peak = jnp.full((rows, keys), DEAD, jnp.float32)
    for i, (ref, j) in enumerate(pieces):
        marks = ref[j, 2 * keys : 2 * keys + 1, :].astype(jnp.float32)
        found = lax.dot_general(
            queries, ref[j, :keys, :], (((1,), (1,)), ((), ())), preferred_element_type=jnp.float32
        )
        found = found + marks
        scores[:, i * keys : (i + 1) * keys] = found
        peak = jnp.maximum(peak, found)
    peak = jnp.max(peak, axis=1, keepdims=True)
    total = jnp.zeros((rows, keys), jnp.float32)
    mixed = jnp.zeros((rows, out_ref.shape[2]), jnp.float32)
    for i, (ref, j) in enumerate(pieces):
        soft = jnp.exp(scores[:, i * keys : (i + 1) * keys] - peak)
        total = total + soft
        mixed = mixed + jnp.dot(
            soft.astype(jnp.bfloat16), ref[j, keys : 2 * keys, :], preferred_element_type=jnp.float32
        )
    out_ref[0] = (mixed / jnp.sum(total, axis=1, keepdims=True)).astype(jnp.bfloat16)


def attend(slabs, z, blocks):
    dim = slabs.shape[2]
    rows = slabs.shape[1] - MARK_ROWS
    keys = sum(b.shape[0] for b in blocks) * (blocks[0].shape[1] - MARK_ROWS) // 2
    return pl.pallas_call(
        attend_kernel,
        grid_spec=pltpu.PrefetchScalarGridSpec(
            num_scalar_prefetch=1,
            grid=(2,),
            in_specs=[
                pl.BlockSpec((1, rows, dim), lambda i, place: ((place[0] + 2 - i) % 4, 0, 0))
            ]
            + [pl.BlockSpec(b.shape, lambda i, place: (0, 0, 0)) for b in blocks],
            out_specs=pl.BlockSpec((1, rows, dim), lambda i, place: (i, 0, 0)),
            scratch_shapes=[pltpu.VMEM((rows, keys), jnp.float32)],
        ),
        out_shape=jax.ShapeDtypeStruct((2, rows, dim), jnp.bfloat16),
        compiler_params=pltpu.CompilerParams(vmem_limit_bytes=VMEM),
    )(z.reshape(1), slabs, *blocks)


def project_kernel(place_ref, c0, c1, c2, c3, w_ref, *rest):
    out_refs, context = rest[:-1], rest[-1]
    step = pl.program_id(0)
    dim = c0.shape[1]

    @pl.when(step == 0)
    def _():
        for d, ref in enumerate((c0, c1, c2, c3)):
            head = (place_ref[0] + 4 - d) % 4
            context[:, pl.ds(pl.multiple_of(head * dim, dim), dim)] = ref[...]

    mixed = lax.dot_general(
        context[...], w_ref[...], (((1,), (1,)), ((), ())), preferred_element_type=jnp.float32
    )
    for d, ref in enumerate(out_refs):

        @pl.when(step == d)
        def _(ref=ref):
            ref[...] = mixed.astype(ref.dtype)


def project(contexts, own, place, first, count, dtype):
    rows, dim = contexts[0].shape
    width = own.shape[0] // 4
    whole = pl.BlockSpec((rows, dim), lambda i, place: (0, 0))
    return pl.pallas_call(
        project_kernel,
        grid_spec=pltpu.PrefetchScalarGridSpec(
            num_scalar_prefetch=1,
            grid=(count,),
            in_specs=[whole] * 4
            + [pl.BlockSpec((width, own.shape[1]), lambda i, place: ((place[1] + first + i) % 4, 0))],
            out_specs=[pl.BlockSpec((rows, width), lambda i, place: (0, 0))] * count,
            scratch_shapes=[pltpu.VMEM((rows, 4 * dim), jnp.bfloat16)],
        ),
        out_shape=[jax.ShapeDtypeStruct((rows, width), dtype)] * count,
        compiler_params=pltpu.CompilerParams(vmem_limit_bytes=VMEM),
    )(place, *contexts, own)


def pick(stacked, index):
    return lax.dynamic_index_in_dim(stacked, index % stacked.shape[0], 0, keepdims=False)


def local(targets, memory, pad_counts, norm_gains, proj_weights):
    segment, ctx, x = (lax.axis_index(axis) for axis in AXES)
    core, y, low = ctx % 2, (ctx // 2) % 4, ctx // 8
    z = 2 * segment + low
    model, width = proj_weights.shape[1], proj_weights.shape[3]
    heads = HEADS // 4
    dim = width // heads
    rows = targets.shape[0]
    half = model // 2

    piece = half // 16
    share = lax.dynamic_slice_in_dim(proj_weights[0], ((1 - low) * 8 + ctx % 8) * piece, piece, 0)
    share = share[:, 1, :]
    down = lambda x, y, z, c: (x, y, 3 - z, c)
    share = moved(share, down, lambda x, y, z, c: z >= 2)
    encoder = lambda x, y, z, c: z < 2
    swapped = moved(share, lambda x, y, z, c: (x, y, 1 - z, c), encoder)
    first = low == 0
    share = jnp.stack([jnp.where(first, share, swapped), jnp.where(first, swapped, share)])
    gathered = jnp.zeros((2, 4, 2, piece, width), jnp.bfloat16)
    for d in (0, 1, 3, 2):
        got = share if d == 0 else along_y(share, d, encoder)
        twin = other_core(got, encoder)
        for c, part in ((core, got), (1 - core, twin)):
            gathered = lax.dynamic_update_slice(
                gathered, part[:, None, None], (0, (y - d) % 4, c, 0, 0)
            )

    slabs, own = lax.cond(
        segment == 0,
        lambda: (
            encode(memory, pad_counts, norm_gains, proj_weights, heads, dim),
            jnp.zeros((half, width), jnp.bfloat16),
        ),
        lambda: tuple(query(targets, norm_gains, proj_weights, heads, dim)),
    )
    arrived = {0: pick(slabs, z)}
    for d in (2, 1, 3):
        arrived[d] = along_z(pick(slabs, z + d), d)
    arrived = jnp.stack([arrived[d] for d in range(4)])
    block = jnp.stack([pick(arrived, z), pick(arrived, z - 1)])
    blocks = [block] + [along_y(block, d) for d in (2, 1, 3)]
    blocks = blocks + [other_core(b) for b in blocks]
    context = attend(arrived, z, blocks)

    contexts = {0: pick(context, low)}
    for d in (2, 1, 3):
        contexts[d] = along_z(pick(context, low + d), d)
    contexts = [contexts[d] for d in range(4)]
    place = jnp.stack([z, x])
    own = jnp.where(segment == 1, own, gathered.reshape(half, width))
    far = project(contexts, own, place, 1, 3, jnp.bfloat16)
    (near,) = project(contexts, own, place, 0, 1, jnp.float32)
    far = {d: along_x(far[d - 1], d) for d in (2, 1, 3)}
    out_width = model // 8
    residual = lax.dynamic_slice_in_dim(targets, (segment * 4 + x) * out_width, out_width, 1)
    summed = residual.astype(jnp.float32) + near
    for d in (1, 2, 3):
        summed = summed + far[d].astype(jnp.float32)
    return summed.astype(jnp.bfloat16)


def solution(mesh):
    placed = (
        P("ctx", None),
        P("ctx", None),
        P("ctx"),
        P("segment", None),
        P("segment", None, None, "mp"),
    )
    return jax.shard_map(
        local, mesh=mesh, in_specs=placed, out_specs=P("ctx", ("segment", "mp")), check_vma=False
    )
```

time: 320 us -> 175 us (0.55)
  the two profiles are of different devices: /device:TPU:38 before, /device:TPU:57 now
where the time goes in v1:
time: 175 us; the launch traced here: 174 us
  waiting for transfers between devices  59.7 us (34%)
  starting transfers between devices  53.3 us (30%)
  Pallas kernels  38.8 us (22%)
  local copies, waits for them, and re-layouts  13.8 us (8%)
  other arithmetic  7.85 us (4%)
    ppermute x25, waiting for transfers between devices, moved(): return lax.ppermute(block, AXES, route)  59.7 us
    ppermute x25, starting transfers between devices, moved(): return lax.ppermute(block, AXES, route)  53.3 us
    pallas_call x1, Pallas kernels, attend(): pl.pallas_call(attend_kernel, grid_spec=pltpu.PrefetchScalarGridSpec(num_...  14.5 us
    pallas_call x1, Pallas kernels, encode(): pl.pallas_call(encode_kernel, grid=(model // depth,), in_specs=[pl.BlockS...  13.9 us
    pallas_call x2, Pallas kernels, project(): pl.pallas_call(project_kernel, grid_spec=pltpu.PrefetchScalarGridSpec(num...  10.4 us
    dynamic_update_slice x7, local copies, waits for them, and re-layouts, local(): lax.dynamic_update_slice(gathered, part[:, None, None], (0, (y - d) % 4,...  5.53 us
  transfers between devices with their start and end apart: 25, of which 11 were waited for; matrix products, arithmetic and copies ran while one was open for 9% of the time, Pallas kernels for 11%

profile of v1, /device:TPU:57, one launch (start us, length us, event | category | flops | bytes accessed | tf_op | source)
XLA Modules:
  0.0 174.0 jit_solution(5214644637008291193)
XLA Ops:
  0.0 16.4 %conditional.1 = ((bf16[4,528,256]{2,1,0:T(8,128)(2,1)S(1)}, bf16[2048,1024]{1,0:T(8,128)(2,1)})) conditional(s32[]{:T(128)} %convert_element_type.19, (bf16[512,4096]{1,0:T(8,128)(2,1)}, f32[1,4096]{1,0:T(1,128)}, bf16[1,4096,2,1024]{3,2,1,0:T(2,128)(2,1)}) %tuple.12, (s32[1]{0:T(128)}, bf16[256,4096]{1,0:T(8,128)(2,1)}, f32[1,4096]{1,0:T(1,128)}, ...), branch_computations={%region_0.1_spmd, %region_1.2_spmd} | conditional | bytes 4194330 | solution.py:285
  0.0 13.9 %branch_1_fun.1 = bf16[4,528,256]{2,1,0:T(8,128)(2,1)S(1)} custom-call(s32[1]{0:T(128)} %get-tuple-element.38.pad_ref, bf16[256,4096]{1,0:T(8,128)(2,1)} %get-tuple-element.39.x_ref, f32[1,4096]{1,0:T(1,128)} %get-tuple-element.24.gain_ref, bf16[1,4096,2,1024]{3,2,1,0:T(2,128)(2,1)} %get-tuple-element.25.w_ref), custom_call_target="tpu_custom_call" | custom-call | tf_op jit(solution)/shard_map/cond/branch_1_fun/pallas_call | solution.py:94
  13.9 2.5 %broadcast.20 = bf16[2048,1024]{1,0:T(8,128)(2,1)} broadcast(bf16[]{:T(256)} %constant.154.clone), dimensions={} | broadcast | bytes 4194306 | tf_op jit(solution)/shard_map/broadcast.1
  16.5 3.4 %collective-permute-start.1 = (bf16[528,256]{1,0:T(8,128)(2,1)S(1)}, bf16[528,256]{1,0:T(8,128)(2,1)S(1)}, u32[]{:S(2)}, u32[]{:S(2)}) collective-permute-start(bf16[528,256]{1,0:T(8,128)(2,1)S(1)} %get-tuple-element.44), channel_id=1, source_target_pairs={{0,64},{1,65},{2,66},{3,67},{4,68},{5,69},{6,70},{7,71},{8,72},{9,... | collective-permute-start | bytes 811016 | tf_op jit(solution)/shard_map/ppermute | solution.py:32
  19.9 2.0 %collective-permute-start = (bf16[528,256]{1,0:T(8,128)(2,1)S(1)}, bf16[528,256]{1,0:T(8,128)(2,1)S(1)}, u32[]{:S(2)}, u32[]{:S(2)}) collective-permute-start(bf16[528,256]{1,0:T(8,128)(2,1)S(1)} %get-tuple-element.45), channel_id=1, source_target_pairs={{0,32},{1,33},{2,34},{3,35},{4,36},{5,37},{6,38},{7,39},{8,40},{9,... | collective-permute-start | bytes 811016 | tf_op jit(solution)/shard_map/ppermute | solution.py:32
  24.7 13.4 %collective-permute-done.13 = bf16[128,1024]{1,0:T(8,128)(2,1)S(1)} collective-permute-done((bf16[128,1024]{1,0:T(8,128)(2,1)S(1)}, bf16[128,1024]{1,0:T(8,128)(2,1)S(1)}, u32[]{:S(2)}, u32[]{:S(2)}) %collective-permute-start.13) | collective-permute-done | bytes 262176 | tf_op jit(solution)/shard_map/ppermute | solution.py:32
  38.2 5.1 %collective-permute-start.14 = (bf16[128,1024]{1,0:T(8,128)(2,1)S(1)}, bf16[128,1024]{1,0:T(8,128)(2,1)}, u32[]{:S(2)}, u32[]{:S(2)}) collective-permute-start(bf16[128,1024]{1,0:T(8,128)(2,1)S(1)} %collective-permute-done.13), channel_id=1, source_target_pairs={{0,32},{1,33},{2,34},{3,35},{4,36},{5,37},{6,38},{7,39},{8,40},{9,... | collective-permute-start | bytes 786440 | tf_op jit(solution)/shard_map/ppermute | solution.py:32
  44.6 1.9 %collective-permute-start.4 = (bf16[2,528,256]{2,1,0:T(8,128)(2,1)S(1)}, bf16[2,528,256]{2,1,0:T(8,128)(2,1)S(1)}, u32[]{:S(2)}, u32[]{:S(2)}) collective-permute-start(bf16[2,528,256]{2,1,0:T(8,128)(2,1)S(1)} %pad_maximum_fusion.1.refs_0_), channel_id=1, source_target_pairs={{0,8},{1,9},{2,10},{3,11},{4,12},{5,13},{6,14},{7,15},{8,16},{9,17... | collective-permute-start | bytes 1622024 | tf_op jit(solution)/shard_map/ppermute | solution.py:32
  51.0 3.3 %collective-permute-start.15 = (bf16[2,128,1024]{2,1,0:T(8,128)(2,1)}, bf16[2,128,1024]{2,1,0:T(8,128)(2,1)}, u32[]{:S(2)}, u32[]{:S(2)}) collective-permute-start(bf16[2,128,1024]{2,1,0:T(8,128)(2,1)} %pad_maximum_fusion.2), channel_id=1, source_target_pairs={{0,4},{1,5},{2,6},{3,7},{4,0},{5,1},{6,2},{7,3},{8,12},{9,13},{10,... | collective-permute-start | bytes 1572872 | tf_op jit(solution)/shard_map/ppermute | solution.py:32
  54.4 3.5 %collective-permute-done.3.refs_1_ = bf16[2,528,256]{2,1,0:T(8,128)(2,1)S(1)} collective-permute-done((bf16[2,528,256]{2,1,0:T(8,128)(2,1)S(1)}, bf16[2,528,256]{2,1,0:T(8,128)(2,1)S(1)}, u32[]{:S(2)}, u32[]{:S(2)}) %collective-permute-start.3) | collective-permute-done | bytes 540704 | tf_op jit(solution)/shard_map/ppermute | solution.py:32
  57.9 1.9 %collective-permute-start.16 = (bf16[2,128,1024]{2,1,0:T(8,128)(2,1)}, bf16[2,128,1024]{2,1,0:T(8,128)(2,1)}, u32[]{:S(2)}, u32[]{:S(2)}) collective-permute-start(bf16[2,128,1024]{2,1,0:T(8,128)(2,1)} %pad_maximum_fusion.2), channel_id=1, source_target_pairs={{0,8},{1,9},{2,10},{3,11},{4,12},{5,13},{6,14},{7,15},{8,16},{9,17... | collective-permute-start | bytes 1572872 | tf_op jit(solution)/shard_map/ppermute | solution.py:32
  59.8 7.7 %collective-permute-done.4.refs_2_ = bf16[2,528,256]{2,1,0:T(8,128)(2,1)S(1)} collective-permute-done((bf16[2,528,256]{2,1,0:T(8,128)(2,1)S(1)}, bf16[2,528,256]{2,1,0:T(8,128)(2,1)S(1)}, u32[]{:S(2)}, u32[]{:S(2)}) %collective-permute-start.4) | collective-permute-done | bytes 540704 | tf_op jit(solution)/shard_map/ppermute | solution.py:32
  67.5 4.3 %collective-permute-start.18 = (bf16[2,128,1024]{2,1,0:T(8,128)(2,1)}, bf16[2,128,1024]{2,1,0:T(8,128)(2,1)}, u32[]{:S(2)}, u32[]{:S(2)}) collective-permute-start(bf16[2,128,1024]{2,1,0:T(8,128)(2,1)} %pad_maximum_fusion.2), channel_id=1, source_target_pairs={{0,24},{1,25},{2,26},{3,27},{4,28},{5,29},{6,30},{7,31},{8,0},{9,1... | collective-permute-start | bytes 1572872 | tf_op jit(solution)/shard_map/ppermute | solution.py:32
  72.6 4.1 %collective-permute-start.20 = (bf16[2,128,1024]{2,1,0:T(8,128)(2,1)}, bf16[2,128,1024]{2,1,0:T(8,128)(2,1)}, u32[]{:S(2)}, u32[]{:S(2)}) collective-permute-start(bf16[2,128,1024]{2,1,0:T(8,128)(2,1)} %pad_maximum_fusion.2), channel_id=1, source_target_pairs={{0,16},{1,17},{2,18},{3,19},{4,20},{5,21},{6,22},{7,23},{8,24},{9,... | collective-permute-start | bytes 1572872 | tf_op jit(solution)/shard_map/ppermute | solution.py:32
  76.7 2.5 %collective-permute-start.7 = (bf16[2,528,256]{2,1,0:T(8,128)(2,1)S(1)}, bf16[2,528,256]{2,1,0:T(8,128)(2,1)S(1)}, u32[]{:S(2)}, u32[]{:S(2)}) collective-permute-start(bf16[2,528,256]{2,1,0:T(8,128)(2,1)S(1)} %collective-permute-done.3.refs_1_), channel_id=1, source_target_pairs={{0,4},{1,5},{2,6},{3,7},{4,0},{5,1},{6,2},{7,3},{8,12},{9,13},{10,... | collective-permute-start | bytes 1622024 | tf_op jit(solution)/shard_map/ppermute | solution.py:32
  79.8 2.2 %collective-permute-start.9 = (bf16[2,528,256]{2,1,0:T(8,128)(2,1)}, bf16[2,528,256]{2,1,0:T(8,128)(2,1)}, u32[]{:S(2)}, u32[]{:S(2)}) collective-permute-start(bf16[2,528,256]{2,1,0:T(8,128)(2,1)} %collective-permute-done.5.refs_3_), channel_id=1, source_target_pairs={{0,4},{1,5},{2,6},{3,7},{4,0},{5,1},{6,2},{7,3},{8,12},{9,13},{10,... | collective-permute-start | bytes 1622024 | tf_op jit(solution)/shard_map/ppermute | solution.py:32
  82.6 6.4 %collective-permute-start.17 = (bf16[2,128,1024]{2,1,0:T(8,128)(2,1)}, bf16[2,128,1024]{2,1,0:T(8,128)(2,1)}, u32[]{:S(2)}, u32[]{:S(2)}) collective-permute-start(bf16[2,128,1024]{2,1,0:T(8,128)(2,1)} %collective-permute-done.16), channel_id=1, source_target_pairs={{0,4},{1,5},{2,6},{3,7},{4,0},{5,1},{6,2},{7,3},{8,12},{9,13},{10,... | collective-permute-start | bytes 1572872 | tf_op jit(solution)/shard_map/ppermute | solution.py:32
  91.2 4.4 %collective-permute-done.20 = bf16[2,128,1024]{2,1,0:T(8,128)(2,1)} collective-permute-done((bf16[2,128,1024]{2,1,0:T(8,128)(2,1)}, bf16[2,128,1024]{2,1,0:T(8,128)(2,1)}, u32[]{:S(2)}, u32[]{:S(2)}) %collective-permute-start.20) | collective-permute-done | bytes 524320 | tf_op jit(solution)/shard_map/ppermute | solution.py:32
  95.6 4.6 %collective-permute-start.19 = (bf16[2,128,1024]{2,1,0:T(8,128)(2,1)}, bf16[2,128,1024]{2,1,0:T(8,128)(2,1)S(1)}, u32[]{:S(2)}, u32[]{:S(2)}) collective-permute-start(bf16[2,128,1024]{2,1,0:T(8,128)(2,1)} %collective-permute-done.18), channel_id=1, source_target_pairs={{0,4},{1,5},{2,6},{3,7},{4,0},{5,1},{6,2},{7,3},{8,12},{9,13},{10,... | collective-permute-start | bytes 1572872 | tf_op jit(solution)/shard_map/ppermute | solution.py:32
  100.3 2.1 %collective-permute-start.21 = (bf16[2,128,1024]{2,1,0:T(8,128)(2,1)}, bf16[2,128,1024]{2,1,0:T(8,128)(2,1)S(1)}, u32[]{:S(2)}, u32[]{:S(2)}) collective-permute-start(bf16[2,128,1024]{2,1,0:T(8,128)(2,1)} %collective-permute-done.20), channel_id=1, source_target_pairs={{0,4},{1,5},{2,6},{3,7},{4,0},{5,1},{6,2},{7,3},{8,12},{9,13},{10,... | collective-permute-start | bytes 1572872 | tf_op jit(solution)/shard_map/ppermute | solution.py:32
  103.2 14.5 %shard_map.57 = bf16[2,512,256]{2,1,0:T(8,128)(2,1)} custom-call(s32[1]{0:T(128)} %bitcast.place_ref, bf16[4,528,256]{2,1,0:T(8,128)(2,1)} %copy-done, bf16[2,528,256]{2,1,0:T(8,128)(2,1)} %copy-done.2, bf16[2,528,256]{2,1,0:T(8,128)(2,1)} %copy-done.6, bf16[2,528,256]{2,1,0:T(8,128)(2,1)} %copy-done.7, bf16[2,528,256]{2,1,0:T(8,128)(2,1)} %collective-permute-done.5.refs_3_, ...), custom_call_target="tpu_custom_call" | custom-call | tf_op jit(solution)/shard_map/pallas_call | solution.py:196
  117.8 2.1 %dynamic-slice_bitcast_fusion.3 = (bf16[512,256]{1,0:T(8,128)(2,1)S(1)}, bf16[512,256]{1,0:T(8,128)(2,1)S(1)}, bf16[512,256]{1,0:T(8,128)(2,1)S(1)}, bf16[512,256]{1,0:T(8,128)(2,1)}) fusion(bf16[2,512,256]{2,1,0:T(8,128)(2,1)} %shard_map.57, s32[]{:T(128)S(6)} %select_n.187, s32[]{:T(128)S(6)} %select_n.185, s32[]{:T(128)S(6)} %select_n.183, s32[]{:T(128)S(6)} %select_n.181), kind=kLoop, calls=%fused_computation.20 | loop fusion | bytes 2097168 | tf_op jit(solution)/shard_map/jit(dynamic_index_in_dim)/squeeze | solution.py:254
  119.9 1.8 %collective-permute-start.11 = (bf16[512,256]{1,0:T(8,128)(2,1)S(1)}, bf16[512,256]{1,0:T(8,128)(2,1)S(1)}, u32[]{:S(2)}, u32[]{:S(2)}) collective-permute-start(bf16[512,256]{1,0:T(8,128)(2,1)S(1)} %get-tuple-element.49), channel_id=1, source_target_pairs={{0,64},{1,65},{2,66},{3,67},{4,68},{5,69},{6,70},{7,71},{8,72},{9,... | collective-permute-start | bytes 786440 | tf_op jit(solution)/shard_map/ppermute | solution.py:32
  125.1 2.7 %bitcast_select_fusion.w_ref = bf16[2048,1024]{1,0:T(8,128)(2,1)} fusion(bf16[2048,1024]{1,0:T(8,128)(2,1)S(1)} %copy-done.1, bf16[2,4,2,128,1024]{4,3,2,1,0:T(8,128)(2,1)S(1)} %bitcast_dynamic-update-slice_fusion, pred[]{:T(512)S(6)} %eq.32), kind=kLoop, calls=%fused_computation | loop fusion | flops 2097152 | bytes 12582913 | tf_op jit(solution)/shard_map/jit(_where)/select_n | solution.py:307
  128.8 6.4 %collective-permute-done.12.c3 = bf16[512,256]{1,0:T(8,128)(2,1)S(1)} collective-permute-done((bf16[512,256]{1,0:T(8,128)(2,1)S(1)}, bf16[512,256]{1,0:T(8,128)(2,1)S(1)}, u32[]{:S(2)}, u32[]{:S(2)}) %collective-permute-start.12) | collective-permute-done | bytes 262176 | tf_op jit(solution)/shard_map/ppermute | solution.py:32
  135.9 6.3 %shard_map.59 = (bf16[512,512]{1,0:T(8,128)(2,1)}, bf16[512,512]{1,0:T(8,128)(2,1)}, bf16[512,512]{1,0:T(8,128)(2,1)}) custom-call(s32[2]{0:T(128)} %pad_add_fusion.place_ref, bf16[512,256]{1,0:T(8,128)(2,1)} %get-tuple-element.51.c0, bf16[512,256]{1,0:T(8,128)(2,1)} %copy-done.3, bf16[512,256]{1,0:T(8,128)(2,1)} %copy-done.4, bf16[512,256]{1,0:T(8,128)(2,1)} %copy-done.5, ...), custom_call_target="tpu_custom_call" | custom-call | tf_op jit(solution)/shard_map/pallas_call | solution.py:238
  142.3 2.5 %collective-permute-start.24 = (bf16[512,512]{1,0:T(8,128)(2,1)}, bf16[512,512]{1,0:T(8,128)(2,1)S(1)}, u32[]{:S(2)}, u32[]{:S(2)}) collective-permute-start(bf16[512,512]{1,0:T(8,128)(2,1)} %get-tuple-element.35), channel_id=1, source_target_pairs={{0,3},{1,0},{2,1},{3,2},{4,7},{5,4},{6,5},{7,6},{8,11},{9,8},{10,9... | collective-permute-start | bytes 1572872 | tf_op jit(solution)/shard_map/ppermute | solution.py:32
  145.9 4.0 %shard_map.58 = f32[512,512]{1,0:T(8,128)} custom-call(s32[2]{0:T(128)} %pad_add_fusion.place_ref, bf16[512,256]{1,0:T(8,128)(2,1)} %get-tuple-element.51.c0, bf16[512,256]{1,0:T(8,128)(2,1)} %copy-done.3, bf16[512,256]{1,0:T(8,128)(2,1)} %copy-done.4, bf16[512,256]{1,0:T(8,128)(2,1)} %copy-done.5, bf16[2048,1024]{1,0:T(8,128)(2,1)} %bitcast_select_fusion.w_ref), custom_call_target="tpu_custom_call" | custom-call | tf_op jit(solution)/shard_map/pallas_call | solution.py:238
  149.9 6.8 %collective-permute-done.24 = bf16[512,512]{1,0:T(8,128)(2,1)S(1)} collective-permute-done((bf16[512,512]{1,0:T(8,128)(2,1)}, bf16[512,512]{1,0:T(8,128)(2,1)S(1)}, u32[]{:S(2)}, u32[]{:S(2)}) %collective-permute-start.24) | collective-permute-done | bytes 524320 | tf_op jit(solution)/shard_map/ppermute | solution.py:32
  156.7 2.5 %collective-permute-done.23 = bf16[512,512]{1,0:T(8,128)(2,1)S(1)} collective-permute-done((bf16[512,512]{1,0:T(8,128)(2,1)}, bf16[512,512]{1,0:T(8,128)(2,1)S(1)}, u32[]{:S(2)}, u32[]{:S(2)}) %collective-permute-start.23) | collective-permute-done | bytes 524320 | tf_op jit(solution)/shard_map/ppermute | solution.py:32
  159.2 12.3 %collective-permute-done.22 = bf16[512,512]{1,0:T(8,128)(2,1)S(1)} collective-permute-done((bf16[512,512]{1,0:T(8,128)(2,1)}, bf16[512,512]{1,0:T(8,128)(2,1)S(1)}, u32[]{:S(2)}, u32[]{:S(2)}) %collective-permute-start.22) | collective-permute-done | bytes 524320 | tf_op jit(solution)/shard_map/ppermute | solution.py:32
  171.5 2.5 %add_convert_fusion = bf16[512,512]{1,0:T(8,128)(2,1)} fusion(bf16[512,512]{1,0:T(8,128)(2,1)S(1)} %collective-permute-done.24, bf16[512,512]{1,0:T(8,128)(2,1)S(1)} %collective-permute-done.23, bf16[512,512]{1,0:T(8,128)(2,1)S(1)} %collective-permute-done.22, f32[512,512]{1,0:T(8,128)} %shard_map.58, bf16[512,4096]{1,0:T(8,128)(2,1)} %param.7, s32[]{:T(128)S(6)} %select_n.168), kind=kLoop, calls=%fused_computation.2 | loop fusion | flops 2359296 | bytes 3670020 | tf_op jit(solution)/shard_map/convert_element_type | solution.py:316
  (66 shorter events, 19.8 us)
Async XLA Ops:
  16.5 26.8 %collective-permute-start.2 = (bf16[528,256]{1,0:T(8,128)(2,1)S(1)}, bf16[528,256]{1,0:T(8,128)(2,1)S(1)}, u32[]{:S(2)}, u32[]{:S(2)}) collective-permute-start(bf16[528,256]{1,0:T(8,128)(2,1)S(1)} %get-tuple-element.43), channel_id=1, source_target_pairs={{0,96},{1,97},{2,98},{3,99},{4,100},{5,101},{6,102},{7,103},{8,104... | collective-permute-start | bytes 811016 | tf_op jit(solution)/shard_map/ppermute | solution.py:32
  16.5 26.7 %collective-permute-start.1 = (bf16[528,256]{1,0:T(8,128)(2,1)S(1)}, bf16[528,256]{1,0:T(8,128)(2,1)S(1)}, u32[]{:S(2)}, u32[]{:S(2)}) collective-permute-start(bf16[528,256]{1,0:T(8,128)(2,1)S(1)} %get-tuple-element.44), channel_id=1, source_target_pairs={{0,64},{1,65},{2,66},{3,67},{4,68},{5,69},{6,70},{7,71},{8,72},{9,... | collective-permute-start | bytes 811016 | tf_op jit(solution)/shard_map/ppermute | solution.py:32
  19.9 23.4 %collective-permute-start = (bf16[528,256]{1,0:T(8,128)(2,1)S(1)}, bf16[528,256]{1,0:T(8,128)(2,1)S(1)}, u32[]{:S(2)}, u32[]{:S(2)}) collective-permute-start(bf16[528,256]{1,0:T(8,128)(2,1)S(1)} %get-tuple-element.45), channel_id=1, source_target_pairs={{0,32},{1,33},{2,34},{3,35},{4,36},{5,37},{6,38},{7,39},{8,40},{9,... | collective-permute-start | bytes 811016 | tf_op jit(solution)/shard_map/ppermute | solution.py:32
  23.4 14.8 %collective-permute-start.13 = (bf16[128,1024]{1,0:T(8,128)(2,1)S(1)}, bf16[128,1024]{1,0:T(8,128)(2,1)S(1)}, u32[]{:S(2)}, u32[]{:S(2)}) collective-permute-start(bf16[128,1024]{1,0:T(8,128)(2,1)S(1)} %slice_bitcast_fusion), channel_id=1, source_target_pairs={{64,32},{65,33},{66,34},{67,35},{68,36},{69,37},{70,38},{71,39},{7... | collective-permute-start | bytes 786440 | tf_op jit(solution)/shard_map/ppermute | solution.py:32
  38.2 11.0 %collective-permute-start.14 = (bf16[128,1024]{1,0:T(8,128)(2,1)S(1)}, bf16[128,1024]{1,0:T(8,128)(2,1)}, u32[]{:S(2)}, u32[]{:S(2)}) collective-permute-start(bf16[128,1024]{1,0:T(8,128)(2,1)S(1)} %collective-permute-done.13), channel_id=1, source_target_pairs={{0,32},{1,33},{2,34},{3,35},{4,36},{5,37},{6,38},{7,39},{8,40},{9,... | collective-permute-start | bytes 786440 | tf_op jit(solution)/shard_map/ppermute | solution.py:32
  43.4 39.1 %copy-start = (bf16[4,528,256]{2,1,0:T(8,128)(2,1)}, bf16[4,528,256]{2,1,0:T(8,128)(2,1)S(1)}, u32[]{:S(2)}) copy-start(bf16[4,528,256]{2,1,0:T(8,128)(2,1)S(1)} %pad_maximum_fusion.q_ref) | copy-start | bytes 3244036
  43.6 46.6 %copy-start.2 = (bf16[2,528,256]{2,1,0:T(8,128)(2,1)}, bf16[2,528,256]{2,1,0:T(8,128)(2,1)S(1)}, u32[]{:S(2)}) copy-start(bf16[2,528,256]{2,1,0:T(8,128)(2,1)S(1)} %pad_maximum_fusion.1.refs_0_) | copy-start | bytes 1622020
  43.6 14.3 %collective-permute-start.3 = (bf16[2,528,256]{2,1,0:T(8,128)(2,1)S(1)}, bf16[2,528,256]{2,1,0:T(8,128)(2,1)S(1)}, u32[]{:S(2)}, u32[]{:S(2)}) collective-permute-start(bf16[2,528,256]{2,1,0:T(8,128)(2,1)S(1)} %pad_maximum_fusion.1.refs_0_), channel_id=1, source_target_pairs={{0,16},{1,17},{2,18},{3,19},{4,20},{5,21},{6,22},{7,23},{8,24},{9,... | collective-permute-start | bytes 1622024 | tf_op jit(solution)/shard_map/ppermute | solution.py:32
  44.6 22.9 %collective-permute-start.4 = (bf16[2,528,256]{2,1,0:T(8,128)(2,1)S(1)}, bf16[2,528,256]{2,1,0:T(8,128)(2,1)S(1)}, u32[]{:S(2)}, u32[]{:S(2)}) collective-permute-start(bf16[2,528,256]{2,1,0:T(8,128)(2,1)S(1)} %pad_maximum_fusion.1.refs_0_), channel_id=1, source_target_pairs={{0,8},{1,9},{2,10},{3,11},{4,12},{5,13},{6,14},{7,15},{8,16},{9,17... | collective-permute-start | bytes 1622024 | tf_op jit(solution)/shard_map/ppermute | solution.py:32
  46.5 26.1 %collective-permute-start.5 = (bf16[2,528,256]{2,1,0:T(8,128)(2,1)S(1)}, bf16[2,528,256]{2,1,0:T(8,128)(2,1)}, u32[]{:S(2)}, u32[]{:S(2)}) collective-permute-start(bf16[2,528,256]{2,1,0:T(8,128)(2,1)S(1)} %pad_maximum_fusion.1.refs_0_), channel_id=1, source_target_pairs={{0,24},{1,25},{2,26},{3,27},{4,28},{5,29},{6,30},{7,31},{8,0},{9,1... | collective-permute-start | bytes 1622024 | tf_op jit(solution)/shard_map/ppermute | solution.py:32
  46.5 30.2 %collective-permute-start.6 = (bf16[2,528,256]{2,1,0:T(8,128)(2,1)S(1)}, bf16[2,528,256]{2,1,0:T(8,128)(2,1)}, u32[]{:S(2)}, u32[]{:S(2)}) collective-permute-start(bf16[2,528,256]{2,1,0:T(8,128)(2,1)S(1)} %pad_maximum_fusion.1.refs_0_), channel_id=1, source_target_pairs={{0,4},{1,5},{2,6},{3,7},{4,0},{5,1},{6,2},{7,3},{8,12},{9,13},{10,... | collective-permute-start | bytes 1622024 | tf_op jit(solution)/shard_map/ppermute | solution.py:32
  51.0 28.1 %collective-permute-start.15 = (bf16[2,128,1024]{2,1,0:T(8,128)(2,1)}, bf16[2,128,1024]{2,1,0:T(8,128)(2,1)}, u32[]{:S(2)}, u32[]{:S(2)}) collective-permute-start(bf16[2,128,1024]{2,1,0:T(8,128)(2,1)} %pad_maximum_fusion.2), channel_id=1, source_target_pairs={{0,4},{1,5},{2,6},{3,7},{4,0},{5,1},{6,2},{7,3},{8,12},{9,13},{10,... | collective-permute-start | bytes 1572872 | tf_op jit(solution)/shard_map/ppermute | solution.py:32
  57.8 45.4 %copy-start.6 = (bf16[2,528,256]{2,1,0:T(8,128)(2,1)}, bf16[2,528,256]{2,1,0:T(8,128)(2,1)S(1)}, u32[]{:S(2)}) copy-start(bf16[2,528,256]{2,1,0:T(8,128)(2,1)S(1)} %collective-permute-done.3.refs_1_) | copy-start | bytes 1622020
  57.9 22.0 %collective-permute-start.16 = (bf16[2,128,1024]{2,1,0:T(8,128)(2,1)}, bf16[2,128,1024]{2,1,0:T(8,128)(2,1)}, u32[]{:S(2)}, u32[]{:S(2)}) collective-permute-start(bf16[2,128,1024]{2,1,0:T(8,128)(2,1)} %pad_maximum_fusion.2), channel_id=1, source_target_pairs={{0,8},{1,9},{2,10},{3,11},{4,12},{5,13},{6,14},{7,15},{8,16},{9,17... | collective-permute-start | bytes 1572872 | tf_op jit(solution)/shard_map/ppermute | solution.py:32
  67.5 35.8 %copy-start.7 = (bf16[2,528,256]{2,1,0:T(8,128)(2,1)}, bf16[2,528,256]{2,1,0:T(8,128)(2,1)S(1)}, u32[]{:S(2)}) copy-start(bf16[2,528,256]{2,1,0:T(8,128)(2,1)S(1)} %collective-permute-done.4.refs_2_) | copy-start | bytes 1622020
  67.5 15.1 %collective-permute-start.18 = (bf16[2,128,1024]{2,1,0:T(8,128)(2,1)}, bf16[2,128,1024]{2,1,0:T(8,128)(2,1)}, u32[]{:S(2)}, u32[]{:S(2)}) collective-permute-start(bf16[2,128,1024]{2,1,0:T(8,128)(2,1)} %pad_maximum_fusion.2), channel_id=1, source_target_pairs={{0,24},{1,25},{2,26},{3,27},{4,28},{5,29},{6,30},{7,31},{8,0},{9,1... | collective-permute-start | bytes 1572872 | tf_op jit(solution)/shard_map/ppermute | solution.py:32
  72.6 23.1 %collective-permute-start.20 = (bf16[2,128,1024]{2,1,0:T(8,128)(2,1)}, bf16[2,128,1024]{2,1,0:T(8,128)(2,1)}, u32[]{:S(2)}, u32[]{:S(2)}) collective-permute-start(bf16[2,128,1024]{2,1,0:T(8,128)(2,1)} %pad_maximum_fusion.2), channel_id=1, source_target_pairs={{0,16},{1,17},{2,18},{3,19},{4,20},{5,21},{6,22},{7,23},{8,24},{9,... | collective-permute-start | bytes 1572872 | tf_op jit(solution)/shard_map/ppermute | solution.py:32
  76.7 23.6 %collective-permute-start.7 = (bf16[2,528,256]{2,1,0:T(8,128)(2,1)S(1)}, bf16[2,528,256]{2,1,0:T(8,128)(2,1)S(1)}, u32[]{:S(2)}, u32[]{:S(2)}) collective-permute-start(bf16[2,528,256]{2,1,0:T(8,128)(2,1)S(1)} %collective-permute-done.3.refs_1_), channel_id=1, source_target_pairs={{0,4},{1,5},{2,6},{3,7},{4,0},{5,1},{6,2},{7,3},{8,12},{9,13},{10,... | collective-permute-start | bytes 1622024 | tf_op jit(solution)/shard_map/ppermute | solution.py:32
  79.1 23.3 %collective-permute-start.8 = (bf16[2,528,256]{2,1,0:T(8,128)(2,1)S(1)}, bf16[2,528,256]{2,1,0:T(8,128)(2,1)S(1)}, u32[]{:S(2)}, u32[]{:S(2)}) collective-permute-start(bf16[2,528,256]{2,1,0:T(8,128)(2,1)S(1)} %collective-permute-done.4.refs_2_), channel_id=1, source_target_pairs={{0,4},{1,5},{2,6},{3,7},{4,0},{5,1},{6,2},{7,3},{8,12},{9,13},{10,... | collective-permute-start | bytes 1622024 | tf_op jit(solution)/shard_map/ppermute | solution.py:32
  79.8 23.4 %collective-permute-start.9 = (bf16[2,528,256]{2,1,0:T(8,128)(2,1)}, bf16[2,528,256]{2,1,0:T(8,128)(2,1)}, u32[]{:S(2)}, u32[]{:S(2)}) collective-permute-start(bf16[2,528,256]{2,1,0:T(8,128)(2,1)} %collective-permute-done.5.refs_3_), channel_id=1, source_target_pairs={{0,4},{1,5},{2,6},{3,7},{4,0},{5,1},{6,2},{7,3},{8,12},{9,13},{10,... | collective-permute-start | bytes 1622024 | tf_op jit(solution)/shard_map/ppermute | solution.py:32
  82.6 39.1 %collective-permute-start.17 = (bf16[2,128,1024]{2,1,0:T(8,128)(2,1)}, bf16[2,128,1024]{2,1,0:T(8,128)(2,1)}, u32[]{:S(2)}, u32[]{:S(2)}) collective-permute-start(bf16[2,128,1024]{2,1,0:T(8,128)(2,1)} %collective-permute-done.16), channel_id=1, source_target_pairs={{0,4},{1,5},{2,6},{3,7},{4,0},{5,1},{6,2},{7,3},{8,12},{9,13},{10,... | collective-permute-start | bytes 1572872 | tf_op jit(solution)/shard_map/ppermute | solution.py:32
  95.6 28.2 %collective-permute-start.19 = (bf16[2,128,1024]{2,1,0:T(8,128)(2,1)}, bf16[2,128,1024]{2,1,0:T(8,128)(2,1)S(1)}, u32[]{:S(2)}, u32[]{:S(2)}) collective-permute-start(bf16[2,128,1024]{2,1,0:T(8,128)(2,1)} %collective-permute-done.18), channel_id=1, source_target_pairs={{0,4},{1,5},{2,6},{3,7},{4,0},{5,1},{6,2},{7,3},{8,12},{9,13},{10,... | collective-permute-start | bytes 1572872 | tf_op jit(solution)/shard_map/ppermute | solution.py:32
  100.3 24.7 %collective-permute-start.21 = (bf16[2,128,1024]{2,1,0:T(8,128)(2,1)}, bf16[2,128,1024]{2,1,0:T(8,128)(2,1)S(1)}, u32[]{:S(2)}, u32[]{:S(2)}) collective-permute-start(bf16[2,128,1024]{2,1,0:T(8,128)(2,1)} %collective-permute-done.20), channel_id=1, source_target_pairs={{0,4},{1,5},{2,6},{3,7},{4,0},{5,1},{6,2},{7,3},{8,12},{9,13},{10,... | collective-permute-start | bytes 1572872 | tf_op jit(solution)/shard_map/ppermute | solution.py:32
  117.8 7.3 %copy-start.1 = (bf16[2048,1024]{1,0:T(8,128)(2,1)S(1)}, bf16[2048,1024]{1,0:T(8,128)(2,1)}, u32[]{:S(2)}) copy-start(bf16[2048,1024]{1,0:T(8,128)(2,1)} %get-tuple-element.32) | copy-start | bytes 12582916
  119.9 7.9 %collective-permute-start.10 = (bf16[512,256]{1,0:T(8,128)(2,1)S(1)}, bf16[512,256]{1,0:T(8,128)(2,1)S(1)}, u32[]{:S(2)}, u32[]{:S(2)}) collective-permute-start(bf16[512,256]{1,0:T(8,128)(2,1)S(1)} %get-tuple-element.50), channel_id=1, source_target_pairs={{0,32},{1,33},{2,34},{3,35},{4,36},{5,37},{6,38},{7,39},{8,40},{9,... | collective-permute-start | bytes 786440 | tf_op jit(solution)/shard_map/ppermute | solution.py:32
  119.9 8.9 %collective-permute-start.11 = (bf16[512,256]{1,0:T(8,128)(2,1)S(1)}, bf16[512,256]{1,0:T(8,128)(2,1)S(1)}, u32[]{:S(2)}, u32[]{:S(2)}) collective-permute-start(bf16[512,256]{1,0:T(8,128)(2,1)S(1)} %get-tuple-element.49), channel_id=1, source_target_pairs={{0,64},{1,65},{2,66},{3,67},{4,68},{5,69},{6,70},{7,71},{8,72},{9,... | collective-permute-start | bytes 786440 | tf_op jit(solution)/shard_map/ppermute | solution.py:32
  121.7 13.5 %collective-permute-start.12 = (bf16[512,256]{1,0:T(8,128)(2,1)S(1)}, bf16[512,256]{1,0:T(8,128)(2,1)S(1)}, u32[]{:S(2)}, u32[]{:S(2)}) collective-permute-start(bf16[512,256]{1,0:T(8,128)(2,1)S(1)} %get-tuple-element.48), channel_id=1, source_target_pairs={{0,96},{1,97},{2,98},{3,99},{4,100},{5,101},{6,102},{7,103},{8,104... | collective-permute-start | bytes 786440 | tf_op jit(solution)/shard_map/ppermute | solution.py:32
  127.8 7.4 %copy-start.3 = (bf16[512,256]{1,0:T(8,128)(2,1)}, bf16[512,256]{1,0:T(8,128)(2,1)S(1)}, u32[]{:S(2)}) copy-start(bf16[512,256]{1,0:T(8,128)(2,1)S(1)} %collective-permute-done.10.c1) | copy-start | bytes 786436
  128.8 6.4 %copy-start.4 = (bf16[512,256]{1,0:T(8,128)(2,1)}, bf16[512,256]{1,0:T(8,128)(2,1)S(1)}, u32[]{:S(2)}) copy-start(bf16[512,256]{1,0:T(8,128)(2,1)S(1)} %collective-permute-done.11.c2) | copy-start | bytes 786436
  142.3 14.4 %collective-permute-start.24 = (bf16[512,512]{1,0:T(8,128)(2,1)}, bf16[512,512]{1,0:T(8,128)(2,1)S(1)}, u32[]{:S(2)}, u32[]{:S(2)}) collective-permute-start(bf16[512,512]{1,0:T(8,128)(2,1)} %get-tuple-element.35), channel_id=1, source_target_pairs={{0,3},{1,0},{2,1},{3,2},{4,7},{5,4},{6,5},{7,6},{8,11},{9,8},{10,9... | collective-permute-start | bytes 1572872 | tf_op jit(solution)/shard_map/ppermute | solution.py:32
  144.7 14.4 %collective-permute-start.23 = (bf16[512,512]{1,0:T(8,128)(2,1)}, bf16[512,512]{1,0:T(8,128)(2,1)S(1)}, u32[]{:S(2)}, u32[]{:S(2)}) collective-permute-start(bf16[512,512]{1,0:T(8,128)(2,1)} %get-tuple-element.34), channel_id=1, source_target_pairs={{0,2},{1,3},{2,0},{3,1},{4,6},{5,7},{6,4},{7,5},{8,10},{9,11},{10,... | collective-permute-start | bytes 1572872 | tf_op jit(solution)/shard_map/ppermute | solution.py:32
  145.2 26.3 %collective-permute-start.22 = (bf16[512,512]{1,0:T(8,128)(2,1)}, bf16[512,512]{1,0:T(8,128)(2,1)S(1)}, u32[]{:S(2)}, u32[]{:S(2)}) collective-permute-start(bf16[512,512]{1,0:T(8,128)(2,1)} %get-tuple-element.33), channel_id=1, source_target_pairs={{0,1},{1,2},{2,3},{3,0},{4,5},{5,6},{6,7},{7,4},{8,9},{9,10},{10,1... | collective-permute-start | bytes 1572872 | tf_op jit(solution)/shard_map/ppermute | solution.py:32
  (3 other events, 4.4 us)

commit v2 on v0

v2 whole, which is shorter than its diff:
```python
import functools

import jax
import jax.numpy as jnp
from jax import lax
from jax.experimental import pallas as pl
from jax.experimental.pallas import tpu as pltpu
from jax.sharding import PartitionSpec as P

HEADS = 16
AXES = ("segment", "ctx", "mp")
MARK_ROWS = 16
DEAD = -1e30
VMEM = 56 * 2**20
ATTEND_VMEM = 40 * 2**20
LIGHT = pl.CostEstimate(flops=0, bytes_accessed=1024, transcendentals=0)


def device_of(x, y, z, core):
    return (z // 2) * 64 + (z % 2) * 32 + y * 8 + core * 4 + x


def place_of(i):
    return i % 4, (i // 8) % 4, (i // 64) * 2 + (i // 32) % 2, (i // 4) % 2


def moved(block, step, senders=lambda x, y, z, core: True):
    route = []
    for i in range(128):
        place = place_of(i)
        if senders(*place):
            x, y, z, core = step(*place)
            route.append((i, device_of(x % 4, y % 4, z % 4, core % 2)))
    return lax.ppermute(block, AXES, route)


def along_x(block, d):
    return moved(block, lambda x, y, z, c: (x + d, y, z, c))


def along_y(block, d, senders=lambda x, y, z, core: True):
    return moved(block, lambda x, y, z, c: (x, y + d, z, c), senders)


def along_z(block, d):
    return moved(block, lambda x, y, z, c: (x, y, z + d, c))


def other_core(block, senders=lambda x, y, z, core: True):
    return moved(block, lambda x, y, z, c: (x, y, z, c + 1), senders)


def norm_rows(hidden_rows, gain_row):
    widened = hidden_rows.astype(jnp.float32)
    inverse = lax.rsqrt(jnp.mean(widened * widened, axis=-1, keepdims=True) + 1e-06)
    return (widened * inverse * gain_row).astype(jnp.bfloat16)


def section_kernel(info_ref, memory, targets, gain_ref, w_ref, *refs):
    *out_refs, normed, x_rows, total, arrival = refs
    k, steps = pl.program_id(0), pl.num_programs(0)
    depth, width = w_ref.shape[1], w_ref.shape[3]
    rows = total.shape[0]
    half = rows // 2
    dim = out_refs[0].shape[1]
    encoder = info_ref[0] < 2

    def normalise(source, count):
        copy = pltpu.make_async_copy(source, x_rows.at[pl.ds(0, count)], arrival)
        copy.start()
        copy.wait()
        for top in range(0, count, 64):
            part = norm_rows(x_rows[pl.ds(top, 64), :], gain_ref[...])
            for j in range(normed.shape[0]):
                normed[j, pl.ds(top, 64), :] = part[:, j * depth : (j + 1) * depth]

    @pl.when((k == 0) & encoder)
    def _():
        normalise(memory, half)

    @pl.when((k == 0) & jnp.logical_not(encoder))
    def _():
        normalise(targets, rows)

    def add(rows_of, found):
        @pl.when(k == 0)
        def _():
            total[rows_of, :] = found

        @pl.when(k > 0)
        def _():
            total[rows_of, :] += found

    @pl.when(encoder)
    def _():
        both = w_ref[0].reshape(depth, 2 * width)
        found = jnp.dot(normed[k, :half, :], both, preferred_element_type=jnp.float32)
        add(pl.ds(0, half), found[:, :width])
        add(pl.ds(half, half), found[:, width:])

    @pl.when(jnp.logical_not(encoder))
    def _():
        both = w_ref[0].reshape(depth, 2 * width)
        found = jnp.dot(normed[k], both[:, :width], preferred_element_type=jnp.float32)
        add(pl.ds(0, rows), found)

    @pl.when(k == steps - 1)
    def _():
        position = lax.broadcasted_iota(jnp.int32, (MARK_ROWS, dim), 1)
        marks = jnp.where(position < half - info_ref[1], 0.0, DEAD).astype(jnp.bfloat16)
        for d, ref in enumerate(out_refs):
            head = (info_ref[0] + d) % 4
            ref[:rows, :] = total[:, pl.ds(pl.multiple_of(head * dim, dim), dim)].astype(jnp.bfloat16)
            ref[rows:, :] = marks


def section(info, memory, targets, gains, weights, dim):
    rows, model = targets.shape
    width = weights.shape[3]
    depth = 1024
    steps = model // depth
    slab = (rows + MARK_ROWS, dim)
    anywhere = pl.BlockSpec(memory_space=pl.ANY)
    return pl.pallas_call(
        section_kernel,
        grid_spec=pltpu.PrefetchScalarGridSpec(
            num_scalar_prefetch=1,
            grid=(steps,),
            in_specs=[
                anywhere,
                anywhere,
                pl.BlockSpec((1, model), lambda k, info: (0, 0)),
                pl.BlockSpec((1, depth, 2, width), lambda k, info: (0, k, 0, 0)),
            ],
            out_specs=[pl.BlockSpec(slab, lambda k, info: (0, 0))] * 4,
            scratch_shapes=[
                pltpu.VMEM((steps, rows, depth), jnp.bfloat16),
                pltpu.VMEM((rows, model), jnp.bfloat16),
                pltpu.VMEM((rows, width), jnp.float32),
                pltpu.SemaphoreType.DMA,
            ],
        ),
        out_shape=[jax.ShapeDtypeStruct(slab, jnp.bfloat16)] * 4,
        cost_estimate=LIGHT,
        compiler_params=pltpu.CompilerParams(vmem_limit_bytes=VMEM),
    )(info, memory, targets, gains, weights)


def second_half_kernel(start_ref, w_ref, *out_refs):
    depth, width = w_ref.shape[1], w_ref.shape[3]
    found = w_ref[0].reshape(depth, 2 * width)[:, width:]
    for j, ref in enumerate(out_refs):
        size = ref.shape[0]
        ref[...] = found[j * size : (j + 1) * size]


def second_half(weights, start, depth, steps, pieces):
    width = weights.shape[3]
    return pl.pallas_call(
        second_half_kernel,
        grid_spec=pltpu.PrefetchScalarGridSpec(
            num_scalar_prefetch=1,
            grid=(steps,),
            in_specs=[pl.BlockSpec((1, depth, 2, width), lambda k, start: (0, start[0] + k, 0, 0))],
            out_specs=[pl.BlockSpec((depth // pieces, width), lambda k, start: (k, 0))] * pieces,
        ),
        out_shape=[jax.ShapeDtypeStruct((steps * depth // pieces, width), jnp.bfloat16)] * pieces,
        cost_estimate=LIGHT,
        compiler_params=pltpu.CompilerParams(vmem_limit_bytes=VMEM),
    )(start.reshape(1), weights)


def attend_kernel(first, half, chunk, chunks, z_ref, *refs):
    if first:
        *slabs, acc_ref, peak_ref, total_ref, queries, keys, values, marks = refs
    else:
        *slabs, acc_ref, peak_ref, total_ref, out_a, out_b, queries, keys, values, marks = refs
    q_slabs, blocks = slabs[:4], slabs[4:]
    size = (blocks[0].shape[1] - MARK_ROWS) // 2
    z = z_ref[0]
    pieces = [ref.at[n] for ref in blocks for n in range(ref.shape[0])]
    for j, ref in enumerate(pieces):
        keys[j * size : (j + 1) * size, :] = ref[:size, :]
        values[j * size : (j + 1) * size, :] = ref[size : 2 * size, :]
        marks[:, j * size : (j + 1) * size] = ref[2 * size : 2 * size + 8, :].astype(jnp.float32)

    def run(at):
        base = at * 2 * half

        def take(index, when, top):
            @pl.when(when)
            def _():
                queries[pl.ds(top, half), :] = q_slabs[index][at * half : (at + 1) * half, :]

        take(2, z < 2, 0)
        take(0, z >= 2, 0)
        inner = (z == 1) | (z == 2)
        take(3, inner, half)
        take(1, jnp.logical_not(inner), half)

        part = 256
        for top in range(0, 2 * half, part):
            scores = lax.dot_general(
                queries[top : top + part, :],
                keys[...],
                (((1,), (1,)), ((), ())),
                preferred_element_type=jnp.float32,
            )
            scores = scores + marks[0:1, :]
            peak = jnp.max(scores, axis=1, keepdims=True)
            mine = slice(base + top, base + top + part)
            if not first:
                before = peak_ref[mine, :1]
                peak = jnp.maximum(peak, before)
                scale = jnp.exp(before - peak)
            soft = jnp.exp(scores - peak)
            total = jnp.sum(soft, axis=1, keepdims=True)
            mixed = jnp.dot(
                soft.astype(jnp.bfloat16), values[...], preferred_element_type=jnp.float32
            )
            if first:
                acc_ref[mine, :] = mixed
                peak_ref[mine, :] = jnp.broadcast_to(peak, (part, 128))
                total_ref[mine, :] = jnp.broadcast_to(total, (part, 128))
            else:
                mixed = mixed + scale * acc_ref[mine, :]
                total = total + scale * total_ref[mine, :1]
                found = (mixed / total).astype(jnp.bfloat16)
                if top < half:
                    out_a[top : top + part, :] = found
                else:
                    out_b[top - half : top - half + part, :] = found

    for at in range(chunks) if first else (chunk,):
        run(at)


def attend(z, q_slabs, blocks, chunks, state=None, chunk=0):
    rows, dim = q_slabs[0].shape[0] - MARK_ROWS, q_slabs[0].shape[1]
    half = rows // chunks
    first = state is None
    keys = sum(b.shape[0] for b in blocks) * (blocks[0].shape[1] - MARK_ROWS) // 2
    vmem = pl.BlockSpec(memory_space=pltpu.VMEM)
    if first:
        out_shape = [jax.ShapeDtypeStruct((2 * rows, last), jnp.float32) for last in (dim, 128, 128)]
    else:
        out_shape = [jax.ShapeDtypeStruct((half, dim), jnp.bfloat16)] * 2
    operands = [*q_slabs, *blocks, *(() if first else state)]
    return pl.pallas_call(
        functools.partial(attend_kernel, first, half, chunk, chunks),
        in_specs=[pl.BlockSpec(memory_space=pltpu.SMEM)] + [vmem] * len(operands),
        out_specs=[vmem] * len(out_shape),
        scratch_shapes=[
            pltpu.VMEM((2 * half, dim), jnp.bfloat16),
            pltpu.VMEM((keys, dim), jnp.bfloat16),
            pltpu.VMEM((keys, dim), jnp.bfloat16),
            pltpu.VMEM((8, keys), jnp.float32),
        ],
        out_shape=out_shape,
        cost_estimate=LIGHT,
        compiler_params=pltpu.CompilerParams(vmem_limit_bytes=ATTEND_VMEM),
    )(z.reshape(1), *operands)


def project_kernel(first, place_ref, c0, c1, c2, c3, *refs):
    sources, rest = refs[:5], refs[5:]
    *out_refs, held, context, arrived = rest
    z, x, core, held_set = place_ref[0], place_ref[1], place_ref[2], place_ref[3]
    dim, width = c0.shape[1], held.shape[1]
    for d, ref in enumerate((c0, c1, c2, c3)):
        head = (z + 4 - d) % 4
        context[:, pl.ds(pl.multiple_of(head * dim, dim), dim)] = ref[...]

    def fetch(j, action):
        wanted = (x + first + j) % 4
        kind = jnp.where(wanted // 2 == core, 0, 2) + jnp.where(wanted % 2 == held_set, 0, 1)

        @pl.when(z >= 2)
        def _():
            top = pl.multiple_of(wanted * width, width)
            action(pltpu.make_async_copy(sources[4].at[pl.ds(top, width)], held.at[j], arrived.at[j]))

        for n in range(4):

            @pl.when((z < 2) & (kind == n))
            def _(n=n):
                action(pltpu.make_async_copy(sources[n], held.at[j], arrived.at[j]))

    for j in range(len(out_refs)):
        fetch(j, lambda copy: copy.start())
    for j, ref in enumerate(out_refs):
        fetch(j, lambda copy: copy.wait())
        mixed = lax.dot_general(
            context[...], held[j], (((1,), (1,)), ((), ())), preferred_element_type=jnp.float32
        )
        ref[...] = mixed.astype(ref.dtype)


def project(place, contexts, sources, first, count, dtype):
    rows, dim = contexts[0].shape
    width = sources[4].shape[0] // 4
    vmem = pl.BlockSpec(memory_space=pltpu.VMEM)
    return pl.pallas_call(
        functools.partial(project_kernel, first),
        in_specs=[pl.BlockSpec(memory_space=pltpu.SMEM)]
        + [vmem] * 4
        + [pl.BlockSpec(memory_space=pl.ANY)] * 5,
        out_specs=[vmem] * count,
        out_shape=[jax.ShapeDtypeStruct((rows, width), dtype)] * count,
        scratch_shapes=[
            pltpu.VMEM((count, width, 4 * dim), jnp.bfloat16),
            pltpu.VMEM((rows, 4 * dim), jnp.bfloat16),
            pltpu.SemaphoreType.DMA((count,)),
        ],
        cost_estimate=LIGHT,
        compiler_params=pltpu.CompilerParams(vmem_limit_bytes=VMEM),
    )(place, *contexts, *sources)


def after(value, *others):
    return lax.optimization_barrier((value, *others))[0]


def local(targets, memory, pad_counts, norm_gains, proj_weights):
    segment, ctx, x = (lax.axis_index(axis) for axis in AXES)
    core, y, low = ctx % 2, (ctx // 2) % 4, ctx // 8
    z = 2 * segment + low
    model, width = proj_weights.shape[1], proj_weights.shape[3]
    dim = width * 4 // HEADS
    rows = targets.shape[0]
    half = model // 2
    chunks = 2
    down = lambda x, y, z, c: (x, y, 3 - z, c)
    encoder = lambda x, y, z, c: z < 2
    decoder = lambda x, y, z, c: z >= 2
    flip = lambda x, y, z, c: (x, y, 1 - z, c)
    is_encoder = segment == 0

    info = jnp.stack([z, pad_counts[0]])
    own, *to = section(info, memory, targets, norm_gains, proj_weights, dim)
    r1, r3, r2 = along_z(to[0], 1), along_z(to[2], 3), along_z(to[1], 2)

    held_set = (low + y) % 2
    (share,) = second_half(after(proj_weights, own), core * 2 + 1 - held_set, half // 4, 1, 1)
    p = moved(share, down, decoder)

    early = jnp.where(is_encoder, own, jnp.where(z == 2, r1, r3))
    late = jnp.where(z == 0, r3, jnp.where(z == 1, r1, r2))
    pair = jnp.stack([after(early, share), late])
    y1, y3 = along_y(pair, 1), along_y(pair, 3)
    (mine,) = second_half(after(proj_weights, pair), jnp.int32(2), half // 2, 2, 1)
    y1, y3, mine, p = lax.optimization_barrier((y1, y3, mine, p))
    far0, far1 = along_y(y1[0], 1), along_y(y3[1], 3)
    slabs = [own, r1, r2, r3]
    blocks = [pair, y1, y3]
    state = attend(z, slabs, blocks + [other_core(b) for b in blocks], chunks)

    quarter = half // 8
    far0, far1, *state = lax.optimization_barrier((far0, far1, *state))
    sz = moved(p[:quarter], flip, encoder)
    sy = moved(p[quarter:], lambda x, y, z, c: (x, y ^ 1, z, c), encoder)
    blocks = [far0[None], far1[None]]
    blocks = blocks + [other_core(b) for b in blocks]
    place = jnp.stack([z, x, core, held_set])

    first_part = attend(z, slabs, blocks, chunks, state, 0)
    second_part = attend(after(z, first_part[0]), slabs, blocks, chunks, state, 1)
    moving = []
    for ca, cb in (first_part, second_part):
        moving.append([ca, along_z(cb, 1), along_z(ca, 2), along_z(cb, 3)])
    twin = other_core(after(p, state[0]), encoder)
    moving[0], sz, sy, _ = lax.optimization_barrier((moving[0], sz, sy, second_part[0]))
    s = jnp.concatenate([sz, sy])
    sources = [p, s, twin, other_core(s, encoder), mine]
    finished = []
    out_width = model // 8
    residual = lax.dynamic_slice_in_dim(targets, (segment * 4 + x) * out_width, out_width, 1)
    for chunk, contexts in enumerate(moving):
        far = project(place, contexts, sources, 1, 3, jnp.bfloat16)
        (near,) = project(place, contexts, sources, 0, 1, jnp.float32)
        part = rows // chunks
        summed = residual[chunk * part : (chunk + 1) * part].astype(jnp.float32) + near
        for d in (1, 3, 2):
            summed = summed + along_x(far[d - 1], d).astype(jnp.float32)
        finished.append(summed.astype(jnp.bfloat16))
    return jnp.concatenate(finished)


def solution(mesh):
    placed = (
        P("ctx", None),
        P("ctx", None),
        P("ctx"),
        P("segment", None),
        P("segment", None, None, "mp"),
    )
    return jax.shard_map(
        local, mesh=mesh, in_specs=placed, out_specs=P("ctx", ("segment", "mp")), check_vma=False
    )
```

time: 320 us -> 136 us (0.42)
  waiting for transfers between devices: 238 us -> 36.9 us
  Pallas kernels: 0 us -> 49.2 us
  starting transfers between devices: 1.4 us -> 41.5 us
  local copies, waits for them, and re-layouts: 36.4 us -> 0.81 us
  blocking collectives: 18.5 us -> 0 us
  between operations: 14.1 us -> 1.04 us
  matrix products: 5.51 us -> 0 us
    reduce_scatter x1 -> x0, waiting for transfers between devices: 150 us -> none  [local(): lax.psum_scatter(partial_out.astype(jnp.bfloat16), ('segment', 'mp'), sca...]
    all_gather x1 -> x0, waiting for transfers between devices: 65.5 us -> none  [local(): lax.all_gather(arrived, 'ctx', axis=0, tiled=True)]
    pallas_call x0 -> x10, Pallas kernels: none -> 49.2 us  [the longest x4 16.5 us: project(): pl.pallas_call(functools.partial(project_kernel, first), in_specs=[pl.Blo...]
    ppermute x1 -> x29, starting transfers between devices: 1.36 us -> 41.5 us  [moved(): return lax.ppermute(block, AXES, route)]
    all_gather x1 -> x0, blocking collectives: 18.5 us -> none  [local(): lax.all_gather(live_keys, 'ctx', axis=0, tiled=True)]
    unnamed x6 -> x25, local copies, waits for them, and re-layouts: 17.5 us -> 0.67 us
    ppermute x1 -> x29, waiting for transfers between devices: 22.6 us -> 36.9 us  [moved(): return lax.ppermute(block, AXES, route)]
    cond x6 -> x0, local copies, waits for them, and re-layouts: 12.9 us -> none
  transfers between devices with their start and end apart: 3 -> 29, of which waited for: 3 -> 13; matrix products, arithmetic and copies ran while one was open for 5% -> 1% of each run, Pallas kernels for 0% -> 23%
where the time goes in v2:
time: 136 us; the launch traced here: 133 us
  Pallas kernels  49.2 us (36%)
  starting transfers between devices  41.5 us (31%)
  waiting for transfers between devices  36.9 us (27%)
  other arithmetic  3.85 us (3%)
    ppermute x29, starting transfers between devices, moved(): return lax.ppermute(block, AXES, route)  41.5 us
    ppermute x29, waiting for transfers between devices, moved(): return lax.ppermute(block, AXES, route)  36.9 us
    pallas_call x4, Pallas kernels, project(): pl.pallas_call(functools.partial(project_kernel, first), in_specs=[pl.Blo...  16.5 us
    pallas_call x1, Pallas kernels, section(): pl.pallas_call(section_kernel, grid_spec=pltpu.PrefetchScalarGridSpec(num...  14.5 us
    pallas_call x3, Pallas kernels, attend(): pl.pallas_call(functools.partial(attend_kernel, first, half, chunk, chunk...  10 us
    pallas_call x2, Pallas kernels, second_half(): pl.pallas_call(second_half_kernel, grid_spec=pltpu.PrefetchScalarGridSpec...  8.25 us
  transfers between devices with their start and end apart: 29, of which 13 were waited for; matrix products, arithmetic and copies ran while one was open for 1% of the time, Pallas kernels for 23%

profile of v2, /device:TPU:38, one launch (start us, length us, event | category | flops | bytes accessed | tf_op | source)
XLA Modules:
  0.0 133.3 jit_solution(6924775464319719227)
XLA Ops:
  1.3 14.5 %shard_map.55 = (bf16[528,256]{1,0:T(8,128)(2,1)}, bf16[528,256]{1,0:T(8,128)(2,1)}, bf16[528,256]{1,0:T(8,128)(2,1)}, bf16[528,256]{1,0:T(8,128)(2,1)}) custom-call(s32[2]{0:T(128)} %pad_add_fusion.1.info_ref, bf16[256,4096]{1,0:T(8,128)(2,1)} %memory.1, bf16[512,4096]{1,0:T(8,128)(2,1)} %targets.1, f32[1,4096]{1,0:T(1,128)} %gain_ref.1, ...), custom_call_target="tpu_custom_call" | custom-call | bytes 1024 | tf_op jit(solution)/shard_map/pallas_call | solution.py:124
  15.8 3.3 %collective-permute-start = (bf16[528,256]{1,0:T(8,128)(2,1)}, bf16[528,256]{1,0:T(8,128)(2,1)S(1)}, u32[]{:S(2)}, u32[]{:S(2)}) collective-permute-start(bf16[528,256]{1,0:T(8,128)(2,1)} %get-tuple-element.43), channel_id=1, source_target_pairs={{0,32},{1,33},{2,34},{3,35},{4,36},{5,37},{6,38},{7,39},{8,40},{9,... | collective-permute-start | bytes 811016 | tf_op jit(solution)/shard_map/ppermute | solution.py:34
  20.3 2.5 %collective-permute-start.2 = (bf16[528,256]{1,0:T(8,128)(2,1)}, bf16[528,256]{1,0:T(8,128)(2,1)S(1)}, u32[]{:S(2)}, u32[]{:S(2)}) collective-permute-start(bf16[528,256]{1,0:T(8,128)(2,1)} %get-tuple-element.45), channel_id=1, source_target_pairs={{0,96},{1,97},{2,98},{3,99},{4,100},{5,101},{6,102},{7,103},{8,104... | collective-permute-start | bytes 811016 | tf_op jit(solution)/shard_map/ppermute | solution.py:34
  22.8 2.9 %shard_map.56 = bf16[512,1024]{1,0:T(8,128)(2,1)} custom-call(s32[1]{0:T(128)} %bitcast.4.start_ref, bf16[1,4096,2,1024]{3,2,1,0:T(2,128)(2,1)} %w_ref.3), custom_call_target="tpu_custom_call" | custom-call | bytes 1024 | tf_op jit(solution)/shard_map/pallas_call | solution.py:159
  27.0 3.9 %collective-permute-done.refs_1_ = bf16[528,256]{1,0:T(8,128)(2,1)S(1)} collective-permute-done((bf16[528,256]{1,0:T(8,128)(2,1)}, bf16[528,256]{1,0:T(8,128)(2,1)S(1)}, u32[]{:S(2)}, u32[]{:S(2)}) %collective-permute-start) | collective-permute-done | bytes 270368 | tf_op jit(solution)/shard_map/ppermute | solution.py:34
  31.0 3.8 %collective-permute-done.2.refs_3_ = bf16[528,256]{1,0:T(8,128)(2,1)S(1)} collective-permute-done((bf16[528,256]{1,0:T(8,128)(2,1)}, bf16[528,256]{1,0:T(8,128)(2,1)S(1)}, u32[]{:S(2)}, u32[]{:S(2)}) %collective-permute-start.2) | collective-permute-done | bytes 270368 | tf_op jit(solution)/shard_map/ppermute | solution.py:34
  34.9 1.6 %collective-permute-start.3 = (bf16[2,528,256]{2,1,0:T(8,128)(2,1)S(1)}, bf16[2,528,256]{2,1,0:T(8,128)(2,1)S(1)}, u32[]{:S(2)}, u32[]{:S(2)}) collective-permute-start(bf16[2,528,256]{2,1,0:T(8,128)(2,1)S(1)} %pad_maximum_fusion.refs_4_), channel_id=1, source_target_pairs={{0,8},{1,9},{2,10},{3,11},{4,12},{5,13},{6,14},{7,15},{8,16},{9,17... | collective-permute-start | bytes 1622024 | tf_op jit(solution)/shard_map/ppermute | solution.py:34
  36.5 1.7 %collective-permute-start.4 = (bf16[2,528,256]{2,1,0:T(8,128)(2,1)S(1)}, bf16[2,528,256]{2,1,0:T(8,128)(2,1)S(1)}, u32[]{:S(2)}, u32[]{:S(2)}) collective-permute-start(bf16[2,528,256]{2,1,0:T(8,128)(2,1)S(1)} %pad_maximum_fusion.refs_4_), channel_id=1, source_target_pairs={{0,24},{1,25},{2,26},{3,27},{4,28},{5,29},{6,30},{7,31},{8,0},{9,1... | collective-permute-start | bytes 1622024 | tf_op jit(solution)/shard_map/ppermute | solution.py:34
  38.2 5.3 %shard_map.57.refs_4_ = bf16[2048,1024]{1,0:T(8,128)(2,1)} custom-call(s32[1]{0:T(128)} %constant.70.clone.1.start_ref, bf16[1,4096,2,1024]{3,2,1,0:T(2,128)(2,1)} %w_ref.3), custom_call_target="tpu_custom_call" | custom-call | bytes 1024 | tf_op jit(solution)/shard_map/pallas_call | solution.py:159
  43.5 6.0 %collective-permute-done.3.refs_5_ = bf16[2,528,256]{2,1,0:T(8,128)(2,1)S(1)} collective-permute-done((bf16[2,528,256]{2,1,0:T(8,128)(2,1)S(1)}, bf16[2,528,256]{2,1,0:T(8,128)(2,1)S(1)}, u32[]{:S(2)}, u32[]{:S(2)}) %collective-permute-start.3) | collective-permute-done | bytes 540704 | tf_op jit(solution)/shard_map/ppermute | solution.py:34
  49.5 7.2 %collective-permute-done.5.refs_0_ = bf16[512,1024]{1,0:T(8,128)(2,1)S(1)} collective-permute-done((bf16[512,1024]{1,0:T(8,128)(2,1)}, bf16[512,1024]{1,0:T(8,128)(2,1)S(1)}, u32[]{:S(2)}, u32[]{:S(2)}) %collective-permute-start.5) | collective-permute-done | bytes 1048608 | tf_op jit(solution)/shard_map/ppermute | solution.py:34
  57.2 1.6 %collective-permute-start.6 = (bf16[528,256]{1,0:T(8,128)(2,1)S(1)}, bf16[528,256]{1,0:T(8,128)(2,1)S(1)}, u32[]{:S(2)}, u32[]{:S(2)}) collective-permute-start(bf16[528,256]{1,0:T(8,128)(2,1)S(1)} %slice_bitcast_fusion.1), channel_id=1, source_target_pairs={{0,8},{1,9},{2,10},{3,11},{4,12},{5,13},{6,14},{7,15},{8,16},{9,17... | collective-permute-start | bytes 811016 | tf_op jit(solution)/shard_map/ppermute | solution.py:34
  58.9 1.7 %collective-permute-start.7 = (bf16[528,256]{1,0:T(8,128)(2,1)S(1)}, bf16[528,256]{1,0:T(8,128)(2,1)S(1)}, u32[]{:S(2)}, u32[]{:S(2)}) collective-permute-start(bf16[528,256]{1,0:T(8,128)(2,1)S(1)} %slice_bitcast_fusion), channel_id=1, source_target_pairs={{0,24},{1,25},{2,26},{3,27},{4,28},{5,29},{6,30},{7,31},{8,0},{9,1... | collective-permute-start | bytes 811016 | tf_op jit(solution)/shard_map/ppermute | solution.py:34
  60.7 2.7 %collective-permute-start.16 = (bf16[256,1024]{1,0:T(8,128)(2,1)S(1)}, bf16[256,1024]{1,0:T(8,128)(2,1)S(1)}, u32[]{:S(2)}, u32[]{:S(2)}) collective-permute-start(bf16[256,1024]{1,0:T(8,128)(2,1)S(1)} %get-tuple-element.82), channel_id=1, source_target_pairs={{0,32},{1,33},{2,34},{3,35},{4,36},{5,37},{6,38},{7,39},{8,40},{9,... | collective-permute-start | bytes 1572872 | tf_op jit(solution)/shard_map/ppermute | solution.py:34
  63.4 2.5 %collective-permute-start.17 = (bf16[256,1024]{1,0:T(8,128)(2,1)S(1)}, bf16[256,1024]{1,0:T(8,128)(2,1)S(1)}, u32[]{:S(2)}, u32[]{:S(2)}) collective-permute-start(bf16[256,1024]{1,0:T(8,128)(2,1)S(1)} %get-tuple-element.81), channel_id=1, source_target_pairs={{0,8},{1,9},{2,10},{3,11},{4,12},{5,13},{6,14},{7,15},{8,0},{9,1},... | collective-permute-start | bytes 1572872 | tf_op jit(solution)/shard_map/ppermute | solution.py:34
  65.9 7.1 %shard_map.58 = (f32[1024,256]{1,0:T(8,128)S(1)}, f32[1024,128]{1,0:T(8,128)S(1)}, f32[1024,128]{1,0:T(8,128)S(1)}) custom-call(s32[1]{0:T(128)} %bitcast.z_ref, bf16[528,256]{1,0:T(8,128)(2,1)S(1)} %copy-done, bf16[528,256]{1,0:T(8,128)(2,1)S(1)} %collective-permute-done.refs_1_, bf16[528,256]{1,0:T(8,128)(2,1)S(1)} %collective-permute-done.1.refs_2_, ...), custom_call_target="tpu_custom_call" | custom-call | bytes 1024 | tf_op jit(solution)/shard_map/pallas_call | solution.py:249
  76.6 3.3 %collective-permute-start.14 = (bf16[256,256]{1,0:T(8,128)(2,1)S(1)}, bf16[256,256]{1,0:T(8,128)(2,1)S(1)}, u32[]{:S(2)}, u32[]{:S(2)}) collective-permute-start(bf16[256,256]{1,0:T(8,128)(2,1)S(1)} %get-tuple-element.64.c0), channel_id=1, source_target_pairs={{0,64},{1,65},{2,66},{3,67},{4,68},{5,69},{6,70},{7,71},{8,72},{9,... | collective-permute-start | bytes 393224 | tf_op jit(solution)/shard_map/ppermute | solution.py:34
  81.4 1.9 %collective-permute-start.18 = (bf16[512,1024]{1,0:T(8,128)(2,1)S(1)}, bf16[512,1024]{1,0:T(8,128)(2,1)}, u32[]{:S(2)}, u32[]{:S(2)}) collective-permute-start(bf16[512,1024]{1,0:T(8,128)(2,1)S(1)} %collective-permute-done.5.refs_0_), channel_id=1, source_target_pairs={{0,4},{1,5},{2,6},{3,7},{4,0},{5,1},{6,2},{7,3},{8,12},{9,13},{10,... | collective-permute-start | bytes 3145736 | tf_op jit(solution)/shard_map/ppermute | solution.py:34
  84.5 2.0 %collective-permute-done.15.c3 = bf16[256,256]{1,0:T(8,128)(2,1)S(1)} collective-permute-done((bf16[256,256]{1,0:T(8,128)(2,1)S(1)}, bf16[256,256]{1,0:T(8,128)(2,1)S(1)}, u32[]{:S(2)}, u32[]{:S(2)}) %collective-permute-start.15) | collective-permute-done | bytes 131104 | tf_op jit(solution)/shard_map/ppermute | solution.py:34
  86.6 1.9 %collective-permute-start.19 = (bf16[512,1024]{1,0:T(8,128)(2,1)S(1)}, bf16[512,1024]{1,0:T(8,128)(2,1)}, u32[]{:S(2)}, u32[]{:S(2)}) collective-permute-start(bf16[512,1024]{1,0:T(8,128)(2,1)S(1)} %constant_dynamic-update-slice_fusion.refs_1_), channel_id=1, source_target_pairs={{0,4},{1,5},{2,6},{3,7},{4,0},{5,1},{6,2},{7,3},{8,12},{9,13},{10,... | collective-permute-start | bytes 3145736 | tf_op jit(solution)/shard_map/ppermute | solution.py:34
  88.9 3.2 %collective-permute-start.24 = (bf16[256,256]{1,0:T(8,128)(2,1)S(1)}, bf16[256,256]{1,0:T(8,128)(2,1)S(1)}, u32[]{:S(2)}, u32[]{:S(2)}) collective-permute-start(bf16[256,256]{1,0:T(8,128)(2,1)S(1)} %get-tuple-element.63.c0), channel_id=1, source_target_pairs={{0,64},{1,65},{2,66},{3,67},{4,68},{5,69},{6,70},{7,71},{8,72},{9,... | collective-permute-start | bytes 393224 | tf_op jit(solution)/shard_map/ppermute | solution.py:34
  92.1 1.8 %collective-permute-start.25 = (bf16[256,256]{1,0:T(8,128)(2,1)S(1)}, bf16[256,256]{1,0:T(8,128)(2,1)S(1)}, u32[]{:S(2)}, u32[]{:S(2)}) collective-permute-start(bf16[256,256]{1,0:T(8,128)(2,1)S(1)} %get-tuple-element.75), channel_id=1, source_target_pairs={{0,96},{1,97},{2,98},{3,99},{4,100},{5,101},{6,102},{7,103},{8,104... | collective-permute-start | bytes 393224 | tf_op jit(solution)/shard_map/ppermute | solution.py:34
  94.8 1.9 %collective-permute-done.24.c2 = bf16[256,256]{1,0:T(8,128)(2,1)S(1)} collective-permute-done((bf16[256,256]{1,0:T(8,128)(2,1)S(1)}, bf16[256,256]{1,0:T(8,128)(2,1)S(1)}, u32[]{:S(2)}, u32[]{:S(2)}) %collective-permute-start.24) | collective-permute-done | bytes 131104 | tf_op jit(solution)/shard_map/ppermute | solution.py:34
  96.7 2.2 %collective-permute-done.25.c3 = bf16[256,256]{1,0:T(8,128)(2,1)S(1)} collective-permute-done((bf16[256,256]{1,0:T(8,128)(2,1)S(1)}, bf16[256,256]{1,0:T(8,128)(2,1)S(1)}, u32[]{:S(2)}, u32[]{:S(2)}) %collective-permute-start.25) | collective-permute-done | bytes 131104 | tf_op jit(solution)/shard_map/ppermute | solution.py:34
  99.6 4.6 %shard_map.64 = (bf16[256,512]{1,0:T(8,128)(2,1)}, bf16[256,512]{1,0:T(8,128)(2,1)}, bf16[256,512]{1,0:T(8,128)(2,1)}) custom-call(s32[4]{0:T(128)} %pad_add_fusion.place_ref, bf16[256,256]{1,0:T(8,128)(2,1)} %copy-done.2, bf16[256,256]{1,0:T(8,128)(2,1)} %copy-done.9, bf16[256,256]{1,0:T(8,128)(2,1)} %copy-done.10, bf16[256,256]{1,0:T(8,128)(2,1)} %copy-done.11, ...), custom_call_target="tpu_custom_call" | custom-call | bytes 1024 | tf_op jit(solution)/shard_map/pallas_call | solution.py:303
  104.7 1.5 %collective-permute-start.27 = (bf16[256,512]{1,0:T(8,128)(2,1)}, bf16[256,512]{1,0:T(8,128)(2,1)S(1)}, u32[]{:S(2)}, u32[]{:S(2)}) collective-permute-start(bf16[256,512]{1,0:T(8,128)(2,1)} %get-tuple-element.77), channel_id=1, source_target_pairs={{0,3},{1,0},{2,1},{3,2},{4,7},{5,4},{6,5},{7,6},{8,11},{9,8},{10,9... | collective-permute-start | bytes 786440 | tf_op jit(solution)/shard_map/ppermute | solution.py:34
  107.7 4.5 %shard_map.62 = (bf16[256,512]{1,0:T(8,128)(2,1)}, bf16[256,512]{1,0:T(8,128)(2,1)}, bf16[256,512]{1,0:T(8,128)(2,1)}) custom-call(s32[4]{0:T(128)} %pad_add_fusion.place_ref, bf16[256,256]{1,0:T(8,128)(2,1)} %copy-done.1, bf16[256,256]{1,0:T(8,128)(2,1)} %copy-done.6, bf16[256,256]{1,0:T(8,128)(2,1)} %copy-done.7, bf16[256,256]{1,0:T(8,128)(2,1)} %copy-done.8, ...), custom_call_target="tpu_custom_call" | custom-call | bytes 1024 | tf_op jit(solution)/shard_map/pallas_call | solution.py:303
  112.2 2.2 %collective-permute-start.20 = (bf16[256,512]{1,0:T(8,128)(2,1)}, bf16[256,512]{1,0:T(8,128)(2,1)S(1)}, u32[]{:S(2)}, u32[]{:S(2)}) collective-permute-start(bf16[256,512]{1,0:T(8,128)(2,1)} %get-tuple-element.72), channel_id=1, source_target_pairs={{0,1},{1,2},{2,3},{3,0},{4,5},{5,6},{6,7},{7,4},{8,9},{9,10},{10,1... | collective-permute-start | bytes 786440 | tf_op jit(solution)/shard_map/ppermute | solution.py:34
  114.4 2.0 %collective-permute-start.22 = (bf16[256,512]{1,0:T(8,128)(2,1)}, bf16[256,512]{1,0:T(8,128)(2,1)S(1)}, u32[]{:S(2)}, u32[]{:S(2)}) collective-permute-start(bf16[256,512]{1,0:T(8,128)(2,1)} %get-tuple-element.74), channel_id=1, source_target_pairs={{0,2},{1,3},{2,0},{3,1},{4,6},{5,7},{6,4},{7,5},{8,10},{9,11},{10,... | collective-permute-start | bytes 786440 | tf_op jit(solution)/shard_map/ppermute | solution.py:34
  116.4 3.7 %shard_map.63 = f32[256,512]{1,0:T(8,128)} custom-call(s32[4]{0:T(128)} %pad_add_fusion.place_ref, bf16[256,256]{1,0:T(8,128)(2,1)} %copy-done.2, bf16[256,256]{1,0:T(8,128)(2,1)} %copy-done.9, bf16[256,256]{1,0:T(8,128)(2,1)} %copy-done.10, bf16[256,256]{1,0:T(8,128)(2,1)} %copy-done.11, bf16[512,1024]{1,0:T(8,128)(2,1)} %copy-done.3, ...), custom_call_target="tpu_custom_call" | custom-call | bytes 1024 | tf_op jit(solution)/shard_map/pallas_call | solution.py:303
  120.1 3.7 %shard_map.61 = f32[256,512]{1,0:T(8,128)} custom-call(s32[4]{0:T(128)} %pad_add_fusion.place_ref, bf16[256,256]{1,0:T(8,128)(2,1)} %copy-done.1, bf16[256,256]{1,0:T(8,128)(2,1)} %copy-done.6, bf16[256,256]{1,0:T(8,128)(2,1)} %copy-done.7, bf16[256,256]{1,0:T(8,128)(2,1)} %copy-done.8, bf16[512,1024]{1,0:T(8,128)(2,1)} %copy-done.3, ...), custom_call_target="tpu_custom_call" | custom-call | bytes 1024 | tf_op jit(solution)/shard_map/pallas_call | solution.py:303
  124.9 6.0 %collective-permute-done.21 = bf16[256,512]{1,0:T(8,128)(2,1)S(1)} collective-permute-done((bf16[256,512]{1,0:T(8,128)(2,1)}, bf16[256,512]{1,0:T(8,128)(2,1)S(1)}, u32[]{:S(2)}, u32[]{:S(2)}) %collective-permute-start.21) | collective-permute-done | bytes 262176 | tf_op jit(solution)/shard_map/ppermute | solution.py:34
  (71 shorter events, 17.4 us)
Async XLA Ops:
  15.8 15.2 %collective-permute-start = (bf16[528,256]{1,0:T(8,128)(2,1)}, bf16[528,256]{1,0:T(8,128)(2,1)S(1)}, u32[]{:S(2)}, u32[]{:S(2)}) collective-permute-start(bf16[528,256]{1,0:T(8,128)(2,1)} %get-tuple-element.43), channel_id=1, source_target_pairs={{0,32},{1,33},{2,34},{3,35},{4,36},{5,37},{6,38},{7,39},{8,40},{9,... | collective-permute-start | bytes 811016 | tf_op jit(solution)/shard_map/ppermute | solution.py:34
  19.1 11.9 %collective-permute-start.1 = (bf16[528,256]{1,0:T(8,128)(2,1)}, bf16[528,256]{1,0:T(8,128)(2,1)S(1)}, u32[]{:S(2)}, u32[]{:S(2)}) collective-permute-start(bf16[528,256]{1,0:T(8,128)(2,1)} %get-tuple-element.44), channel_id=1, source_target_pairs={{0,64},{1,65},{2,66},{3,67},{4,68},{5,69},{6,70},{7,71},{8,72},{9,... | collective-permute-start | bytes 811016 | tf_op jit(solution)/shard_map/ppermute | solution.py:34
  20.3 14.5 %collective-permute-start.2 = (bf16[528,256]{1,0:T(8,128)(2,1)}, bf16[528,256]{1,0:T(8,128)(2,1)S(1)}, u32[]{:S(2)}, u32[]{:S(2)}) collective-permute-start(bf16[528,256]{1,0:T(8,128)(2,1)} %get-tuple-element.45), channel_id=1, source_target_pairs={{0,96},{1,97},{2,98},{3,99},{4,100},{5,101},{6,102},{7,103},{8,104... | collective-permute-start | bytes 811016 | tf_op jit(solution)/shard_map/ppermute | solution.py:34
  25.7 31.0 %collective-permute-start.5 = (bf16[512,1024]{1,0:T(8,128)(2,1)}, bf16[512,1024]{1,0:T(8,128)(2,1)S(1)}, u32[]{:S(2)}, u32[]{:S(2)}) collective-permute-start(bf16[512,1024]{1,0:T(8,128)(2,1)} %shard_map.56), channel_id=1, source_target_pairs={{64,32},{65,33},{66,34},{67,35},{68,36},{69,37},{70,38},{71,39},{7... | collective-permute-start | bytes 3145736 | tf_op jit(solution)/shard_map/ppermute | solution.py:34
  34.9 14.6 %collective-permute-start.3 = (bf16[2,528,256]{2,1,0:T(8,128)(2,1)S(1)}, bf16[2,528,256]{2,1,0:T(8,128)(2,1)S(1)}, u32[]{:S(2)}, u32[]{:S(2)}) collective-permute-start(bf16[2,528,256]{2,1,0:T(8,128)(2,1)S(1)} %pad_maximum_fusion.refs_4_), channel_id=1, source_target_pairs={{0,8},{1,9},{2,10},{3,11},{4,12},{5,13},{6,14},{7,15},{8,16},{9,17... | collective-permute-start | bytes 1622024 | tf_op jit(solution)/shard_map/ppermute | solution.py:34
  36.5 13.0 %collective-permute-start.4 = (bf16[2,528,256]{2,1,0:T(8,128)(2,1)S(1)}, bf16[2,528,256]{2,1,0:T(8,128)(2,1)S(1)}, u32[]{:S(2)}, u32[]{:S(2)}) collective-permute-start(bf16[2,528,256]{2,1,0:T(8,128)(2,1)S(1)} %pad_maximum_fusion.refs_4_), channel_id=1, source_target_pairs={{0,24},{1,25},{2,26},{3,27},{4,28},{5,29},{6,30},{7,31},{8,0},{9,1... | collective-permute-start | bytes 1622024 | tf_op jit(solution)/shard_map/ppermute | solution.py:34
  38.2 22.5 %collective-permute-start.8 = (bf16[2,528,256]{2,1,0:T(8,128)(2,1)S(1)}, bf16[2,528,256]{2,1,0:T(8,128)(2,1)S(1)}, u32[]{:S(2)}, u32[]{:S(2)}) collective-permute-start(bf16[2,528,256]{2,1,0:T(8,128)(2,1)S(1)} %pad_maximum_fusion.refs_4_), channel_id=1, source_target_pairs={{0,4},{1,5},{2,6},{3,7},{4,0},{5,1},{6,2},{7,3},{8,12},{9,13},{10,... | collective-permute-start | bytes 1622024 | tf_op jit(solution)/shard_map/ppermute | solution.py:34
  56.7 24.7 %copy-start.3 = (bf16[512,1024]{1,0:T(8,128)(2,1)}, bf16[512,1024]{1,0:T(8,128)(2,1)S(1)}, u32[]{:S(2)}) copy-start(bf16[512,1024]{1,0:T(8,128)(2,1)S(1)} %collective-permute-done.5.refs_0_) | copy-start | bytes 3145732
  56.7 6.7 %collective-permute-start.10 = (bf16[2,528,256]{2,1,0:T(8,128)(2,1)S(1)}, bf16[2,528,256]{2,1,0:T(8,128)(2,1)S(1)}, u32[]{:S(2)}, u32[]{:S(2)}) collective-permute-start(bf16[2,528,256]{2,1,0:T(8,128)(2,1)S(1)} %collective-permute-done.4.refs_6_), channel_id=1, source_target_pairs={{0,4},{1,5},{2,6},{3,7},{4,0},{5,1},{6,2},{7,3},{8,12},{9,13},{10,... | collective-permute-start | bytes 1622024 | tf_op jit(solution)/shard_map/ppermute | solution.py:34
  56.7 9.2 %collective-permute-start.9 = (bf16[2,528,256]{2,1,0:T(8,128)(2,1)S(1)}, bf16[2,528,256]{2,1,0:T(8,128)(2,1)S(1)}, u32[]{:S(2)}, u32[]{:S(2)}) collective-permute-start(bf16[2,528,256]{2,1,0:T(8,128)(2,1)S(1)} %collective-permute-done.3.refs_5_), channel_id=1, source_target_pairs={{0,4},{1,5},{2,6},{3,7},{4,0},{5,1},{6,2},{7,3},{8,12},{9,13},{10,... | collective-permute-start | bytes 1622024 | tf_op jit(solution)/shard_map/ppermute | solution.py:34
  57.2 15.8 %collective-permute-start.6 = (bf16[528,256]{1,0:T(8,128)(2,1)S(1)}, bf16[528,256]{1,0:T(8,128)(2,1)S(1)}, u32[]{:S(2)}, u32[]{:S(2)}) collective-permute-start(bf16[528,256]{1,0:T(8,128)(2,1)S(1)} %slice_bitcast_fusion.1), channel_id=1, source_target_pairs={{0,8},{1,9},{2,10},{3,11},{4,12},{5,13},{6,14},{7,15},{8,16},{9,17... | collective-permute-start | bytes 811016 | tf_op jit(solution)/shard_map/ppermute | solution.py:34
  58.9 14.1 %collective-permute-start.7 = (bf16[528,256]{1,0:T(8,128)(2,1)S(1)}, bf16[528,256]{1,0:T(8,128)(2,1)S(1)}, u32[]{:S(2)}, u32[]{:S(2)}) collective-permute-start(bf16[528,256]{1,0:T(8,128)(2,1)S(1)} %slice_bitcast_fusion), channel_id=1, source_target_pairs={{0,24},{1,25},{2,26},{3,27},{4,28},{5,29},{6,30},{7,31},{8,0},{9,1... | collective-permute-start | bytes 811016 | tf_op jit(solution)/shard_map/ppermute | solution.py:34
  60.7 20.7 %collective-permute-start.16 = (bf16[256,1024]{1,0:T(8,128)(2,1)S(1)}, bf16[256,1024]{1,0:T(8,128)(2,1)S(1)}, u32[]{:S(2)}, u32[]{:S(2)}) collective-permute-start(bf16[256,1024]{1,0:T(8,128)(2,1)S(1)} %get-tuple-element.82), channel_id=1, source_target_pairs={{0,32},{1,33},{2,34},{3,35},{4,36},{5,37},{6,38},{7,39},{8,40},{9,... | collective-permute-start | bytes 1572872 | tf_op jit(solution)/shard_map/ppermute | solution.py:34
  63.4 19.9 %collective-permute-start.17 = (bf16[256,1024]{1,0:T(8,128)(2,1)S(1)}, bf16[256,1024]{1,0:T(8,128)(2,1)S(1)}, u32[]{:S(2)}, u32[]{:S(2)}) collective-permute-start(bf16[256,1024]{1,0:T(8,128)(2,1)S(1)} %get-tuple-element.81), channel_id=1, source_target_pairs={{0,8},{1,9},{2,10},{3,11},{4,12},{5,13},{6,14},{7,15},{8,0},{9,1},... | collective-permute-start | bytes 1572872 | tf_op jit(solution)/shard_map/ppermute | solution.py:34
  73.0 1.6 %collective-permute-start.11 = (bf16[1,528,256]{2,1,0:T(8,128)(2,1)S(1)}, bf16[1,528,256]{2,1,0:T(8,128)(2,1)S(1)}, u32[]{:S(2)}, u32[]{:S(2)}) collective-permute-start(bf16[1,528,256]{2,1,0:T(8,128)(2,1)S(1)} %bitcast.15), channel_id=1, source_target_pairs={{0,4},{1,5},{2,6},{3,7},{4,0},{5,1},{6,2},{7,3},{8,12},{9,13},{10,... | collective-permute-start | bytes 811016 | tf_op jit(solution)/shard_map/ppermute | solution.py:34
  73.1 1.9 %collective-permute-start.12 = (bf16[1,528,256]{2,1,0:T(8,128)(2,1)S(1)}, bf16[1,528,256]{2,1,0:T(8,128)(2,1)S(1)}, u32[]{:S(2)}, u32[]{:S(2)}) collective-permute-start(bf16[1,528,256]{2,1,0:T(8,128)(2,1)S(1)} %bitcast.18), channel_id=1, source_target_pairs={{0,4},{1,5},{2,6},{3,7},{4,0},{5,1},{6,2},{7,3},{8,12},{9,13},{10,... | collective-permute-start | bytes 811016 | tf_op jit(solution)/shard_map/ppermute | solution.py:34
  76.5 27.6 %copy-start.1 = (bf16[256,256]{1,0:T(8,128)(2,1)}, bf16[256,256]{1,0:T(8,128)(2,1)S(1)}, u32[]{:S(2)}) copy-start(bf16[256,256]{1,0:T(8,128)(2,1)S(1)} %get-tuple-element.64.c0) | copy-start | bytes 393220
  76.5 6.8 %collective-permute-start.13 = (bf16[256,256]{1,0:T(8,128)(2,1)S(1)}, bf16[256,256]{1,0:T(8,128)(2,1)S(1)}, u32[]{:S(2)}, u32[]{:S(2)}) collective-permute-start(bf16[256,256]{1,0:T(8,128)(2,1)S(1)} %get-tuple-element.60), channel_id=1, source_target_pairs={{0,32},{1,33},{2,34},{3,35},{4,36},{5,37},{6,38},{7,39},{8,40},{9,... | collective-permute-start | bytes 393224 | tf_op jit(solution)/shard_map/ppermute | solution.py:34
  76.6 7.9 %collective-permute-start.14 = (bf16[256,256]{1,0:T(8,128)(2,1)S(1)}, bf16[256,256]{1,0:T(8,128)(2,1)S(1)}, u32[]{:S(2)}, u32[]{:S(2)}) collective-permute-start(bf16[256,256]{1,0:T(8,128)(2,1)S(1)} %get-tuple-element.64.c0), channel_id=1, source_target_pairs={{0,64},{1,65},{2,66},{3,67},{4,68},{5,69},{6,70},{7,71},{8,72},{9,... | collective-permute-start | bytes 393224 | tf_op jit(solution)/shard_map/ppermute | solution.py:34
  79.9 6.6 %collective-permute-start.15 = (bf16[256,256]{1,0:T(8,128)(2,1)S(1)}, bf16[256,256]{1,0:T(8,128)(2,1)S(1)}, u32[]{:S(2)}, u32[]{:S(2)}) collective-permute-start(bf16[256,256]{1,0:T(8,128)(2,1)S(1)} %get-tuple-element.60), channel_id=1, source_target_pairs={{0,96},{1,97},{2,98},{3,99},{4,100},{5,101},{6,102},{7,103},{8,104... | collective-permute-start | bytes 393224 | tf_op jit(solution)/shard_map/ppermute | solution.py:34
  81.4 17.5 %collective-permute-start.18 = (bf16[512,1024]{1,0:T(8,128)(2,1)S(1)}, bf16[512,1024]{1,0:T(8,128)(2,1)}, u32[]{:S(2)}, u32[]{:S(2)}) collective-permute-start(bf16[512,1024]{1,0:T(8,128)(2,1)S(1)} %collective-permute-done.5.refs_0_), channel_id=1, source_target_pairs={{0,4},{1,5},{2,6},{3,7},{4,0},{5,1},{6,2},{7,3},{8,12},{9,13},{10,... | collective-permute-start | bytes 3145736 | tf_op jit(solution)/shard_map/ppermute | solution.py:34
  83.3 20.8 %copy-start.6 = (bf16[256,256]{1,0:T(8,128)(2,1)}, bf16[256,256]{1,0:T(8,128)(2,1)S(1)}, u32[]{:S(2)}) copy-start(bf16[256,256]{1,0:T(8,128)(2,1)S(1)} %collective-permute-done.13.c1) | copy-start | bytes 393220
  86.6 12.3 %collective-permute-start.19 = (bf16[512,1024]{1,0:T(8,128)(2,1)S(1)}, bf16[512,1024]{1,0:T(8,128)(2,1)}, u32[]{:S(2)}, u32[]{:S(2)}) collective-permute-start(bf16[512,1024]{1,0:T(8,128)(2,1)S(1)} %constant_dynamic-update-slice_fusion.refs_1_), channel_id=1, source_target_pairs={{0,4},{1,5},{2,6},{3,7},{4,0},{5,1},{6,2},{7,3},{8,12},{9,13},{10,... | collective-permute-start | bytes 3145736 | tf_op jit(solution)/shard_map/ppermute | solution.py:34
  88.5 6.2 %collective-permute-start.23 = (bf16[256,256]{1,0:T(8,128)(2,1)S(1)}, bf16[256,256]{1,0:T(8,128)(2,1)S(1)}, u32[]{:S(2)}, u32[]{:S(2)}) collective-permute-start(bf16[256,256]{1,0:T(8,128)(2,1)S(1)} %get-tuple-element.75), channel_id=1, source_target_pairs={{0,32},{1,33},{2,34},{3,35},{4,36},{5,37},{6,38},{7,39},{8,40},{9,... | collective-permute-start | bytes 393224 | tf_op jit(solution)/shard_map/ppermute | solution.py:34
  88.9 7.8 %collective-permute-start.24 = (bf16[256,256]{1,0:T(8,128)(2,1)S(1)}, bf16[256,256]{1,0:T(8,128)(2,1)S(1)}, u32[]{:S(2)}, u32[]{:S(2)}) collective-permute-start(bf16[256,256]{1,0:T(8,128)(2,1)S(1)} %get-tuple-element.63.c0), channel_id=1, source_target_pairs={{0,64},{1,65},{2,66},{3,67},{4,68},{5,69},{6,70},{7,71},{8,72},{9,... | collective-permute-start | bytes 393224 | tf_op jit(solution)/shard_map/ppermute | solution.py:34
  92.1 6.8 %collective-permute-start.25 = (bf16[256,256]{1,0:T(8,128)(2,1)S(1)}, bf16[256,256]{1,0:T(8,128)(2,1)S(1)}, u32[]{:S(2)}, u32[]{:S(2)}) collective-permute-start(bf16[256,256]{1,0:T(8,128)(2,1)S(1)} %get-tuple-element.75), channel_id=1, source_target_pairs={{0,96},{1,97},{2,98},{3,99},{4,100},{5,101},{6,102},{7,103},{8,104... | collective-permute-start | bytes 393224 | tf_op jit(solution)/shard_map/ppermute | solution.py:34
  104.2 10.2 %collective-permute-start.26 = (bf16[256,512]{1,0:T(8,128)(2,1)}, bf16[256,512]{1,0:T(8,128)(2,1)S(1)}, u32[]{:S(2)}, u32[]{:S(2)}) collective-permute-start(bf16[256,512]{1,0:T(8,128)(2,1)} %get-tuple-element.76), channel_id=1, source_target_pairs={{0,1},{1,2},{2,3},{3,0},{4,5},{5,6},{6,7},{7,4},{8,9},{9,10},{10,1... | collective-permute-start | bytes 786440 | tf_op jit(solution)/shard_map/ppermute | solution.py:34
  104.7 19.2 %collective-permute-start.27 = (bf16[256,512]{1,0:T(8,128)(2,1)}, bf16[256,512]{1,0:T(8,128)(2,1)S(1)}, u32[]{:S(2)}, u32[]{:S(2)}) collective-permute-start(bf16[256,512]{1,0:T(8,128)(2,1)} %get-tuple-element.77), channel_id=1, source_target_pairs={{0,3},{1,0},{2,1},{3,2},{4,7},{5,4},{6,5},{7,6},{8,11},{9,8},{10,9... | collective-permute-start | bytes 786440 | tf_op jit(solution)/shard_map/ppermute | solution.py:34
  106.3 17.6 %collective-permute-start.28 = (bf16[256,512]{1,0:T(8,128)(2,1)}, bf16[256,512]{1,0:T(8,128)(2,1)S(1)}, u32[]{:S(2)}, u32[]{:S(2)}) collective-permute-start(bf16[256,512]{1,0:T(8,128)(2,1)} %get-tuple-element.78), channel_id=1, source_target_pairs={{0,2},{1,3},{2,0},{3,1},{4,6},{5,7},{6,4},{7,5},{8,10},{9,11},{10,... | collective-permute-start | bytes 786440 | tf_op jit(solution)/shard_map/ppermute | solution.py:34
  112.2 12.7 %collective-permute-start.20 = (bf16[256,512]{1,0:T(8,128)(2,1)}, bf16[256,512]{1,0:T(8,128)(2,1)S(1)}, u32[]{:S(2)}, u32[]{:S(2)}) collective-permute-start(bf16[256,512]{1,0:T(8,128)(2,1)} %get-tuple-element.72), channel_id=1, source_target_pairs={{0,1},{1,2},{2,3},{3,0},{4,5},{5,6},{6,7},{7,4},{8,9},{9,10},{10,1... | collective-permute-start | bytes 786440 | tf_op jit(solution)/shard_map/ppermute | solution.py:34
  114.4 16.5 %collective-permute-start.21 = (bf16[256,512]{1,0:T(8,128)(2,1)}, bf16[256,512]{1,0:T(8,128)(2,1)S(1)}, u32[]{:S(2)}, u32[]{:S(2)}) collective-permute-start(bf16[256,512]{1,0:T(8,128)(2,1)} %get-tuple-element.73), channel_id=1, source_target_pairs={{0,3},{1,0},{2,1},{3,2},{4,7},{5,4},{6,5},{7,6},{8,11},{9,8},{10,9... | collective-permute-start | bytes 786440 | tf_op jit(solution)/shard_map/ppermute | solution.py:34
  114.4 16.5 %collective-permute-start.22 = (bf16[256,512]{1,0:T(8,128)(2,1)}, bf16[256,512]{1,0:T(8,128)(2,1)S(1)}, u32[]{:S(2)}, u32[]{:S(2)}) collective-permute-start(bf16[256,512]{1,0:T(8,128)(2,1)} %get-tuple-element.74), channel_id=1, source_target_pairs={{0,2},{1,3},{2,0},{3,1},{4,6},{5,7},{6,4},{7,5},{8,10},{9,11},{10,... | collective-permute-start | bytes 786440 | tf_op jit(solution)/shard_map/ppermute | solution.py:34
  (9 other events, 97.0 us)

commit v3 on v2

--- a/solution.py
+++ b/solution.py
@@ -56,20 +56,28 @@
     return (widened * inverse * gain_row).astype(jnp.bfloat16)
 
 
-def section_kernel(info_ref, memory, targets, gain_ref, w_ref, *refs):
+def section_kernel(z_ref, pad_ref, memory, targets, gain_ref, w_ref, *refs):
     *out_refs, normed, x_rows, total, arrival = refs
     k, steps = pl.program_id(0), pl.num_programs(0)
     depth, width = w_ref.shape[1], w_ref.shape[3]
     rows = total.shape[0]
     half = rows // 2
     dim = out_refs[0].shape[1]
-    encoder = info_ref[0] < 2
+    encoder = z_ref[0] < 2
 
     def normalise(source, count):
-        copy = pltpu.make_async_copy(source, x_rows.at[pl.ds(0, count)], arrival)
-        copy.start()
-        copy.wait()
+        block = 128
+        copies = [
+            pltpu.make_async_copy(
+                source.at[pl.ds(top, block)], x_rows.at[pl.ds(top, block)], arrival.at[top // block]
+            )
+            for top in range(0, count, block)
+        ]
+        for copy in copies:
+            copy.start()
         for top in range(0, count, 64):
+            if top % block == 0:
+                copies[top // block].wait()
             part = norm_rows(x_rows[pl.ds(top, 64), :], gain_ref[...])
             for j in range(normed.shape[0]):
                 normed[j, pl.ds(top, 64), :] = part[:, j * depth : (j + 1) * depth]
@@ -107,14 +115,14 @@
     @pl.when(k == steps - 1)
     def _():
         position = lax.broadcasted_iota(jnp.int32, (MARK_ROWS, dim), 1)
-        marks = jnp.where(position < half - info_ref[1], 0.0, DEAD).astype(jnp.bfloat16)
+        marks = jnp.where(position < half - pad_ref[0], 0.0, DEAD).astype(jnp.bfloat16)
         for d, ref in enumerate(out_refs):
-            head = (info_ref[0] + d) % 4
+            head = (z_ref[0] + d) % 4
             ref[:rows, :] = total[:, pl.ds(pl.multiple_of(head * dim, dim), dim)].astype(jnp.bfloat16)
             ref[rows:, :] = marks
 
 
-def section(info, memory, targets, gains, weights, dim):
+def section(z, pad_counts, memory, targets, gains, weights, dim):
     rows, model = targets.shape
     width = weights.shape[3]
     depth = 1024
@@ -124,26 +132,26 @@
     return pl.pallas_call(
         section_kernel,
         grid_spec=pltpu.PrefetchScalarGridSpec(
-            num_scalar_prefetch=1,
+            num_scalar_prefetch=2,
             grid=(steps,),
             in_specs=[
                 anywhere,
                 anywhere,
-                pl.BlockSpec((1, model), lambda k, info: (0, 0)),
-                pl.BlockSpec((1, depth, 2, width), lambda k, info: (0, k, 0, 0)),
+                pl.BlockSpec((1, model), lambda k, z, pad: (0, 0)),
+                pl.BlockSpec((1, depth, 2, width), lambda k, z, pad: (0, k, 0, 0)),
             ],
-            out_specs=[pl.BlockSpec(slab, lambda k, info: (0, 0))] * 4,
+            out_specs=[pl.BlockSpec(slab, lambda k, z, pad: (0, 0))] * 4,
             scratch_shapes=[
                 pltpu.VMEM((steps, rows, depth), jnp.bfloat16),
                 pltpu.VMEM((rows, model), jnp.bfloat16),
                 pltpu.VMEM((rows, width), jnp.float32),
-                pltpu.SemaphoreType.DMA,
+                pltpu.SemaphoreType.DMA((rows // 128,)),
             ],
         ),
         out_shape=[jax.ShapeDtypeStruct(slab, jnp.bfloat16)] * 4,
         cost_estimate=LIGHT,
         compiler_params=pltpu.CompilerParams(vmem_limit_bytes=VMEM),
-    )(info, memory, targets, gains, weights)
+    )(z.reshape(1), pad_counts, memory, targets, gains, weights)
 
 
 def second_half_kernel(start_ref, w_ref, *out_refs):
@@ -170,7 +178,7 @@
     )(start.reshape(1), weights)
 
 
-def attend_kernel(first, half, chunk, chunks, z_ref, *refs):
+def attend_kernel(first, half, chunks, z_ref, *refs):
     if first:
         *slabs, acc_ref, peak_ref, total_ref, queries, keys, values, marks = refs
     else:
@@ -227,15 +235,15 @@
                 total = total + scale * total_ref[mine, :1]
                 found = (mixed / total).astype(jnp.bfloat16)
                 if top < half:
-                    out_a[top : top + part, :] = found
+                    out_a[at * half + top : at * half + top + part, :] = found
                 else:
-                    out_b[top - half : top - half + part, :] = found
-
-    for at in range(chunks) if first else (chunk,):
+                    out_b[at * half + top - half : at * half + top - half + part, :] = found
+
+    for at in range(chunks):
         run(at)
 
 
-def attend(z, q_slabs, blocks, chunks, state=None, chunk=0):
+def attend(z, q_slabs, blocks, chunks, state=None):
     rows, dim = q_slabs[0].shape[0] - MARK_ROWS, q_slabs[0].shape[1]
     half = rows // chunks
     first = state is None
@@ -244,10 +252,10 @@
     if first:
         out_shape = [jax.ShapeDtypeStruct((2 * rows, last), jnp.float32) for last in (dim, 128, 128)]
     else:
-        out_shape = [jax.ShapeDtypeStruct((half, dim), jnp.bfloat16)] * 2
+        out_shape = [jax.ShapeDtypeStruct((rows, dim), jnp.bfloat16)] * 2
     operands = [*q_slabs, *blocks, *(() if first else state)]
     return pl.pallas_call(
-        functools.partial(attend_kernel, first, half, chunk, chunks),
+        functools.partial(attend_kernel, first, half, chunks),
         in_specs=[pl.BlockSpec(memory_space=pltpu.SMEM)] + [vmem] * len(operands),
         out_specs=[vmem] * len(out_shape),
         scratch_shapes=[
@@ -262,32 +270,35 @@
     )(z.reshape(1), *operands)
 
 
-def project_kernel(first, place_ref, c0, c1, c2, c3, *refs):
-    sources, rest = refs[:5], refs[5:]
-    *out_refs, held, context, arrived = rest
-    z, x, core, held_set = place_ref[0], place_ref[1], place_ref[2], place_ref[3]
+def project_kernel(first, z_ref, x_ref, core_ref, set_ref, c0, c1, c2, c3, *refs):
+    sources, mine = refs[:8], refs[8]
+    *out_refs, held, context, arrived = refs[9:]
+    z, x, core, held_set = z_ref[0], x_ref[0], core_ref[0], set_ref[0]
     dim, width = c0.shape[1], held.shape[1]
+    part = width // 2
+
+    def fetch(j, action):
+        wanted = (x + first + j) % 4
+        slot, arrival = held.at[j], arrived.at[j]
+
+        @pl.when(z >= 2)
+        def _():
+            top = pl.multiple_of(wanted * width, width)
+            action(pltpu.make_async_copy(mine.at[pl.ds(top, width)], slot, arrival))
+
+        for n in range(4):
+
+            @pl.when((z < 2) & ((wanted + 4 - held_set) % 4 == n))
+            def _(n=n):
+                for source, side in ((sources[n], core), (sources[4 + n], 1 - core)):
+                    top = pl.multiple_of(side * part, part)
+                    action(pltpu.make_async_copy(source, slot.at[pl.ds(top, part)], arrival))
+
+    for j in range(len(out_refs)):
+        fetch(j, lambda copy: copy.start())
     for d, ref in enumerate((c0, c1, c2, c3)):
         head = (z + 4 - d) % 4
         context[:, pl.ds(pl.multiple_of(head * dim, dim), dim)] = ref[...]
-
-    def fetch(j, action):
-        wanted = (x + first + j) % 4
-        kind = jnp.where(wanted // 2 == core, 0, 2) + jnp.where(wanted % 2 == held_set, 0, 1)
-
-        @pl.when(z >= 2)
-        def _():
-            top = pl.multiple_of(wanted * width, width)
-            action(pltpu.make_async_copy(sources[4].at[pl.ds(top, width)], held.at[j], arrived.at[j]))
-
-        for n in range(4):
-
-            @pl.when((z < 2) & (kind == n))
-            def _(n=n):
-                action(pltpu.make_async_copy(sources[n], held.at[j], arrived.at[j]))
-
-    for j in range(len(out_refs)):
-        fetch(j, lambda copy: copy.start())
     for j, ref in enumerate(out_refs):
         fetch(j, lambda copy: copy.wait())
         mixed = lax.dot_general(
@@ -298,13 +309,13 @@
 
 def project(place, contexts, sources, first, count, dtype):
     rows, dim = contexts[0].shape
-    width = sources[4].shape[0] // 4
+    width = sources[-1].shape[0] // 4
     vmem = pl.BlockSpec(memory_space=pltpu.VMEM)
     return pl.pallas_call(
         functools.partial(project_kernel, first),
-        in_specs=[pl.BlockSpec(memory_space=pltpu.SMEM)]
+        in_specs=[pl.BlockSpec(memory_space=pltpu.SMEM)] * 4
         + [vmem] * 4
-        + [pl.BlockSpec(memory_space=pl.ANY)] * 5,
+        + [pl.BlockSpec(memory_space=pl.ANY)] * 9,
         out_specs=[vmem] * count,
         out_shape=[jax.ShapeDtypeStruct((rows, width), dtype)] * count,
         scratch_shapes=[
@@ -314,7 +325,7 @@
         ],
         cost_estimate=LIGHT,
         compiler_params=pltpu.CompilerParams(vmem_limit_bytes=VMEM),
-    )(place, *contexts, *sources)
+    )(*(scalar.reshape(1) for scalar in place), *contexts, *sources)
 
 
 def after(value, *others):
@@ -336,54 +347,47 @@
     flip = lambda x, y, z, c: (x, y, 1 - z, c)
     is_encoder = segment == 0
 
-    info = jnp.stack([z, pad_counts[0]])
-    own, *to = section(info, memory, targets, norm_gains, proj_weights, dim)
+    held_set = (y + 2 * low) % 4
+    wanted_set = (y + 2 * (1 - low)) % 4
+    (share,) = second_half(proj_weights, wanted_set * 2 + core, half // 8, 1, 1)
+    p = moved(share, down, decoder)
+
+    own, *to = section(after(z, share), pad_counts, memory, targets, norm_gains, proj_weights, dim)
+    own, to, p = lax.optimization_barrier((own, to, p))
+    above, below = along_y(p, 3, encoder), along_y(p, 1, encoder)
     r1, r3, r2 = along_z(to[0], 1), along_z(to[2], 3), along_z(to[1], 2)
-
-    held_set = (low + y) % 2
-    (share,) = second_half(after(proj_weights, own), core * 2 + 1 - held_set, half // 4, 1, 1)
-    p = moved(share, down, decoder)
-
     early = jnp.where(is_encoder, own, jnp.where(z == 2, r1, r3))
     late = jnp.where(z == 0, r3, jnp.where(z == 1, r1, r2))
-    pair = jnp.stack([after(early, share), late])
+    pair = jnp.stack([early, late])
+    above_twin = other_core(above, encoder)
+
+    pair, p, above, below, above_twin = lax.optimization_barrier((pair, p, above, below, above_twin))
     y1, y3 = along_y(pair, 1), along_y(pair, 3)
+    across = moved(p, flip, encoder)
+    twin, below_twin = other_core(p, encoder), other_core(below, encoder)
     (mine,) = second_half(after(proj_weights, pair), jnp.int32(2), half // 2, 2, 1)
-    y1, y3, mine, p = lax.optimization_barrier((y1, y3, mine, p))
+
+    y1, y3, twin, below_twin, mine = lax.optimization_barrier((y1, y3, twin, below_twin, mine))
     far0, far1 = along_y(y1[0], 1), along_y(y3[1], 3)
     slabs = [own, r1, r2, r3]
     blocks = [pair, y1, y3]
     state = attend(z, slabs, blocks + [other_core(b) for b in blocks], chunks)
 
-    quarter = half // 8
-    far0, far1, *state = lax.optimization_barrier((far0, far1, *state))
-    sz = moved(p[:quarter], flip, encoder)
-    sy = moved(p[quarter:], lambda x, y, z, c: (x, y ^ 1, z, c), encoder)
+    far0, far1, across, *state = lax.optimization_barrier((far0, far1, across, *state))
+    across_twin = other_core(across, encoder)
     blocks = [far0[None], far1[None]]
     blocks = blocks + [other_core(b) for b in blocks]
-    place = jnp.stack([z, x, core, held_set])
-
-    first_part = attend(z, slabs, blocks, chunks, state, 0)
-    second_part = attend(after(z, first_part[0]), slabs, blocks, chunks, state, 1)
-    moving = []
-    for ca, cb in (first_part, second_part):
-        moving.append([ca, along_z(cb, 1), along_z(ca, 2), along_z(cb, 3)])
-    twin = other_core(after(p, state[0]), encoder)
-    moving[0], sz, sy, _ = lax.optimization_barrier((moving[0], sz, sy, second_part[0]))
-    s = jnp.concatenate([sz, sy])
-    sources = [p, s, twin, other_core(s, encoder), mine]
-    finished = []
+    ca, cb = attend(z, slabs, blocks, chunks, state)
+    contexts = [ca, along_z(cb, 1), along_z(ca, 2), along_z(cb, 3)]
+    sources = [p, above, across, below, twin, above_twin, across_twin, below_twin, mine]
+    place = [z, x, core, held_set]
     out_width = model // 8
     residual = lax.dynamic_slice_in_dim(targets, (segment * 4 + x) * out_width, out_width, 1)
-    for chunk, contexts in enumerate(moving):
-        far = project(place, contexts, sources, 1, 3, jnp.bfloat16)
-        (near,) = project(place, contexts, sources, 0, 1, jnp.float32)
-        part = rows // chunks
-        summed = residual[chunk * part : (chunk + 1) * part].astype(jnp.float32) + near
-        for d in (1, 3, 2):
-            summed = summed + along_x(far[d - 1], d).astype(jnp.float32)
-        finished.append(summed.astype(jnp.bfloat16))
-    return jnp.concatenate(finished)
+    far = project(place, contexts, sources, 1, 3, jnp.bfloat16)
+    (near,) = project([after(z, far[0]), *place[1:]], contexts, sources, 0, 1, jnp.float32)
+    far = {d: along_x(far[d - 1], d) for d in (2, 1, 3)}
+    summed = lax.optimization_barrier(residual.astype(jnp.float32) + near + far[2].astype(jnp.float32))
+    return (summed + far[1].astype(jnp.float32) + far[3].astype(jnp.float32)).astype(jnp.bfloat16)
 
 
 def solution(mesh):

time: 136 us -> 129 us (0.949)
  Pallas kernels: 49.2 us -> 40.4 us
  waiting for transfers between devices: 36.9 us -> 42 us
  starting transfers between devices: 41.5 us -> 38.3 us
    pallas_call x4 -> x2, Pallas kernels: 16.5 us -> 9.64 us  [project(): pl.pallas_call(functools.partial(project_kernel, first), in_specs=[pl.Blo...]
    ppermute x29 -> x26, waiting for transfers between devices: 36.9 us -> 42 us  [moved(): return lax.ppermute(block, AXES, route)]
    ppermute x29 -> x26, starting transfers between devices: 41.5 us -> 38.3 us  [moved(): return lax.ppermute(block, AXES, route)]
    add x0 -> x1, other arithmetic: none -> 1.58 us  [local(): residual.astype(jnp.float32) + near + far[2].astype(jnp.float32)]
    pallas_call x3 -> x2, Pallas kernels: 10 us -> 9.77 us  [attend(): pl.pallas_call(functools.partial(attend_kernel, first, half, chunks), in_...]
  transfers between devices with their start and end apart: 29 -> 26, of which waited for: 13 -> 11; matrix products, arithmetic and copies ran while one was open for 1% -> 2% of each run, Pallas kernels for 23% -> 26%
where the time goes in v3:
time: 129 us; the launch traced here: 127 us
  waiting for transfers between devices  42 us (33%)
  Pallas kernels  40.4 us (31%)
  starting transfers between devices  38.3 us (30%)
  other arithmetic  3.67 us (3%)
  local copies, waits for them, and re-layouts  1.52 us (1%)
    ppermute x26, waiting for transfers between devices, moved(): return lax.ppermute(block, AXES, route)  42 us
    ppermute x26, starting transfers between devices, moved(): return lax.ppermute(block, AXES, route)  38.3 us
    pallas_call x1, Pallas kernels, section(): pl.pallas_call(section_kernel, grid_spec=pltpu.PrefetchScalarGridSpec(num...  13.5 us
    pallas_call x2, Pallas kernels, attend(): pl.pallas_call(functools.partial(attend_kernel, first, half, chunks), in_...  9.77 us
    pallas_call x2, Pallas kernels, project(): pl.pallas_call(functools.partial(project_kernel, first), in_specs=[pl.Blo...  9.64 us
    pallas_call x2, Pallas kernels, second_half(): pl.pallas_call(second_half_kernel, grid_spec=pltpu.PrefetchScalarGridSpec...  7.51 us
  transfers between devices with their start and end apart: 26, of which 11 were waited for; matrix products, arithmetic and copies ran while one was open for 2% of the time, Pallas kernels for 26%

profile of v3, /device:TPU:38, one launch (start us, length us, event | category | flops | bytes accessed | tf_op | source)
XLA Modules:
  0.0 127.0 jit_solution(16155829945500534458)
XLA Ops:
  0.0 2.2 %shard_map.55 = bf16[256,1024]{1,0:T(8,128)(2,1)} custom-call(s32[1]{0:T(128)} %bitcast.4.start_ref, bf16[1,4096,2,1024]{3,2,1,0:T(2,128)(2,1)} %w_ref.4), custom_call_target="tpu_custom_call" | custom-call | bytes 1024 | tf_op jit(solution)/shard_map/pallas_call | solution.py:167
  2.2 1.3 %collective-permute-start = (bf16[256,1024]{1,0:T(8,128)(2,1)}, bf16[256,1024]{1,0:T(8,128)(2,1)S(1)}, u32[]{:S(2)}, u32[]{:S(2)}) collective-permute-start(bf16[256,1024]{1,0:T(8,128)(2,1)} %shard_map.55), channel_id=1, source_target_pairs={{64,32},{65,33},{66,34},{67,35},{68,36},{69,37},{70,38},{71,39},{7... | collective-permute-start | bytes 1572872 | tf_op jit(solution)/shard_map/ppermute | solution.py:34
  4.1 13.5 %shard_map.56 = (bf16[528,256]{1,0:T(8,128)(2,1)}, bf16[528,256]{1,0:T(8,128)(2,1)}, bf16[528,256]{1,0:T(8,128)(2,1)}, bf16[528,256]{1,0:T(8,128)(2,1)}) custom-call(s32[1]{0:T(128)} %bitcast.5.z_ref, s32[1]{0:T(128)S(6)} %copy.6.pad_ref, bf16[256,4096]{1,0:T(8,128)(2,1)} %memory.1, bf16[512,4096]{1,0:T(8,128)(2,1)} %targets.1, f32[1,4096]{1,0:T(1,128)} %gain_ref.1, ...), custom_call_target="tpu_custom_call" | custom-call | bytes 1024 | tf_op jit(solution)/shard_map/pallas_call | solution.py:132
  17.9 4.9 %collective-permute-start.4 = (bf16[256,1024]{1,0:T(8,128)(2,1)S(1)}, bf16[256,1024]{1,0:T(8,128)(2,1)S(1)}, u32[]{:S(2)}, u32[]{:S(2)}) collective-permute-start(bf16[256,1024]{1,0:T(8,128)(2,1)S(1)} %collective-permute-done.refs_0_), channel_id=1, source_target_pairs={{0,24},{1,25},{2,26},{3,27},{4,28},{5,29},{6,30},{7,31},{8,0},{9,1... | collective-permute-start | bytes 1572872 | tf_op jit(solution)/shard_map/ppermute | solution.py:34
  22.9 3.8 %collective-permute-start.2 = (bf16[528,256]{1,0:T(8,128)(2,1)}, bf16[528,256]{1,0:T(8,128)(2,1)S(1)}, u32[]{:S(2)}, u32[]{:S(2)}) collective-permute-start(bf16[528,256]{1,0:T(8,128)(2,1)} %get-tuple-element.48), channel_id=1, source_target_pairs={{0,64},{1,65},{2,66},{3,67},{4,68},{5,69},{6,70},{7,71},{8,72},{9,... | collective-permute-start | bytes 811016 | tf_op jit(solution)/shard_map/ppermute | solution.py:34
  26.8 1.9 %collective-permute-start.5 = (bf16[256,1024]{1,0:T(8,128)(2,1)S(1)}, bf16[256,1024]{1,0:T(8,128)(2,1)S(1)}, u32[]{:S(2)}, u32[]{:S(2)}) collective-permute-start(bf16[256,1024]{1,0:T(8,128)(2,1)S(1)} %collective-permute-done.refs_0_), channel_id=1, source_target_pairs={{0,8},{1,9},{2,10},{3,11},{4,12},{5,13},{6,14},{7,15},{8,16},{9,17... | collective-permute-start | bytes 1572872 | tf_op jit(solution)/shard_map/ppermute | solution.py:34
  28.7 5.0 %collective-permute-done.4.refs_1_ = bf16[256,1024]{1,0:T(8,128)(2,1)S(1)} collective-permute-done((bf16[256,1024]{1,0:T(8,128)(2,1)S(1)}, bf16[256,1024]{1,0:T(8,128)(2,1)S(1)}, u32[]{:S(2)}, u32[]{:S(2)}) %collective-permute-start.4) | collective-permute-done | bytes 524320 | tf_op jit(solution)/shard_map/ppermute | solution.py:34
  33.7 1.9 %collective-permute-start.6 = (bf16[256,1024]{1,0:T(8,128)(2,1)S(1)}, bf16[256,1024]{1,0:T(8,128)(2,1)S(1)}, u32[]{:S(2)}, u32[]{:S(2)}) collective-permute-start(bf16[256,1024]{1,0:T(8,128)(2,1)S(1)} %collective-permute-done.4.refs_1_), channel_id=1, source_target_pairs={{0,4},{1,5},{2,6},{3,7},{4,0},{5,1},{6,2},{7,3},{8,12},{9,13},{10,... | collective-permute-start | bytes 1572872 | tf_op jit(solution)/shard_map/ppermute | solution.py:34
  35.7 2.5 %collective-permute-done.3.refs_3_ = bf16[528,256]{1,0:T(8,128)(2,1)S(1)} collective-permute-done((bf16[528,256]{1,0:T(8,128)(2,1)}, bf16[528,256]{1,0:T(8,128)(2,1)S(1)}, u32[]{:S(2)}, u32[]{:S(2)}) %collective-permute-start.3) | collective-permute-done | bytes 270368 | tf_op jit(solution)/shard_map/ppermute | solution.py:34
  39.3 2.9 %collective-permute-done.5.refs_3_ = bf16[256,1024]{1,0:T(8,128)(2,1)S(1)} collective-permute-done((bf16[256,1024]{1,0:T(8,128)(2,1)S(1)}, bf16[256,1024]{1,0:T(8,128)(2,1)S(1)}, u32[]{:S(2)}, u32[]{:S(2)}) %collective-permute-start.5) | collective-permute-done | bytes 524320 | tf_op jit(solution)/shard_map/ppermute | solution.py:34
  42.2 3.2 %collective-permute-start.8 = (bf16[2,528,256]{2,1,0:T(8,128)(2,1)S(1)}, bf16[2,528,256]{2,1,0:T(8,128)(2,1)S(1)}, u32[]{:S(2)}, u32[]{:S(2)}) collective-permute-start(bf16[2,528,256]{2,1,0:T(8,128)(2,1)S(1)} %pad_maximum_fusion.refs_4_), channel_id=1, source_target_pairs={{0,24},{1,25},{2,26},{3,27},{4,28},{5,29},{6,30},{7,31},{8,0},{9,1... | collective-permute-start | bytes 1622024 | tf_op jit(solution)/shard_map/ppermute | solution.py:34
  45.4 1.9 %collective-permute-start.10 = (bf16[256,1024]{1,0:T(8,128)(2,1)S(1)}, bf16[256,1024]{1,0:T(8,128)(2,1)S(1)}, u32[]{:S(2)}, u32[]{:S(2)}) collective-permute-start(bf16[256,1024]{1,0:T(8,128)(2,1)S(1)} %collective-permute-done.5.refs_3_), channel_id=1, source_target_pairs={{0,4},{1,5},{2,6},{3,7},{4,0},{5,1},{6,2},{7,3},{8,12},{9,13},{10,... | collective-permute-start | bytes 1572872 | tf_op jit(solution)/shard_map/ppermute | solution.py:34
  47.3 2.4 %collective-permute-start.9 = (bf16[256,1024]{1,0:T(8,128)(2,1)S(1)}, bf16[256,1024]{1,0:T(8,128)(2,1)S(1)}, u32[]{:S(2)}, u32[]{:S(2)}) collective-permute-start(bf16[256,1024]{1,0:T(8,128)(2,1)S(1)} %collective-permute-done.refs_0_), channel_id=1, source_target_pairs={{0,4},{1,5},{2,6},{3,7},{4,0},{5,1},{6,2},{7,3},{8,12},{9,13},{10,... | collective-permute-start | bytes 1572872 | tf_op jit(solution)/shard_map/ppermute | solution.py:34
  49.9 5.4 %shard_map.57.refs_8_ = bf16[2048,1024]{1,0:T(8,128)(2,1)} custom-call(s32[1]{0:T(128)} %constant.74.clone.1.start_ref, bf16[1,4096,2,1024]{3,2,1,0:T(2,128)(2,1)} %w_ref.4), custom_call_target="tpu_custom_call" | custom-call | bytes 1024 | tf_op jit(solution)/shard_map/pallas_call | solution.py:167
  55.3 3.1 %collective-permute-start.13 = (bf16[256,1024]{1,0:T(8,128)(2,1)S(1)}, bf16[256,1024]{1,0:T(8,128)(2,1)S(1)}, u32[]{:S(2)}, u32[]{:S(2)}) collective-permute-start(bf16[256,1024]{1,0:T(8,128)(2,1)S(1)} %collective-permute-done.refs_0_), channel_id=1, source_target_pairs={{0,32},{1,33},{2,34},{3,35},{4,36},{5,37},{6,38},{7,39},{8,40},{9,... | collective-permute-start | bytes 1572872 | tf_op jit(solution)/shard_map/ppermute | solution.py:34
  59.8 3.5 %collective-permute-start.12 = (bf16[528,256]{1,0:T(8,128)(2,1)S(1)}, bf16[528,256]{1,0:T(8,128)(2,1)S(1)}, u32[]{:S(2)}, u32[]{:S(2)}) collective-permute-start(bf16[528,256]{1,0:T(8,128)(2,1)S(1)} %slice_bitcast_fusion), channel_id=1, source_target_pairs={{0,24},{1,25},{2,26},{3,27},{4,28},{5,29},{6,30},{7,31},{8,0},{9,1... | collective-permute-start | bytes 811016 | tf_op jit(solution)/shard_map/ppermute | solution.py:34
  63.3 6.9 %shard_map.58 = (f32[1024,256]{1,0:T(8,128)S(1)}, f32[1024,128]{1,0:T(8,128)S(1)}, f32[1024,128]{1,0:T(8,128)S(1)}) custom-call(s32[1]{0:T(128)} %bitcast.z_ref, bf16[528,256]{1,0:T(8,128)(2,1)S(1)} %copy-done, bf16[528,256]{1,0:T(8,128)(2,1)S(1)} %collective-permute-done.1.refs_1_, bf16[528,256]{1,0:T(8,128)(2,1)S(1)} %collective-permute-done.2.refs_2_, ...), custom_call_target="tpu_custom_call" | custom-call | bytes 1024 | tf_op jit(solution)/shard_map/pallas_call | solution.py:257
  70.3 1.2 collective-permute-done.13.refs_2_
  72.1 2.0 %collective-permute-start.22 = (bf16[256,1024]{1,0:T(8,128)(2,1)S(1)}, bf16[256,1024]{1,0:T(8,128)(2,1)S(1)}, u32[]{:S(2)}, u32[]{:S(2)}) collective-permute-start(bf16[256,1024]{1,0:T(8,128)(2,1)S(1)} %collective-permute-done.13.refs_2_), channel_id=1, source_target_pairs={{0,4},{1,5},{2,6},{3,7},{4,0},{5,1},{6,2},{7,3},{8,12},{9,13},{10,... | collective-permute-start | bytes 1572872 | tf_op jit(solution)/shard_map/ppermute | solution.py:34
  74.1 2.8 %shard_map.59 = (bf16[512,256]{1,0:T(8,128)(2,1)S(1)}, bf16[512,256]{1,0:T(8,128)(2,1)S(1)}) custom-call(s32[1]{0:T(128)} %bitcast.z_ref, bf16[528,256]{1,0:T(8,128)(2,1)S(1)} %copy-done, bf16[528,256]{1,0:T(8,128)(2,1)S(1)} %collective-permute-done.1.refs_1_, bf16[528,256]{1,0:T(8,128)(2,1)S(1)} %collective-permute-done.2.refs_2_, ...), custom_call_target="tpu_custom_call" | custom-call | bytes 1024 | tf_op jit(solution)/shard_map/pallas_call | solution.py:257
  77.0 3.3 %collective-permute-start.20 = (bf16[512,256]{1,0:T(8,128)(2,1)S(1)}, bf16[512,256]{1,0:T(8,128)(2,1)S(1)}, u32[]{:S(2)}, u32[]{:S(2)}) collective-permute-start(bf16[512,256]{1,0:T(8,128)(2,1)S(1)} %get-tuple-element.65.c0), channel_id=1, source_target_pairs={{0,64},{1,65},{2,66},{3,67},{4,68},{5,69},{6,70},{7,71},{8,72},{9,... | collective-permute-start | bytes 786440 | tf_op jit(solution)/shard_map/ppermute | solution.py:34
  80.3 5.8 %collective-permute-done.19.c1 = bf16[512,256]{1,0:T(8,128)(2,1)S(1)} collective-permute-done((bf16[512,256]{1,0:T(8,128)(2,1)S(1)}, bf16[512,256]{1,0:T(8,128)(2,1)S(1)}, u32[]{:S(2)}, u32[]{:S(2)}) %collective-permute-start.19) | collective-permute-done | bytes 262176 | tf_op jit(solution)/shard_map/ppermute | solution.py:34
  86.1 1.6 %collective-permute-done.20.c2 = bf16[512,256]{1,0:T(8,128)(2,1)S(1)} collective-permute-done((bf16[512,256]{1,0:T(8,128)(2,1)S(1)}, bf16[512,256]{1,0:T(8,128)(2,1)S(1)}, u32[]{:S(2)}, u32[]{:S(2)}) %collective-permute-start.20) | collective-permute-done | bytes 262176 | tf_op jit(solution)/shard_map/ppermute | solution.py:34
  87.8 5.1 %collective-permute-done.21.c3 = bf16[512,256]{1,0:T(8,128)(2,1)S(1)} collective-permute-done((bf16[512,256]{1,0:T(8,128)(2,1)S(1)}, bf16[512,256]{1,0:T(8,128)(2,1)S(1)}, u32[]{:S(2)}, u32[]{:S(2)}) %collective-permute-start.21) | collective-permute-done | bytes 262176 | tf_op jit(solution)/shard_map/ppermute | solution.py:34
  93.6 5.5 %shard_map.60 = (bf16[512,512]{1,0:T(8,128)(2,1)}, bf16[512,512]{1,0:T(8,128)(2,1)}, bf16[512,512]{1,0:T(8,128)(2,1)}) custom-call(s32[1]{0:T(128)} %bitcast.z_ref, s32[1]{0:T(128)} %bitcast.1.x_ref, s32[1]{0:T(128)} %bitcast.2.core_ref, s32[1]{0:T(128)} %bitcast.3.set_ref, bf16[512,256]{1,0:T(8,128)(2,1)} %copy-done.1, bf16[512,256]{1,0:T(8,128)(2,1)} %copy-done.10, ...), custom_call_target="tpu_custom_call" | custom-call | bytes 1024 | tf_op jit(solution)/shard_map/pallas_call | solution.py:314
  99.1 1.5 %collective-permute-start.23 = (bf16[512,512]{1,0:T(8,128)(2,1)}, bf16[512,512]{1,0:T(8,128)(2,1)S(1)}, u32[]{:S(2)}, u32[]{:S(2)}) collective-permute-start(bf16[512,512]{1,0:T(8,128)(2,1)} %get-tuple-element.75), channel_id=1, source_target_pairs={{0,2},{1,3},{2,0},{3,1},{4,6},{5,7},{6,4},{7,5},{8,10},{9,11},{10,... | collective-permute-start | bytes 1572872 | tf_op jit(solution)/shard_map/ppermute | solution.py:34
  100.5 2.1 %collective-permute-start.24 = (bf16[512,512]{1,0:T(8,128)(2,1)}, bf16[512,512]{1,0:T(8,128)(2,1)S(1)}, u32[]{:S(2)}, u32[]{:S(2)}) collective-permute-start(bf16[512,512]{1,0:T(8,128)(2,1)} %get-tuple-element.73), channel_id=1, source_target_pairs={{0,1},{1,2},{2,3},{3,0},{4,5},{5,6},{6,7},{7,4},{8,9},{9,10},{10,1... | collective-permute-start | bytes 1572872 | tf_op jit(solution)/shard_map/ppermute | solution.py:34
  102.6 4.1 %shard_map.61 = f32[512,512]{1,0:T(8,128)} custom-call(s32[1]{0:T(128)} %bitcast.12.z_ref, s32[1]{0:T(128)} %bitcast.1.x_ref, s32[1]{0:T(128)} %bitcast.2.core_ref, s32[1]{0:T(128)} %bitcast.3.set_ref, bf16[512,256]{1,0:T(8,128)(2,1)} %copy-done.1, bf16[512,256]{1,0:T(8,128)(2,1)} %copy-done.10, bf16[512,256]{1,0:T(8,128)(2,1)} %copy-done.11, ...), custom_call_target="tpu_custom_call" | custom-call | bytes 1024 | tf_op jit(solution)/shard_map/pallas_call | solution.py:314
  106.8 8.9 %collective-permute-done.23 = bf16[512,512]{1,0:T(8,128)(2,1)S(1)} collective-permute-done((bf16[512,512]{1,0:T(8,128)(2,1)}, bf16[512,512]{1,0:T(8,128)(2,1)S(1)}, u32[]{:S(2)}, u32[]{:S(2)}) %collective-permute-start.23) | collective-permute-done | bytes 524320 | tf_op jit(solution)/shard_map/ppermute | solution.py:34
  115.7 1.6 %convert_add_fusion = f32[512,512]{1,0:T(8,128)S(1)} fusion(bf16[512,512]{1,0:T(8,128)(2,1)S(1)} %collective-permute-done.23, f32[512,512]{1,0:T(8,128)} %shard_map.61, bf16[512,4096]{1,0:T(8,128)(2,1)} %targets.1, s32[]{:T(128)S(6)} %select_n.55), kind=kLoop, calls=%fused_computation.1 | loop fusion | flops 1048576 | bytes 3145732 | tf_op jit(solution)/shard_map/add | solution.py:389
  117.3 6.5 %collective-permute-done.24 = bf16[512,512]{1,0:T(8,128)(2,1)S(1)} collective-permute-done((bf16[512,512]{1,0:T(8,128)(2,1)}, bf16[512,512]{1,0:T(8,128)(2,1)S(1)}, u32[]{:S(2)}, u32[]{:S(2)}) %collective-permute-start.24) | collective-permute-done | bytes 524320 | tf_op jit(solution)/shard_map/ppermute | solution.py:34
  123.8 2.2 %collective-permute-done.25 = bf16[512,512]{1,0:T(8,128)(2,1)S(1)} collective-permute-done((bf16[512,512]{1,0:T(8,128)(2,1)}, bf16[512,512]{1,0:T(8,128)(2,1)S(1)}, u32[]{:S(2)}, u32[]{:S(2)}) %collective-permute-start.25) | collective-permute-done | bytes 524320 | tf_op jit(solution)/shard_map/ppermute | solution.py:34
  (59 shorter events, 5.4 us)
Async XLA Ops:
  2.2 15.8 %collective-permute-start = (bf16[256,1024]{1,0:T(8,128)(2,1)}, bf16[256,1024]{1,0:T(8,128)(2,1)S(1)}, u32[]{:S(2)}, u32[]{:S(2)}) collective-permute-start(bf16[256,1024]{1,0:T(8,128)(2,1)} %shard_map.55), channel_id=1, source_target_pairs={{64,32},{65,33},{66,34},{67,35},{68,36},{69,37},{70,38},{71,39},{7... | collective-permute-start | bytes 1572872 | tf_op jit(solution)/shard_map/ppermute | solution.py:34
  17.9 37.3 %copy-start.2 = (bf16[256,1024]{1,0:T(8,128)(2,1)}, bf16[256,1024]{1,0:T(8,128)(2,1)S(1)}, u32[]{:S(2)}) copy-start(bf16[256,1024]{1,0:T(8,128)(2,1)S(1)} %collective-permute-done.refs_0_) | copy-start | bytes 1572868
  17.9 15.8 %collective-permute-start.4 = (bf16[256,1024]{1,0:T(8,128)(2,1)S(1)}, bf16[256,1024]{1,0:T(8,128)(2,1)S(1)}, u32[]{:S(2)}, u32[]{:S(2)}) collective-permute-start(bf16[256,1024]{1,0:T(8,128)(2,1)S(1)} %collective-permute-done.refs_0_), channel_id=1, source_target_pairs={{0,24},{1,25},{2,26},{3,27},{4,28},{5,29},{6,30},{7,31},{8,0},{9,1... | collective-permute-start | bytes 1572872 | tf_op jit(solution)/shard_map/ppermute | solution.py:34
  22.8 12.8 %collective-permute-start.1 = (bf16[528,256]{1,0:T(8,128)(2,1)}, bf16[528,256]{1,0:T(8,128)(2,1)S(1)}, u32[]{:S(2)}, u32[]{:S(2)}) collective-permute-start(bf16[528,256]{1,0:T(8,128)(2,1)} %get-tuple-element.47), channel_id=1, source_target_pairs={{0,32},{1,33},{2,34},{3,35},{4,36},{5,37},{6,38},{7,39},{8,40},{9,... | collective-permute-start | bytes 811016 | tf_op jit(solution)/shard_map/ppermute | solution.py:34
  22.9 12.7 %collective-permute-start.2 = (bf16[528,256]{1,0:T(8,128)(2,1)}, bf16[528,256]{1,0:T(8,128)(2,1)S(1)}, u32[]{:S(2)}, u32[]{:S(2)}) collective-permute-start(bf16[528,256]{1,0:T(8,128)(2,1)} %get-tuple-element.48), channel_id=1, source_target_pairs={{0,64},{1,65},{2,66},{3,67},{4,68},{5,69},{6,70},{7,71},{8,72},{9,... | collective-permute-start | bytes 811016 | tf_op jit(solution)/shard_map/ppermute | solution.py:34
  26.8 11.4 %collective-permute-start.3 = (bf16[528,256]{1,0:T(8,128)(2,1)}, bf16[528,256]{1,0:T(8,128)(2,1)S(1)}, u32[]{:S(2)}, u32[]{:S(2)}) collective-permute-start(bf16[528,256]{1,0:T(8,128)(2,1)} %get-tuple-element.49), channel_id=1, source_target_pairs={{0,96},{1,97},{2,98},{3,99},{4,100},{5,101},{6,102},{7,103},{8,104... | collective-permute-start | bytes 811016 | tf_op jit(solution)/shard_map/ppermute | solution.py:34
  26.8 15.4 %collective-permute-start.5 = (bf16[256,1024]{1,0:T(8,128)(2,1)S(1)}, bf16[256,1024]{1,0:T(8,128)(2,1)S(1)}, u32[]{:S(2)}, u32[]{:S(2)}) collective-permute-start(bf16[256,1024]{1,0:T(8,128)(2,1)S(1)} %collective-permute-done.refs_0_), channel_id=1, source_target_pairs={{0,8},{1,9},{2,10},{3,11},{4,12},{5,13},{6,14},{7,15},{8,16},{9,17... | collective-permute-start | bytes 1572872 | tf_op jit(solution)/shard_map/ppermute | solution.py:34
  33.7 21.5 %copy-start.3 = (bf16[256,1024]{1,0:T(8,128)(2,1)}, bf16[256,1024]{1,0:T(8,128)(2,1)S(1)}, u32[]{:S(2)}) copy-start(bf16[256,1024]{1,0:T(8,128)(2,1)S(1)} %collective-permute-done.4.refs_1_) | copy-start | bytes 1572868
  33.7 8.4 %collective-permute-start.6 = (bf16[256,1024]{1,0:T(8,128)(2,1)S(1)}, bf16[256,1024]{1,0:T(8,128)(2,1)S(1)}, u32[]{:S(2)}, u32[]{:S(2)}) collective-permute-start(bf16[256,1024]{1,0:T(8,128)(2,1)S(1)} %collective-permute-done.4.refs_1_), channel_id=1, source_target_pairs={{0,4},{1,5},{2,6},{3,7},{4,0},{5,1},{6,2},{7,3},{8,12},{9,13},{10,... | collective-permute-start | bytes 1572872 | tf_op jit(solution)/shard_map/ppermute | solution.py:34
  39.3 24.1 %copy-start = (bf16[528,256]{1,0:T(8,128)(2,1)S(1)}, bf16[528,256]{1,0:T(8,128)(2,1)}, u32[]{:S(2)}) copy-start(bf16[528,256]{1,0:T(8,128)(2,1)} %get-tuple-element.46.refs_0_) | copy-start | bytes 811012
  42.1 16.3 %collective-permute-start.7 = (bf16[2,528,256]{2,1,0:T(8,128)(2,1)S(1)}, bf16[2,528,256]{2,1,0:T(8,128)(2,1)S(1)}, u32[]{:S(2)}, u32[]{:S(2)}) collective-permute-start(bf16[2,528,256]{2,1,0:T(8,128)(2,1)S(1)} %pad_maximum_fusion.refs_4_), channel_id=1, source_target_pairs={{0,8},{1,9},{2,10},{3,11},{4,12},{5,13},{6,14},{7,15},{8,16},{9,17... | collective-permute-start | bytes 1622024 | tf_op jit(solution)/shard_map/ppermute | solution.py:34
  42.2 16.2 %collective-permute-start.8 = (bf16[2,528,256]{2,1,0:T(8,128)(2,1)S(1)}, bf16[2,528,256]{2,1,0:T(8,128)(2,1)S(1)}, u32[]{:S(2)}, u32[]{:S(2)}) collective-permute-start(bf16[2,528,256]{2,1,0:T(8,128)(2,1)S(1)} %pad_maximum_fusion.refs_4_), channel_id=1, source_target_pairs={{0,24},{1,25},{2,26},{3,27},{4,28},{5,29},{6,30},{7,31},{8,0},{9,1... | collective-permute-start | bytes 1622024 | tf_op jit(solution)/shard_map/ppermute | solution.py:34
  45.4 9.8 %collective-permute-start.10 = (bf16[256,1024]{1,0:T(8,128)(2,1)S(1)}, bf16[256,1024]{1,0:T(8,128)(2,1)S(1)}, u32[]{:S(2)}, u32[]{:S(2)}) collective-permute-start(bf16[256,1024]{1,0:T(8,128)(2,1)S(1)} %collective-permute-done.5.refs_3_), channel_id=1, source_target_pairs={{0,4},{1,5},{2,6},{3,7},{4,0},{5,1},{6,2},{7,3},{8,12},{9,13},{10,... | collective-permute-start | bytes 1572872 | tf_op jit(solution)/shard_map/ppermute | solution.py:34
  47.3 11.0 %collective-permute-start.9 = (bf16[256,1024]{1,0:T(8,128)(2,1)S(1)}, bf16[256,1024]{1,0:T(8,128)(2,1)S(1)}, u32[]{:S(2)}, u32[]{:S(2)}) collective-permute-start(bf16[256,1024]{1,0:T(8,128)(2,1)S(1)} %collective-permute-done.refs_0_), channel_id=1, source_target_pairs={{0,4},{1,5},{2,6},{3,7},{4,0},{5,1},{6,2},{7,3},{8,12},{9,13},{10,... | collective-permute-start | bytes 1572872 | tf_op jit(solution)/shard_map/ppermute | solution.py:34
  49.8 10.1 %collective-permute-start.14 = (bf16[2,528,256]{2,1,0:T(8,128)(2,1)S(1)}, bf16[2,528,256]{2,1,0:T(8,128)(2,1)S(1)}, u32[]{:S(2)}, u32[]{:S(2)}) collective-permute-start(bf16[2,528,256]{2,1,0:T(8,128)(2,1)S(1)} %pad_maximum_fusion.refs_4_), channel_id=1, source_target_pairs={{0,4},{1,5},{2,6},{3,7},{4,0},{5,1},{6,2},{7,3},{8,12},{9,13},{10,... | collective-permute-start | bytes 1622024 | tf_op jit(solution)/shard_map/ppermute | solution.py:34
  55.2 18.8 %copy-start.6 = (bf16[256,1024]{1,0:T(8,128)(2,1)}, bf16[256,1024]{1,0:T(8,128)(2,1)S(1)}, u32[]{:S(2)}) copy-start(bf16[256,1024]{1,0:T(8,128)(2,1)S(1)} %collective-permute-done.10.refs_7_) | copy-start | bytes 1572868
  55.3 16.2 %collective-permute-start.13 = (bf16[256,1024]{1,0:T(8,128)(2,1)S(1)}, bf16[256,1024]{1,0:T(8,128)(2,1)S(1)}, u32[]{:S(2)}, u32[]{:S(2)}) collective-permute-start(bf16[256,1024]{1,0:T(8,128)(2,1)S(1)} %collective-permute-done.refs_0_), channel_id=1, source_target_pairs={{0,32},{1,33},{2,34},{3,35},{4,36},{5,37},{6,38},{7,39},{8,40},{9,... | collective-permute-start | bytes 1572872 | tf_op jit(solution)/shard_map/ppermute | solution.py:34
  59.2 4.1 %collective-permute-start.15 = (bf16[2,528,256]{2,1,0:T(8,128)(2,1)S(1)}, bf16[2,528,256]{2,1,0:T(8,128)(2,1)S(1)}, u32[]{:S(2)}, u32[]{:S(2)}) collective-permute-start(bf16[2,528,256]{2,1,0:T(8,128)(2,1)S(1)} %collective-permute-done.7.refs_5_), channel_id=1, source_target_pairs={{0,4},{1,5},{2,6},{3,7},{4,0},{5,1},{6,2},{7,3},{8,12},{9,13},{10,... | collective-permute-start | bytes 1622024 | tf_op jit(solution)/shard_map/ppermute | solution.py:34
  59.4 3.9 %collective-permute-start.16 = (bf16[2,528,256]{2,1,0:T(8,128)(2,1)S(1)}, bf16[2,528,256]{2,1,0:T(8,128)(2,1)S(1)}, u32[]{:S(2)}, u32[]{:S(2)}) collective-permute-start(bf16[2,528,256]{2,1,0:T(8,128)(2,1)S(1)} %collective-permute-done.8.refs_6_), channel_id=1, source_target_pairs={{0,4},{1,5},{2,6},{3,7},{4,0},{5,1},{6,2},{7,3},{8,12},{9,13},{10,... | collective-permute-start | bytes 1622024 | tf_op jit(solution)/shard_map/ppermute | solution.py:34
  59.7 11.7 %collective-permute-start.11 = (bf16[528,256]{1,0:T(8,128)(2,1)S(1)}, bf16[528,256]{1,0:T(8,128)(2,1)S(1)}, u32[]{:S(2)}, u32[]{:S(2)}) collective-permute-start(bf16[528,256]{1,0:T(8,128)(2,1)S(1)} %slice_bitcast_fusion.1), channel_id=1, source_target_pairs={{0,8},{1,9},{2,10},{3,11},{4,12},{5,13},{6,14},{7,15},{8,16},{9,17... | collective-permute-start | bytes 811016 | tf_op jit(solution)/shard_map/ppermute | solution.py:34
  59.8 11.6 %collective-permute-start.12 = (bf16[528,256]{1,0:T(8,128)(2,1)S(1)}, bf16[528,256]{1,0:T(8,128)(2,1)S(1)}, u32[]{:S(2)}, u32[]{:S(2)}) collective-permute-start(bf16[528,256]{1,0:T(8,128)(2,1)S(1)} %slice_bitcast_fusion), channel_id=1, source_target_pairs={{0,24},{1,25},{2,26},{3,27},{4,28},{5,29},{6,30},{7,31},{8,0},{9,1... | collective-permute-start | bytes 811016 | tf_op jit(solution)/shard_map/ppermute | solution.py:34
  71.5 21.4 %copy-start.8 = (bf16[256,1024]{1,0:T(8,128)(2,1)}, bf16[256,1024]{1,0:T(8,128)(2,1)S(1)}, u32[]{:S(2)}) copy-start(bf16[256,1024]{1,0:T(8,128)(2,1)S(1)} %collective-permute-done.13.refs_2_) | copy-start | bytes 1572868
  71.5 2.6 %collective-permute-start.17 = (bf16[1,528,256]{2,1,0:T(8,128)(2,1)S(1)}, bf16[1,528,256]{2,1,0:T(8,128)(2,1)S(1)}, u32[]{:S(2)}, u32[]{:S(2)}) collective-permute-start(bf16[1,528,256]{2,1,0:T(8,128)(2,1)S(1)} %bitcast.17), channel_id=1, source_target_pairs={{0,4},{1,5},{2,6},{3,7},{4,0},{5,1},{6,2},{7,3},{8,12},{9,13},{10,... | collective-permute-start | bytes 811016 | tf_op jit(solution)/shard_map/ppermute | solution.py:34
  71.6 2.5 %collective-permute-start.18 = (bf16[1,528,256]{2,1,0:T(8,128)(2,1)S(1)}, bf16[1,528,256]{2,1,0:T(8,128)(2,1)S(1)}, u32[]{:S(2)}, u32[]{:S(2)}) collective-permute-start(bf16[1,528,256]{2,1,0:T(8,128)(2,1)S(1)} %bitcast.19), channel_id=1, source_target_pairs={{0,4},{1,5},{2,6},{3,7},{4,0},{5,1},{6,2},{7,3},{8,12},{9,13},{10,... | collective-permute-start | bytes 811016 | tf_op jit(solution)/shard_map/ppermute | solution.py:34
  72.1 8.2 %collective-permute-start.22 = (bf16[256,1024]{1,0:T(8,128)(2,1)S(1)}, bf16[256,1024]{1,0:T(8,128)(2,1)S(1)}, u32[]{:S(2)}, u32[]{:S(2)}) collective-permute-start(bf16[256,1024]{1,0:T(8,128)(2,1)S(1)} %collective-permute-done.13.refs_2_), channel_id=1, source_target_pairs={{0,4},{1,5},{2,6},{3,7},{4,0},{5,1},{6,2},{7,3},{8,12},{9,13},{10,... | collective-permute-start | bytes 1572872 | tf_op jit(solution)/shard_map/ppermute | solution.py:34
  76.9 15.9 %copy-start.1 = (bf16[512,256]{1,0:T(8,128)(2,1)}, bf16[512,256]{1,0:T(8,128)(2,1)S(1)}, u32[]{:S(2)}) copy-start(bf16[512,256]{1,0:T(8,128)(2,1)S(1)} %get-tuple-element.65.c0) | copy-start | bytes 786436
  76.9 9.2 %collective-permute-start.19 = (bf16[512,256]{1,0:T(8,128)(2,1)S(1)}, bf16[512,256]{1,0:T(8,128)(2,1)S(1)}, u32[]{:S(2)}, u32[]{:S(2)}) collective-permute-start(bf16[512,256]{1,0:T(8,128)(2,1)S(1)} %get-tuple-element.66), channel_id=1, source_target_pairs={{0,32},{1,33},{2,34},{3,35},{4,36},{5,37},{6,38},{7,39},{8,40},{9,... | collective-permute-start | bytes 786440 | tf_op jit(solution)/shard_map/ppermute | solution.py:34
  77.0 10.7 %collective-permute-start.20 = (bf16[512,256]{1,0:T(8,128)(2,1)S(1)}, bf16[512,256]{1,0:T(8,128)(2,1)S(1)}, u32[]{:S(2)}, u32[]{:S(2)}) collective-permute-start(bf16[512,256]{1,0:T(8,128)(2,1)S(1)} %get-tuple-element.65.c0), channel_id=1, source_target_pairs={{0,64},{1,65},{2,66},{3,67},{4,68},{5,69},{6,70},{7,71},{8,72},{9,... | collective-permute-start | bytes 786440 | tf_op jit(solution)/shard_map/ppermute | solution.py:34
  80.3 12.6 %collective-permute-start.21 = (bf16[512,256]{1,0:T(8,128)(2,1)S(1)}, bf16[512,256]{1,0:T(8,128)(2,1)S(1)}, u32[]{:S(2)}, u32[]{:S(2)}) collective-permute-start(bf16[512,256]{1,0:T(8,128)(2,1)S(1)} %get-tuple-element.66), channel_id=1, source_target_pairs={{0,96},{1,97},{2,98},{3,99},{4,100},{5,101},{6,102},{7,103},{8,104... | collective-permute-start | bytes 786440 | tf_op jit(solution)/shard_map/ppermute | solution.py:34
  99.1 16.6 %collective-permute-start.23 = (bf16[512,512]{1,0:T(8,128)(2,1)}, bf16[512,512]{1,0:T(8,128)(2,1)S(1)}, u32[]{:S(2)}, u32[]{:S(2)}) collective-permute-start(bf16[512,512]{1,0:T(8,128)(2,1)} %get-tuple-element.75), channel_id=1, source_target_pairs={{0,2},{1,3},{2,0},{3,1},{4,6},{5,7},{6,4},{7,5},{8,10},{9,11},{10,... | collective-permute-start | bytes 1572872 | tf_op jit(solution)/shard_map/ppermute | solution.py:34
  100.5 23.3 %collective-permute-start.24 = (bf16[512,512]{1,0:T(8,128)(2,1)}, bf16[512,512]{1,0:T(8,128)(2,1)S(1)}, u32[]{:S(2)}, u32[]{:S(2)}) collective-permute-start(bf16[512,512]{1,0:T(8,128)(2,1)} %get-tuple-element.73), channel_id=1, source_target_pairs={{0,1},{1,2},{2,3},{3,0},{4,5},{5,6},{6,7},{7,4},{8,9},{9,10},{10,1... | collective-permute-start | bytes 1572872 | tf_op jit(solution)/shard_map/ppermute | solution.py:34
  102.6 23.3 %collective-permute-start.25 = (bf16[512,512]{1,0:T(8,128)(2,1)}, bf16[512,512]{1,0:T(8,128)(2,1)S(1)}, u32[]{:S(2)}, u32[]{:S(2)}) collective-permute-start(bf16[512,512]{1,0:T(8,128)(2,1)} %get-tuple-element.76), channel_id=1, source_target_pairs={{0,3},{1,0},{2,1},{3,2},{4,7},{5,4},{6,5},{7,6},{8,11},{9,8},{10,9... | collective-permute-start | bytes 1572872 | tf_op jit(solution)/shard_map/ppermute | solution.py:34
  (7 other events, 52.2 us)

commit v4 on v3

--- a/solution.py
+++ b/solution.py
@@ -13,6 +13,7 @@
 DEAD = -1e30
 VMEM = 56 * 2**20
 ATTEND_VMEM = 40 * 2**20
+SMALL_VMEM = 24 * 2**20
 LIGHT = pl.CostEstimate(flops=0, bytes_accessed=1024, transcendentals=0)
 
 
@@ -56,14 +57,15 @@
     return (widened * inverse * gain_row).astype(jnp.bfloat16)
 
 
-def section_kernel(z_ref, pad_ref, memory, targets, gain_ref, w_ref, *refs):
+def section_kernel(pad_ref, memory, targets, gain_ref, w_ref, *refs):
     *out_refs, normed, x_rows, total, arrival = refs
     k, steps = pl.program_id(0), pl.num_programs(0)
     depth, width = w_ref.shape[1], w_ref.shape[3]
     rows = total.shape[0]
     half = rows // 2
     dim = out_refs[0].shape[1]
-    encoder = z_ref[0] < 2
+    z = position()[2]
+    encoder = z < 2
 
     def normalise(source, count):
         block = 128
@@ -117,12 +119,12 @@
         position = lax.broadcasted_iota(jnp.int32, (MARK_ROWS, dim), 1)
         marks = jnp.where(position < half - pad_ref[0], 0.0, DEAD).astype(jnp.bfloat16)
         for d, ref in enumerate(out_refs):
-            head = (z_ref[0] + d) % 4
+            head = (z + d) % 4
             ref[:rows, :] = total[:, pl.ds(pl.multiple_of(head * dim, dim), dim)].astype(jnp.bfloat16)
             ref[rows:, :] = marks
 
 
-def section(z, pad_counts, memory, targets, gains, weights, dim):
+def section(pad_counts, memory, targets, gains, weights, dim):
     rows, model = targets.shape
     width = weights.shape[3]
     depth = 1024
@@ -132,15 +134,15 @@
     return pl.pallas_call(
         section_kernel,
         grid_spec=pltpu.PrefetchScalarGridSpec(
-            num_scalar_prefetch=2,
+            num_scalar_prefetch=1,
             grid=(steps,),
             in_specs=[
                 anywhere,
                 anywhere,
-                pl.BlockSpec((1, model), lambda k, z, pad: (0, 0)),
-                pl.BlockSpec((1, depth, 2, width), lambda k, z, pad: (0, k, 0, 0)),
+                pl.BlockSpec((1, model), lambda k, pad: (0, 0)),
+                pl.BlockSpec((1, depth, 2, width), lambda k, pad: (0, k, 0, 0)),
             ],
-            out_specs=[pl.BlockSpec(slab, lambda k, z, pad: (0, 0))] * 4,
+            out_specs=[pl.BlockSpec(slab, lambda k, pad: (0, 0))] * 4,
             scratch_shapes=[
                 pltpu.VMEM((steps, rows, depth), jnp.bfloat16),
                 pltpu.VMEM((rows, model), jnp.bfloat16),
@@ -151,7 +153,7 @@
         out_shape=[jax.ShapeDtypeStruct(slab, jnp.bfloat16)] * 4,
         cost_estimate=LIGHT,
         compiler_params=pltpu.CompilerParams(vmem_limit_bytes=VMEM),
-    )(z.reshape(1), pad_counts, memory, targets, gains, weights)
+    )(pad_counts, memory, targets, gains, weights)
 
 
 def second_half_kernel(start_ref, w_ref, *out_refs):
@@ -178,14 +180,14 @@
     )(start.reshape(1), weights)
 
 
-def attend_kernel(first, half, chunks, z_ref, *refs):
+def attend_kernel(first, half, chunks, *refs):
     if first:
         *slabs, acc_ref, peak_ref, total_ref, queries, keys, values, marks = refs
     else:
         *slabs, acc_ref, peak_ref, total_ref, out_a, out_b, queries, keys, values, marks = refs
     q_slabs, blocks = slabs[:4], slabs[4:]
     size = (blocks[0].shape[1] - MARK_ROWS) // 2
-    z = z_ref[0]
+    z = position()[2]
     pieces = [ref.at[n] for ref in blocks for n in range(ref.shape[0])]
     for j, ref in enumerate(pieces):
         keys[j * size : (j + 1) * size, :] = ref[:size, :]
@@ -243,7 +245,7 @@
         run(at)
 
 
-def attend(z, q_slabs, blocks, chunks, state=None):
+def attend(q_slabs, blocks, chunks, state=None):
     rows, dim = q_slabs[0].shape[0] - MARK_ROWS, q_slabs[0].shape[1]
     half = rows // chunks
     first = state is None
@@ -256,7 +258,7 @@
     operands = [*q_slabs, *blocks, *(() if first else state)]
     return pl.pallas_call(
         functools.partial(attend_kernel, first, half, chunks),
-        in_specs=[pl.BlockSpec(memory_space=pltpu.SMEM)] + [vmem] * len(operands),
+        in_specs=[vmem] * len(operands),
         out_specs=[vmem] * len(out_shape),
         scratch_shapes=[
             pltpu.VMEM((2 * half, dim), jnp.bfloat16),
@@ -267,18 +269,18 @@
         out_shape=out_shape,
         cost_estimate=LIGHT,
         compiler_params=pltpu.CompilerParams(vmem_limit_bytes=ATTEND_VMEM),
-    )(z.reshape(1), *operands)
-
-
-def project_kernel(first, z_ref, x_ref, core_ref, set_ref, c0, c1, c2, c3, *refs):
-    sources, mine = refs[:8], refs[8]
-    *out_refs, held, context, arrived = refs[9:]
-    z, x, core, held_set = z_ref[0], x_ref[0], core_ref[0], set_ref[0]
-    dim, width = c0.shape[1], held.shape[1]
+    )(*operands)
+
+
+def assemble_kernel(*refs):
+    sources, mine, held, arrived = refs[:4], refs[4], refs[5], refs[6]
+    x, y, z, core = position()
+    odd = y % 2
+    count, width = held.shape[:2]
     part = width // 2
 
     def fetch(j, action):
-        wanted = (x + first + j) % 4
+        wanted = (x + j) % count
         slot, arrival = held.at[j], arrived.at[j]
 
         @pl.when(z >= 2)
@@ -286,46 +288,92 @@
             top = pl.multiple_of(wanted * width, width)
             action(pltpu.make_async_copy(mine.at[pl.ds(top, width)], slot, arrival))
 
-        for n in range(4):
-
-            @pl.when((z < 2) & ((wanted + 4 - held_set) % 4 == n))
+        for n in range(2):
+
+            @pl.when((z < 2) & ((wanted // 2 + z) % 2 == n))
             def _(n=n):
-                for source, side in ((sources[n], core), (sources[4 + n], 1 - core)):
+                for source, side in ((sources[n], core), (sources[2 + n], 1 - core)):
                     top = pl.multiple_of(side * part, part)
-                    action(pltpu.make_async_copy(source, slot.at[pl.ds(top, part)], arrival))
-
-    for j in range(len(out_refs)):
+                    block = source.at[(wanted + odd) % 2]
+                    action(pltpu.make_async_copy(block, slot.at[pl.ds(top, part)], arrival))
+
+    for j in range(count):
         fetch(j, lambda copy: copy.start())
+    for j in range(count):
+        fetch(j, lambda copy: copy.wait())
+
+
+def assemble(sources):
+    count, (features, width) = 4, sources[4].shape
+    shape = (count, features // count, width)
+    return pl.pallas_call(
+        assemble_kernel,
+        in_specs=[pl.BlockSpec(memory_space=pl.ANY)] * 5,
+        out_specs=pl.BlockSpec(memory_space=pltpu.VMEM),
+        out_shape=jax.ShapeDtypeStruct(shape, jnp.bfloat16),
+        scratch_shapes=[pltpu.SemaphoreType.DMA((count,))],
+        cost_estimate=LIGHT,
+        compiler_params=pltpu.CompilerParams(vmem_limit_bytes=SMALL_VMEM),
+    )(*sources)
+
+
+def project_kernel(distances, c0, c1, c2, c3, held, *refs):
+    *out_refs, context = refs
+    z = position()[2]
+    dim = c0.shape[1]
     for d, ref in enumerate((c0, c1, c2, c3)):
         head = (z + 4 - d) % 4
         context[:, pl.ds(pl.multiple_of(head * dim, dim), dim)] = ref[...]
-    for j, ref in enumerate(out_refs):
-        fetch(j, lambda copy: copy.wait())
+    parts = len(out_refs) // len(distances)
+    for j, distance in enumerate(distances):
         mixed = lax.dot_general(
-            context[...], held[j], (((1,), (1,)), ((), ())), preferred_element_type=jnp.float32
+            context[...], held[distance], (((1,), (1,)), ((), ())), preferred_element_type=jnp.float32
         )
-        ref[...] = mixed.astype(ref.dtype)
-
-
-def project(place, contexts, sources, first, count, dtype):
+        for n, ref in enumerate(out_refs[j * parts : (j + 1) * parts]):
+            size = ref.shape[0]
+            ref[...] = mixed[n * size : (n + 1) * size].astype(ref.dtype)
+
+
+def project(contexts, features, distances, dtype, parts=1):
     rows, dim = contexts[0].shape
-    width = sources[-1].shape[0] // 4
+    width = features.shape[1]
+    outs = len(distances) * parts
     vmem = pl.BlockSpec(memory_space=pltpu.VMEM)
     return pl.pallas_call(
-        functools.partial(project_kernel, first),
-        in_specs=[pl.BlockSpec(memory_space=pltpu.SMEM)] * 4
-        + [vmem] * 4
-        + [pl.BlockSpec(memory_space=pl.ANY)] * 9,
-        out_specs=[vmem] * count,
-        out_shape=[jax.ShapeDtypeStruct((rows, width), dtype)] * count,
-        scratch_shapes=[
-            pltpu.VMEM((count, width, 4 * dim), jnp.bfloat16),
-            pltpu.VMEM((rows, 4 * dim), jnp.bfloat16),
-            pltpu.SemaphoreType.DMA((count,)),
-        ],
-        cost_estimate=LIGHT,
-        compiler_params=pltpu.CompilerParams(vmem_limit_bytes=VMEM),
-    )(*(scalar.reshape(1) for scalar in place), *contexts, *sources)
+        functools.partial(project_kernel, distances),
+        in_specs=[vmem] * 5,
+        out_specs=[vmem] * outs,
+        out_shape=[jax.ShapeDtypeStruct((rows // parts, width), dtype)] * outs,
+        scratch_shapes=[pltpu.VMEM((rows, 4 * dim), jnp.bfloat16)],
+        cost_estimate=LIGHT,
+        compiler_params=pltpu.CompilerParams(vmem_limit_bytes=SMALL_VMEM),
+    )(*contexts, features)
+
+
+def joined_kernel(up_ref, down_ref, upward, downward, up_out, down_out):
+    half = upward.shape[0]
+    up_out[:half, :] = (up_ref[:half, :] + upward[...].astype(jnp.float32)).astype(jnp.bfloat16)
+    up_out[half:, :] = up_ref[half:, :].astype(jnp.bfloat16)
+    down_out[:half, :] = down_ref[:half, :].astype(jnp.bfloat16)
+    down_out[half:, :] = (down_ref[half:, :] + downward[...].astype(jnp.float32)).astype(jnp.bfloat16)
+
+
+def joined(up, down, upward, downward):
+    vmem = pl.BlockSpec(memory_space=pltpu.VMEM)
+    return pl.pallas_call(
+        joined_kernel,
+        in_specs=[vmem] * 4,
+        out_specs=[vmem] * 2,
+        out_shape=[jax.ShapeDtypeStruct(up.shape, jnp.bfloat16)] * 2,
+        cost_estimate=LIGHT,
+        compiler_params=pltpu.CompilerParams(vmem_limit_bytes=SMALL_VMEM),
+    )(up, down, upward, downward)
+
+
+def position():
+    segment, ctx, x = (lax.axis_index(axis) for axis in AXES)
+    core, y, low = ctx % 2, (ctx // 2) % 4, ctx // 8
+    return x, y, 2 * segment + low, core
 
 
 def after(value, *others):
@@ -347,47 +395,52 @@
     flip = lambda x, y, z, c: (x, y, 1 - z, c)
     is_encoder = segment == 0
 
-    held_set = (y + 2 * low) % 4
-    wanted_set = (y + 2 * (1 - low)) % 4
+    odd = y % 2
+    wanted_set = 2 * (1 - low) + odd
     (share,) = second_half(proj_weights, wanted_set * 2 + core, half // 8, 1, 1)
     p = moved(share, down, decoder)
 
-    own, *to = section(after(z, share), pad_counts, memory, targets, norm_gains, proj_weights, dim)
+    own, *to = section(after(pad_counts, share), memory, targets, norm_gains, proj_weights, dim)
     own, to, p = lax.optimization_barrier((own, to, p))
-    above, below = along_y(p, 3, encoder), along_y(p, 1, encoder)
+    beside = moved(p, lambda x, y, z, c: (x, y ^ 1, z, c), encoder)
     r1, r3, r2 = along_z(to[0], 1), along_z(to[2], 3), along_z(to[1], 2)
     early = jnp.where(is_encoder, own, jnp.where(z == 2, r1, r3))
     late = jnp.where(z == 0, r3, jnp.where(z == 1, r1, r2))
     pair = jnp.stack([early, late])
-    above_twin = other_core(above, encoder)
-
-    pair, p, above, below, above_twin = lax.optimization_barrier((pair, p, above, below, above_twin))
+    pair, p, beside = lax.optimization_barrier((pair, p, beside))
+
     y1, y3 = along_y(pair, 1), along_y(pair, 3)
-    across = moved(p, flip, encoder)
-    twin, below_twin = other_core(p, encoder), other_core(below, encoder)
+    lower = jnp.stack([p, beside])
+    lower_twin = other_core(lower, encoder)
+    upper = moved(lower, flip, encoder)
     (mine,) = second_half(after(proj_weights, pair), jnp.int32(2), half // 2, 2, 1)
-
-    y1, y3, twin, below_twin, mine = lax.optimization_barrier((y1, y3, twin, below_twin, mine))
+    y1, y3, mine, lower_twin = lax.optimization_barrier((y1, y3, mine, lower_twin))
+
     far0, far1 = along_y(y1[0], 1), along_y(y3[1], 3)
     slabs = [own, r1, r2, r3]
     blocks = [pair, y1, y3]
-    state = attend(z, slabs, blocks + [other_core(b) for b in blocks], chunks)
-
-    far0, far1, across, *state = lax.optimization_barrier((far0, far1, across, *state))
-    across_twin = other_core(across, encoder)
+    state = attend(slabs, blocks + [other_core(b) for b in blocks], chunks)
+    far0, far1, *state = lax.optimization_barrier((far0, far1, *state))
+
     blocks = [far0[None], far1[None]]
     blocks = blocks + [other_core(b) for b in blocks]
-    ca, cb = attend(z, slabs, blocks, chunks, state)
+    ca, cb = attend(slabs, blocks, chunks, state)
+    upper_twin = other_core(after(upper, ca), encoder)
     contexts = [ca, along_z(cb, 1), along_z(ca, 2), along_z(cb, 3)]
-    sources = [p, above, across, below, twin, above_twin, across_twin, below_twin, mine]
-    place = [z, x, core, held_set]
+    sources = [lower, upper, lower_twin, upper_twin, mine]
     out_width = model // 8
     residual = lax.dynamic_slice_in_dim(targets, (segment * 4 + x) * out_width, out_width, 1)
-    far = project(place, contexts, sources, 1, 3, jnp.bfloat16)
-    (near,) = project([after(z, far[0]), *place[1:]], contexts, sources, 0, 1, jnp.float32)
-    far = {d: along_x(far[d - 1], d) for d in (2, 1, 3)}
-    summed = lax.optimization_barrier(residual.astype(jnp.float32) + near + far[2].astype(jnp.float32))
-    return (summed + far[1].astype(jnp.float32) + far[3].astype(jnp.float32)).astype(jnp.bfloat16)
+    features = assemble(sources)
+    upward, downward = project(contexts, features, (2,), jnp.bfloat16, 2)
+    contexts[0], upward, downward = lax.optimization_barrier((contexts[0], upward, downward))
+    up, down = project(contexts, features, (1, 3), jnp.float32)
+    up, down = joined(up, down, along_x(upward, 1), along_x(downward, 3))
+    contexts[0], up, down = lax.optimization_barrier((contexts[0], up, down))
+    (near,) = project(contexts, features, (0,), jnp.float32)
+    summed = lax.optimization_barrier(residual.astype(jnp.float32) + near)
+    for block, d in ((up, 1), (down, 3)):
+        summed = summed + along_x(block, d).astype(jnp.float32)
+    return summed.astype(jnp.bfloat16)
 
 
 def solution(mesh):

time: 129 us -> 118 us (0.915); the launches traced: 127 us -> 117 us
  Pallas kernels: 40.4 us -> 34.7 us
  starting transfers between devices: 38.3 us -> 34.4 us
    pallas_call x2 -> x5, Pallas kernels: 9.64 us -> 3.71 us  [the longest x3 3.09 us: project(): pl.pallas_call(functools.partial(project_kernel, distances), in_specs=[vm...]
    ppermute x26 -> x24, starting transfers between devices: 38.3 us -> 34.4 us  [moved(): return lax.ppermute(block, AXES, route)]
    ppermute x26 -> x24, waiting for transfers between devices: 42 us -> 41.7 us  [moved(): return lax.ppermute(block, AXES, route)]
  transfers between devices with their start and end apart: 26 -> 24, of which waited for: 11 -> 14; matrix products, arithmetic and copies ran while one was open for 2% -> 2% of each run, Pallas kernels for 26% -> 27%
where the time goes in v4:
time: 118 us; the launch traced here: 117 us
  waiting for transfers between devices  41.7 us (35%)
  Pallas kernels  34.7 us (29%)
  starting transfers between devices  34.4 us (29%)
  other arithmetic  3.39 us (3%)
  local copies, waits for them, and re-layouts  2.24 us (2%)
    ppermute x24, waiting for transfers between devices, moved(): return lax.ppermute(block, AXES, route)  41.7 us
    ppermute x24, starting transfers between devices, moved(): return lax.ppermute(block, AXES, route)  34.4 us
    pallas_call x1, Pallas kernels, section(): pl.pallas_call(section_kernel, grid_spec=pltpu.PrefetchScalarGridSpec(num...  13.5 us
    pallas_call x2, Pallas kernels, attend(): pl.pallas_call(functools.partial(attend_kernel, first, half, chunks), in_...  9.95 us
    pallas_call x2, Pallas kernels, second_half(): pl.pallas_call(second_half_kernel, grid_spec=pltpu.PrefetchScalarGridSpec...  7.52 us
    pallas_call x3, Pallas kernels, project(): pl.pallas_call(functools.partial(project_kernel, distances), in_specs=[vm...  3.09 us
  transfers between devices with their start and end apart: 24, of which 14 were waited for; matrix products, arithmetic and copies ran while one was open for 2% of the time, Pallas kernels for 27%

profile of v4, /device:TPU:38, one launch (start us, length us, event | category | flops | bytes accessed | tf_op | source)
XLA Modules:
  0.0 117.2 jit_solution(14730228057149123527)
XLA Ops:
  0.0 2.2 %shard_map.55 = bf16[256,1024]{1,0:T(8,128)(2,1)} custom-call(s32[1]{0:T(128)} %bitcast.start_ref, bf16[1,4096,2,1024]{3,2,1,0:T(2,128)(2,1)} %w_ref.4), custom_call_target="tpu_custom_call" | custom-call | bytes 1024 | tf_op jit(solution)/shard_map/pallas_call | solution.py:169
  2.2 1.3 %collective-permute-start = (bf16[256,1024]{1,0:T(8,128)(2,1)}, bf16[256,1024]{1,0:T(8,128)(2,1)S(1)}, u32[]{:S(2)}, u32[]{:S(2)}) collective-permute-start(bf16[256,1024]{1,0:T(8,128)(2,1)} %shard_map.55), channel_id=1, source_target_pairs={{64,32},{65,33},{66,34},{67,35},{68,36},{69,37},{70,38},{71,39},{7... | collective-permute-start | bytes 1572872 | tf_op jit(solution)/shard_map/ppermute | solution.py:35
  4.1 13.5 %shard_map.56 = (bf16[528,256]{1,0:T(8,128)(2,1)}, bf16[528,256]{1,0:T(8,128)(2,1)}, bf16[528,256]{1,0:T(8,128)(2,1)}, bf16[528,256]{1,0:T(8,128)(2,1)}) custom-call(s32[1]{0:T(128)S(6)} %copy.6.pad_ref, bf16[256,4096]{1,0:T(8,128)(2,1)} %memory.1, bf16[512,4096]{1,0:T(8,128)(2,1)} %targets.1, f32[1,4096]{1,0:T(1,128)} %gain_ref.1, ...), custom_call_target="tpu_custom_call" | custom-call | bytes 1024 | tf_op jit(solution)/shard_map/pallas_call | solution.py:134
  17.9 3.2 %collective-permute-start.1 = (bf16[528,256]{1,0:T(8,128)(2,1)}, bf16[528,256]{1,0:T(8,128)(2,1)S(1)}, u32[]{:S(2)}, u32[]{:S(2)}) collective-permute-start(bf16[528,256]{1,0:T(8,128)(2,1)} %get-tuple-element.52), channel_id=1, source_target_pairs={{0,32},{1,33},{2,34},{3,35},{4,36},{5,37},{6,38},{7,39},{8,40},{9,... | collective-permute-start | bytes 811016 | tf_op jit(solution)/shard_map/ppermute | solution.py:35
  21.8 2.3 %collective-permute-start.3 = (bf16[528,256]{1,0:T(8,128)(2,1)}, bf16[528,256]{1,0:T(8,128)(2,1)S(1)}, u32[]{:S(2)}, u32[]{:S(2)}) collective-permute-start(bf16[528,256]{1,0:T(8,128)(2,1)} %get-tuple-element.54), channel_id=1, source_target_pairs={{0,96},{1,97},{2,98},{3,99},{4,100},{5,101},{6,102},{7,103},{8,104... | collective-permute-start | bytes 811016 | tf_op jit(solution)/shard_map/ppermute | solution.py:35
  24.0 3.5 %collective-permute-start.4 = (bf16[256,1024]{1,0:T(8,128)(2,1)S(1)}, bf16[256,1024]{1,0:T(8,128)(2,1)S(1)}, u32[]{:S(2)}, u32[]{:S(2)}) collective-permute-start(bf16[256,1024]{1,0:T(8,128)(2,1)S(1)} %collective-permute-done), channel_id=1, source_target_pairs={{0,8},{1,9},{2,10},{3,11},{4,12},{5,13},{6,14},{7,15},{8,0},{9,1},... | collective-permute-start | bytes 1572872 | tf_op jit(solution)/shard_map/ppermute | solution.py:35
  27.5 5.1 %collective-permute-done.1.refs_1_ = bf16[528,256]{1,0:T(8,128)(2,1)S(1)} collective-permute-done((bf16[528,256]{1,0:T(8,128)(2,1)}, bf16[528,256]{1,0:T(8,128)(2,1)S(1)}, u32[]{:S(2)}, u32[]{:S(2)}) %collective-permute-start.1) | collective-permute-done | bytes 270368 | tf_op jit(solution)/shard_map/ppermute | solution.py:35
  32.6 2.8 %collective-permute-done.3.refs_3_ = bf16[528,256]{1,0:T(8,128)(2,1)S(1)} collective-permute-done((bf16[528,256]{1,0:T(8,128)(2,1)}, bf16[528,256]{1,0:T(8,128)(2,1)S(1)}, u32[]{:S(2)}, u32[]{:S(2)}) %collective-permute-start.3) | collective-permute-done | bytes 270368 | tf_op jit(solution)/shard_map/ppermute | solution.py:35
  36.5 2.2 %collective-permute-done.4 = bf16[256,1024]{1,0:T(8,128)(2,1)S(1)} collective-permute-done((bf16[256,1024]{1,0:T(8,128)(2,1)S(1)}, bf16[256,1024]{1,0:T(8,128)(2,1)S(1)}, u32[]{:S(2)}, u32[]{:S(2)}) %collective-permute-start.4) | collective-permute-done | bytes 524320 | tf_op jit(solution)/shard_map/ppermute | solution.py:35
  38.8 2.1 %collective-permute-start.7 = (bf16[2,256,1024]{2,1,0:T(8,128)(2,1)S(1)}, bf16[2,256,1024]{2,1,0:T(8,128)(2,1)S(1)}, u32[]{:S(2)}, u32[]{:S(2)}) collective-permute-start(bf16[2,256,1024]{2,1,0:T(8,128)(2,1)S(1)} %pad_maximum_fusion.refs_0_), channel_id=1, source_target_pairs={{0,4},{1,5},{2,6},{3,7},{4,0},{5,1},{6,2},{7,3},{8,12},{9,13},{10,... | collective-permute-start | bytes 3145736 | tf_op jit(solution)/shard_map/ppermute | solution.py:35
  40.9 1.6 %collective-permute-start.5 = (bf16[2,528,256]{2,1,0:T(8,128)(2,1)S(1)}, bf16[2,528,256]{2,1,0:T(8,128)(2,1)S(1)}, u32[]{:S(2)}, u32[]{:S(2)}) collective-permute-start(bf16[2,528,256]{2,1,0:T(8,128)(2,1)S(1)} %pad_maximum_fusion.1.refs_4_), channel_id=1, source_target_pairs={{0,8},{1,9},{2,10},{3,11},{4,12},{5,13},{6,14},{7,15},{8,16},{9,17... | collective-permute-start | bytes 1622024 | tf_op jit(solution)/shard_map/ppermute | solution.py:35
  42.6 1.7 %collective-permute-start.6 = (bf16[2,528,256]{2,1,0:T(8,128)(2,1)S(1)}, bf16[2,528,256]{2,1,0:T(8,128)(2,1)S(1)}, u32[]{:S(2)}, u32[]{:S(2)}) collective-permute-start(bf16[2,528,256]{2,1,0:T(8,128)(2,1)S(1)} %pad_maximum_fusion.1.refs_4_), channel_id=1, source_target_pairs={{0,24},{1,25},{2,26},{3,27},{4,28},{5,29},{6,30},{7,31},{8,0},{9,1... | collective-permute-start | bytes 1622024 | tf_op jit(solution)/shard_map/ppermute | solution.py:35
  44.3 3.3 %collective-permute-start.18 = (bf16[2,256,1024]{2,1,0:T(8,128)(2,1)S(1)}, bf16[2,256,1024]{2,1,0:T(8,128)(2,1)S(1)}, u32[]{:S(2)}, u32[]{:S(2)}) collective-permute-start(bf16[2,256,1024]{2,1,0:T(8,128)(2,1)S(1)} %pad_maximum_fusion.refs_0_), channel_id=1, source_target_pairs={{0,32},{1,33},{2,34},{3,35},{4,36},{5,37},{6,38},{7,39},{8,40},{9,... | collective-permute-start | bytes 3145736 | tf_op jit(solution)/shard_map/ppermute | solution.py:35
  47.6 5.4 %shard_map.57.refs_4_ = bf16[2048,1024]{1,0:T(8,128)(2,1)} custom-call(s32[1]{0:T(128)} %constant.70.clone.1.start_ref, bf16[1,4096,2,1024]{3,2,1,0:T(2,128)(2,1)} %w_ref.4), custom_call_target="tpu_custom_call" | custom-call | bytes 1024 | tf_op jit(solution)/shard_map/pallas_call | solution.py:169
  53.0 3.9 %collective-permute-done.5.refs_5_ = bf16[2,528,256]{2,1,0:T(8,128)(2,1)S(1)} collective-permute-done((bf16[2,528,256]{2,1,0:T(8,128)(2,1)S(1)}, bf16[2,528,256]{2,1,0:T(8,128)(2,1)S(1)}, u32[]{:S(2)}, u32[]{:S(2)}) %collective-permute-start.5) | collective-permute-done | bytes 540704 | tf_op jit(solution)/shard_map/ppermute | solution.py:35
  57.5 1.6 %collective-permute-start.8 = (bf16[528,256]{1,0:T(8,128)(2,1)S(1)}, bf16[528,256]{1,0:T(8,128)(2,1)S(1)}, u32[]{:S(2)}, u32[]{:S(2)}) collective-permute-start(bf16[528,256]{1,0:T(8,128)(2,1)S(1)} %slice_bitcast_fusion.1), channel_id=1, source_target_pairs={{0,8},{1,9},{2,10},{3,11},{4,12},{5,13},{6,14},{7,15},{8,16},{9,17... | collective-permute-start | bytes 811016 | tf_op jit(solution)/shard_map/ppermute | solution.py:35
  59.2 1.9 %collective-permute-start.9 = (bf16[528,256]{1,0:T(8,128)(2,1)S(1)}, bf16[528,256]{1,0:T(8,128)(2,1)S(1)}, u32[]{:S(2)}, u32[]{:S(2)}) collective-permute-start(bf16[528,256]{1,0:T(8,128)(2,1)S(1)} %slice_bitcast_fusion), channel_id=1, source_target_pairs={{0,24},{1,25},{2,26},{3,27},{4,28},{5,29},{6,30},{7,31},{8,0},{9,1... | collective-permute-start | bytes 811016 | tf_op jit(solution)/shard_map/ppermute | solution.py:35
  61.1 7.1 %shard_map.58 = (f32[1024,256]{1,0:T(8,128)S(1)}, f32[1024,128]{1,0:T(8,128)S(1)}, f32[1024,128]{1,0:T(8,128)S(1)}) custom-call(bf16[528,256]{1,0:T(8,128)(2,1)S(1)} %copy-done.3, bf16[528,256]{1,0:T(8,128)(2,1)S(1)} %collective-permute-done.1.refs_1_, bf16[528,256]{1,0:T(8,128)(2,1)S(1)} %collective-permute-done.2.refs_2_, ...), custom_call_target="tpu_custom_call" | custom-call | bytes 1024 | tf_op jit(solution)/shard_map/pallas_call | solution.py:259
  70.3 2.8 %shard_map.59 = (bf16[512,256]{1,0:T(8,128)(2,1)S(1)}, bf16[512,256]{1,0:T(8,128)(2,1)S(1)}) custom-call(bf16[528,256]{1,0:T(8,128)(2,1)S(1)} %copy-done.3, bf16[528,256]{1,0:T(8,128)(2,1)S(1)} %collective-permute-done.1.refs_1_, bf16[528,256]{1,0:T(8,128)(2,1)S(1)} %collective-permute-done.2.refs_2_, bf16[528,256]{1,0:T(8,128)(2,1)S(1)} %collective-permute-done.3.refs_3_, ...), custom_call_target="tpu_custom_call" | custom-call | bytes 1024 | tf_op jit(solution)/shard_map/pallas_call | solution.py:259
  73.1 2.0 %collective-permute-start.19 = (bf16[2,256,1024]{2,1,0:T(8,128)(2,1)S(1)}, bf16[2,256,1024]{2,1,0:T(8,128)(2,1)S(1)}, u32[]{:S(2)}, u32[]{:S(2)}) collective-permute-start(bf16[2,256,1024]{2,1,0:T(8,128)(2,1)S(1)} %collective-permute-done.18.refs_1_), channel_id=1, source_target_pairs={{0,4},{1,5},{2,6},{3,7},{4,0},{5,1},{6,2},{7,3},{8,12},{9,13},{10,... | collective-permute-start | bytes 3145736 | tf_op jit(solution)/shard_map/ppermute | solution.py:35
  75.2 3.5 %collective-permute-start.16 = (bf16[512,256]{1,0:T(8,128)(2,1)S(1)}, bf16[512,256]{1,0:T(8,128)(2,1)S(1)}, u32[]{:S(2)}, u32[]{:S(2)}) collective-permute-start(bf16[512,256]{1,0:T(8,128)(2,1)S(1)} %get-tuple-element.84.c0), channel_id=1, source_target_pairs={{0,64},{1,65},{2,66},{3,67},{4,68},{5,69},{6,70},{7,71},{8,72},{9,... | collective-permute-start | bytes 786440 | tf_op jit(solution)/shard_map/ppermute | solution.py:35
  79.3 5.1 %collective-permute-done.15.c1 = bf16[512,256]{1,0:T(8,128)(2,1)S(1)} collective-permute-done((bf16[512,256]{1,0:T(8,128)(2,1)S(1)}, bf16[512,256]{1,0:T(8,128)(2,1)S(1)}, u32[]{:S(2)}, u32[]{:S(2)}) %collective-permute-start.15) | collective-permute-done | bytes 262176 | tf_op jit(solution)/shard_map/ppermute | solution.py:35
  84.4 1.6 %collective-permute-done.16.c2 = bf16[512,256]{1,0:T(8,128)(2,1)S(1)} collective-permute-done((bf16[512,256]{1,0:T(8,128)(2,1)S(1)}, bf16[512,256]{1,0:T(8,128)(2,1)S(1)}, u32[]{:S(2)}, u32[]{:S(2)}) %collective-permute-start.16) | collective-permute-done | bytes 262176 | tf_op jit(solution)/shard_map/ppermute | solution.py:35
  86.0 5.0 %collective-permute-done.17.c3 = bf16[512,256]{1,0:T(8,128)(2,1)S(1)} collective-permute-done((bf16[512,256]{1,0:T(8,128)(2,1)S(1)}, bf16[512,256]{1,0:T(8,128)(2,1)S(1)}, u32[]{:S(2)}, u32[]{:S(2)}) %collective-permute-start.17) | collective-permute-done | bytes 262176 | tf_op jit(solution)/shard_map/ppermute | solution.py:35
  92.7 1.5 %collective-permute-start.21 = (bf16[256,512]{1,0:T(8,128)(2,1)S(1)}, bf16[256,512]{1,0:T(8,128)(2,1)S(1)}, u32[]{:S(2)}, u32[]{:S(2)}) collective-permute-start(bf16[256,512]{1,0:T(8,128)(2,1)S(1)} %get-tuple-element.81), channel_id=1, source_target_pairs={{0,3},{1,0},{2,1},{3,2},{4,7},{5,4},{6,5},{7,6},{8,11},{9,8},{10,9... | collective-permute-start | bytes 786440 | tf_op jit(solution)/shard_map/ppermute | solution.py:35
  94.2 1.4 %shard_map.62 = (f32[512,512]{1,0:T(8,128)S(1)}, f32[512,512]{1,0:T(8,128)S(1)}) custom-call(bf16[512,256]{1,0:T(8,128)(2,1)S(1)} %get-tuple-element.84.c0, bf16[512,256]{1,0:T(8,128)(2,1)S(1)} %collective-permute-done.15.c1, bf16[512,256]{1,0:T(8,128)(2,1)S(1)} %collective-permute-done.16.c2, bf16[512,256]{1,0:T(8,128)(2,1)S(1)} %collective-permute-done.17.c3, ...), custom_call_target="tpu_custom_call" | custom-call | bytes 1024 | tf_op jit(solution)/shard_map/pallas_call | solution.py:342
  95.6 4.8 %collective-permute-done.20.upward = bf16[256,512]{1,0:T(8,128)(2,1)S(1)} collective-permute-done((bf16[256,512]{1,0:T(8,128)(2,1)S(1)}, bf16[256,512]{1,0:T(8,128)(2,1)S(1)}, u32[]{:S(2)}, u32[]{:S(2)}) %collective-permute-start.20) | collective-permute-done | bytes 262176 | tf_op jit(solution)/shard_map/ppermute | solution.py:35
  100.4 1.4 %collective-permute-done.21.downward = bf16[256,512]{1,0:T(8,128)(2,1)S(1)} collective-permute-done((bf16[256,512]{1,0:T(8,128)(2,1)S(1)}, bf16[256,512]{1,0:T(8,128)(2,1)S(1)}, u32[]{:S(2)}, u32[]{:S(2)}) %collective-permute-start.21) | collective-permute-done | bytes 262176 | tf_op jit(solution)/shard_map/ppermute | solution.py:35
  102.3 1.7 %collective-permute-start.23 = (bf16[512,512]{1,0:T(8,128)(2,1)S(1)}, bf16[512,512]{1,0:T(8,128)(2,1)S(1)}, u32[]{:S(2)}, u32[]{:S(2)}) collective-permute-start(bf16[512,512]{1,0:T(8,128)(2,1)S(1)} %get-tuple-element.86), channel_id=1, source_target_pairs={{0,3},{1,0},{2,1},{3,2},{4,7},{5,4},{6,5},{7,6},{8,11},{9,8},{10,9... | collective-permute-start | bytes 1572872 | tf_op jit(solution)/shard_map/ppermute | solution.py:35
  104.1 2.2 %copy-done.1 = bf16[4,512,1024]{2,1,0:T(8,128)(2,1)S(1)} copy-done((bf16[4,512,1024]{2,1,0:T(8,128)(2,1)S(1)}, bf16[4,512,1024]{2,1,0:T(8,128)(2,1)}, u32[]{:S(2)}) %copy-start.1) | copy-done | bytes 4194328
  108.3 6.4 %collective-permute-done.22 = bf16[512,512]{1,0:T(8,128)(2,1)S(1)} collective-permute-done((bf16[512,512]{1,0:T(8,128)(2,1)S(1)}, bf16[512,512]{1,0:T(8,128)(2,1)S(1)}, u32[]{:S(2)}, u32[]{:S(2)}) %collective-permute-start.22) | collective-permute-done | bytes 524320 | tf_op jit(solution)/shard_map/ppermute | solution.py:35
  114.7 1.5 %collective-permute-done.23 = bf16[512,512]{1,0:T(8,128)(2,1)S(1)} collective-permute-done((bf16[512,512]{1,0:T(8,128)(2,1)S(1)}, bf16[512,512]{1,0:T(8,128)(2,1)S(1)}, u32[]{:S(2)}, u32[]{:S(2)}) %collective-permute-start.23) | collective-permute-done | bytes 524320 | tf_op jit(solution)/shard_map/ppermute | solution.py:35
  (41 shorter events, 10.6 us)
Async XLA Ops:
  2.2 15.8 %collective-permute-start = (bf16[256,1024]{1,0:T(8,128)(2,1)}, bf16[256,1024]{1,0:T(8,128)(2,1)S(1)}, u32[]{:S(2)}, u32[]{:S(2)}) collective-permute-start(bf16[256,1024]{1,0:T(8,128)(2,1)} %shard_map.55), channel_id=1, source_target_pairs={{64,32},{65,33},{66,34},{67,35},{68,36},{69,37},{70,38},{71,39},{7... | collective-permute-start | bytes 1572872 | tf_op jit(solution)/shard_map/ppermute | solution.py:35
  17.9 14.7 %collective-permute-start.1 = (bf16[528,256]{1,0:T(8,128)(2,1)}, bf16[528,256]{1,0:T(8,128)(2,1)S(1)}, u32[]{:S(2)}, u32[]{:S(2)}) collective-permute-start(bf16[528,256]{1,0:T(8,128)(2,1)} %get-tuple-element.52), channel_id=1, source_target_pairs={{0,32},{1,33},{2,34},{3,35},{4,36},{5,37},{6,38},{7,39},{8,40},{9,... | collective-permute-start | bytes 811016 | tf_op jit(solution)/shard_map/ppermute | solution.py:35
  21.1 11.6 %collective-permute-start.2 = (bf16[528,256]{1,0:T(8,128)(2,1)}, bf16[528,256]{1,0:T(8,128)(2,1)S(1)}, u32[]{:S(2)}, u32[]{:S(2)}) collective-permute-start(bf16[528,256]{1,0:T(8,128)(2,1)} %get-tuple-element.53), channel_id=1, source_target_pairs={{0,64},{1,65},{2,66},{3,67},{4,68},{5,69},{6,70},{7,71},{8,72},{9,... | collective-permute-start | bytes 811016 | tf_op jit(solution)/shard_map/ppermute | solution.py:35
  21.8 13.7 %collective-permute-start.3 = (bf16[528,256]{1,0:T(8,128)(2,1)}, bf16[528,256]{1,0:T(8,128)(2,1)S(1)}, u32[]{:S(2)}, u32[]{:S(2)}) collective-permute-start(bf16[528,256]{1,0:T(8,128)(2,1)} %get-tuple-element.54), channel_id=1, source_target_pairs={{0,96},{1,97},{2,98},{3,99},{4,100},{5,101},{6,102},{7,103},{8,104... | collective-permute-start | bytes 811016 | tf_op jit(solution)/shard_map/ppermute | solution.py:35
  24.0 14.7 %collective-permute-start.4 = (bf16[256,1024]{1,0:T(8,128)(2,1)S(1)}, bf16[256,1024]{1,0:T(8,128)(2,1)S(1)}, u32[]{:S(2)}, u32[]{:S(2)}) collective-permute-start(bf16[256,1024]{1,0:T(8,128)(2,1)S(1)} %collective-permute-done), channel_id=1, source_target_pairs={{0,8},{1,9},{2,10},{3,11},{4,12},{5,13},{6,14},{7,15},{8,0},{9,1},... | collective-permute-start | bytes 1572872 | tf_op jit(solution)/shard_map/ppermute | solution.py:35
  38.8 22.3 %copy-start.3 = (bf16[528,256]{1,0:T(8,128)(2,1)S(1)}, bf16[528,256]{1,0:T(8,128)(2,1)}, u32[]{:S(2)}) copy-start(bf16[528,256]{1,0:T(8,128)(2,1)} %get-tuple-element.51.refs_0_) | copy-start | bytes 811012
  38.8 18.1 %collective-permute-start.7 = (bf16[2,256,1024]{2,1,0:T(8,128)(2,1)S(1)}, bf16[2,256,1024]{2,1,0:T(8,128)(2,1)S(1)}, u32[]{:S(2)}, u32[]{:S(2)}) collective-permute-start(bf16[2,256,1024]{2,1,0:T(8,128)(2,1)S(1)} %pad_maximum_fusion.refs_0_), channel_id=1, source_target_pairs={{0,4},{1,5},{2,6},{3,7},{4,0},{5,1},{6,2},{7,3},{8,12},{9,13},{10,... | collective-permute-start | bytes 3145736 | tf_op jit(solution)/shard_map/ppermute | solution.py:35
  40.9 16.0 %collective-permute-start.5 = (bf16[2,528,256]{2,1,0:T(8,128)(2,1)S(1)}, bf16[2,528,256]{2,1,0:T(8,128)(2,1)S(1)}, u32[]{:S(2)}, u32[]{:S(2)}) collective-permute-start(bf16[2,528,256]{2,1,0:T(8,128)(2,1)S(1)} %pad_maximum_fusion.1.refs_4_), channel_id=1, source_target_pairs={{0,8},{1,9},{2,10},{3,11},{4,12},{5,13},{6,14},{7,15},{8,16},{9,17... | collective-permute-start | bytes 1622024 | tf_op jit(solution)/shard_map/ppermute | solution.py:35
  42.6 14.4 %collective-permute-start.6 = (bf16[2,528,256]{2,1,0:T(8,128)(2,1)S(1)}, bf16[2,528,256]{2,1,0:T(8,128)(2,1)S(1)}, u32[]{:S(2)}, u32[]{:S(2)}) collective-permute-start(bf16[2,528,256]{2,1,0:T(8,128)(2,1)S(1)} %pad_maximum_fusion.1.refs_4_), channel_id=1, source_target_pairs={{0,24},{1,25},{2,26},{3,27},{4,28},{5,29},{6,30},{7,31},{8,0},{9,1... | collective-permute-start | bytes 1622024 | tf_op jit(solution)/shard_map/ppermute | solution.py:35
  44.2 14.9 %collective-permute-start.10 = (bf16[2,528,256]{2,1,0:T(8,128)(2,1)S(1)}, bf16[2,528,256]{2,1,0:T(8,128)(2,1)S(1)}, u32[]{:S(2)}, u32[]{:S(2)}) collective-permute-start(bf16[2,528,256]{2,1,0:T(8,128)(2,1)S(1)} %pad_maximum_fusion.1.refs_4_), channel_id=1, source_target_pairs={{0,4},{1,5},{2,6},{3,7},{4,0},{5,1},{6,2},{7,3},{8,12},{9,13},{10,... | collective-permute-start | bytes 1622024 | tf_op jit(solution)/shard_map/ppermute | solution.py:35
  44.3 28.8 %collective-permute-start.18 = (bf16[2,256,1024]{2,1,0:T(8,128)(2,1)S(1)}, bf16[2,256,1024]{2,1,0:T(8,128)(2,1)S(1)}, u32[]{:S(2)}, u32[]{:S(2)}) collective-permute-start(bf16[2,256,1024]{2,1,0:T(8,128)(2,1)S(1)} %pad_maximum_fusion.refs_0_), channel_id=1, source_target_pairs={{0,32},{1,33},{2,34},{3,35},{4,36},{5,37},{6,38},{7,39},{8,40},{9,... | collective-permute-start | bytes 3145736 | tf_op jit(solution)/shard_map/ppermute | solution.py:35
  57.0 4.1 %collective-permute-start.11 = (bf16[2,528,256]{2,1,0:T(8,128)(2,1)S(1)}, bf16[2,528,256]{2,1,0:T(8,128)(2,1)S(1)}, u32[]{:S(2)}, u32[]{:S(2)}) collective-permute-start(bf16[2,528,256]{2,1,0:T(8,128)(2,1)S(1)} %collective-permute-done.5.refs_5_), channel_id=1, source_target_pairs={{0,4},{1,5},{2,6},{3,7},{4,0},{5,1},{6,2},{7,3},{8,12},{9,13},{10,... | collective-permute-start | bytes 1622024 | tf_op jit(solution)/shard_map/ppermute | solution.py:35
  57.0 4.1 %collective-permute-start.12 = (bf16[2,528,256]{2,1,0:T(8,128)(2,1)S(1)}, bf16[2,528,256]{2,1,0:T(8,128)(2,1)S(1)}, u32[]{:S(2)}, u32[]{:S(2)}) collective-permute-start(bf16[2,528,256]{2,1,0:T(8,128)(2,1)S(1)} %collective-permute-done.6.refs_6_), channel_id=1, source_target_pairs={{0,4},{1,5},{2,6},{3,7},{4,0},{5,1},{6,2},{7,3},{8,12},{9,13},{10,... | collective-permute-start | bytes 1622024 | tf_op jit(solution)/shard_map/ppermute | solution.py:35
  57.5 10.7 %collective-permute-start.8 = (bf16[528,256]{1,0:T(8,128)(2,1)S(1)}, bf16[528,256]{1,0:T(8,128)(2,1)S(1)}, u32[]{:S(2)}, u32[]{:S(2)}) collective-permute-start(bf16[528,256]{1,0:T(8,128)(2,1)S(1)} %slice_bitcast_fusion.1), channel_id=1, source_target_pairs={{0,8},{1,9},{2,10},{3,11},{4,12},{5,13},{6,14},{7,15},{8,16},{9,17... | collective-permute-start | bytes 811016 | tf_op jit(solution)/shard_map/ppermute | solution.py:35
  59.2 19.6 %copy-start.2 = (bf16[2048,1024]{1,0:T(8,128)(2,1)S(1)}, bf16[2048,1024]{1,0:T(8,128)(2,1)}, u32[]{:S(2)}) copy-start(bf16[2048,1024]{1,0:T(8,128)(2,1)} %shard_map.57.refs_4_) | copy-start | bytes 12582916
  59.2 9.1 %collective-permute-start.9 = (bf16[528,256]{1,0:T(8,128)(2,1)S(1)}, bf16[528,256]{1,0:T(8,128)(2,1)S(1)}, u32[]{:S(2)}, u32[]{:S(2)}) collective-permute-start(bf16[528,256]{1,0:T(8,128)(2,1)S(1)} %slice_bitcast_fusion), channel_id=1, source_target_pairs={{0,24},{1,25},{2,26},{3,27},{4,28},{5,29},{6,30},{7,31},{8,0},{9,1... | collective-permute-start | bytes 811016 | tf_op jit(solution)/shard_map/ppermute | solution.py:35
  68.2 1.6 %collective-permute-start.13 = (bf16[1,528,256]{2,1,0:T(8,128)(2,1)S(1)}, bf16[1,528,256]{2,1,0:T(8,128)(2,1)S(1)}, u32[]{:S(2)}, u32[]{:S(2)}) collective-permute-start(bf16[1,528,256]{2,1,0:T(8,128)(2,1)S(1)} %bitcast.13), channel_id=1, source_target_pairs={{0,4},{1,5},{2,6},{3,7},{4,0},{5,1},{6,2},{7,3},{8,12},{9,13},{10,... | collective-permute-start | bytes 811016 | tf_op jit(solution)/shard_map/ppermute | solution.py:35
  68.3 1.9 %collective-permute-start.14 = (bf16[1,528,256]{2,1,0:T(8,128)(2,1)S(1)}, bf16[1,528,256]{2,1,0:T(8,128)(2,1)S(1)}, u32[]{:S(2)}, u32[]{:S(2)}) collective-permute-start(bf16[1,528,256]{2,1,0:T(8,128)(2,1)S(1)} %bitcast.15), channel_id=1, source_target_pairs={{0,4},{1,5},{2,6},{3,7},{4,0},{5,1},{6,2},{7,3},{8,12},{9,13},{10,... | collective-permute-start | bytes 811016 | tf_op jit(solution)/shard_map/ppermute | solution.py:35
  73.1 5.7 %collective-permute-start.19 = (bf16[2,256,1024]{2,1,0:T(8,128)(2,1)S(1)}, bf16[2,256,1024]{2,1,0:T(8,128)(2,1)S(1)}, u32[]{:S(2)}, u32[]{:S(2)}) collective-permute-start(bf16[2,256,1024]{2,1,0:T(8,128)(2,1)S(1)} %collective-permute-done.18.refs_1_), channel_id=1, source_target_pairs={{0,4},{1,5},{2,6},{3,7},{4,0},{5,1},{6,2},{7,3},{8,12},{9,13},{10,... | collective-permute-start | bytes 3145736 | tf_op jit(solution)/shard_map/ppermute | solution.py:35
  75.2 9.2 %collective-permute-start.15 = (bf16[512,256]{1,0:T(8,128)(2,1)S(1)}, bf16[512,256]{1,0:T(8,128)(2,1)S(1)}, u32[]{:S(2)}, u32[]{:S(2)}) collective-permute-start(bf16[512,256]{1,0:T(8,128)(2,1)S(1)} %get-tuple-element.71), channel_id=1, source_target_pairs={{0,32},{1,33},{2,34},{3,35},{4,36},{5,37},{6,38},{7,39},{8,40},{9,... | collective-permute-start | bytes 786440 | tf_op jit(solution)/shard_map/ppermute | solution.py:35
  75.2 10.8 %collective-permute-start.16 = (bf16[512,256]{1,0:T(8,128)(2,1)S(1)}, bf16[512,256]{1,0:T(8,128)(2,1)S(1)}, u32[]{:S(2)}, u32[]{:S(2)}) collective-permute-start(bf16[512,256]{1,0:T(8,128)(2,1)S(1)} %get-tuple-element.84.c0), channel_id=1, source_target_pairs={{0,64},{1,65},{2,66},{3,67},{4,68},{5,69},{6,70},{7,71},{8,72},{9,... | collective-permute-start | bytes 786440 | tf_op jit(solution)/shard_map/ppermute | solution.py:35
  78.8 12.3 %collective-permute-start.17 = (bf16[512,256]{1,0:T(8,128)(2,1)S(1)}, bf16[512,256]{1,0:T(8,128)(2,1)S(1)}, u32[]{:S(2)}, u32[]{:S(2)}) collective-permute-start(bf16[512,256]{1,0:T(8,128)(2,1)S(1)} %get-tuple-element.71), channel_id=1, source_target_pairs={{0,96},{1,97},{2,98},{3,99},{4,100},{5,101},{6,102},{7,103},{8,104... | collective-permute-start | bytes 786440 | tf_op jit(solution)/shard_map/ppermute | solution.py:35
  79.3 16.3 %copy-start = (bf16[4,512,1024]{2,1,0:T(8,128)(2,1)}, bf16[4,512,1024]{2,1,0:T(8,128)(2,1)S(1)}, u32[]{:S(2)}) copy-start(bf16[4,512,1024]{2,1,0:T(8,128)(2,1)S(1)} %shard_map.60.held) | copy-start | bytes 12582916
  91.9 8.5 %collective-permute-start.20 = (bf16[256,512]{1,0:T(8,128)(2,1)S(1)}, bf16[256,512]{1,0:T(8,128)(2,1)S(1)}, u32[]{:S(2)}, u32[]{:S(2)}) collective-permute-start(bf16[256,512]{1,0:T(8,128)(2,1)S(1)} %get-tuple-element.80), channel_id=1, source_target_pairs={{0,1},{1,2},{2,3},{3,0},{4,5},{5,6},{6,7},{7,4},{8,9},{9,10},{10,1... | collective-permute-start | bytes 786440 | tf_op jit(solution)/shard_map/ppermute | solution.py:35
  92.7 9.2 %collective-permute-start.21 = (bf16[256,512]{1,0:T(8,128)(2,1)S(1)}, bf16[256,512]{1,0:T(8,128)(2,1)S(1)}, u32[]{:S(2)}, u32[]{:S(2)}) collective-permute-start(bf16[256,512]{1,0:T(8,128)(2,1)S(1)} %get-tuple-element.81), channel_id=1, source_target_pairs={{0,3},{1,0},{2,1},{3,2},{4,7},{5,4},{6,5},{7,6},{8,11},{9,8},{10,9... | collective-permute-start | bytes 786440 | tf_op jit(solution)/shard_map/ppermute | solution.py:35
  102.0 12.7 %collective-permute-start.22 = (bf16[512,512]{1,0:T(8,128)(2,1)S(1)}, bf16[512,512]{1,0:T(8,128)(2,1)S(1)}, u32[]{:S(2)}, u32[]{:S(2)}) collective-permute-start(bf16[512,512]{1,0:T(8,128)(2,1)S(1)} %get-tuple-element.85), channel_id=1, source_target_pairs={{0,1},{1,2},{2,3},{3,0},{4,5},{5,6},{6,7},{7,4},{8,9},{9,10},{10,1... | collective-permute-start | bytes 1572872 | tf_op jit(solution)/shard_map/ppermute | solution.py:35
  102.3 13.9 %collective-permute-start.23 = (bf16[512,512]{1,0:T(8,128)(2,1)S(1)}, bf16[512,512]{1,0:T(8,128)(2,1)S(1)}, u32[]{:S(2)}, u32[]{:S(2)}) collective-permute-start(bf16[512,512]{1,0:T(8,128)(2,1)S(1)} %get-tuple-element.86), channel_id=1, source_target_pairs={{0,3},{1,0},{2,1},{3,2},{4,7},{5,4},{6,5},{7,6},{8,11},{9,8},{10,9... | collective-permute-start | bytes 1572872 | tf_op jit(solution)/shard_map/ppermute | solution.py:35
  104.1 2.2 %copy-start.1 = (bf16[4,512,1024]{2,1,0:T(8,128)(2,1)S(1)}, bf16[4,512,1024]{2,1,0:T(8,128)(2,1)}, u32[]{:S(2)}) copy-start(bf16[4,512,1024]{2,1,0:T(8,128)(2,1)} %copy-done) | copy-start | bytes 12582916

commit v5 on v4

--- a/solution.py
+++ b/solution.py
@@ -407,14 +407,13 @@
     early = jnp.where(is_encoder, own, jnp.where(z == 2, r1, r3))
     late = jnp.where(z == 0, r3, jnp.where(z == 1, r1, r2))
     pair = jnp.stack([early, late])
-    pair, p, beside = lax.optimization_barrier((pair, p, beside))
+    pair, p = lax.optimization_barrier((pair, p))
 
     y1, y3 = along_y(pair, 1), along_y(pair, 3)
     lower = jnp.stack([p, beside])
-    lower_twin = other_core(lower, encoder)
     upper = moved(lower, flip, encoder)
     (mine,) = second_half(after(proj_weights, pair), jnp.int32(2), half // 2, 2, 1)
-    y1, y3, mine, lower_twin = lax.optimization_barrier((y1, y3, mine, lower_twin))
+    y1, y3, mine = lax.optimization_barrier((y1, y3, mine))
 
     far0, far1 = along_y(y1[0], 1), along_y(y3[1], 3)
     slabs = [own, r1, r2, r3]
@@ -425,6 +424,7 @@
     blocks = [far0[None], far1[None]]
     blocks = blocks + [other_core(b) for b in blocks]
     ca, cb = attend(slabs, blocks, chunks, state)
+    lower_twin = other_core(after(lower, state[0]), encoder)
     upper_twin = other_core(after(upper, ca), encoder)
     contexts = [ca, along_z(cb, 1), along_z(ca, 2), along_z(cb, 3)]
     sources = [lower, upper, lower_twin, upper_twin, mine]

time: 118 us -> 112 us (0.949)
  waiting for transfers between devices: 41.7 us -> 37.8 us
  starting transfers between devices: 34.4 us -> 33.1 us
    ppermute x24, waiting for transfers between devices: 41.7 us -> 37.8 us  [moved(): return lax.ppermute(block, AXES, route)]
    ppermute x24, starting transfers between devices: 34.4 us -> 33.1 us  [moved(): return lax.ppermute(block, AXES, route)]
  transfers between devices with their start and end apart: 24 -> 24, of which waited for: 14 -> 11; matrix products, arithmetic and copies ran while one was open for 2% -> 2% of each run, Pallas kernels for 27% -> 28%
where the time goes in v5:
time: 112 us
  waiting for transfers between devices  37.8 us (34%)
  Pallas kernels  34.4 us (31%)
  starting transfers between devices  33.1 us (30%)
  other arithmetic  3.39 us (3%)
  local copies, waits for them, and re-layouts  2.24 us (2%)
    ppermute x24, waiting for transfers between devices, moved(): return lax.ppermute(block, AXES, route)  37.8 us
    ppermute x24, starting transfers between devices, moved(): return lax.ppermute(block, AXES, route)  33.1 us
    pallas_call x1, Pallas kernels, section(): pl.pallas_call(section_kernel, grid_spec=pltpu.PrefetchScalarGridSpec(num...  13.5 us
    pallas_call x2, Pallas kernels, attend(): pl.pallas_call(functools.partial(attend_kernel, first, half, chunks), in_...  9.74 us
    pallas_call x2, Pallas kernels, second_half(): pl.pallas_call(second_half_kernel, grid_spec=pltpu.PrefetchScalarGridSpec...  7.52 us
    pallas_call x3, Pallas kernels, project(): pl.pallas_call(functools.partial(project_kernel, distances), in_specs=[vm...  3.09 us
  transfers between devices with their start and end apart: 24, of which 11 were waited for; matrix products, arithmetic and copies ran while one was open for 2% of the time, Pallas kernels for 28%

profile of v5, /device:TPU:38, one launch (start us, length us, event | category | flops | bytes accessed | tf_op | source)
XLA Modules:
  0.0 111.9 jit_solution(6989624849168573479)
XLA Ops:
  0.0 2.2 %shard_map.55 = bf16[256,1024]{1,0:T(8,128)(2,1)} custom-call(s32[1]{0:T(128)} %bitcast.start_ref, bf16[1,4096,2,1024]{3,2,1,0:T(2,128)(2,1)} %w_ref.4), custom_call_target="tpu_custom_call" | custom-call | bytes 1024 | tf_op jit(solution)/shard_map/pallas_call | solution.py:169
  2.2 1.3 %collective-permute-start = (bf16[256,1024]{1,0:T(8,128)(2,1)}, bf16[256,1024]{1,0:T(8,128)(2,1)S(1)}, u32[]{:S(2)}, u32[]{:S(2)}) collective-permute-start(bf16[256,1024]{1,0:T(8,128)(2,1)} %shard_map.55), channel_id=1, source_target_pairs={{64,32},{65,33},{66,34},{67,35},{68,36},{69,37},{70,38},{71,39},{7... | collective-permute-start | bytes 1572872 | tf_op jit(solution)/shard_map/ppermute | solution.py:35
  4.1 13.5 %shard_map.56 = (bf16[528,256]{1,0:T(8,128)(2,1)}, bf16[528,256]{1,0:T(8,128)(2,1)}, bf16[528,256]{1,0:T(8,128)(2,1)}, bf16[528,256]{1,0:T(8,128)(2,1)}) custom-call(s32[1]{0:T(128)S(6)} %copy.6.pad_ref, bf16[256,4096]{1,0:T(8,128)(2,1)} %memory.1, bf16[512,4096]{1,0:T(8,128)(2,1)} %targets.1, f32[1,4096]{1,0:T(1,128)} %gain_ref.1, ...), custom_call_target="tpu_custom_call" | custom-call | bytes 1024 | tf_op jit(solution)/shard_map/pallas_call | solution.py:134
  17.9 3.2 %collective-permute-start.1 = (bf16[528,256]{1,0:T(8,128)(2,1)}, bf16[528,256]{1,0:T(8,128)(2,1)S(1)}, u32[]{:S(2)}, u32[]{:S(2)}) collective-permute-start(bf16[528,256]{1,0:T(8,128)(2,1)} %get-tuple-element.51), channel_id=1, source_target_pairs={{0,32},{1,33},{2,34},{3,35},{4,36},{5,37},{6,38},{7,39},{8,40},{9,... | collective-permute-start | bytes 811016 | tf_op jit(solution)/shard_map/ppermute | solution.py:35
  21.8 2.3 %collective-permute-start.3 = (bf16[528,256]{1,0:T(8,128)(2,1)}, bf16[528,256]{1,0:T(8,128)(2,1)S(1)}, u32[]{:S(2)}, u32[]{:S(2)}) collective-permute-start(bf16[528,256]{1,0:T(8,128)(2,1)} %get-tuple-element.53), channel_id=1, source_target_pairs={{0,96},{1,97},{2,98},{3,99},{4,100},{5,101},{6,102},{7,103},{8,104... | collective-permute-start | bytes 811016 | tf_op jit(solution)/shard_map/ppermute | solution.py:35
  24.0 3.5 %collective-permute-start.16 = (bf16[256,1024]{1,0:T(8,128)(2,1)S(1)}, bf16[256,1024]{1,0:T(8,128)(2,1)S(1)}, u32[]{:S(2)}, u32[]{:S(2)}) collective-permute-start(bf16[256,1024]{1,0:T(8,128)(2,1)S(1)} %collective-permute-done), channel_id=1, source_target_pairs={{0,8},{1,9},{2,10},{3,11},{4,12},{5,13},{6,14},{7,15},{8,0},{9,1},... | collective-permute-start | bytes 1572872 | tf_op jit(solution)/shard_map/ppermute | solution.py:35
  27.5 5.1 %collective-permute-done.1.refs_1_ = bf16[528,256]{1,0:T(8,128)(2,1)S(1)} collective-permute-done((bf16[528,256]{1,0:T(8,128)(2,1)}, bf16[528,256]{1,0:T(8,128)(2,1)S(1)}, u32[]{:S(2)}, u32[]{:S(2)}) %collective-permute-start.1) | collective-permute-done | bytes 270368 | tf_op jit(solution)/shard_map/ppermute | solution.py:35
  32.6 2.8 %collective-permute-done.3.refs_3_ = bf16[528,256]{1,0:T(8,128)(2,1)S(1)} collective-permute-done((bf16[528,256]{1,0:T(8,128)(2,1)}, bf16[528,256]{1,0:T(8,128)(2,1)S(1)}, u32[]{:S(2)}, u32[]{:S(2)}) %collective-permute-start.3) | collective-permute-done | bytes 270368 | tf_op jit(solution)/shard_map/ppermute | solution.py:35
  36.5 1.6 %collective-permute-start.4 = (bf16[2,528,256]{2,1,0:T(8,128)(2,1)S(1)}, bf16[2,528,256]{2,1,0:T(8,128)(2,1)S(1)}, u32[]{:S(2)}, u32[]{:S(2)}) collective-permute-start(bf16[2,528,256]{2,1,0:T(8,128)(2,1)S(1)} %pad_maximum_fusion.1.refs_4_), channel_id=1, source_target_pairs={{0,8},{1,9},{2,10},{3,11},{4,12},{5,13},{6,14},{7,15},{8,16},{9,17... | collective-permute-start | bytes 1622024 | tf_op jit(solution)/shard_map/ppermute | solution.py:35
  38.2 1.7 %collective-permute-start.5 = (bf16[2,528,256]{2,1,0:T(8,128)(2,1)S(1)}, bf16[2,528,256]{2,1,0:T(8,128)(2,1)S(1)}, u32[]{:S(2)}, u32[]{:S(2)}) collective-permute-start(bf16[2,528,256]{2,1,0:T(8,128)(2,1)S(1)} %pad_maximum_fusion.1.refs_4_), channel_id=1, source_target_pairs={{0,24},{1,25},{2,26},{3,27},{4,28},{5,29},{6,30},{7,31},{8,0},{9,1... | collective-permute-start | bytes 1622024 | tf_op jit(solution)/shard_map/ppermute | solution.py:35
  40.0 2.8 %collective-permute-start.17 = (bf16[2,256,1024]{2,1,0:T(8,128)(2,1)S(1)}, bf16[2,256,1024]{2,1,0:T(8,128)(2,1)S(1)}, u32[]{:S(2)}, u32[]{:S(2)}) collective-permute-start(bf16[2,256,1024]{2,1,0:T(8,128)(2,1)S(1)} %pad_maximum_fusion.refs_0_), channel_id=1, source_target_pairs={{0,32},{1,33},{2,34},{3,35},{4,36},{5,37},{6,38},{7,39},{8,40},{9,... | collective-permute-start | bytes 3145736 | tf_op jit(solution)/shard_map/ppermute | solution.py:35
  42.8 5.4 %shard_map.57.refs_4_ = bf16[2048,1024]{1,0:T(8,128)(2,1)} custom-call(s32[1]{0:T(128)} %constant.70.clone.1.start_ref, bf16[1,4096,2,1024]{3,2,1,0:T(2,128)(2,1)} %w_ref.4), custom_call_target="tpu_custom_call" | custom-call | bytes 1024 | tf_op jit(solution)/shard_map/pallas_call | solution.py:169
  48.2 3.0 %collective-permute-done.4.refs_5_ = bf16[2,528,256]{2,1,0:T(8,128)(2,1)S(1)} collective-permute-done((bf16[2,528,256]{2,1,0:T(8,128)(2,1)S(1)}, bf16[2,528,256]{2,1,0:T(8,128)(2,1)S(1)}, u32[]{:S(2)}, u32[]{:S(2)}) %collective-permute-start.4) | collective-permute-done | bytes 540704 | tf_op jit(solution)/shard_map/ppermute | solution.py:35
  51.8 1.6 %collective-permute-start.6 = (bf16[528,256]{1,0:T(8,128)(2,1)S(1)}, bf16[528,256]{1,0:T(8,128)(2,1)S(1)}, u32[]{:S(2)}, u32[]{:S(2)}) collective-permute-start(bf16[528,256]{1,0:T(8,128)(2,1)S(1)} %slice_bitcast_fusion.1), channel_id=1, source_target_pairs={{0,8},{1,9},{2,10},{3,11},{4,12},{5,13},{6,14},{7,15},{8,16},{9,17... | collective-permute-start | bytes 811016 | tf_op jit(solution)/shard_map/ppermute | solution.py:35
  53.5 1.9 %collective-permute-start.7 = (bf16[528,256]{1,0:T(8,128)(2,1)S(1)}, bf16[528,256]{1,0:T(8,128)(2,1)S(1)}, u32[]{:S(2)}, u32[]{:S(2)}) collective-permute-start(bf16[528,256]{1,0:T(8,128)(2,1)S(1)} %slice_bitcast_fusion), channel_id=1, source_target_pairs={{0,24},{1,25},{2,26},{3,27},{4,28},{5,29},{6,30},{7,31},{8,0},{9,1... | collective-permute-start | bytes 811016 | tf_op jit(solution)/shard_map/ppermute | solution.py:35
  55.4 6.9 %shard_map.58 = (f32[1024,256]{1,0:T(8,128)S(1)}, f32[1024,128]{1,0:T(8,128)S(1)}, f32[1024,128]{1,0:T(8,128)S(1)}) custom-call(bf16[528,256]{1,0:T(8,128)(2,1)S(1)} %copy-done.3, bf16[528,256]{1,0:T(8,128)(2,1)S(1)} %collective-permute-done.1.refs_1_, bf16[528,256]{1,0:T(8,128)(2,1)S(1)} %collective-permute-done.2.refs_2_, ...), custom_call_target="tpu_custom_call" | custom-call | bytes 1024 | tf_op jit(solution)/shard_map/pallas_call | solution.py:259
  62.9 2.0 %collective-permute-start.18 = (bf16[2,256,1024]{2,1,0:T(8,128)(2,1)S(1)}, bf16[2,256,1024]{2,1,0:T(8,128)(2,1)S(1)}, u32[]{:S(2)}, u32[]{:S(2)}) collective-permute-start(bf16[2,256,1024]{2,1,0:T(8,128)(2,1)S(1)} %pad_maximum_fusion.refs_0_), channel_id=1, source_target_pairs={{0,4},{1,5},{2,6},{3,7},{4,0},{5,1},{6,2},{7,3},{8,12},{9,13},{10,... | collective-permute-start | bytes 3145736 | tf_op jit(solution)/shard_map/ppermute | solution.py:35
  65.0 2.8 %shard_map.59 = (bf16[512,256]{1,0:T(8,128)(2,1)S(1)}, bf16[512,256]{1,0:T(8,128)(2,1)S(1)}) custom-call(bf16[528,256]{1,0:T(8,128)(2,1)S(1)} %copy-done.3, bf16[528,256]{1,0:T(8,128)(2,1)S(1)} %collective-permute-done.1.refs_1_, bf16[528,256]{1,0:T(8,128)(2,1)S(1)} %collective-permute-done.2.refs_2_, bf16[528,256]{1,0:T(8,128)(2,1)S(1)} %collective-permute-done.3.refs_3_, ...), custom_call_target="tpu_custom_call" | custom-call | bytes 1024 | tf_op jit(solution)/shard_map/pallas_call | solution.py:259
  67.8 2.3 %collective-permute-start.19 = (bf16[2,256,1024]{2,1,0:T(8,128)(2,1)S(1)}, bf16[2,256,1024]{2,1,0:T(8,128)(2,1)S(1)}, u32[]{:S(2)}, u32[]{:S(2)}) collective-permute-start(bf16[2,256,1024]{2,1,0:T(8,128)(2,1)S(1)} %collective-permute-done.17.refs_1_), channel_id=1, source_target_pairs={{0,4},{1,5},{2,6},{3,7},{4,0},{5,1},{6,2},{7,3},{8,12},{9,13},{10,... | collective-permute-start | bytes 3145736 | tf_op jit(solution)/shard_map/ppermute | solution.py:35
  70.2 2.7 %collective-permute-start.14 = (bf16[512,256]{1,0:T(8,128)(2,1)S(1)}, bf16[512,256]{1,0:T(8,128)(2,1)S(1)}, u32[]{:S(2)}, u32[]{:S(2)}) collective-permute-start(bf16[512,256]{1,0:T(8,128)(2,1)S(1)} %get-tuple-element.82.c0), channel_id=1, source_target_pairs={{0,64},{1,65},{2,66},{3,67},{4,68},{5,69},{6,70},{7,71},{8,72},{9,... | collective-permute-start | bytes 786440 | tf_op jit(solution)/shard_map/ppermute | solution.py:35
  73.4 6.0 %collective-permute-done.13.c1 = bf16[512,256]{1,0:T(8,128)(2,1)S(1)} collective-permute-done((bf16[512,256]{1,0:T(8,128)(2,1)S(1)}, bf16[512,256]{1,0:T(8,128)(2,1)S(1)}, u32[]{:S(2)}, u32[]{:S(2)}) %collective-permute-start.13) | collective-permute-done | bytes 262176 | tf_op jit(solution)/shard_map/ppermute | solution.py:35
  79.3 1.6 %collective-permute-done.14.c2 = bf16[512,256]{1,0:T(8,128)(2,1)S(1)} collective-permute-done((bf16[512,256]{1,0:T(8,128)(2,1)S(1)}, bf16[512,256]{1,0:T(8,128)(2,1)S(1)}, u32[]{:S(2)}, u32[]{:S(2)}) %collective-permute-start.14) | collective-permute-done | bytes 262176 | tf_op jit(solution)/shard_map/ppermute | solution.py:35
  81.0 4.7 %collective-permute-done.15.c3 = bf16[512,256]{1,0:T(8,128)(2,1)S(1)} collective-permute-done((bf16[512,256]{1,0:T(8,128)(2,1)S(1)}, bf16[512,256]{1,0:T(8,128)(2,1)S(1)}, u32[]{:S(2)}, u32[]{:S(2)}) %collective-permute-start.15) | collective-permute-done | bytes 262176 | tf_op jit(solution)/shard_map/ppermute | solution.py:35
  87.3 1.6 %collective-permute-start.21 = (bf16[256,512]{1,0:T(8,128)(2,1)S(1)}, bf16[256,512]{1,0:T(8,128)(2,1)S(1)}, u32[]{:S(2)}, u32[]{:S(2)}) collective-permute-start(bf16[256,512]{1,0:T(8,128)(2,1)S(1)} %get-tuple-element.79), channel_id=1, source_target_pairs={{0,3},{1,0},{2,1},{3,2},{4,7},{5,4},{6,5},{7,6},{8,11},{9,8},{10,9... | collective-permute-start | bytes 786440 | tf_op jit(solution)/shard_map/ppermute | solution.py:35
  88.9 1.4 %shard_map.62 = (f32[512,512]{1,0:T(8,128)S(1)}, f32[512,512]{1,0:T(8,128)S(1)}) custom-call(bf16[512,256]{1,0:T(8,128)(2,1)S(1)} %get-tuple-element.82.c0, bf16[512,256]{1,0:T(8,128)(2,1)S(1)} %collective-permute-done.13.c1, bf16[512,256]{1,0:T(8,128)(2,1)S(1)} %collective-permute-done.14.c2, bf16[512,256]{1,0:T(8,128)(2,1)S(1)} %collective-permute-done.15.c3, ...), custom_call_target="tpu_custom_call" | custom-call | bytes 1024 | tf_op jit(solution)/shard_map/pallas_call | solution.py:342
  90.3 4.8 %collective-permute-done.20.upward = bf16[256,512]{1,0:T(8,128)(2,1)S(1)} collective-permute-done((bf16[256,512]{1,0:T(8,128)(2,1)S(1)}, bf16[256,512]{1,0:T(8,128)(2,1)S(1)}, u32[]{:S(2)}, u32[]{:S(2)}) %collective-permute-start.20) | collective-permute-done | bytes 262176 | tf_op jit(solution)/shard_map/ppermute | solution.py:35
  95.1 1.4 %collective-permute-done.21.downward = bf16[256,512]{1,0:T(8,128)(2,1)S(1)} collective-permute-done((bf16[256,512]{1,0:T(8,128)(2,1)S(1)}, bf16[256,512]{1,0:T(8,128)(2,1)S(1)}, u32[]{:S(2)}, u32[]{:S(2)}) %collective-permute-start.21) | collective-permute-done | bytes 262176 | tf_op jit(solution)/shard_map/ppermute | solution.py:35
  97.0 1.7 %collective-permute-start.23 = (bf16[512,512]{1,0:T(8,128)(2,1)S(1)}, bf16[512,512]{1,0:T(8,128)(2,1)S(1)}, u32[]{:S(2)}, u32[]{:S(2)}) collective-permute-start(bf16[512,512]{1,0:T(8,128)(2,1)S(1)} %get-tuple-element.84), channel_id=1, source_target_pairs={{0,3},{1,0},{2,1},{3,2},{4,7},{5,4},{6,5},{7,6},{8,11},{9,8},{10,9... | collective-permute-start | bytes 1572872 | tf_op jit(solution)/shard_map/ppermute | solution.py:35
  98.7 2.2 %copy-done.1 = bf16[4,512,1024]{2,1,0:T(8,128)(2,1)S(1)} copy-done((bf16[4,512,1024]{2,1,0:T(8,128)(2,1)S(1)}, bf16[4,512,1024]{2,1,0:T(8,128)(2,1)}, u32[]{:S(2)}) %copy-start.1) | copy-done | bytes 4194328
  101.7 1.2 %convert_add_fusion = f32[512,512]{1,0:T(8,128)S(1)} fusion(f32[512,512]{1,0:T(8,128)S(1)} %shard_map.64, bf16[512,4096]{1,0:T(8,128)(2,1)} %targets.1, s32[]{:T(128)S(6)} %select_n.51), kind=kLoop, calls=%fused_computation.2 | loop fusion | flops 524288 | bytes 2621444 | tf_op jit(solution)/shard_map/add | solution.py:440
  102.9 6.4 %collective-permute-done.22 = bf16[512,512]{1,0:T(8,128)(2,1)S(1)} collective-permute-done((bf16[512,512]{1,0:T(8,128)(2,1)S(1)}, bf16[512,512]{1,0:T(8,128)(2,1)S(1)}, u32[]{:S(2)}, u32[]{:S(2)}) %collective-permute-start.22) | collective-permute-done | bytes 524320 | tf_op jit(solution)/shard_map/ppermute | solution.py:35
  109.3 1.5 %collective-permute-done.23 = bf16[512,512]{1,0:T(8,128)(2,1)S(1)} collective-permute-done((bf16[512,512]{1,0:T(8,128)(2,1)S(1)}, bf16[512,512]{1,0:T(8,128)(2,1)S(1)}, u32[]{:S(2)}, u32[]{:S(2)}) %collective-permute-start.23) | collective-permute-done | bytes 524320 | tf_op jit(solution)/shard_map/ppermute | solution.py:35
  (41 shorter events, 7.9 us)
Async XLA Ops:
  2.2 15.8 %collective-permute-start = (bf16[256,1024]{1,0:T(8,128)(2,1)}, bf16[256,1024]{1,0:T(8,128)(2,1)S(1)}, u32[]{:S(2)}, u32[]{:S(2)}) collective-permute-start(bf16[256,1024]{1,0:T(8,128)(2,1)} %shard_map.55), channel_id=1, source_target_pairs={{64,32},{65,33},{66,34},{67,35},{68,36},{69,37},{70,38},{71,39},{7... | collective-permute-start | bytes 1572872 | tf_op jit(solution)/shard_map/ppermute | solution.py:35
  17.9 14.7 %collective-permute-start.1 = (bf16[528,256]{1,0:T(8,128)(2,1)}, bf16[528,256]{1,0:T(8,128)(2,1)S(1)}, u32[]{:S(2)}, u32[]{:S(2)}) collective-permute-start(bf16[528,256]{1,0:T(8,128)(2,1)} %get-tuple-element.51), channel_id=1, source_target_pairs={{0,32},{1,33},{2,34},{3,35},{4,36},{5,37},{6,38},{7,39},{8,40},{9,... | collective-permute-start | bytes 811016 | tf_op jit(solution)/shard_map/ppermute | solution.py:35
  21.1 11.6 %collective-permute-start.2 = (bf16[528,256]{1,0:T(8,128)(2,1)}, bf16[528,256]{1,0:T(8,128)(2,1)S(1)}, u32[]{:S(2)}, u32[]{:S(2)}) collective-permute-start(bf16[528,256]{1,0:T(8,128)(2,1)} %get-tuple-element.52), channel_id=1, source_target_pairs={{0,64},{1,65},{2,66},{3,67},{4,68},{5,69},{6,70},{7,71},{8,72},{9,... | collective-permute-start | bytes 811016 | tf_op jit(solution)/shard_map/ppermute | solution.py:35
  21.8 13.7 %collective-permute-start.3 = (bf16[528,256]{1,0:T(8,128)(2,1)}, bf16[528,256]{1,0:T(8,128)(2,1)S(1)}, u32[]{:S(2)}, u32[]{:S(2)}) collective-permute-start(bf16[528,256]{1,0:T(8,128)(2,1)} %get-tuple-element.53), channel_id=1, source_target_pairs={{0,96},{1,97},{2,98},{3,99},{4,100},{5,101},{6,102},{7,103},{8,104... | collective-permute-start | bytes 811016 | tf_op jit(solution)/shard_map/ppermute | solution.py:35
  24.0 15.8 %collective-permute-start.16 = (bf16[256,1024]{1,0:T(8,128)(2,1)S(1)}, bf16[256,1024]{1,0:T(8,128)(2,1)S(1)}, u32[]{:S(2)}, u32[]{:S(2)}) collective-permute-start(bf16[256,1024]{1,0:T(8,128)(2,1)S(1)} %collective-permute-done), channel_id=1, source_target_pairs={{0,8},{1,9},{2,10},{3,11},{4,12},{5,13},{6,14},{7,15},{8,0},{9,1},... | collective-permute-start | bytes 1572872 | tf_op jit(solution)/shard_map/ppermute | solution.py:35
  36.5 14.7 %collective-permute-start.4 = (bf16[2,528,256]{2,1,0:T(8,128)(2,1)S(1)}, bf16[2,528,256]{2,1,0:T(8,128)(2,1)S(1)}, u32[]{:S(2)}, u32[]{:S(2)}) collective-permute-start(bf16[2,528,256]{2,1,0:T(8,128)(2,1)S(1)} %pad_maximum_fusion.1.refs_4_), channel_id=1, source_target_pairs={{0,8},{1,9},{2,10},{3,11},{4,12},{5,13},{6,14},{7,15},{8,16},{9,17... | collective-permute-start | bytes 1622024 | tf_op jit(solution)/shard_map/ppermute | solution.py:35
  38.2 13.1 %collective-permute-start.5 = (bf16[2,528,256]{2,1,0:T(8,128)(2,1)S(1)}, bf16[2,528,256]{2,1,0:T(8,128)(2,1)S(1)}, u32[]{:S(2)}, u32[]{:S(2)}) collective-permute-start(bf16[2,528,256]{2,1,0:T(8,128)(2,1)S(1)} %pad_maximum_fusion.1.refs_4_), channel_id=1, source_target_pairs={{0,24},{1,25},{2,26},{3,27},{4,28},{5,29},{6,30},{7,31},{8,0},{9,1... | collective-permute-start | bytes 1622024 | tf_op jit(solution)/shard_map/ppermute | solution.py:35
  39.8 13.6 %collective-permute-start.8 = (bf16[2,528,256]{2,1,0:T(8,128)(2,1)S(1)}, bf16[2,528,256]{2,1,0:T(8,128)(2,1)S(1)}, u32[]{:S(2)}, u32[]{:S(2)}) collective-permute-start(bf16[2,528,256]{2,1,0:T(8,128)(2,1)S(1)} %pad_maximum_fusion.1.refs_4_), channel_id=1, source_target_pairs={{0,4},{1,5},{2,6},{3,7},{4,0},{5,1},{6,2},{7,3},{8,12},{9,13},{10,... | collective-permute-start | bytes 1622024 | tf_op jit(solution)/shard_map/ppermute | solution.py:35
  39.9 15.4 %copy-start.3 = (bf16[528,256]{1,0:T(8,128)(2,1)S(1)}, bf16[528,256]{1,0:T(8,128)(2,1)}, u32[]{:S(2)}) copy-start(bf16[528,256]{1,0:T(8,128)(2,1)} %get-tuple-element.50.refs_0_) | copy-start | bytes 811012
  40.0 27.8 %collective-permute-start.17 = (bf16[2,256,1024]{2,1,0:T(8,128)(2,1)S(1)}, bf16[2,256,1024]{2,1,0:T(8,128)(2,1)S(1)}, u32[]{:S(2)}, u32[]{:S(2)}) collective-permute-start(bf16[2,256,1024]{2,1,0:T(8,128)(2,1)S(1)} %pad_maximum_fusion.refs_0_), channel_id=1, source_target_pairs={{0,32},{1,33},{2,34},{3,35},{4,36},{5,37},{6,38},{7,39},{8,40},{9,... | collective-permute-start | bytes 3145736 | tf_op jit(solution)/shard_map/ppermute | solution.py:35
  51.2 4.1 %collective-permute-start.10 = (bf16[2,528,256]{2,1,0:T(8,128)(2,1)S(1)}, bf16[2,528,256]{2,1,0:T(8,128)(2,1)S(1)}, u32[]{:S(2)}, u32[]{:S(2)}) collective-permute-start(bf16[2,528,256]{2,1,0:T(8,128)(2,1)S(1)} %collective-permute-done.5.refs_6_), channel_id=1, source_target_pairs={{0,4},{1,5},{2,6},{3,7},{4,0},{5,1},{6,2},{7,3},{8,12},{9,13},{10,... | collective-permute-start | bytes 1622024 | tf_op jit(solution)/shard_map/ppermute | solution.py:35
  51.2 4.1 %collective-permute-start.9 = (bf16[2,528,256]{2,1,0:T(8,128)(2,1)S(1)}, bf16[2,528,256]{2,1,0:T(8,128)(2,1)S(1)}, u32[]{:S(2)}, u32[]{:S(2)}) collective-permute-start(bf16[2,528,256]{2,1,0:T(8,128)(2,1)S(1)} %collective-permute-done.4.refs_5_), channel_id=1, source_target_pairs={{0,4},{1,5},{2,6},{3,7},{4,0},{5,1},{6,2},{7,3},{8,12},{9,13},{10,... | collective-permute-start | bytes 1622024 | tf_op jit(solution)/shard_map/ppermute | solution.py:35
  51.8 10.6 %collective-permute-start.6 = (bf16[528,256]{1,0:T(8,128)(2,1)S(1)}, bf16[528,256]{1,0:T(8,128)(2,1)S(1)}, u32[]{:S(2)}, u32[]{:S(2)}) collective-permute-start(bf16[528,256]{1,0:T(8,128)(2,1)S(1)} %slice_bitcast_fusion.1), channel_id=1, source_target_pairs={{0,8},{1,9},{2,10},{3,11},{4,12},{5,13},{6,14},{7,15},{8,16},{9,17... | collective-permute-start | bytes 811016 | tf_op jit(solution)/shard_map/ppermute | solution.py:35
  53.4 19.4 %copy-start.2 = (bf16[2048,1024]{1,0:T(8,128)(2,1)S(1)}, bf16[2048,1024]{1,0:T(8,128)(2,1)}, u32[]{:S(2)}) copy-start(bf16[2048,1024]{1,0:T(8,128)(2,1)} %shard_map.57.refs_4_) | copy-start | bytes 12582916
  53.5 8.9 %collective-permute-start.7 = (bf16[528,256]{1,0:T(8,128)(2,1)S(1)}, bf16[528,256]{1,0:T(8,128)(2,1)S(1)}, u32[]{:S(2)}, u32[]{:S(2)}) collective-permute-start(bf16[528,256]{1,0:T(8,128)(2,1)S(1)} %slice_bitcast_fusion), channel_id=1, source_target_pairs={{0,24},{1,25},{2,26},{3,27},{4,28},{5,29},{6,30},{7,31},{8,0},{9,1... | collective-permute-start | bytes 811016 | tf_op jit(solution)/shard_map/ppermute | solution.py:35
  62.3 2.6 %collective-permute-start.11 = (bf16[1,528,256]{2,1,0:T(8,128)(2,1)S(1)}, bf16[1,528,256]{2,1,0:T(8,128)(2,1)S(1)}, u32[]{:S(2)}, u32[]{:S(2)}) collective-permute-start(bf16[1,528,256]{2,1,0:T(8,128)(2,1)S(1)} %bitcast.13), channel_id=1, source_target_pairs={{0,4},{1,5},{2,6},{3,7},{4,0},{5,1},{6,2},{7,3},{8,12},{9,13},{10,... | collective-permute-start | bytes 811016 | tf_op jit(solution)/shard_map/ppermute | solution.py:35
  62.4 2.5 %collective-permute-start.12 = (bf16[1,528,256]{2,1,0:T(8,128)(2,1)S(1)}, bf16[1,528,256]{2,1,0:T(8,128)(2,1)S(1)}, u32[]{:S(2)}, u32[]{:S(2)}) collective-permute-start(bf16[1,528,256]{2,1,0:T(8,128)(2,1)S(1)} %bitcast.15), channel_id=1, source_target_pairs={{0,4},{1,5},{2,6},{3,7},{4,0},{5,1},{6,2},{7,3},{8,12},{9,13},{10,... | collective-permute-start | bytes 811016 | tf_op jit(solution)/shard_map/ppermute | solution.py:35
  62.9 9.9 %collective-permute-start.18 = (bf16[2,256,1024]{2,1,0:T(8,128)(2,1)S(1)}, bf16[2,256,1024]{2,1,0:T(8,128)(2,1)S(1)}, u32[]{:S(2)}, u32[]{:S(2)}) collective-permute-start(bf16[2,256,1024]{2,1,0:T(8,128)(2,1)S(1)} %pad_maximum_fusion.refs_0_), channel_id=1, source_target_pairs={{0,4},{1,5},{2,6},{3,7},{4,0},{5,1},{6,2},{7,3},{8,12},{9,13},{10,... | collective-permute-start | bytes 3145736 | tf_op jit(solution)/shard_map/ppermute | solution.py:35
  67.8 5.1 %collective-permute-start.19 = (bf16[2,256,1024]{2,1,0:T(8,128)(2,1)S(1)}, bf16[2,256,1024]{2,1,0:T(8,128)(2,1)S(1)}, u32[]{:S(2)}, u32[]{:S(2)}) collective-permute-start(bf16[2,256,1024]{2,1,0:T(8,128)(2,1)S(1)} %collective-permute-done.17.refs_1_), channel_id=1, source_target_pairs={{0,4},{1,5},{2,6},{3,7},{4,0},{5,1},{6,2},{7,3},{8,12},{9,13},{10,... | collective-permute-start | bytes 3145736 | tf_op jit(solution)/shard_map/ppermute | solution.py:35
  70.1 9.2 %collective-permute-start.13 = (bf16[512,256]{1,0:T(8,128)(2,1)S(1)}, bf16[512,256]{1,0:T(8,128)(2,1)S(1)}, u32[]{:S(2)}, u32[]{:S(2)}) collective-permute-start(bf16[512,256]{1,0:T(8,128)(2,1)S(1)} %get-tuple-element.68), channel_id=1, source_target_pairs={{0,32},{1,33},{2,34},{3,35},{4,36},{5,37},{6,38},{7,39},{8,40},{9,... | collective-permute-start | bytes 786440 | tf_op jit(solution)/shard_map/ppermute | solution.py:35
  70.2 10.8 %collective-permute-start.14 = (bf16[512,256]{1,0:T(8,128)(2,1)S(1)}, bf16[512,256]{1,0:T(8,128)(2,1)S(1)}, u32[]{:S(2)}, u32[]{:S(2)}) collective-permute-start(bf16[512,256]{1,0:T(8,128)(2,1)S(1)} %get-tuple-element.82.c0), channel_id=1, source_target_pairs={{0,64},{1,65},{2,66},{3,67},{4,68},{5,69},{6,70},{7,71},{8,72},{9,... | collective-permute-start | bytes 786440 | tf_op jit(solution)/shard_map/ppermute | solution.py:35
  72.8 12.8 %collective-permute-start.15 = (bf16[512,256]{1,0:T(8,128)(2,1)S(1)}, bf16[512,256]{1,0:T(8,128)(2,1)S(1)}, u32[]{:S(2)}, u32[]{:S(2)}) collective-permute-start(bf16[512,256]{1,0:T(8,128)(2,1)S(1)} %get-tuple-element.68), channel_id=1, source_target_pairs={{0,96},{1,97},{2,98},{3,99},{4,100},{5,101},{6,102},{7,103},{8,104... | collective-permute-start | bytes 786440 | tf_op jit(solution)/shard_map/ppermute | solution.py:35
  73.4 16.9 %copy-start = (bf16[4,512,1024]{2,1,0:T(8,128)(2,1)}, bf16[4,512,1024]{2,1,0:T(8,128)(2,1)S(1)}, u32[]{:S(2)}) copy-start(bf16[4,512,1024]{2,1,0:T(8,128)(2,1)S(1)} %shard_map.60.held) | copy-start | bytes 12582916
  86.5 8.5 %collective-permute-start.20 = (bf16[256,512]{1,0:T(8,128)(2,1)S(1)}, bf16[256,512]{1,0:T(8,128)(2,1)S(1)}, u32[]{:S(2)}, u32[]{:S(2)}) collective-permute-start(bf16[256,512]{1,0:T(8,128)(2,1)S(1)} %get-tuple-element.78), channel_id=1, source_target_pairs={{0,1},{1,2},{2,3},{3,0},{4,5},{5,6},{6,7},{7,4},{8,9},{9,10},{10,1... | collective-permute-start | bytes 786440 | tf_op jit(solution)/shard_map/ppermute | solution.py:35
  87.3 9.2 %collective-permute-start.21 = (bf16[256,512]{1,0:T(8,128)(2,1)S(1)}, bf16[256,512]{1,0:T(8,128)(2,1)S(1)}, u32[]{:S(2)}, u32[]{:S(2)}) collective-permute-start(bf16[256,512]{1,0:T(8,128)(2,1)S(1)} %get-tuple-element.79), channel_id=1, source_target_pairs={{0,3},{1,0},{2,1},{3,2},{4,7},{5,4},{6,5},{7,6},{8,11},{9,8},{10,9... | collective-permute-start | bytes 786440 | tf_op jit(solution)/shard_map/ppermute | solution.py:35
  96.6 12.7 %collective-permute-start.22 = (bf16[512,512]{1,0:T(8,128)(2,1)S(1)}, bf16[512,512]{1,0:T(8,128)(2,1)S(1)}, u32[]{:S(2)}, u32[]{:S(2)}) collective-permute-start(bf16[512,512]{1,0:T(8,128)(2,1)S(1)} %get-tuple-element.83), channel_id=1, source_target_pairs={{0,1},{1,2},{2,3},{3,0},{4,5},{5,6},{6,7},{7,4},{8,9},{9,10},{10,1... | collective-permute-start | bytes 1572872 | tf_op jit(solution)/shard_map/ppermute | solution.py:35
  97.0 13.9 %collective-permute-start.23 = (bf16[512,512]{1,0:T(8,128)(2,1)S(1)}, bf16[512,512]{1,0:T(8,128)(2,1)S(1)}, u32[]{:S(2)}, u32[]{:S(2)}) collective-permute-start(bf16[512,512]{1,0:T(8,128)(2,1)S(1)} %get-tuple-element.84), channel_id=1, source_target_pairs={{0,3},{1,0},{2,1},{3,2},{4,7},{5,4},{6,5},{7,6},{8,11},{9,8},{10,9... | collective-permute-start | bytes 1572872 | tf_op jit(solution)/shard_map/ppermute | solution.py:35
  98.7 2.2 %copy-start.1 = (bf16[4,512,1024]{2,1,0:T(8,128)(2,1)S(1)}, bf16[4,512,1024]{2,1,0:T(8,128)(2,1)}, u32[]{:S(2)}) copy-start(bf16[4,512,1024]{2,1,0:T(8,128)(2,1)} %copy-done) | copy-start | bytes 12582916

commit v6 on v5

--- a/solution.py
+++ b/solution.py
@@ -178,6 +178,30 @@
         cost_estimate=LIGHT,
         compiler_params=pltpu.CompilerParams(vmem_limit_bytes=VMEM),
     )(start.reshape(1), weights)
+
+
+def share_kernel(w_ref, out_ref, held, arrived):
+    x, y, z, core = position()
+    size, width = out_ref.shape
+    index = (2 * (1 - z % 2) + y % 2) * 2 + core
+    top = pl.multiple_of(index * size, size)
+    copy = pltpu.make_async_copy(w_ref.at[0, pl.ds(top, size)], held, arrived)
+    copy.start()
+    copy.wait()
+    out_ref[...] = held[...].reshape(size, 2 * width)[:, width:]
+
+
+def share_of(weights, size):
+    width = weights.shape[3]
+    return pl.pallas_call(
+        share_kernel,
+        in_specs=[pl.BlockSpec(memory_space=pl.ANY)],
+        out_specs=pl.BlockSpec(memory_space=pltpu.VMEM),
+        out_shape=jax.ShapeDtypeStruct((size, width), jnp.bfloat16),
+        scratch_shapes=[pltpu.VMEM((size, 2, width), jnp.bfloat16), pltpu.SemaphoreType.DMA],
+        cost_estimate=LIGHT,
+        compiler_params=pltpu.CompilerParams(vmem_limit_bytes=VMEM),
+    )(weights)
 
 
 def attend_kernel(first, half, chunks, *refs):
@@ -334,16 +358,17 @@
             ref[...] = mixed[n * size : (n + 1) * size].astype(ref.dtype)
 
 
-def project(contexts, features, distances, dtype, parts=1):
+def project(contexts, features, distances, dtypes):
     rows, dim = contexts[0].shape
     width = features.shape[1]
-    outs = len(distances) * parts
+    outs = len(dtypes)
+    parts = outs // len(distances)
     vmem = pl.BlockSpec(memory_space=pltpu.VMEM)
     return pl.pallas_call(
         functools.partial(project_kernel, distances),
         in_specs=[vmem] * 5,
         out_specs=[vmem] * outs,
-        out_shape=[jax.ShapeDtypeStruct((rows // parts, width), dtype)] * outs,
+        out_shape=[jax.ShapeDtypeStruct((rows // parts, width), dtype) for dtype in dtypes],
         scratch_shapes=[pltpu.VMEM((rows, 4 * dim), jnp.bfloat16)],
         cost_estimate=LIGHT,
         compiler_params=pltpu.CompilerParams(vmem_limit_bytes=SMALL_VMEM),
@@ -351,23 +376,41 @@
 
 
 def joined_kernel(up_ref, down_ref, upward, downward, up_out, down_out):
-    half = upward.shape[0]
-    up_out[:half, :] = (up_ref[:half, :] + upward[...].astype(jnp.float32)).astype(jnp.bfloat16)
-    up_out[half:, :] = up_ref[half:, :].astype(jnp.bfloat16)
-    down_out[:half, :] = down_ref[:half, :].astype(jnp.bfloat16)
-    down_out[half:, :] = (down_ref[half:, :] + downward[...].astype(jnp.float32)).astype(jnp.bfloat16)
-
-
-def joined(up, down, upward, downward):
+    up_out[...] = (up_ref[...] + upward[...].astype(jnp.float32)).astype(jnp.bfloat16)
+    down_out[...] = (down_ref[...] + downward[...].astype(jnp.float32)).astype(jnp.bfloat16)
+
+
+def joined(*operands):
     vmem = pl.BlockSpec(memory_space=pltpu.VMEM)
     return pl.pallas_call(
         joined_kernel,
         in_specs=[vmem] * 4,
         out_specs=[vmem] * 2,
-        out_shape=[jax.ShapeDtypeStruct(up.shape, jnp.bfloat16)] * 2,
+        out_shape=[jax.ShapeDtypeStruct(operands[2].shape, jnp.bfloat16)] * 2,
         cost_estimate=LIGHT,
         compiler_params=pltpu.CompilerParams(vmem_limit_bytes=SMALL_VMEM),
-    )(up, down, upward, downward)
+    )(*operands)
+
+
+def finish_kernel(residual, near_top, near_end, up_top, up_end, down_top, down_end, out_ref):
+    half = up_top.shape[0]
+    for top, near, one, other in ((0, near_top, up_top, down_top), (half, near_end, up_end, down_end)):
+        rows = slice(top, top + half)
+        found = residual[rows, :].astype(jnp.float32) + near[...]
+        found = found + one[...].astype(jnp.float32) + other[...].astype(jnp.float32)
+        out_ref[rows, :] = found.astype(jnp.bfloat16)
+
+
+def finish(residual, *parts):
+    vmem = pl.BlockSpec(memory_space=pltpu.VMEM)
+    return pl.pallas_call(
+        finish_kernel,
+        in_specs=[vmem] * 7,
+        out_specs=vmem,
+        out_shape=jax.ShapeDtypeStruct(residual.shape, jnp.bfloat16),
+        cost_estimate=LIGHT,
+        compiler_params=pltpu.CompilerParams(vmem_limit_bytes=SMALL_VMEM),
+    )(residual, *parts)
 
 
 def position():
@@ -395,9 +438,7 @@
     flip = lambda x, y, z, c: (x, y, 1 - z, c)
     is_encoder = segment == 0
 
-    odd = y % 2
-    wanted_set = 2 * (1 - low) + odd
-    (share,) = second_half(proj_weights, wanted_set * 2 + core, half // 8, 1, 1)
+    share = share_of(proj_weights, half // 8)
     p = moved(share, down, decoder)
 
     own, *to = section(after(pad_counts, share), memory, targets, norm_gains, proj_weights, dim)
@@ -431,16 +472,17 @@
     out_width = model // 8
     residual = lax.dynamic_slice_in_dim(targets, (segment * 4 + x) * out_width, out_width, 1)
     features = assemble(sources)
-    upward, downward = project(contexts, features, (2,), jnp.bfloat16, 2)
+    wide, narrow = jnp.float32, jnp.bfloat16
+    wide, narrow = jnp.float32, jnp.bfloat16
+    upward, downward = project(contexts, features, (2,), (narrow, narrow))
     contexts[0], upward, downward = lax.optimization_barrier((contexts[0], upward, downward))
-    up, down = project(contexts, features, (1, 3), jnp.float32)
-    up, down = joined(up, down, along_x(upward, 1), along_x(downward, 3))
-    contexts[0], up, down = lax.optimization_barrier((contexts[0], up, down))
-    (near,) = project(contexts, features, (0,), jnp.float32)
-    summed = lax.optimization_barrier(residual.astype(jnp.float32) + near)
-    for block, d in ((up, 1), (down, 3)):
-        summed = summed + along_x(block, d).astype(jnp.float32)
-    return summed.astype(jnp.bfloat16)
+    up_top, up_end, down_top, down_end, near_top, near_end = project(
+        contexts, features, (1, 3, 0), (wide, narrow, narrow, wide, wide, wide)
+    )
+    up_end, down_top = along_x(up_end, 1), along_x(down_top, 3)
+    up_top, down_end = joined(up_top, down_end, along_x(upward, 1), along_x(downward, 3))
+    up_top, down_end = along_x(up_top, 1), along_x(down_end, 3)
+    return finish(residual, near_top, near_end, up_top, up_end, down_top, down_end)
 
 
 def solution(mesh):

time: 112 us -> 109 us (0.973)
  waiting for transfers between devices: 37.8 us -> 35.2 us
  other arithmetic: 3.39 us -> 1.18 us
  starting transfers between devices: 33.1 us -> 35.2 us
  local copies, waits for them, and re-layouts: 2.24 us -> 1.12 us
    pallas_call x0 -> x2, Pallas kernels: none -> 3.18 us  [the longest x1 2.16 us: share_of(): pl.pallas_call(share_kernel, in_specs=[pl.BlockSpec(memory_space=pl.ANY)]...]
    ppermute x24 -> x26, waiting for transfers between devices: 37.8 us -> 35.2 us  [moved(): return lax.ppermute(block, AXES, route)]
    unnamed x8 -> x4, local copies, waits for them, and re-layouts: 2.2 us -> 0.01 us
    pallas_call x2 -> x1, Pallas kernels: 7.52 us -> 5.36 us  [second_half(): pl.pallas_call(second_half_kernel, grid_spec=pltpu.PrefetchScalarGridSpec...]
    ppermute x24 -> x26, starting transfers between devices: 33.1 us -> 35.2 us  [moved(): return lax.ppermute(block, AXES, route)]
    add x1 -> x0, other arithmetic: 1.2 us -> none  [local(): summed = lax.optimization_barrier(residual.astype(jnp.float32) + near)]
    pallas_call x3 -> x2, Pallas kernels: 3.09 us -> 2.77 us  [project(): pl.pallas_call(functools.partial(project_kernel, distances), in_specs=[vm...]
  transfers between devices with their start and end apart: 24 -> 26, of which waited for: 11 -> 13; matrix products, arithmetic and copies ran while one was open for 2% -> 2% of each run, Pallas kernels for 28% -> 29%
where the time goes in v6:
time: 109 us
  Pallas kernels  35.3 us (32%)
  starting transfers between devices  35.2 us (32%)
  waiting for transfers between devices  35.2 us (32%)
  other arithmetic  1.18 us (1%)
  local copies, waits for them, and re-layouts  1.12 us (1%)
    ppermute x26, starting transfers between devices, moved(): return lax.ppermute(block, AXES, route)  35.2 us
    ppermute x26, waiting for transfers between devices, moved(): return lax.ppermute(block, AXES, route)  35.2 us
    pallas_call x1, Pallas kernels, section(): pl.pallas_call(section_kernel, grid_spec=pltpu.PrefetchScalarGridSpec(num...  13.5 us
    pallas_call x2, Pallas kernels, attend(): pl.pallas_call(functools.partial(attend_kernel, first, half, chunks), in_...  9.96 us
    pallas_call x1, Pallas kernels, second_half(): pl.pallas_call(second_half_kernel, grid_spec=pltpu.PrefetchScalarGridSpec...  5.36 us
    pallas_call x2, Pallas kernels, project(): pl.pallas_call(functools.partial(project_kernel, distances), in_specs=[vm...  2.77 us
  transfers between devices with their start and end apart: 26, of which 13 were waited for; matrix products, arithmetic and copies ran while one was open for 2% of the time, Pallas kernels for 29%

profile of v6, /device:TPU:38, one launch (start us, length us, event | category | flops | bytes accessed | tf_op | source)
XLA Modules:
  0.0 109.0 jit_solution(12698937420253682199)
XLA Ops:
  0.0 2.2 %shard_map.55 = bf16[256,1024]{1,0:T(8,128)(2,1)} custom-call(bf16[1,4096,2,1024]{3,2,1,0:T(2,128)(2,1)} %w_ref.4), custom_call_target="tpu_custom_call" | custom-call | bytes 1024 | tf_op jit(solution)/shard_map/pallas_call | solution.py:196
  2.2 1.3 %collective-permute-start = (bf16[256,1024]{1,0:T(8,128)(2,1)}, bf16[256,1024]{1,0:T(8,128)(2,1)S(1)}, u32[]{:S(2)}, u32[]{:S(2)}) collective-permute-start(bf16[256,1024]{1,0:T(8,128)(2,1)} %shard_map.55), channel_id=1, source_target_pairs={{64,32},{65,33},{66,34},{67,35},{68,36},{69,37},{70,38},{71,39},{7... | collective-permute-start | bytes 1572872 | tf_op jit(solution)/shard_map/ppermute | solution.py:35
  4.1 13.5 %shard_map.56 = (bf16[528,256]{1,0:T(8,128)(2,1)}, bf16[528,256]{1,0:T(8,128)(2,1)}, bf16[528,256]{1,0:T(8,128)(2,1)}, bf16[528,256]{1,0:T(8,128)(2,1)}) custom-call(s32[1]{0:T(128)S(6)} %copy.6.pad_ref, bf16[256,4096]{1,0:T(8,128)(2,1)} %memory.1, bf16[512,4096]{1,0:T(8,128)(2,1)} %targets.1, f32[1,4096]{1,0:T(1,128)} %gain_ref.1, ...), custom_call_target="tpu_custom_call" | custom-call | bytes 1024 | tf_op jit(solution)/shard_map/pallas_call | solution.py:134
  17.9 3.2 %collective-permute-start.1 = (bf16[528,256]{1,0:T(8,128)(2,1)}, bf16[528,256]{1,0:T(8,128)(2,1)S(1)}, u32[]{:S(2)}, u32[]{:S(2)}) collective-permute-start(bf16[528,256]{1,0:T(8,128)(2,1)} %get-tuple-element.52), channel_id=1, source_target_pairs={{0,32},{1,33},{2,34},{3,35},{4,36},{5,37},{6,38},{7,39},{8,40},{9,... | collective-permute-start | bytes 811016 | tf_op jit(solution)/shard_map/ppermute | solution.py:35
  21.8 2.3 %collective-permute-start.3 = (bf16[528,256]{1,0:T(8,128)(2,1)}, bf16[528,256]{1,0:T(8,128)(2,1)S(1)}, u32[]{:S(2)}, u32[]{:S(2)}) collective-permute-start(bf16[528,256]{1,0:T(8,128)(2,1)} %get-tuple-element.54), channel_id=1, source_target_pairs={{0,96},{1,97},{2,98},{3,99},{4,100},{5,101},{6,102},{7,103},{8,104... | collective-permute-start | bytes 811016 | tf_op jit(solution)/shard_map/ppermute | solution.py:35
  24.1 3.5 %collective-permute-start.16 = (bf16[256,1024]{1,0:T(8,128)(2,1)S(1)}, bf16[256,1024]{1,0:T(8,128)(2,1)S(1)}, u32[]{:S(2)}, u32[]{:S(2)}) collective-permute-start(bf16[256,1024]{1,0:T(8,128)(2,1)S(1)} %collective-permute-done), channel_id=1, source_target_pairs={{0,8},{1,9},{2,10},{3,11},{4,12},{5,13},{6,14},{7,15},{8,0},{9,1},... | collective-permute-start | bytes 1572872 | tf_op jit(solution)/shard_map/ppermute | solution.py:35
  27.5 5.1 %collective-permute-done.1.refs_1_ = bf16[528,256]{1,0:T(8,128)(2,1)S(1)} collective-permute-done((bf16[528,256]{1,0:T(8,128)(2,1)}, bf16[528,256]{1,0:T(8,128)(2,1)S(1)}, u32[]{:S(2)}, u32[]{:S(2)}) %collective-permute-start.1) | collective-permute-done | bytes 270368 | tf_op jit(solution)/shard_map/ppermute | solution.py:35
  32.7 2.8 %collective-permute-done.3.refs_3_ = bf16[528,256]{1,0:T(8,128)(2,1)S(1)} collective-permute-done((bf16[528,256]{1,0:T(8,128)(2,1)}, bf16[528,256]{1,0:T(8,128)(2,1)S(1)}, u32[]{:S(2)}, u32[]{:S(2)}) %collective-permute-start.3) | collective-permute-done | bytes 270368 | tf_op jit(solution)/shard_map/ppermute | solution.py:35
  36.6 1.6 %collective-permute-start.4 = (bf16[2,528,256]{2,1,0:T(8,128)(2,1)S(1)}, bf16[2,528,256]{2,1,0:T(8,128)(2,1)S(1)}, u32[]{:S(2)}, u32[]{:S(2)}) collective-permute-start(bf16[2,528,256]{2,1,0:T(8,128)(2,1)S(1)} %pad_maximum_fusion.1.refs_4_), channel_id=1, source_target_pairs={{0,8},{1,9},{2,10},{3,11},{4,12},{5,13},{6,14},{7,15},{8,16},{9,17... | collective-permute-start | bytes 1622024 | tf_op jit(solution)/shard_map/ppermute | solution.py:35
  38.2 1.7 %collective-permute-start.5 = (bf16[2,528,256]{2,1,0:T(8,128)(2,1)S(1)}, bf16[2,528,256]{2,1,0:T(8,128)(2,1)S(1)}, u32[]{:S(2)}, u32[]{:S(2)}) collective-permute-start(bf16[2,528,256]{2,1,0:T(8,128)(2,1)S(1)} %pad_maximum_fusion.1.refs_4_), channel_id=1, source_target_pairs={{0,24},{1,25},{2,26},{3,27},{4,28},{5,29},{6,30},{7,31},{8,0},{9,1... | collective-permute-start | bytes 1622024 | tf_op jit(solution)/shard_map/ppermute | solution.py:35
  40.0 2.8 %collective-permute-start.17 = (bf16[2,256,1024]{2,1,0:T(8,128)(2,1)S(1)}, bf16[2,256,1024]{2,1,0:T(8,128)(2,1)S(1)}, u32[]{:S(2)}, u32[]{:S(2)}) collective-permute-start(bf16[2,256,1024]{2,1,0:T(8,128)(2,1)S(1)} %pad_maximum_fusion.refs_0_), channel_id=1, source_target_pairs={{0,32},{1,33},{2,34},{3,35},{4,36},{5,37},{6,38},{7,39},{8,40},{9,... | collective-permute-start | bytes 3145736 | tf_op jit(solution)/shard_map/ppermute | solution.py:35
  42.8 5.4 %shard_map.57.refs_4_ = bf16[2048,1024]{1,0:T(8,128)(2,1)} custom-call(s32[1]{0:T(128)} %constant.42.clone.1.start_ref, bf16[1,4096,2,1024]{3,2,1,0:T(2,128)(2,1)} %w_ref.4), custom_call_target="tpu_custom_call" | custom-call | bytes 1024 | tf_op jit(solution)/shard_map/pallas_call | solution.py:169
  48.2 3.0 %collective-permute-done.4.refs_5_ = bf16[2,528,256]{2,1,0:T(8,128)(2,1)S(1)} collective-permute-done((bf16[2,528,256]{2,1,0:T(8,128)(2,1)S(1)}, bf16[2,528,256]{2,1,0:T(8,128)(2,1)S(1)}, u32[]{:S(2)}, u32[]{:S(2)}) %collective-permute-start.4) | collective-permute-done | bytes 540704 | tf_op jit(solution)/shard_map/ppermute | solution.py:35
  51.8 1.6 %collective-permute-start.6 = (bf16[528,256]{1,0:T(8,128)(2,1)S(1)}, bf16[528,256]{1,0:T(8,128)(2,1)S(1)}, u32[]{:S(2)}, u32[]{:S(2)}) collective-permute-start(bf16[528,256]{1,0:T(8,128)(2,1)S(1)} %slice_bitcast_fusion.1), channel_id=1, source_target_pairs={{0,8},{1,9},{2,10},{3,11},{4,12},{5,13},{6,14},{7,15},{8,16},{9,17... | collective-permute-start | bytes 811016 | tf_op jit(solution)/shard_map/ppermute | solution.py:35
  53.5 1.9 %collective-permute-start.7 = (bf16[528,256]{1,0:T(8,128)(2,1)S(1)}, bf16[528,256]{1,0:T(8,128)(2,1)S(1)}, u32[]{:S(2)}, u32[]{:S(2)}) collective-permute-start(bf16[528,256]{1,0:T(8,128)(2,1)S(1)} %slice_bitcast_fusion), channel_id=1, source_target_pairs={{0,24},{1,25},{2,26},{3,27},{4,28},{5,29},{6,30},{7,31},{8,0},{9,1... | collective-permute-start | bytes 811016 | tf_op jit(solution)/shard_map/ppermute | solution.py:35
  55.4 7.1 %shard_map.58 = (f32[1024,256]{1,0:T(8,128)S(1)}, f32[1024,128]{1,0:T(8,128)S(1)}, f32[1024,128]{1,0:T(8,128)S(1)}) custom-call(bf16[528,256]{1,0:T(8,128)(2,1)S(1)} %copy-done.1, bf16[528,256]{1,0:T(8,128)(2,1)S(1)} %collective-permute-done.1.refs_1_, bf16[528,256]{1,0:T(8,128)(2,1)S(1)} %collective-permute-done.2.refs_2_, ...), custom_call_target="tpu_custom_call" | custom-call | bytes 1024 | tf_op jit(solution)/shard_map/pallas_call | solution.py:283
  63.1 2.0 %collective-permute-start.18 = (bf16[2,256,1024]{2,1,0:T(8,128)(2,1)S(1)}, bf16[2,256,1024]{2,1,0:T(8,128)(2,1)S(1)}, u32[]{:S(2)}, u32[]{:S(2)}) collective-permute-start(bf16[2,256,1024]{2,1,0:T(8,128)(2,1)S(1)} %pad_maximum_fusion.refs_0_), channel_id=1, source_target_pairs={{0,4},{1,5},{2,6},{3,7},{4,0},{5,1},{6,2},{7,3},{8,12},{9,13},{10,... | collective-permute-start | bytes 3145736 | tf_op jit(solution)/shard_map/ppermute | solution.py:35
  65.1 2.9 %shard_map.59 = (bf16[512,256]{1,0:T(8,128)(2,1)S(1)}, bf16[512,256]{1,0:T(8,128)(2,1)S(1)}) custom-call(bf16[528,256]{1,0:T(8,128)(2,1)S(1)} %copy-done.1, bf16[528,256]{1,0:T(8,128)(2,1)S(1)} %collective-permute-done.1.refs_1_, bf16[528,256]{1,0:T(8,128)(2,1)S(1)} %collective-permute-done.2.refs_2_, bf16[528,256]{1,0:T(8,128)(2,1)S(1)} %collective-permute-done.3.refs_3_, ...), custom_call_target="tpu_custom_call" | custom-call | bytes 1024 | tf_op jit(solution)/shard_map/pallas_call | solution.py:283
  68.0 2.3 %collective-permute-start.19 = (bf16[2,256,1024]{2,1,0:T(8,128)(2,1)S(1)}, bf16[2,256,1024]{2,1,0:T(8,128)(2,1)S(1)}, u32[]{:S(2)}, u32[]{:S(2)}) collective-permute-start(bf16[2,256,1024]{2,1,0:T(8,128)(2,1)S(1)} %collective-permute-done.17.refs_1_), channel_id=1, source_target_pairs={{0,4},{1,5},{2,6},{3,7},{4,0},{5,1},{6,2},{7,3},{8,12},{9,13},{10,... | collective-permute-start | bytes 3145736 | tf_op jit(solution)/shard_map/ppermute | solution.py:35
  70.4 2.7 %collective-permute-start.14 = (bf16[512,256]{1,0:T(8,128)(2,1)S(1)}, bf16[512,256]{1,0:T(8,128)(2,1)S(1)}, u32[]{:S(2)}, u32[]{:S(2)}) collective-permute-start(bf16[512,256]{1,0:T(8,128)(2,1)S(1)} %get-tuple-element.76.c0), channel_id=1, source_target_pairs={{0,64},{1,65},{2,66},{3,67},{4,68},{5,69},{6,70},{7,71},{8,72},{9,... | collective-permute-start | bytes 786440 | tf_op jit(solution)/shard_map/ppermute | solution.py:35
  73.6 6.0 %collective-permute-done.13.c1 = bf16[512,256]{1,0:T(8,128)(2,1)S(1)} collective-permute-done((bf16[512,256]{1,0:T(8,128)(2,1)S(1)}, bf16[512,256]{1,0:T(8,128)(2,1)S(1)}, u32[]{:S(2)}, u32[]{:S(2)}) %collective-permute-start.13) | collective-permute-done | bytes 262176 | tf_op jit(solution)/shard_map/ppermute | solution.py:35
  79.6 1.6 %collective-permute-done.14.c2 = bf16[512,256]{1,0:T(8,128)(2,1)S(1)} collective-permute-done((bf16[512,256]{1,0:T(8,128)(2,1)S(1)}, bf16[512,256]{1,0:T(8,128)(2,1)S(1)}, u32[]{:S(2)}, u32[]{:S(2)}) %collective-permute-start.14) | collective-permute-done | bytes 262176 | tf_op jit(solution)/shard_map/ppermute | solution.py:35
  81.2 4.7 %collective-permute-done.15.c3 = bf16[512,256]{1,0:T(8,128)(2,1)S(1)} collective-permute-done((bf16[512,256]{1,0:T(8,128)(2,1)S(1)}, bf16[512,256]{1,0:T(8,128)(2,1)S(1)}, u32[]{:S(2)}, u32[]{:S(2)}) %collective-permute-start.15) | collective-permute-done | bytes 262176 | tf_op jit(solution)/shard_map/ppermute | solution.py:35
  87.6 1.5 %collective-permute-start.21 = (bf16[256,512]{1,0:T(8,128)(2,1)S(1)}, bf16[256,512]{1,0:T(8,128)(2,1)S(1)}, u32[]{:S(2)}, u32[]{:S(2)}) collective-permute-start(bf16[256,512]{1,0:T(8,128)(2,1)S(1)} %get-tuple-element.82), channel_id=1, source_target_pairs={{0,3},{1,0},{2,1},{3,2},{4,7},{5,4},{6,5},{7,6},{8,11},{9,8},{10,9... | collective-permute-start | bytes 786440 | tf_op jit(solution)/shard_map/ppermute | solution.py:35
  89.1 1.9 %shard_map.62 = (f32[256,512]{1,0:T(8,128)S(1)}, bf16[256,512]{1,0:T(8,128)(2,1)S(1)}, bf16[256,512]{1,0:T(8,128)(2,1)S(1)}, f32[256,512]{1,0:T(8,128)S(1)}, f32...) custom-call(bf16[512,256]{1,0:T(8,128)(2,1)S(1)} %get-tuple-element.76.c0, bf16[512,256]{1,0:T(8,128)(2,1)S(1)} %collective-permute-done.13.c1, ...), custom_call_target="tpu_custom_call" | custom-call | bytes 1024 | tf_op jit(solution)/shard_map/pallas_call | solution.py:367
  91.0 1.8 %collective-permute-start.23 = (bf16[256,512]{1,0:T(8,128)(2,1)S(1)}, bf16[256,512]{1,0:T(8,128)(2,1)S(1)}, u32[]{:S(2)}, u32[]{:S(2)}) collective-permute-start(bf16[256,512]{1,0:T(8,128)(2,1)S(1)} %get-tuple-element.84), channel_id=1, source_target_pairs={{0,1},{1,2},{2,3},{3,0},{4,5},{5,6},{6,7},{7,4},{8,9},{9,10},{10,1... | collective-permute-start | bytes 786440 | tf_op jit(solution)/shard_map/ppermute | solution.py:35
  93.1 3.1 %collective-permute-done.20.upward = bf16[256,512]{1,0:T(8,128)(2,1)S(1)} collective-permute-done((bf16[256,512]{1,0:T(8,128)(2,1)S(1)}, bf16[256,512]{1,0:T(8,128)(2,1)S(1)}, u32[]{:S(2)}, u32[]{:S(2)}) %collective-permute-start.20) | collective-permute-done | bytes 262176 | tf_op jit(solution)/shard_map/ppermute | solution.py:35
  96.2 1.3 %collective-permute-done.21.downward = bf16[256,512]{1,0:T(8,128)(2,1)S(1)} collective-permute-done((bf16[256,512]{1,0:T(8,128)(2,1)S(1)}, bf16[256,512]{1,0:T(8,128)(2,1)S(1)}, u32[]{:S(2)}, u32[]{:S(2)}) %collective-permute-start.21) | collective-permute-done | bytes 262176 | tf_op jit(solution)/shard_map/ppermute | solution.py:35
  98.4 1.4 %collective-permute-start.25 = (bf16[256,512]{1,0:T(8,128)(2,1)S(1)}, bf16[256,512]{1,0:T(8,128)(2,1)S(1)}, u32[]{:S(2)}, u32[]{:S(2)}) collective-permute-start(bf16[256,512]{1,0:T(8,128)(2,1)S(1)} %get-tuple-element.86), channel_id=1, source_target_pairs={{0,3},{1,0},{2,1},{3,2},{4,7},{5,4},{6,5},{7,6},{8,11},{9,8},{10,9... | collective-permute-start | bytes 786440 | tf_op jit(solution)/shard_map/ppermute | solution.py:35
  101.9 1.3 %collective-permute-done.24.down_top = bf16[256,512]{1,0:T(8,128)(2,1)S(1)} collective-permute-done((bf16[256,512]{1,0:T(8,128)(2,1)S(1)}, bf16[256,512]{1,0:T(8,128)(2,1)S(1)}, u32[]{:S(2)}, u32[]{:S(2)}) %collective-permute-start.24) | collective-permute-done | bytes 262176 | tf_op jit(solution)/shard_map/ppermute | solution.py:35
  103.2 3.3 %collective-permute-done.22.up_top = bf16[256,512]{1,0:T(8,128)(2,1)S(1)} collective-permute-done((bf16[256,512]{1,0:T(8,128)(2,1)S(1)}, bf16[256,512]{1,0:T(8,128)(2,1)S(1)}, u32[]{:S(2)}, u32[]{:S(2)}) %collective-permute-start.22) | collective-permute-done | bytes 262176 | tf_op jit(solution)/shard_map/ppermute | solution.py:35
  106.5 1.4 %collective-permute-done.25.down_end = bf16[256,512]{1,0:T(8,128)(2,1)S(1)} collective-permute-done((bf16[256,512]{1,0:T(8,128)(2,1)S(1)}, bf16[256,512]{1,0:T(8,128)(2,1)S(1)}, u32[]{:S(2)}, u32[]{:S(2)}) %collective-permute-start.25) | collective-permute-done | bytes 262176 | tf_op jit(solution)/shard_map/ppermute | solution.py:35
  (40 shorter events, 9.8 us)
Async XLA Ops:
  2.2 15.8 %collective-permute-start = (bf16[256,1024]{1,0:T(8,128)(2,1)}, bf16[256,1024]{1,0:T(8,128)(2,1)S(1)}, u32[]{:S(2)}, u32[]{:S(2)}) collective-permute-start(bf16[256,1024]{1,0:T(8,128)(2,1)} %shard_map.55), channel_id=1, source_target_pairs={{64,32},{65,33},{66,34},{67,35},{68,36},{69,37},{70,38},{71,39},{7... | collective-permute-start | bytes 1572872 | tf_op jit(solution)/shard_map/ppermute | solution.py:35
  17.9 14.7 %collective-permute-start.1 = (bf16[528,256]{1,0:T(8,128)(2,1)}, bf16[528,256]{1,0:T(8,128)(2,1)S(1)}, u32[]{:S(2)}, u32[]{:S(2)}) collective-permute-start(bf16[528,256]{1,0:T(8,128)(2,1)} %get-tuple-element.52), channel_id=1, source_target_pairs={{0,32},{1,33},{2,34},{3,35},{4,36},{5,37},{6,38},{7,39},{8,40},{9,... | collective-permute-start | bytes 811016 | tf_op jit(solution)/shard_map/ppermute | solution.py:35
  21.1 11.6 %collective-permute-start.2 = (bf16[528,256]{1,0:T(8,128)(2,1)}, bf16[528,256]{1,0:T(8,128)(2,1)S(1)}, u32[]{:S(2)}, u32[]{:S(2)}) collective-permute-start(bf16[528,256]{1,0:T(8,128)(2,1)} %get-tuple-element.53), channel_id=1, source_target_pairs={{0,64},{1,65},{2,66},{3,67},{4,68},{5,69},{6,70},{7,71},{8,72},{9,... | collective-permute-start | bytes 811016 | tf_op jit(solution)/shard_map/ppermute | solution.py:35
  21.8 13.7 %collective-permute-start.3 = (bf16[528,256]{1,0:T(8,128)(2,1)}, bf16[528,256]{1,0:T(8,128)(2,1)S(1)}, u32[]{:S(2)}, u32[]{:S(2)}) collective-permute-start(bf16[528,256]{1,0:T(8,128)(2,1)} %get-tuple-element.54), channel_id=1, source_target_pairs={{0,96},{1,97},{2,98},{3,99},{4,100},{5,101},{6,102},{7,103},{8,104... | collective-permute-start | bytes 811016 | tf_op jit(solution)/shard_map/ppermute | solution.py:35
  24.1 15.8 %collective-permute-start.16 = (bf16[256,1024]{1,0:T(8,128)(2,1)S(1)}, bf16[256,1024]{1,0:T(8,128)(2,1)S(1)}, u32[]{:S(2)}, u32[]{:S(2)}) collective-permute-start(bf16[256,1024]{1,0:T(8,128)(2,1)S(1)} %collective-permute-done), channel_id=1, source_target_pairs={{0,8},{1,9},{2,10},{3,11},{4,12},{5,13},{6,14},{7,15},{8,0},{9,1},... | collective-permute-start | bytes 1572872 | tf_op jit(solution)/shard_map/ppermute | solution.py:35
  36.6 14.7 %collective-permute-start.4 = (bf16[2,528,256]{2,1,0:T(8,128)(2,1)S(1)}, bf16[2,528,256]{2,1,0:T(8,128)(2,1)S(1)}, u32[]{:S(2)}, u32[]{:S(2)}) collective-permute-start(bf16[2,528,256]{2,1,0:T(8,128)(2,1)S(1)} %pad_maximum_fusion.1.refs_4_), channel_id=1, source_target_pairs={{0,8},{1,9},{2,10},{3,11},{4,12},{5,13},{6,14},{7,15},{8,16},{9,17... | collective-permute-start | bytes 1622024 | tf_op jit(solution)/shard_map/ppermute | solution.py:35
  38.2 13.0 %collective-permute-start.5 = (bf16[2,528,256]{2,1,0:T(8,128)(2,1)S(1)}, bf16[2,528,256]{2,1,0:T(8,128)(2,1)S(1)}, u32[]{:S(2)}, u32[]{:S(2)}) collective-permute-start(bf16[2,528,256]{2,1,0:T(8,128)(2,1)S(1)} %pad_maximum_fusion.1.refs_4_), channel_id=1, source_target_pairs={{0,24},{1,25},{2,26},{3,27},{4,28},{5,29},{6,30},{7,31},{8,0},{9,1... | collective-permute-start | bytes 1622024 | tf_op jit(solution)/shard_map/ppermute | solution.py:35
  39.9 13.6 %collective-permute-start.8 = (bf16[2,528,256]{2,1,0:T(8,128)(2,1)S(1)}, bf16[2,528,256]{2,1,0:T(8,128)(2,1)S(1)}, u32[]{:S(2)}, u32[]{:S(2)}) collective-permute-start(bf16[2,528,256]{2,1,0:T(8,128)(2,1)S(1)} %pad_maximum_fusion.1.refs_4_), channel_id=1, source_target_pairs={{0,4},{1,5},{2,6},{3,7},{4,0},{5,1},{6,2},{7,3},{8,12},{9,13},{10,... | collective-permute-start | bytes 1622024 | tf_op jit(solution)/shard_map/ppermute | solution.py:35
  40.0 15.4 %copy-start.1 = (bf16[528,256]{1,0:T(8,128)(2,1)S(1)}, bf16[528,256]{1,0:T(8,128)(2,1)}, u32[]{:S(2)}) copy-start(bf16[528,256]{1,0:T(8,128)(2,1)} %get-tuple-element.51.refs_0_) | copy-start | bytes 811012
  40.0 28.0 %collective-permute-start.17 = (bf16[2,256,1024]{2,1,0:T(8,128)(2,1)S(1)}, bf16[2,256,1024]{2,1,0:T(8,128)(2,1)S(1)}, u32[]{:S(2)}, u32[]{:S(2)}) collective-permute-start(bf16[2,256,1024]{2,1,0:T(8,128)(2,1)S(1)} %pad_maximum_fusion.refs_0_), channel_id=1, source_target_pairs={{0,32},{1,33},{2,34},{3,35},{4,36},{5,37},{6,38},{7,39},{8,40},{9,... | collective-permute-start | bytes 3145736 | tf_op jit(solution)/shard_map/ppermute | solution.py:35
  51.3 4.1 %collective-permute-start.10 = (bf16[2,528,256]{2,1,0:T(8,128)(2,1)S(1)}, bf16[2,528,256]{2,1,0:T(8,128)(2,1)S(1)}, u32[]{:S(2)}, u32[]{:S(2)}) collective-permute-start(bf16[2,528,256]{2,1,0:T(8,128)(2,1)S(1)} %collective-permute-done.5.refs_6_), channel_id=1, source_target_pairs={{0,4},{1,5},{2,6},{3,7},{4,0},{5,1},{6,2},{7,3},{8,12},{9,13},{10,... | collective-permute-start | bytes 1622024 | tf_op jit(solution)/shard_map/ppermute | solution.py:35
  51.3 4.1 %collective-permute-start.9 = (bf16[2,528,256]{2,1,0:T(8,128)(2,1)S(1)}, bf16[2,528,256]{2,1,0:T(8,128)(2,1)S(1)}, u32[]{:S(2)}, u32[]{:S(2)}) collective-permute-start(bf16[2,528,256]{2,1,0:T(8,128)(2,1)S(1)} %collective-permute-done.4.refs_5_), channel_id=1, source_target_pairs={{0,4},{1,5},{2,6},{3,7},{4,0},{5,1},{6,2},{7,3},{8,12},{9,13},{10,... | collective-permute-start | bytes 1622024 | tf_op jit(solution)/shard_map/ppermute | solution.py:35
  51.8 10.7 %collective-permute-start.6 = (bf16[528,256]{1,0:T(8,128)(2,1)S(1)}, bf16[528,256]{1,0:T(8,128)(2,1)S(1)}, u32[]{:S(2)}, u32[]{:S(2)}) collective-permute-start(bf16[528,256]{1,0:T(8,128)(2,1)S(1)} %slice_bitcast_fusion.1), channel_id=1, source_target_pairs={{0,8},{1,9},{2,10},{3,11},{4,12},{5,13},{6,14},{7,15},{8,16},{9,17... | collective-permute-start | bytes 811016 | tf_op jit(solution)/shard_map/ppermute | solution.py:35
  53.5 19.7 %copy-start = (bf16[2048,1024]{1,0:T(8,128)(2,1)S(1)}, bf16[2048,1024]{1,0:T(8,128)(2,1)}, u32[]{:S(2)}) copy-start(bf16[2048,1024]{1,0:T(8,128)(2,1)} %shard_map.57.refs_4_) | copy-start | bytes 12582916
  53.5 9.1 %collective-permute-start.7 = (bf16[528,256]{1,0:T(8,128)(2,1)S(1)}, bf16[528,256]{1,0:T(8,128)(2,1)S(1)}, u32[]{:S(2)}, u32[]{:S(2)}) collective-permute-start(bf16[528,256]{1,0:T(8,128)(2,1)S(1)} %slice_bitcast_fusion), channel_id=1, source_target_pairs={{0,24},{1,25},{2,26},{3,27},{4,28},{5,29},{6,30},{7,31},{8,0},{9,1... | collective-permute-start | bytes 811016 | tf_op jit(solution)/shard_map/ppermute | solution.py:35
  62.5 2.6 %collective-permute-start.11 = (bf16[1,528,256]{2,1,0:T(8,128)(2,1)S(1)}, bf16[1,528,256]{2,1,0:T(8,128)(2,1)S(1)}, u32[]{:S(2)}, u32[]{:S(2)}) collective-permute-start(bf16[1,528,256]{2,1,0:T(8,128)(2,1)S(1)} %bitcast.12), channel_id=1, source_target_pairs={{0,4},{1,5},{2,6},{3,7},{4,0},{5,1},{6,2},{7,3},{8,12},{9,13},{10,... | collective-permute-start | bytes 811016 | tf_op jit(solution)/shard_map/ppermute | solution.py:35
  62.6 2.5 %collective-permute-start.12 = (bf16[1,528,256]{2,1,0:T(8,128)(2,1)S(1)}, bf16[1,528,256]{2,1,0:T(8,128)(2,1)S(1)}, u32[]{:S(2)}, u32[]{:S(2)}) collective-permute-start(bf16[1,528,256]{2,1,0:T(8,128)(2,1)S(1)} %bitcast.14), channel_id=1, source_target_pairs={{0,4},{1,5},{2,6},{3,7},{4,0},{5,1},{6,2},{7,3},{8,12},{9,13},{10,... | collective-permute-start | bytes 811016 | tf_op jit(solution)/shard_map/ppermute | solution.py:35
  63.1 10.0 %collective-permute-start.18 = (bf16[2,256,1024]{2,1,0:T(8,128)(2,1)S(1)}, bf16[2,256,1024]{2,1,0:T(8,128)(2,1)S(1)}, u32[]{:S(2)}, u32[]{:S(2)}) collective-permute-start(bf16[2,256,1024]{2,1,0:T(8,128)(2,1)S(1)} %pad_maximum_fusion.refs_0_), channel_id=1, source_target_pairs={{0,4},{1,5},{2,6},{3,7},{4,0},{5,1},{6,2},{7,3},{8,12},{9,13},{10,... | collective-permute-start | bytes 3145736 | tf_op jit(solution)/shard_map/ppermute | solution.py:35
  68.0 5.1 %collective-permute-start.19 = (bf16[2,256,1024]{2,1,0:T(8,128)(2,1)S(1)}, bf16[2,256,1024]{2,1,0:T(8,128)(2,1)S(1)}, u32[]{:S(2)}, u32[]{:S(2)}) collective-permute-start(bf16[2,256,1024]{2,1,0:T(8,128)(2,1)S(1)} %collective-permute-done.17.refs_1_), channel_id=1, source_target_pairs={{0,4},{1,5},{2,6},{3,7},{4,0},{5,1},{6,2},{7,3},{8,12},{9,13},{10,... | collective-permute-start | bytes 3145736 | tf_op jit(solution)/shard_map/ppermute | solution.py:35
  70.3 9.2 %collective-permute-start.13 = (bf16[512,256]{1,0:T(8,128)(2,1)S(1)}, bf16[512,256]{1,0:T(8,128)(2,1)S(1)}, u32[]{:S(2)}, u32[]{:S(2)}) collective-permute-start(bf16[512,256]{1,0:T(8,128)(2,1)S(1)} %get-tuple-element.69), channel_id=1, source_target_pairs={{0,32},{1,33},{2,34},{3,35},{4,36},{5,37},{6,38},{7,39},{8,40},{9,... | collective-permute-start | bytes 786440 | tf_op jit(solution)/shard_map/ppermute | solution.py:35
  70.4 10.8 %collective-permute-start.14 = (bf16[512,256]{1,0:T(8,128)(2,1)S(1)}, bf16[512,256]{1,0:T(8,128)(2,1)S(1)}, u32[]{:S(2)}, u32[]{:S(2)}) collective-permute-start(bf16[512,256]{1,0:T(8,128)(2,1)S(1)} %get-tuple-element.76.c0), channel_id=1, source_target_pairs={{0,64},{1,65},{2,66},{3,67},{4,68},{5,69},{6,70},{7,71},{8,72},{9,... | collective-permute-start | bytes 786440 | tf_op jit(solution)/shard_map/ppermute | solution.py:35
  73.1 12.8 %collective-permute-start.15 = (bf16[512,256]{1,0:T(8,128)(2,1)S(1)}, bf16[512,256]{1,0:T(8,128)(2,1)S(1)}, u32[]{:S(2)}, u32[]{:S(2)}) collective-permute-start(bf16[512,256]{1,0:T(8,128)(2,1)S(1)} %get-tuple-element.69), channel_id=1, source_target_pairs={{0,96},{1,97},{2,98},{3,99},{4,100},{5,101},{6,102},{7,103},{8,104... | collective-permute-start | bytes 786440 | tf_op jit(solution)/shard_map/ppermute | solution.py:35
  86.8 9.5 %collective-permute-start.20 = (bf16[256,512]{1,0:T(8,128)(2,1)S(1)}, bf16[256,512]{1,0:T(8,128)(2,1)S(1)}, u32[]{:S(2)}, u32[]{:S(2)}) collective-permute-start(bf16[256,512]{1,0:T(8,128)(2,1)S(1)} %get-tuple-element.81), channel_id=1, source_target_pairs={{0,1},{1,2},{2,3},{3,0},{4,5},{5,6},{6,7},{7,4},{8,9},{9,10},{10,1... | collective-permute-start | bytes 786440 | tf_op jit(solution)/shard_map/ppermute | solution.py:35
  87.6 10.0 %collective-permute-start.21 = (bf16[256,512]{1,0:T(8,128)(2,1)S(1)}, bf16[256,512]{1,0:T(8,128)(2,1)S(1)}, u32[]{:S(2)}, u32[]{:S(2)}) collective-permute-start(bf16[256,512]{1,0:T(8,128)(2,1)S(1)} %get-tuple-element.82), channel_id=1, source_target_pairs={{0,3},{1,0},{2,1},{3,2},{4,7},{5,4},{6,5},{7,6},{8,11},{9,8},{10,9... | collective-permute-start | bytes 786440 | tf_op jit(solution)/shard_map/ppermute | solution.py:35
  91.0 10.8 %collective-permute-start.23 = (bf16[256,512]{1,0:T(8,128)(2,1)S(1)}, bf16[256,512]{1,0:T(8,128)(2,1)S(1)}, u32[]{:S(2)}, u32[]{:S(2)}) collective-permute-start(bf16[256,512]{1,0:T(8,128)(2,1)S(1)} %get-tuple-element.84), channel_id=1, source_target_pairs={{0,1},{1,2},{2,3},{3,0},{4,5},{5,6},{6,7},{7,4},{8,9},{9,10},{10,1... | collective-permute-start | bytes 786440 | tf_op jit(solution)/shard_map/ppermute | solution.py:35
  92.8 10.4 %collective-permute-start.24 = (bf16[256,512]{1,0:T(8,128)(2,1)S(1)}, bf16[256,512]{1,0:T(8,128)(2,1)S(1)}, u32[]{:S(2)}, u32[]{:S(2)}) collective-permute-start(bf16[256,512]{1,0:T(8,128)(2,1)S(1)} %get-tuple-element.85), channel_id=1, source_target_pairs={{0,3},{1,0},{2,1},{3,2},{4,7},{5,4},{6,5},{7,6},{8,11},{9,8},{10,9... | collective-permute-start | bytes 786440 | tf_op jit(solution)/shard_map/ppermute | solution.py:35
  97.7 8.9 %collective-permute-start.22 = (bf16[256,512]{1,0:T(8,128)(2,1)S(1)}, bf16[256,512]{1,0:T(8,128)(2,1)S(1)}, u32[]{:S(2)}, u32[]{:S(2)}) collective-permute-start(bf16[256,512]{1,0:T(8,128)(2,1)S(1)} %get-tuple-element.83), channel_id=1, source_target_pairs={{0,1},{1,2},{2,3},{3,0},{4,5},{5,6},{6,7},{7,4},{8,9},{9,10},{10,1... | collective-permute-start | bytes 786440 | tf_op jit(solution)/shard_map/ppermute | solution.py:35
  98.4 9.5 %collective-permute-start.25 = (bf16[256,512]{1,0:T(8,128)(2,1)S(1)}, bf16[256,512]{1,0:T(8,128)(2,1)S(1)}, u32[]{:S(2)}, u32[]{:S(2)}) collective-permute-start(bf16[256,512]{1,0:T(8,128)(2,1)S(1)} %get-tuple-element.86), channel_id=1, source_target_pairs={{0,3},{1,0},{2,1},{3,2},{4,7},{5,4},{6,5},{7,6},{8,11},{9,8},{10,9... | collective-permute-start | bytes 786440 | tf_op jit(solution)/shard_map/ppermute | solution.py:35

commit v7 on v6

--- a/solution.py
+++ b/solution.py
@@ -57,15 +57,18 @@
     return (widened * inverse * gain_row).astype(jnp.bfloat16)
 
 
-def section_kernel(pad_ref, memory, targets, gain_ref, w_ref, *refs):
-    *out_refs, normed, x_rows, total, arrival = refs
-    k, steps = pl.program_id(0), pl.num_programs(0)
-    depth, width = w_ref.shape[1], w_ref.shape[3]
+def section_kernel(pad_ref, memory, targets, gain_ref, weights, *refs):
+    *out_refs, normed, x_rows, total, blocks, arrival, block_arrival = refs
+    steps, depth, _, width = blocks.shape
     rows = total.shape[0]
     half = rows // 2
     dim = out_refs[0].shape[1]
     z = position()[2]
     encoder = z < 2
+
+    def block_copy(k):
+        source = weights.at[0, pl.ds(pl.multiple_of(k * depth, depth), depth)]
+        return pltpu.make_async_copy(source, blocks.at[k], block_arrival.at[k])
 
     def normalise(source, count):
         block = 128
@@ -77,6 +80,8 @@
         ]
         for copy in copies:
             copy.start()
+        for k in range(steps // 2):
+            block_copy(k).start()
         for top in range(0, count, 64):
             if top % block == 0:
                 copies[top // block].wait()
@@ -84,44 +89,40 @@
             for j in range(normed.shape[0]):
                 normed[j, pl.ds(top, 64), :] = part[:, j * depth : (j + 1) * depth]
 
-    @pl.when((k == 0) & encoder)
+    @pl.when(encoder)
     def _():
         normalise(memory, half)
 
-    @pl.when((k == 0) & jnp.logical_not(encoder))
+    @pl.when(jnp.logical_not(encoder))
     def _():
         normalise(targets, rows)
 
-    def add(rows_of, found):
-        @pl.when(k == 0)
+    for k in range(steps // 2, steps):
+        block_copy(k).start()
+    total[...] = jnp.zeros_like(total)
+
+    @pl.loop(0, steps)
+    def _(k):
+        block_copy(k).wait()
+
+        @pl.when(encoder)
         def _():
-            total[rows_of, :] = found
-
-        @pl.when(k > 0)
+            both = blocks[k].reshape(depth, 2 * width)
+            found = jnp.dot(normed[k, :half, :], both, preferred_element_type=jnp.float32)
+            total[:half, :] += found[:, :width]
+            total[half:, :] += found[:, width:]
+
+        @pl.when(jnp.logical_not(encoder))
         def _():
-            total[rows_of, :] += found
-
-    @pl.when(encoder)
-    def _():
-        both = w_ref[0].reshape(depth, 2 * width)
-        found = jnp.dot(normed[k, :half, :], both, preferred_element_type=jnp.float32)
-        add(pl.ds(0, half), found[:, :width])
-        add(pl.ds(half, half), found[:, width:])
-
-    @pl.when(jnp.logical_not(encoder))
-    def _():
-        both = w_ref[0].reshape(depth, 2 * width)
-        found = jnp.dot(normed[k], both[:, :width], preferred_element_type=jnp.float32)
-        add(pl.ds(0, rows), found)
-
-    @pl.when(k == steps - 1)
-    def _():
-        position = lax.broadcasted_iota(jnp.int32, (MARK_ROWS, dim), 1)
-        marks = jnp.where(position < half - pad_ref[0], 0.0, DEAD).astype(jnp.bfloat16)
-        for d, ref in enumerate(out_refs):
-            head = (z + d) % 4
-            ref[:rows, :] = total[:, pl.ds(pl.multiple_of(head * dim, dim), dim)].astype(jnp.bfloat16)
-            ref[rows:, :] = marks
+            both = blocks[k].reshape(depth, 2 * width)
+            total[...] += jnp.dot(normed[k], both[:, :width], preferred_element_type=jnp.float32)
+
+    columns = lax.broadcasted_iota(jnp.int32, (MARK_ROWS, dim), 1)
+    marks = jnp.where(columns < half - pad_ref[0], 0.0, DEAD).astype(jnp.bfloat16)
+    for d, ref in enumerate(out_refs):
+        head = (z + d) % 4
+        ref[:rows, :] = total[:, pl.ds(pl.multiple_of(head * dim, dim), dim)].astype(jnp.bfloat16)
+        ref[rows:, :] = marks
 
 
 def section(pad_counts, memory, targets, gains, weights, dim):
@@ -131,25 +132,19 @@
     steps = model // depth
     slab = (rows + MARK_ROWS, dim)
     anywhere = pl.BlockSpec(memory_space=pl.ANY)
+    vmem = pl.BlockSpec(memory_space=pltpu.VMEM)
     return pl.pallas_call(
         section_kernel,
-        grid_spec=pltpu.PrefetchScalarGridSpec(
-            num_scalar_prefetch=1,
-            grid=(steps,),
-            in_specs=[
-                anywhere,
-                anywhere,
-                pl.BlockSpec((1, model), lambda k, pad: (0, 0)),
-                pl.BlockSpec((1, depth, 2, width), lambda k, pad: (0, k, 0, 0)),
-            ],
-            out_specs=[pl.BlockSpec(slab, lambda k, pad: (0, 0))] * 4,
-            scratch_shapes=[
-                pltpu.VMEM((steps, rows, depth), jnp.bfloat16),
-                pltpu.VMEM((rows, model), jnp.bfloat16),
-                pltpu.VMEM((rows, width), jnp.float32),
-                pltpu.SemaphoreType.DMA((rows // 128,)),
-            ],
-        ),
+        in_specs=[pl.BlockSpec(memory_space=pltpu.SMEM), anywhere, anywhere, vmem, anywhere],
+        out_specs=[vmem] * 4,
+        scratch_shapes=[
+            pltpu.VMEM((steps, rows, depth), jnp.bfloat16),
+            pltpu.VMEM((rows, model), jnp.bfloat16),
+            pltpu.VMEM((rows, width), jnp.float32),
+            pltpu.VMEM((steps, depth, 2, width), jnp.bfloat16),
+            pltpu.SemaphoreType.DMA((rows // 128,)),
+            pltpu.SemaphoreType.DMA((steps,)),
+        ],
         out_shape=[jax.ShapeDtypeStruct(slab, jnp.bfloat16)] * 4,
         cost_estimate=LIGHT,
         compiler_params=pltpu.CompilerParams(vmem_limit_bytes=VMEM),
@@ -442,7 +437,7 @@
     p = moved(share, down, decoder)
 
     own, *to = section(after(pad_counts, share), memory, targets, norm_gains, proj_weights, dim)
-    own, to, p = lax.optimization_barrier((own, to, p))
+    p = after(p, own)
     beside = moved(p, lambda x, y, z, c: (x, y ^ 1, z, c), encoder)
     r1, r3, r2 = along_z(to[0], 1), along_z(to[2], 3), along_z(to[1], 2)
     early = jnp.where(is_encoder, own, jnp.where(z == 2, r1, r3))

time: 109 us -> 106 us (0.972)
  Pallas kernels: 35.3 us -> 33.6 us
  starting transfers between devices: 35.2 us -> 34.1 us
    pallas_call x1, Pallas kernels: 13.5 us -> 11.5 us  [section(): pl.pallas_call(section_kernel, in_specs=[pl.BlockSpec(memory_space=pltpu....]
    ppermute x26, starting transfers between devices: 35.2 us -> 34.1 us  [moved(): return lax.ppermute(block, AXES, route)]
  transfers between devices with their start and end apart: 26 -> 26, of which waited for: 13 -> 12; matrix products, arithmetic and copies ran while one was open for 2% -> 2% of each run, Pallas kernels for 29% -> 28%
where the time goes in v7:
time: 106 us
  waiting for transfers between devices  35 us (33%)
  starting transfers between devices  34.1 us (32%)
  Pallas kernels  33.6 us (32%)
  other arithmetic  1.18 us (1%)
  local copies, waits for them, and re-layouts  1.12 us (1%)
    ppermute x26, waiting for transfers between devices, moved(): return lax.ppermute(block, AXES, route)  35 us
    ppermute x26, starting transfers between devices, moved(): return lax.ppermute(block, AXES, route)  34.1 us
    pallas_call x1, Pallas kernels, section(): pl.pallas_call(section_kernel, in_specs=[pl.BlockSpec(memory_space=pltpu....  11.5 us
    pallas_call x2, Pallas kernels, attend(): pl.pallas_call(functools.partial(attend_kernel, first, half, chunks), in_...  10.1 us
    pallas_call x1, Pallas kernels, second_half(): pl.pallas_call(second_half_kernel, grid_spec=pltpu.PrefetchScalarGridSpec...  5.36 us
    pallas_call x2, Pallas kernels, project(): pl.pallas_call(functools.partial(project_kernel, distances), in_specs=[vm...  2.77 us
    pallas_call x1, Pallas kernels, share_of(): pl.pallas_call(share_kernel, in_specs=[pl.BlockSpec(memory_space=pl.ANY)]...  2.16 us
  transfers between devices with their start and end apart: 26, of which 12 were waited for; matrix products, arithmetic and copies ran while one was open for 2% of the time, Pallas kernels for 28%

profile of v7, /device:TPU:38, one launch (start us, length us, event | category | flops | bytes accessed | tf_op | source)
XLA Modules:
  0.0 105.9 jit_solution(303361126010536977)
XLA Ops:
  0.0 2.2 %shard_map.55 = bf16[256,1024]{1,0:T(8,128)(2,1)} custom-call(bf16[1,4096,2,1024]{3,2,1,0:T(2,128)(2,1)} %w_ref.2), custom_call_target="tpu_custom_call" | custom-call | bytes 1024 | tf_op jit(solution)/shard_map/pallas_call | solution.py:191
  2.2 1.3 %collective-permute-start.3 = (bf16[256,1024]{1,0:T(8,128)(2,1)}, bf16[256,1024]{1,0:T(8,128)(2,1)S(1)}, u32[]{:S(2)}, u32[]{:S(2)}) collective-permute-start(bf16[256,1024]{1,0:T(8,128)(2,1)} %shard_map.55), channel_id=1, source_target_pairs={{64,32},{65,33},{66,34},{67,35},{68,36},{69,37},{70,38},{71,39},{7... | collective-permute-start | bytes 1572872 | tf_op jit(solution)/shard_map/ppermute | solution.py:35
  4.1 11.5 %shard_map.56 = (bf16[528,256]{1,0:T(8,128)(2,1)}, bf16[528,256]{1,0:T(8,128)(2,1)}, bf16[528,256]{1,0:T(8,128)(2,1)}, bf16[528,256]{1,0:T(8,128)(2,1)}) custom-call(s32[1]{0:T(128)S(6)} %copy.6.pad_ref, bf16[256,4096]{1,0:T(8,128)(2,1)} %memory.1, bf16[512,4096]{1,0:T(8,128)(2,1)} %targets.1, f32[1,4096]{1,0:T(1,128)} %gain_ref.1, ...), custom_call_target="tpu_custom_call" | custom-call | bytes 1024 | tf_op jit(solution)/shard_map/pallas_call | solution.py:136
  15.7 2.5 %collective-permute-start = (bf16[528,256]{1,0:T(8,128)(2,1)}, bf16[528,256]{1,0:T(8,128)(2,1)S(1)}, u32[]{:S(2)}, u32[]{:S(2)}) collective-permute-start(bf16[528,256]{1,0:T(8,128)(2,1)} %get-tuple-element.44), channel_id=1, source_target_pairs={{0,32},{1,33},{2,34},{3,35},{4,36},{5,37},{6,38},{7,39},{8,40},{9,... | collective-permute-start | bytes 811016 | tf_op jit(solution)/shard_map/ppermute | solution.py:35
  18.5 2.5 %collective-permute-start.2 = (bf16[528,256]{1,0:T(8,128)(2,1)}, bf16[528,256]{1,0:T(8,128)(2,1)S(1)}, u32[]{:S(2)}, u32[]{:S(2)}) collective-permute-start(bf16[528,256]{1,0:T(8,128)(2,1)} %get-tuple-element.46), channel_id=1, source_target_pairs={{0,96},{1,97},{2,98},{3,99},{4,100},{5,101},{6,102},{7,103},{8,104... | collective-permute-start | bytes 811016 | tf_op jit(solution)/shard_map/ppermute | solution.py:35
  21.1 3.5 %collective-permute-start.16 = (bf16[256,1024]{1,0:T(8,128)(2,1)S(1)}, bf16[256,1024]{1,0:T(8,128)(2,1)S(1)}, u32[]{:S(2)}, u32[]{:S(2)}) collective-permute-start(bf16[256,1024]{1,0:T(8,128)(2,1)S(1)} %collective-permute-done.3), channel_id=1, source_target_pairs={{0,8},{1,9},{2,10},{3,11},{4,12},{5,13},{6,14},{7,15},{8,0},{9,1},... | collective-permute-start | bytes 1572872 | tf_op jit(solution)/shard_map/ppermute | solution.py:35
  24.6 5.1 %collective-permute-done.refs_1_ = bf16[528,256]{1,0:T(8,128)(2,1)S(1)} collective-permute-done((bf16[528,256]{1,0:T(8,128)(2,1)}, bf16[528,256]{1,0:T(8,128)(2,1)S(1)}, u32[]{:S(2)}, u32[]{:S(2)}) %collective-permute-start) | collective-permute-done | bytes 270368 | tf_op jit(solution)/shard_map/ppermute | solution.py:35
  29.7 2.8 %collective-permute-done.2.refs_3_ = bf16[528,256]{1,0:T(8,128)(2,1)S(1)} collective-permute-done((bf16[528,256]{1,0:T(8,128)(2,1)}, bf16[528,256]{1,0:T(8,128)(2,1)S(1)}, u32[]{:S(2)}, u32[]{:S(2)}) %collective-permute-start.2) | collective-permute-done | bytes 270368 | tf_op jit(solution)/shard_map/ppermute | solution.py:35
  33.6 1.6 %collective-permute-start.4 = (bf16[2,528,256]{2,1,0:T(8,128)(2,1)S(1)}, bf16[2,528,256]{2,1,0:T(8,128)(2,1)S(1)}, u32[]{:S(2)}, u32[]{:S(2)}) collective-permute-start(bf16[2,528,256]{2,1,0:T(8,128)(2,1)S(1)} %pad_maximum_fusion.1.refs_4_), channel_id=1, source_target_pairs={{0,8},{1,9},{2,10},{3,11},{4,12},{5,13},{6,14},{7,15},{8,16},{9,17... | collective-permute-start | bytes 1622024 | tf_op jit(solution)/shard_map/ppermute | solution.py:35
  35.2 1.7 %collective-permute-start.5 = (bf16[2,528,256]{2,1,0:T(8,128)(2,1)S(1)}, bf16[2,528,256]{2,1,0:T(8,128)(2,1)S(1)}, u32[]{:S(2)}, u32[]{:S(2)}) collective-permute-start(bf16[2,528,256]{2,1,0:T(8,128)(2,1)S(1)} %pad_maximum_fusion.1.refs_4_), channel_id=1, source_target_pairs={{0,24},{1,25},{2,26},{3,27},{4,28},{5,29},{6,30},{7,31},{8,0},{9,1... | collective-permute-start | bytes 1622024 | tf_op jit(solution)/shard_map/ppermute | solution.py:35
  37.0 2.8 %collective-permute-start.17 = (bf16[2,256,1024]{2,1,0:T(8,128)(2,1)S(1)}, bf16[2,256,1024]{2,1,0:T(8,128)(2,1)S(1)}, u32[]{:S(2)}, u32[]{:S(2)}) collective-permute-start(bf16[2,256,1024]{2,1,0:T(8,128)(2,1)S(1)} %pad_maximum_fusion.refs_0_), channel_id=1, source_target_pairs={{0,32},{1,33},{2,34},{3,35},{4,36},{5,37},{6,38},{7,39},{8,40},{9,... | collective-permute-start | bytes 3145736 | tf_op jit(solution)/shard_map/ppermute | solution.py:35
  39.9 5.4 %shard_map.57.refs_4_ = bf16[2048,1024]{1,0:T(8,128)(2,1)} custom-call(s32[1]{0:T(128)} %constant.42.clone.1.start_ref, bf16[1,4096,2,1024]{3,2,1,0:T(2,128)(2,1)} %w_ref.2), custom_call_target="tpu_custom_call" | custom-call | bytes 1024 | tf_op jit(solution)/shard_map/pallas_call | solution.py:164
  45.2 3.0 %collective-permute-done.4.refs_5_ = bf16[2,528,256]{2,1,0:T(8,128)(2,1)S(1)} collective-permute-done((bf16[2,528,256]{2,1,0:T(8,128)(2,1)S(1)}, bf16[2,528,256]{2,1,0:T(8,128)(2,1)S(1)}, u32[]{:S(2)}, u32[]{:S(2)}) %collective-permute-start.4) | collective-permute-done | bytes 540704 | tf_op jit(solution)/shard_map/ppermute | solution.py:35
  48.8 1.6 %collective-permute-start.6 = (bf16[528,256]{1,0:T(8,128)(2,1)S(1)}, bf16[528,256]{1,0:T(8,128)(2,1)S(1)}, u32[]{:S(2)}, u32[]{:S(2)}) collective-permute-start(bf16[528,256]{1,0:T(8,128)(2,1)S(1)} %slice_bitcast_fusion.1), channel_id=1, source_target_pairs={{0,8},{1,9},{2,10},{3,11},{4,12},{5,13},{6,14},{7,15},{8,16},{9,17... | collective-permute-start | bytes 811016 | tf_op jit(solution)/shard_map/ppermute | solution.py:35
  50.5 1.7 %collective-permute-start.7 = (bf16[528,256]{1,0:T(8,128)(2,1)S(1)}, bf16[528,256]{1,0:T(8,128)(2,1)S(1)}, u32[]{:S(2)}, u32[]{:S(2)}) collective-permute-start(bf16[528,256]{1,0:T(8,128)(2,1)S(1)} %slice_bitcast_fusion), channel_id=1, source_target_pairs={{0,24},{1,25},{2,26},{3,27},{4,28},{5,29},{6,30},{7,31},{8,0},{9,1... | collective-permute-start | bytes 811016 | tf_op jit(solution)/shard_map/ppermute | solution.py:35
  52.3 7.3 %shard_map.58 = (f32[1024,256]{1,0:T(8,128)S(1)}, f32[1024,128]{1,0:T(8,128)S(1)}, f32[1024,128]{1,0:T(8,128)S(1)}) custom-call(bf16[528,256]{1,0:T(8,128)(2,1)S(1)} %copy-done.1, bf16[528,256]{1,0:T(8,128)(2,1)S(1)} %collective-permute-done.refs_1_, bf16[528,256]{1,0:T(8,128)(2,1)S(1)} %collective-permute-done.1.refs_2_, ...), custom_call_target="tpu_custom_call" | custom-call | bytes 1024 | tf_op jit(solution)/shard_map/pallas_call | solution.py:278
  60.2 2.0 %collective-permute-start.18 = (bf16[2,256,1024]{2,1,0:T(8,128)(2,1)S(1)}, bf16[2,256,1024]{2,1,0:T(8,128)(2,1)S(1)}, u32[]{:S(2)}, u32[]{:S(2)}) collective-permute-start(bf16[2,256,1024]{2,1,0:T(8,128)(2,1)S(1)} %pad_maximum_fusion.refs_0_), channel_id=1, source_target_pairs={{0,4},{1,5},{2,6},{3,7},{4,0},{5,1},{6,2},{7,3},{8,12},{9,13},{10,... | collective-permute-start | bytes 3145736 | tf_op jit(solution)/shard_map/ppermute | solution.py:35
  62.2 2.9 %shard_map.59 = (bf16[512,256]{1,0:T(8,128)(2,1)S(1)}, bf16[512,256]{1,0:T(8,128)(2,1)S(1)}) custom-call(bf16[528,256]{1,0:T(8,128)(2,1)S(1)} %copy-done.1, bf16[528,256]{1,0:T(8,128)(2,1)S(1)} %collective-permute-done.refs_1_, bf16[528,256]{1,0:T(8,128)(2,1)S(1)} %collective-permute-done.1.refs_2_, bf16[528,256]{1,0:T(8,128)(2,1)S(1)} %collective-permute-done.2.refs_3_, ...), custom_call_target="tpu_custom_call" | custom-call | bytes 1024 | tf_op jit(solution)/shard_map/pallas_call | solution.py:278
  65.1 2.3 %collective-permute-start.19 = (bf16[2,256,1024]{2,1,0:T(8,128)(2,1)S(1)}, bf16[2,256,1024]{2,1,0:T(8,128)(2,1)S(1)}, u32[]{:S(2)}, u32[]{:S(2)}) collective-permute-start(bf16[2,256,1024]{2,1,0:T(8,128)(2,1)S(1)} %collective-permute-done.17.refs_1_), channel_id=1, source_target_pairs={{0,4},{1,5},{2,6},{3,7},{4,0},{5,1},{6,2},{7,3},{8,12},{9,13},{10,... | collective-permute-start | bytes 3145736 | tf_op jit(solution)/shard_map/ppermute | solution.py:35
  67.5 2.6 %collective-permute-start.14 = (bf16[512,256]{1,0:T(8,128)(2,1)S(1)}, bf16[512,256]{1,0:T(8,128)(2,1)S(1)}, u32[]{:S(2)}, u32[]{:S(2)}) collective-permute-start(bf16[512,256]{1,0:T(8,128)(2,1)S(1)} %get-tuple-element.68.c0), channel_id=1, source_target_pairs={{0,64},{1,65},{2,66},{3,67},{4,68},{5,69},{6,70},{7,71},{8,72},{9,... | collective-permute-start | bytes 786440 | tf_op jit(solution)/shard_map/ppermute | solution.py:35
  70.6 6.0 %collective-permute-done.13.c1 = bf16[512,256]{1,0:T(8,128)(2,1)S(1)} collective-permute-done((bf16[512,256]{1,0:T(8,128)(2,1)S(1)}, bf16[512,256]{1,0:T(8,128)(2,1)S(1)}, u32[]{:S(2)}, u32[]{:S(2)}) %collective-permute-start.13) | collective-permute-done | bytes 262176 | tf_op jit(solution)/shard_map/ppermute | solution.py:35
  76.6 1.6 %collective-permute-done.14.c2 = bf16[512,256]{1,0:T(8,128)(2,1)S(1)} collective-permute-done((bf16[512,256]{1,0:T(8,128)(2,1)S(1)}, bf16[512,256]{1,0:T(8,128)(2,1)S(1)}, u32[]{:S(2)}, u32[]{:S(2)}) %collective-permute-start.14) | collective-permute-done | bytes 262176 | tf_op jit(solution)/shard_map/ppermute | solution.py:35
  78.3 4.7 %collective-permute-done.15.c3 = bf16[512,256]{1,0:T(8,128)(2,1)S(1)} collective-permute-done((bf16[512,256]{1,0:T(8,128)(2,1)S(1)}, bf16[512,256]{1,0:T(8,128)(2,1)S(1)}, u32[]{:S(2)}, u32[]{:S(2)}) %collective-permute-start.15) | collective-permute-done | bytes 262176 | tf_op jit(solution)/shard_map/ppermute | solution.py:35
  84.4 1.5 %collective-permute-start.21 = (bf16[256,512]{1,0:T(8,128)(2,1)S(1)}, bf16[256,512]{1,0:T(8,128)(2,1)S(1)}, u32[]{:S(2)}, u32[]{:S(2)}) collective-permute-start(bf16[256,512]{1,0:T(8,128)(2,1)S(1)} %get-tuple-element.74), channel_id=1, source_target_pairs={{0,3},{1,0},{2,1},{3,2},{4,7},{5,4},{6,5},{7,6},{8,11},{9,8},{10,9... | collective-permute-start | bytes 786440 | tf_op jit(solution)/shard_map/ppermute | solution.py:35
  85.9 1.9 %shard_map.62 = (f32[256,512]{1,0:T(8,128)S(1)}, bf16[256,512]{1,0:T(8,128)(2,1)S(1)}, bf16[256,512]{1,0:T(8,128)(2,1)S(1)}, f32[256,512]{1,0:T(8,128)S(1)}, f32...) custom-call(bf16[512,256]{1,0:T(8,128)(2,1)S(1)} %get-tuple-element.68.c0, bf16[512,256]{1,0:T(8,128)(2,1)S(1)} %collective-permute-done.13.c1, ...), custom_call_target="tpu_custom_call" | custom-call | bytes 1024 | tf_op jit(solution)/shard_map/pallas_call | solution.py:362
  87.8 1.8 %collective-permute-start.23 = (bf16[256,512]{1,0:T(8,128)(2,1)S(1)}, bf16[256,512]{1,0:T(8,128)(2,1)S(1)}, u32[]{:S(2)}, u32[]{:S(2)}) collective-permute-start(bf16[256,512]{1,0:T(8,128)(2,1)S(1)} %get-tuple-element.76), channel_id=1, source_target_pairs={{0,1},{1,2},{2,3},{3,0},{4,5},{5,6},{6,7},{7,4},{8,9},{9,10},{10,1... | collective-permute-start | bytes 786440 | tf_op jit(solution)/shard_map/ppermute | solution.py:35
  89.9 3.1 %collective-permute-done.20.upward = bf16[256,512]{1,0:T(8,128)(2,1)S(1)} collective-permute-done((bf16[256,512]{1,0:T(8,128)(2,1)S(1)}, bf16[256,512]{1,0:T(8,128)(2,1)S(1)}, u32[]{:S(2)}, u32[]{:S(2)}) %collective-permute-start.20) | collective-permute-done | bytes 262176 | tf_op jit(solution)/shard_map/ppermute | solution.py:35
  93.1 1.4 %collective-permute-done.21.downward = bf16[256,512]{1,0:T(8,128)(2,1)S(1)} collective-permute-done((bf16[256,512]{1,0:T(8,128)(2,1)S(1)}, bf16[256,512]{1,0:T(8,128)(2,1)S(1)}, u32[]{:S(2)}, u32[]{:S(2)}) %collective-permute-start.21) | collective-permute-done | bytes 262176 | tf_op jit(solution)/shard_map/ppermute | solution.py:35
  95.2 1.5 %collective-permute-start.25 = (bf16[256,512]{1,0:T(8,128)(2,1)S(1)}, bf16[256,512]{1,0:T(8,128)(2,1)S(1)}, u32[]{:S(2)}, u32[]{:S(2)}) collective-permute-start(bf16[256,512]{1,0:T(8,128)(2,1)S(1)} %get-tuple-element.78), channel_id=1, source_target_pairs={{0,3},{1,0},{2,1},{3,2},{4,7},{5,4},{6,5},{7,6},{8,11},{9,8},{10,9... | collective-permute-start | bytes 786440 | tf_op jit(solution)/shard_map/ppermute | solution.py:35
  98.7 1.4 %collective-permute-done.24.down_top = bf16[256,512]{1,0:T(8,128)(2,1)S(1)} collective-permute-done((bf16[256,512]{1,0:T(8,128)(2,1)S(1)}, bf16[256,512]{1,0:T(8,128)(2,1)S(1)}, u32[]{:S(2)}, u32[]{:S(2)}) %collective-permute-start.24) | collective-permute-done | bytes 262176 | tf_op jit(solution)/shard_map/ppermute | solution.py:35
  100.1 3.2 %collective-permute-done.22.up_top = bf16[256,512]{1,0:T(8,128)(2,1)S(1)} collective-permute-done((bf16[256,512]{1,0:T(8,128)(2,1)S(1)}, bf16[256,512]{1,0:T(8,128)(2,1)S(1)}, u32[]{:S(2)}, u32[]{:S(2)}) %collective-permute-start.22) | collective-permute-done | bytes 262176 | tf_op jit(solution)/shard_map/ppermute | solution.py:35
  103.4 1.5 %collective-permute-done.25.down_end = bf16[256,512]{1,0:T(8,128)(2,1)S(1)} collective-permute-done((bf16[256,512]{1,0:T(8,128)(2,1)S(1)}, bf16[256,512]{1,0:T(8,128)(2,1)S(1)}, u32[]{:S(2)}, u32[]{:S(2)}) %collective-permute-start.25) | collective-permute-done | bytes 262176 | tf_op jit(solution)/shard_map/ppermute | solution.py:35
  (40 shorter events, 8.8 us)
Async XLA Ops:
  2.2 18.9 %collective-permute-start.3 = (bf16[256,1024]{1,0:T(8,128)(2,1)}, bf16[256,1024]{1,0:T(8,128)(2,1)S(1)}, u32[]{:S(2)}, u32[]{:S(2)}) collective-permute-start(bf16[256,1024]{1,0:T(8,128)(2,1)} %shard_map.55), channel_id=1, source_target_pairs={{64,32},{65,33},{66,34},{67,35},{68,36},{69,37},{70,38},{71,39},{7... | collective-permute-start | bytes 1572872 | tf_op jit(solution)/shard_map/ppermute | solution.py:35
  15.7 14.1 %collective-permute-start = (bf16[528,256]{1,0:T(8,128)(2,1)}, bf16[528,256]{1,0:T(8,128)(2,1)S(1)}, u32[]{:S(2)}, u32[]{:S(2)}) collective-permute-start(bf16[528,256]{1,0:T(8,128)(2,1)} %get-tuple-element.44), channel_id=1, source_target_pairs={{0,32},{1,33},{2,34},{3,35},{4,36},{5,37},{6,38},{7,39},{8,40},{9,... | collective-permute-start | bytes 811016 | tf_op jit(solution)/shard_map/ppermute | solution.py:35
  18.1 11.6 %collective-permute-start.1 = (bf16[528,256]{1,0:T(8,128)(2,1)}, bf16[528,256]{1,0:T(8,128)(2,1)S(1)}, u32[]{:S(2)}, u32[]{:S(2)}) collective-permute-start(bf16[528,256]{1,0:T(8,128)(2,1)} %get-tuple-element.45), channel_id=1, source_target_pairs={{0,64},{1,65},{2,66},{3,67},{4,68},{5,69},{6,70},{7,71},{8,72},{9,... | collective-permute-start | bytes 811016 | tf_op jit(solution)/shard_map/ppermute | solution.py:35
  18.5 13.9 %collective-permute-start.2 = (bf16[528,256]{1,0:T(8,128)(2,1)}, bf16[528,256]{1,0:T(8,128)(2,1)S(1)}, u32[]{:S(2)}, u32[]{:S(2)}) collective-permute-start(bf16[528,256]{1,0:T(8,128)(2,1)} %get-tuple-element.46), channel_id=1, source_target_pairs={{0,96},{1,97},{2,98},{3,99},{4,100},{5,101},{6,102},{7,103},{8,104... | collective-permute-start | bytes 811016 | tf_op jit(solution)/shard_map/ppermute | solution.py:35
  21.1 15.8 %collective-permute-start.16 = (bf16[256,1024]{1,0:T(8,128)(2,1)S(1)}, bf16[256,1024]{1,0:T(8,128)(2,1)S(1)}, u32[]{:S(2)}, u32[]{:S(2)}) collective-permute-start(bf16[256,1024]{1,0:T(8,128)(2,1)S(1)} %collective-permute-done.3), channel_id=1, source_target_pairs={{0,8},{1,9},{2,10},{3,11},{4,12},{5,13},{6,14},{7,15},{8,0},{9,1},... | collective-permute-start | bytes 1572872 | tf_op jit(solution)/shard_map/ppermute | solution.py:35
  33.6 14.7 %collective-permute-start.4 = (bf16[2,528,256]{2,1,0:T(8,128)(2,1)S(1)}, bf16[2,528,256]{2,1,0:T(8,128)(2,1)S(1)}, u32[]{:S(2)}, u32[]{:S(2)}) collective-permute-start(bf16[2,528,256]{2,1,0:T(8,128)(2,1)S(1)} %pad_maximum_fusion.1.refs_4_), channel_id=1, source_target_pairs={{0,8},{1,9},{2,10},{3,11},{4,12},{5,13},{6,14},{7,15},{8,16},{9,17... | collective-permute-start | bytes 1622024 | tf_op jit(solution)/shard_map/ppermute | solution.py:35
  35.2 13.1 %collective-permute-start.5 = (bf16[2,528,256]{2,1,0:T(8,128)(2,1)S(1)}, bf16[2,528,256]{2,1,0:T(8,128)(2,1)S(1)}, u32[]{:S(2)}, u32[]{:S(2)}) collective-permute-start(bf16[2,528,256]{2,1,0:T(8,128)(2,1)S(1)} %pad_maximum_fusion.1.refs_4_), channel_id=1, source_target_pairs={{0,24},{1,25},{2,26},{3,27},{4,28},{5,29},{6,30},{7,31},{8,0},{9,1... | collective-permute-start | bytes 1622024 | tf_op jit(solution)/shard_map/ppermute | solution.py:35
  36.9 13.6 %collective-permute-start.8 = (bf16[2,528,256]{2,1,0:T(8,128)(2,1)S(1)}, bf16[2,528,256]{2,1,0:T(8,128)(2,1)S(1)}, u32[]{:S(2)}, u32[]{:S(2)}) collective-permute-start(bf16[2,528,256]{2,1,0:T(8,128)(2,1)S(1)} %pad_maximum_fusion.1.refs_4_), channel_id=1, source_target_pairs={{0,4},{1,5},{2,6},{3,7},{4,0},{5,1},{6,2},{7,3},{8,12},{9,13},{10,... | collective-permute-start | bytes 1622024 | tf_op jit(solution)/shard_map/ppermute | solution.py:35
  37.0 15.3 %copy-start.1 = (bf16[528,256]{1,0:T(8,128)(2,1)S(1)}, bf16[528,256]{1,0:T(8,128)(2,1)}, u32[]{:S(2)}) copy-start(bf16[528,256]{1,0:T(8,128)(2,1)} %get-tuple-element.43.refs_0_) | copy-start | bytes 811012
  37.0 28.0 %collective-permute-start.17 = (bf16[2,256,1024]{2,1,0:T(8,128)(2,1)S(1)}, bf16[2,256,1024]{2,1,0:T(8,128)(2,1)S(1)}, u32[]{:S(2)}, u32[]{:S(2)}) collective-permute-start(bf16[2,256,1024]{2,1,0:T(8,128)(2,1)S(1)} %pad_maximum_fusion.refs_0_), channel_id=1, source_target_pairs={{0,32},{1,33},{2,34},{3,35},{4,36},{5,37},{6,38},{7,39},{8,40},{9,... | collective-permute-start | bytes 3145736 | tf_op jit(solution)/shard_map/ppermute | solution.py:35
  48.3 4.0 %collective-permute-start.10 = (bf16[2,528,256]{2,1,0:T(8,128)(2,1)S(1)}, bf16[2,528,256]{2,1,0:T(8,128)(2,1)S(1)}, u32[]{:S(2)}, u32[]{:S(2)}) collective-permute-start(bf16[2,528,256]{2,1,0:T(8,128)(2,1)S(1)} %collective-permute-done.5.refs_6_), channel_id=1, source_target_pairs={{0,4},{1,5},{2,6},{3,7},{4,0},{5,1},{6,2},{7,3},{8,12},{9,13},{10,... | collective-permute-start | bytes 1622024 | tf_op jit(solution)/shard_map/ppermute | solution.py:35
  48.3 4.0 %collective-permute-start.9 = (bf16[2,528,256]{2,1,0:T(8,128)(2,1)S(1)}, bf16[2,528,256]{2,1,0:T(8,128)(2,1)S(1)}, u32[]{:S(2)}, u32[]{:S(2)}) collective-permute-start(bf16[2,528,256]{2,1,0:T(8,128)(2,1)S(1)} %collective-permute-done.4.refs_5_), channel_id=1, source_target_pairs={{0,4},{1,5},{2,6},{3,7},{4,0},{5,1},{6,2},{7,3},{8,12},{9,13},{10,... | collective-permute-start | bytes 1622024 | tf_op jit(solution)/shard_map/ppermute | solution.py:35
  48.8 10.7 %collective-permute-start.6 = (bf16[528,256]{1,0:T(8,128)(2,1)S(1)}, bf16[528,256]{1,0:T(8,128)(2,1)S(1)}, u32[]{:S(2)}, u32[]{:S(2)}) collective-permute-start(bf16[528,256]{1,0:T(8,128)(2,1)S(1)} %slice_bitcast_fusion.1), channel_id=1, source_target_pairs={{0,8},{1,9},{2,10},{3,11},{4,12},{5,13},{6,14},{7,15},{8,16},{9,17... | collective-permute-start | bytes 811016 | tf_op jit(solution)/shard_map/ppermute | solution.py:35
  50.5 19.6 %copy-start = (bf16[2048,1024]{1,0:T(8,128)(2,1)S(1)}, bf16[2048,1024]{1,0:T(8,128)(2,1)}, u32[]{:S(2)}) copy-start(bf16[2048,1024]{1,0:T(8,128)(2,1)} %shard_map.57.refs_4_) | copy-start | bytes 12582916
  50.5 9.1 %collective-permute-start.7 = (bf16[528,256]{1,0:T(8,128)(2,1)S(1)}, bf16[528,256]{1,0:T(8,128)(2,1)S(1)}, u32[]{:S(2)}, u32[]{:S(2)}) collective-permute-start(bf16[528,256]{1,0:T(8,128)(2,1)S(1)} %slice_bitcast_fusion), channel_id=1, source_target_pairs={{0,24},{1,25},{2,26},{3,27},{4,28},{5,29},{6,30},{7,31},{8,0},{9,1... | collective-permute-start | bytes 811016 | tf_op jit(solution)/shard_map/ppermute | solution.py:35
  59.6 2.6 %collective-permute-start.11 = (bf16[1,528,256]{2,1,0:T(8,128)(2,1)S(1)}, bf16[1,528,256]{2,1,0:T(8,128)(2,1)S(1)}, u32[]{:S(2)}, u32[]{:S(2)}) collective-permute-start(bf16[1,528,256]{2,1,0:T(8,128)(2,1)S(1)} %bitcast.12), channel_id=1, source_target_pairs={{0,4},{1,5},{2,6},{3,7},{4,0},{5,1},{6,2},{7,3},{8,12},{9,13},{10,... | collective-permute-start | bytes 811016 | tf_op jit(solution)/shard_map/ppermute | solution.py:35
  59.7 2.5 %collective-permute-start.12 = (bf16[1,528,256]{2,1,0:T(8,128)(2,1)S(1)}, bf16[1,528,256]{2,1,0:T(8,128)(2,1)S(1)}, u32[]{:S(2)}, u32[]{:S(2)}) collective-permute-start(bf16[1,528,256]{2,1,0:T(8,128)(2,1)S(1)} %bitcast.14), channel_id=1, source_target_pairs={{0,4},{1,5},{2,6},{3,7},{4,0},{5,1},{6,2},{7,3},{8,12},{9,13},{10,... | collective-permute-start | bytes 811016 | tf_op jit(solution)/shard_map/ppermute | solution.py:35
  60.2 10.0 %collective-permute-start.18 = (bf16[2,256,1024]{2,1,0:T(8,128)(2,1)S(1)}, bf16[2,256,1024]{2,1,0:T(8,128)(2,1)S(1)}, u32[]{:S(2)}, u32[]{:S(2)}) collective-permute-start(bf16[2,256,1024]{2,1,0:T(8,128)(2,1)S(1)} %pad_maximum_fusion.refs_0_), channel_id=1, source_target_pairs={{0,4},{1,5},{2,6},{3,7},{4,0},{5,1},{6,2},{7,3},{8,12},{9,13},{10,... | collective-permute-start | bytes 3145736 | tf_op jit(solution)/shard_map/ppermute | solution.py:35
  65.1 5.1 %collective-permute-start.19 = (bf16[2,256,1024]{2,1,0:T(8,128)(2,1)S(1)}, bf16[2,256,1024]{2,1,0:T(8,128)(2,1)S(1)}, u32[]{:S(2)}, u32[]{:S(2)}) collective-permute-start(bf16[2,256,1024]{2,1,0:T(8,128)(2,1)S(1)} %collective-permute-done.17.refs_1_), channel_id=1, source_target_pairs={{0,4},{1,5},{2,6},{3,7},{4,0},{5,1},{6,2},{7,3},{8,12},{9,13},{10,... | collective-permute-start | bytes 3145736 | tf_op jit(solution)/shard_map/ppermute | solution.py:35
  67.4 9.2 %collective-permute-start.13 = (bf16[512,256]{1,0:T(8,128)(2,1)S(1)}, bf16[512,256]{1,0:T(8,128)(2,1)S(1)}, u32[]{:S(2)}, u32[]{:S(2)}) collective-permute-start(bf16[512,256]{1,0:T(8,128)(2,1)S(1)} %get-tuple-element.61), channel_id=1, source_target_pairs={{0,32},{1,33},{2,34},{3,35},{4,36},{5,37},{6,38},{7,39},{8,40},{9,... | collective-permute-start | bytes 786440 | tf_op jit(solution)/shard_map/ppermute | solution.py:35
  67.5 10.8 %collective-permute-start.14 = (bf16[512,256]{1,0:T(8,128)(2,1)S(1)}, bf16[512,256]{1,0:T(8,128)(2,1)S(1)}, u32[]{:S(2)}, u32[]{:S(2)}) collective-permute-start(bf16[512,256]{1,0:T(8,128)(2,1)S(1)} %get-tuple-element.68.c0), channel_id=1, source_target_pairs={{0,64},{1,65},{2,66},{3,67},{4,68},{5,69},{6,70},{7,71},{8,72},{9,... | collective-permute-start | bytes 786440 | tf_op jit(solution)/shard_map/ppermute | solution.py:35
  70.1 12.9 %collective-permute-start.15 = (bf16[512,256]{1,0:T(8,128)(2,1)S(1)}, bf16[512,256]{1,0:T(8,128)(2,1)S(1)}, u32[]{:S(2)}, u32[]{:S(2)}) collective-permute-start(bf16[512,256]{1,0:T(8,128)(2,1)S(1)} %get-tuple-element.61), channel_id=1, source_target_pairs={{0,96},{1,97},{2,98},{3,99},{4,100},{5,101},{6,102},{7,103},{8,104... | collective-permute-start | bytes 786440 | tf_op jit(solution)/shard_map/ppermute | solution.py:35
  83.8 9.2 %collective-permute-start.20 = (bf16[256,512]{1,0:T(8,128)(2,1)S(1)}, bf16[256,512]{1,0:T(8,128)(2,1)S(1)}, u32[]{:S(2)}, u32[]{:S(2)}) collective-permute-start(bf16[256,512]{1,0:T(8,128)(2,1)S(1)} %get-tuple-element.73), channel_id=1, source_target_pairs={{0,1},{1,2},{2,3},{3,0},{4,5},{5,6},{6,7},{7,4},{8,9},{9,10},{10,1... | collective-permute-start | bytes 786440 | tf_op jit(solution)/shard_map/ppermute | solution.py:35
  84.4 10.1 %collective-permute-start.21 = (bf16[256,512]{1,0:T(8,128)(2,1)S(1)}, bf16[256,512]{1,0:T(8,128)(2,1)S(1)}, u32[]{:S(2)}, u32[]{:S(2)}) collective-permute-start(bf16[256,512]{1,0:T(8,128)(2,1)S(1)} %get-tuple-element.74), channel_id=1, source_target_pairs={{0,3},{1,0},{2,1},{3,2},{4,7},{5,4},{6,5},{7,6},{8,11},{9,8},{10,9... | collective-permute-start | bytes 786440 | tf_op jit(solution)/shard_map/ppermute | solution.py:35
  87.8 10.8 %collective-permute-start.23 = (bf16[256,512]{1,0:T(8,128)(2,1)S(1)}, bf16[256,512]{1,0:T(8,128)(2,1)S(1)}, u32[]{:S(2)}, u32[]{:S(2)}) collective-permute-start(bf16[256,512]{1,0:T(8,128)(2,1)S(1)} %get-tuple-element.76), channel_id=1, source_target_pairs={{0,1},{1,2},{2,3},{3,0},{4,5},{5,6},{6,7},{7,4},{8,9},{9,10},{10,1... | collective-permute-start | bytes 786440 | tf_op jit(solution)/shard_map/ppermute | solution.py:35
  89.6 10.5 %collective-permute-start.24 = (bf16[256,512]{1,0:T(8,128)(2,1)S(1)}, bf16[256,512]{1,0:T(8,128)(2,1)S(1)}, u32[]{:S(2)}, u32[]{:S(2)}) collective-permute-start(bf16[256,512]{1,0:T(8,128)(2,1)S(1)} %get-tuple-element.77), channel_id=1, source_target_pairs={{0,3},{1,0},{2,1},{3,2},{4,7},{5,4},{6,5},{7,6},{8,11},{9,8},{10,9... | collective-permute-start | bytes 786440 | tf_op jit(solution)/shard_map/ppermute | solution.py:35
  94.6 8.8 %collective-permute-start.22 = (bf16[256,512]{1,0:T(8,128)(2,1)S(1)}, bf16[256,512]{1,0:T(8,128)(2,1)S(1)}, u32[]{:S(2)}, u32[]{:S(2)}) collective-permute-start(bf16[256,512]{1,0:T(8,128)(2,1)S(1)} %get-tuple-element.75), channel_id=1, source_target_pairs={{0,1},{1,2},{2,3},{3,0},{4,5},{5,6},{6,7},{7,4},{8,9},{9,10},{10,1... | collective-permute-start | bytes 786440 | tf_op jit(solution)/shard_map/ppermute | solution.py:35
  95.2 9.6 %collective-permute-start.25 = (bf16[256,512]{1,0:T(8,128)(2,1)S(1)}, bf16[256,512]{1,0:T(8,128)(2,1)S(1)}, u32[]{:S(2)}, u32[]{:S(2)}) collective-permute-start(bf16[256,512]{1,0:T(8,128)(2,1)S(1)} %get-tuple-element.78), channel_id=1, source_target_pairs={{0,3},{1,0},{2,1},{3,2},{4,7},{5,4},{6,5},{7,6},{8,11},{9,8},{10,9... | collective-permute-start | bytes 786440 | tf_op jit(solution)/shard_map/ppermute | solution.py:35

commit v8 on v7

--- a/solution.py
+++ b/solution.py
@@ -211,7 +211,7 @@
     for j, ref in enumerate(pieces):
         keys[j * size : (j + 1) * size, :] = ref[:size, :]
         values[j * size : (j + 1) * size, :] = ref[size : 2 * size, :]
-        marks[:, j * size : (j + 1) * size] = ref[2 * size : 2 * size + 8, :].astype(jnp.float32)
+        marks[:, j * size : (j + 1) * size] = ref[2 * size : 2 * size + MARK_ROWS, :].astype(jnp.float32)
 
     def run(at):
         base = at * 2 * half
@@ -283,7 +283,7 @@
             pltpu.VMEM((2 * half, dim), jnp.bfloat16),
             pltpu.VMEM((keys, dim), jnp.bfloat16),
             pltpu.VMEM((keys, dim), jnp.bfloat16),
-            pltpu.VMEM((8, keys), jnp.float32),
+            pltpu.VMEM((MARK_ROWS, keys), jnp.float32),
         ],
         out_shape=out_shape,
         cost_estimate=LIGHT,

time: 106 us -> 106 us (level)
  no operation moved by 1% of the time
where the time goes in v8:
time: 106 us
  waiting for transfers between devices  35 us (33%)
  starting transfers between devices  34.1 us (32%)
  Pallas kernels  33.6 us (32%)
  other arithmetic  1.18 us (1%)
  local copies, waits for them, and re-layouts  1.12 us (1%)
    ppermute x26, waiting for transfers between devices, moved(): return lax.ppermute(block, AXES, route)  35 us
    ppermute x26, starting transfers between devices, moved(): return lax.ppermute(block, AXES, route)  34.1 us
    pallas_call x1, Pallas kernels, section(): pl.pallas_call(section_kernel, in_specs=[pl.BlockSpec(memory_space=pltpu....  11.5 us
    pallas_call x2, Pallas kernels, attend(): pl.pallas_call(functools.partial(attend_kernel, first, half, chunks), in_...  10.1 us
    pallas_call x1, Pallas kernels, second_half(): pl.pallas_call(second_half_kernel, grid_spec=pltpu.PrefetchScalarGridSpec...  5.36 us
    pallas_call x2, Pallas kernels, project(): pl.pallas_call(functools.partial(project_kernel, distances), in_specs=[vm...  2.77 us
    pallas_call x1, Pallas kernels, share_of(): pl.pallas_call(share_kernel, in_specs=[pl.BlockSpec(memory_space=pl.ANY)]...  2.16 us
  transfers between devices with their start and end apart: 26, of which 12 were waited for; matrix products, arithmetic and copies ran while one was open for 2% of the time, Pallas kernels for 28%

profile of v8, /device:TPU:38, one launch (start us, length us, event | category | flops | bytes accessed | tf_op | source)
XLA Modules:
  0.0 105.9 jit_solution(14806755650526011886)
XLA Ops:
  0.0 2.2 %shard_map.55 = bf16[256,1024]{1,0:T(8,128)(2,1)} custom-call(bf16[1,4096,2,1024]{3,2,1,0:T(2,128)(2,1)} %w_ref.2), custom_call_target="tpu_custom_call" | custom-call | bytes 1024 | tf_op jit(solution)/shard_map/pallas_call | solution.py:191
  2.2 1.3 %collective-permute-start.3 = (bf16[256,1024]{1,0:T(8,128)(2,1)}, bf16[256,1024]{1,0:T(8,128)(2,1)S(1)}, u32[]{:S(2)}, u32[]{:S(2)}) collective-permute-start(bf16[256,1024]{1,0:T(8,128)(2,1)} %shard_map.55), channel_id=1, source_target_pairs={{64,32},{65,33},{66,34},{67,35},{68,36},{69,37},{70,38},{71,39},{7... | collective-permute-start | bytes 1572872 | tf_op jit(solution)/shard_map/ppermute | solution.py:35
  4.1 11.5 %shard_map.56 = (bf16[528,256]{1,0:T(8,128)(2,1)}, bf16[528,256]{1,0:T(8,128)(2,1)}, bf16[528,256]{1,0:T(8,128)(2,1)}, bf16[528,256]{1,0:T(8,128)(2,1)}) custom-call(s32[1]{0:T(128)S(6)} %copy.6.pad_ref, bf16[256,4096]{1,0:T(8,128)(2,1)} %memory.1, bf16[512,4096]{1,0:T(8,128)(2,1)} %targets.1, f32[1,4096]{1,0:T(1,128)} %gain_ref.1, ...), custom_call_target="tpu_custom_call" | custom-call | bytes 1024 | tf_op jit(solution)/shard_map/pallas_call | solution.py:136
  15.7 2.5 %collective-permute-start = (bf16[528,256]{1,0:T(8,128)(2,1)}, bf16[528,256]{1,0:T(8,128)(2,1)S(1)}, u32[]{:S(2)}, u32[]{:S(2)}) collective-permute-start(bf16[528,256]{1,0:T(8,128)(2,1)} %get-tuple-element.44), channel_id=1, source_target_pairs={{0,32},{1,33},{2,34},{3,35},{4,36},{5,37},{6,38},{7,39},{8,40},{9,... | collective-permute-start | bytes 811016 | tf_op jit(solution)/shard_map/ppermute | solution.py:35
  18.5 2.5 %collective-permute-start.2 = (bf16[528,256]{1,0:T(8,128)(2,1)}, bf16[528,256]{1,0:T(8,128)(2,1)S(1)}, u32[]{:S(2)}, u32[]{:S(2)}) collective-permute-start(bf16[528,256]{1,0:T(8,128)(2,1)} %get-tuple-element.46), channel_id=1, source_target_pairs={{0,96},{1,97},{2,98},{3,99},{4,100},{5,101},{6,102},{7,103},{8,104... | collective-permute-start | bytes 811016 | tf_op jit(solution)/shard_map/ppermute | solution.py:35
  21.1 3.5 %collective-permute-start.16 = (bf16[256,1024]{1,0:T(8,128)(2,1)S(1)}, bf16[256,1024]{1,0:T(8,128)(2,1)S(1)}, u32[]{:S(2)}, u32[]{:S(2)}) collective-permute-start(bf16[256,1024]{1,0:T(8,128)(2,1)S(1)} %collective-permute-done.3), channel_id=1, source_target_pairs={{0,8},{1,9},{2,10},{3,11},{4,12},{5,13},{6,14},{7,15},{8,0},{9,1},... | collective-permute-start | bytes 1572872 | tf_op jit(solution)/shard_map/ppermute | solution.py:35
  24.6 5.1 %collective-permute-done.refs_1_ = bf16[528,256]{1,0:T(8,128)(2,1)S(1)} collective-permute-done((bf16[528,256]{1,0:T(8,128)(2,1)}, bf16[528,256]{1,0:T(8,128)(2,1)S(1)}, u32[]{:S(2)}, u32[]{:S(2)}) %collective-permute-start) | collective-permute-done | bytes 270368 | tf_op jit(solution)/shard_map/ppermute | solution.py:35
  29.7 2.8 %collective-permute-done.2.refs_3_ = bf16[528,256]{1,0:T(8,128)(2,1)S(1)} collective-permute-done((bf16[528,256]{1,0:T(8,128)(2,1)}, bf16[528,256]{1,0:T(8,128)(2,1)S(1)}, u32[]{:S(2)}, u32[]{:S(2)}) %collective-permute-start.2) | collective-permute-done | bytes 270368 | tf_op jit(solution)/shard_map/ppermute | solution.py:35
  33.6 1.6 %collective-permute-start.4 = (bf16[2,528,256]{2,1,0:T(8,128)(2,1)S(1)}, bf16[2,528,256]{2,1,0:T(8,128)(2,1)S(1)}, u32[]{:S(2)}, u32[]{:S(2)}) collective-permute-start(bf16[2,528,256]{2,1,0:T(8,128)(2,1)S(1)} %pad_maximum_fusion.1.refs_4_), channel_id=1, source_target_pairs={{0,8},{1,9},{2,10},{3,11},{4,12},{5,13},{6,14},{7,15},{8,16},{9,17... | collective-permute-start | bytes 1622024 | tf_op jit(solution)/shard_map/ppermute | solution.py:35
  35.2 1.7 %collective-permute-start.5 = (bf16[2,528,256]{2,1,0:T(8,128)(2,1)S(1)}, bf16[2,528,256]{2,1,0:T(8,128)(2,1)S(1)}, u32[]{:S(2)}, u32[]{:S(2)}) collective-permute-start(bf16[2,528,256]{2,1,0:T(8,128)(2,1)S(1)} %pad_maximum_fusion.1.refs_4_), channel_id=1, source_target_pairs={{0,24},{1,25},{2,26},{3,27},{4,28},{5,29},{6,30},{7,31},{8,0},{9,1... | collective-permute-start | bytes 1622024 | tf_op jit(solution)/shard_map/ppermute | solution.py:35
  37.0 2.8 %collective-permute-start.17 = (bf16[2,256,1024]{2,1,0:T(8,128)(2,1)S(1)}, bf16[2,256,1024]{2,1,0:T(8,128)(2,1)S(1)}, u32[]{:S(2)}, u32[]{:S(2)}) collective-permute-start(bf16[2,256,1024]{2,1,0:T(8,128)(2,1)S(1)} %pad_maximum_fusion.refs_0_), channel_id=1, source_target_pairs={{0,32},{1,33},{2,34},{3,35},{4,36},{5,37},{6,38},{7,39},{8,40},{9,... | collective-permute-start | bytes 3145736 | tf_op jit(solution)/shard_map/ppermute | solution.py:35
  39.9 5.4 %shard_map.57.refs_4_ = bf16[2048,1024]{1,0:T(8,128)(2,1)} custom-call(s32[1]{0:T(128)} %constant.42.clone.1.start_ref, bf16[1,4096,2,1024]{3,2,1,0:T(2,128)(2,1)} %w_ref.2), custom_call_target="tpu_custom_call" | custom-call | bytes 1024 | tf_op jit(solution)/shard_map/pallas_call | solution.py:164
  45.2 3.0 %collective-permute-done.4.refs_5_ = bf16[2,528,256]{2,1,0:T(8,128)(2,1)S(1)} collective-permute-done((bf16[2,528,256]{2,1,0:T(8,128)(2,1)S(1)}, bf16[2,528,256]{2,1,0:T(8,128)(2,1)S(1)}, u32[]{:S(2)}, u32[]{:S(2)}) %collective-permute-start.4) | collective-permute-done | bytes 540704 | tf_op jit(solution)/shard_map/ppermute | solution.py:35
  48.8 1.6 %collective-permute-start.6 = (bf16[528,256]{1,0:T(8,128)(2,1)S(1)}, bf16[528,256]{1,0:T(8,128)(2,1)S(1)}, u32[]{:S(2)}, u32[]{:S(2)}) collective-permute-start(bf16[528,256]{1,0:T(8,128)(2,1)S(1)} %slice_bitcast_fusion.1), channel_id=1, source_target_pairs={{0,8},{1,9},{2,10},{3,11},{4,12},{5,13},{6,14},{7,15},{8,16},{9,17... | collective-permute-start | bytes 811016 | tf_op jit(solution)/shard_map/ppermute | solution.py:35
  50.5 1.7 %collective-permute-start.7 = (bf16[528,256]{1,0:T(8,128)(2,1)S(1)}, bf16[528,256]{1,0:T(8,128)(2,1)S(1)}, u32[]{:S(2)}, u32[]{:S(2)}) collective-permute-start(bf16[528,256]{1,0:T(8,128)(2,1)S(1)} %slice_bitcast_fusion), channel_id=1, source_target_pairs={{0,24},{1,25},{2,26},{3,27},{4,28},{5,29},{6,30},{7,31},{8,0},{9,1... | collective-permute-start | bytes 811016 | tf_op jit(solution)/shard_map/ppermute | solution.py:35
  52.3 7.3 %shard_map.58 = (f32[1024,256]{1,0:T(8,128)S(1)}, f32[1024,128]{1,0:T(8,128)S(1)}, f32[1024,128]{1,0:T(8,128)S(1)}) custom-call(bf16[528,256]{1,0:T(8,128)(2,1)S(1)} %copy-done.1, bf16[528,256]{1,0:T(8,128)(2,1)S(1)} %collective-permute-done.refs_1_, bf16[528,256]{1,0:T(8,128)(2,1)S(1)} %collective-permute-done.1.refs_2_, ...), custom_call_target="tpu_custom_call" | custom-call | bytes 1024 | tf_op jit(solution)/shard_map/pallas_call | solution.py:278
  60.2 2.0 %collective-permute-start.18 = (bf16[2,256,1024]{2,1,0:T(8,128)(2,1)S(1)}, bf16[2,256,1024]{2,1,0:T(8,128)(2,1)S(1)}, u32[]{:S(2)}, u32[]{:S(2)}) collective-permute-start(bf16[2,256,1024]{2,1,0:T(8,128)(2,1)S(1)} %pad_maximum_fusion.refs_0_), channel_id=1, source_target_pairs={{0,4},{1,5},{2,6},{3,7},{4,0},{5,1},{6,2},{7,3},{8,12},{9,13},{10,... | collective-permute-start | bytes 3145736 | tf_op jit(solution)/shard_map/ppermute | solution.py:35
  62.2 2.9 %shard_map.59 = (bf16[512,256]{1,0:T(8,128)(2,1)S(1)}, bf16[512,256]{1,0:T(8,128)(2,1)S(1)}) custom-call(bf16[528,256]{1,0:T(8,128)(2,1)S(1)} %copy-done.1, bf16[528,256]{1,0:T(8,128)(2,1)S(1)} %collective-permute-done.refs_1_, bf16[528,256]{1,0:T(8,128)(2,1)S(1)} %collective-permute-done.1.refs_2_, bf16[528,256]{1,0:T(8,128)(2,1)S(1)} %collective-permute-done.2.refs_3_, ...), custom_call_target="tpu_custom_call" | custom-call | bytes 1024 | tf_op jit(solution)/shard_map/pallas_call | solution.py:278
  65.1 2.3 %collective-permute-start.19 = (bf16[2,256,1024]{2,1,0:T(8,128)(2,1)S(1)}, bf16[2,256,1024]{2,1,0:T(8,128)(2,1)S(1)}, u32[]{:S(2)}, u32[]{:S(2)}) collective-permute-start(bf16[2,256,1024]{2,1,0:T(8,128)(2,1)S(1)} %collective-permute-done.17.refs_1_), channel_id=1, source_target_pairs={{0,4},{1,5},{2,6},{3,7},{4,0},{5,1},{6,2},{7,3},{8,12},{9,13},{10,... | collective-permute-start | bytes 3145736 | tf_op jit(solution)/shard_map/ppermute | solution.py:35
  67.5 2.6 %collective-permute-start.14 = (bf16[512,256]{1,0:T(8,128)(2,1)S(1)}, bf16[512,256]{1,0:T(8,128)(2,1)S(1)}, u32[]{:S(2)}, u32[]{:S(2)}) collective-permute-start(bf16[512,256]{1,0:T(8,128)(2,1)S(1)} %get-tuple-element.68.c0), channel_id=1, source_target_pairs={{0,64},{1,65},{2,66},{3,67},{4,68},{5,69},{6,70},{7,71},{8,72},{9,... | collective-permute-start | bytes 786440 | tf_op jit(solution)/shard_map/ppermute | solution.py:35
  70.6 6.0 %collective-permute-done.13.c1 = bf16[512,256]{1,0:T(8,128)(2,1)S(1)} collective-permute-done((bf16[512,256]{1,0:T(8,128)(2,1)S(1)}, bf16[512,256]{1,0:T(8,128)(2,1)S(1)}, u32[]{:S(2)}, u32[]{:S(2)}) %collective-permute-start.13) | collective-permute-done | bytes 262176 | tf_op jit(solution)/shard_map/ppermute | solution.py:35
  76.6 1.6 %collective-permute-done.14.c2 = bf16[512,256]{1,0:T(8,128)(2,1)S(1)} collective-permute-done((bf16[512,256]{1,0:T(8,128)(2,1)S(1)}, bf16[512,256]{1,0:T(8,128)(2,1)S(1)}, u32[]{:S(2)}, u32[]{:S(2)}) %collective-permute-start.14) | collective-permute-done | bytes 262176 | tf_op jit(solution)/shard_map/ppermute | solution.py:35
  78.3 4.7 %collective-permute-done.15.c3 = bf16[512,256]{1,0:T(8,128)(2,1)S(1)} collective-permute-done((bf16[512,256]{1,0:T(8,128)(2,1)S(1)}, bf16[512,256]{1,0:T(8,128)(2,1)S(1)}, u32[]{:S(2)}, u32[]{:S(2)}) %collective-permute-start.15) | collective-permute-done | bytes 262176 | tf_op jit(solution)/shard_map/ppermute | solution.py:35
  84.4 1.5 %collective-permute-start.21 = (bf16[256,512]{1,0:T(8,128)(2,1)S(1)}, bf16[256,512]{1,0:T(8,128)(2,1)S(1)}, u32[]{:S(2)}, u32[]{:S(2)}) collective-permute-start(bf16[256,512]{1,0:T(8,128)(2,1)S(1)} %get-tuple-element.74), channel_id=1, source_target_pairs={{0,3},{1,0},{2,1},{3,2},{4,7},{5,4},{6,5},{7,6},{8,11},{9,8},{10,9... | collective-permute-start | bytes 786440 | tf_op jit(solution)/shard_map/ppermute | solution.py:35
  85.9 1.9 %shard_map.62 = (f32[256,512]{1,0:T(8,128)S(1)}, bf16[256,512]{1,0:T(8,128)(2,1)S(1)}, bf16[256,512]{1,0:T(8,128)(2,1)S(1)}, f32[256,512]{1,0:T(8,128)S(1)}, f32...) custom-call(bf16[512,256]{1,0:T(8,128)(2,1)S(1)} %get-tuple-element.68.c0, bf16[512,256]{1,0:T(8,128)(2,1)S(1)} %collective-permute-done.13.c1, ...), custom_call_target="tpu_custom_call" | custom-call | bytes 1024 | tf_op jit(solution)/shard_map/pallas_call | solution.py:362
  87.8 1.8 %collective-permute-start.23 = (bf16[256,512]{1,0:T(8,128)(2,1)S(1)}, bf16[256,512]{1,0:T(8,128)(2,1)S(1)}, u32[]{:S(2)}, u32[]{:S(2)}) collective-permute-start(bf16[256,512]{1,0:T(8,128)(2,1)S(1)} %get-tuple-element.76), channel_id=1, source_target_pairs={{0,1},{1,2},{2,3},{3,0},{4,5},{5,6},{6,7},{7,4},{8,9},{9,10},{10,1... | collective-permute-start | bytes 786440 | tf_op jit(solution)/shard_map/ppermute | solution.py:35
  89.9 3.1 %collective-permute-done.20.upward = bf16[256,512]{1,0:T(8,128)(2,1)S(1)} collective-permute-done((bf16[256,512]{1,0:T(8,128)(2,1)S(1)}, bf16[256,512]{1,0:T(8,128)(2,1)S(1)}, u32[]{:S(2)}, u32[]{:S(2)}) %collective-permute-start.20) | collective-permute-done | bytes 262176 | tf_op jit(solution)/shard_map/ppermute | solution.py:35
  93.1 1.4 %collective-permute-done.21.downward = bf16[256,512]{1,0:T(8,128)(2,1)S(1)} collective-permute-done((bf16[256,512]{1,0:T(8,128)(2,1)S(1)}, bf16[256,512]{1,0:T(8,128)(2,1)S(1)}, u32[]{:S(2)}, u32[]{:S(2)}) %collective-permute-start.21) | collective-permute-done | bytes 262176 | tf_op jit(solution)/shard_map/ppermute | solution.py:35
  95.2 1.5 %collective-permute-start.25 = (bf16[256,512]{1,0:T(8,128)(2,1)S(1)}, bf16[256,512]{1,0:T(8,128)(2,1)S(1)}, u32[]{:S(2)}, u32[]{:S(2)}) collective-permute-start(bf16[256,512]{1,0:T(8,128)(2,1)S(1)} %get-tuple-element.78), channel_id=1, source_target_pairs={{0,3},{1,0},{2,1},{3,2},{4,7},{5,4},{6,5},{7,6},{8,11},{9,8},{10,9... | collective-permute-start | bytes 786440 | tf_op jit(solution)/shard_map/ppermute | solution.py:35
  98.7 1.4 %collective-permute-done.24.down_top = bf16[256,512]{1,0:T(8,128)(2,1)S(1)} collective-permute-done((bf16[256,512]{1,0:T(8,128)(2,1)S(1)}, bf16[256,512]{1,0:T(8,128)(2,1)S(1)}, u32[]{:S(2)}, u32[]{:S(2)}) %collective-permute-start.24) | collective-permute-done | bytes 262176 | tf_op jit(solution)/shard_map/ppermute | solution.py:35
  100.1 3.2 %collective-permute-done.22.up_top = bf16[256,512]{1,0:T(8,128)(2,1)S(1)} collective-permute-done((bf16[256,512]{1,0:T(8,128)(2,1)S(1)}, bf16[256,512]{1,0:T(8,128)(2,1)S(1)}, u32[]{:S(2)}, u32[]{:S(2)}) %collective-permute-start.22) | collective-permute-done | bytes 262176 | tf_op jit(solution)/shard_map/ppermute | solution.py:35
  103.4 1.5 %collective-permute-done.25.down_end = bf16[256,512]{1,0:T(8,128)(2,1)S(1)} collective-permute-done((bf16[256,512]{1,0:T(8,128)(2,1)S(1)}, bf16[256,512]{1,0:T(8,128)(2,1)S(1)}, u32[]{:S(2)}, u32[]{:S(2)}) %collective-permute-start.25) | collective-permute-done | bytes 262176 | tf_op jit(solution)/shard_map/ppermute | solution.py:35
  (40 shorter events, 8.8 us)
Async XLA Ops:
  2.2 18.9 %collective-permute-start.3 = (bf16[256,1024]{1,0:T(8,128)(2,1)}, bf16[256,1024]{1,0:T(8,128)(2,1)S(1)}, u32[]{:S(2)}, u32[]{:S(2)}) collective-permute-start(bf16[256,1024]{1,0:T(8,128)(2,1)} %shard_map.55), channel_id=1, source_target_pairs={{64,32},{65,33},{66,34},{67,35},{68,36},{69,37},{70,38},{71,39},{7... | collective-permute-start | bytes 1572872 | tf_op jit(solution)/shard_map/ppermute | solution.py:35
  15.7 14.1 %collective-permute-start = (bf16[528,256]{1,0:T(8,128)(2,1)}, bf16[528,256]{1,0:T(8,128)(2,1)S(1)}, u32[]{:S(2)}, u32[]{:S(2)}) collective-permute-start(bf16[528,256]{1,0:T(8,128)(2,1)} %get-tuple-element.44), channel_id=1, source_target_pairs={{0,32},{1,33},{2,34},{3,35},{4,36},{5,37},{6,38},{7,39},{8,40},{9,... | collective-permute-start | bytes 811016 | tf_op jit(solution)/shard_map/ppermute | solution.py:35
  18.1 11.6 %collective-permute-start.1 = (bf16[528,256]{1,0:T(8,128)(2,1)}, bf16[528,256]{1,0:T(8,128)(2,1)S(1)}, u32[]{:S(2)}, u32[]{:S(2)}) collective-permute-start(bf16[528,256]{1,0:T(8,128)(2,1)} %get-tuple-element.45), channel_id=1, source_target_pairs={{0,64},{1,65},{2,66},{3,67},{4,68},{5,69},{6,70},{7,71},{8,72},{9,... | collective-permute-start | bytes 811016 | tf_op jit(solution)/shard_map/ppermute | solution.py:35
  18.5 13.9 %collective-permute-start.2 = (bf16[528,256]{1,0:T(8,128)(2,1)}, bf16[528,256]{1,0:T(8,128)(2,1)S(1)}, u32[]{:S(2)}, u32[]{:S(2)}) collective-permute-start(bf16[528,256]{1,0:T(8,128)(2,1)} %get-tuple-element.46), channel_id=1, source_target_pairs={{0,96},{1,97},{2,98},{3,99},{4,100},{5,101},{6,102},{7,103},{8,104... | collective-permute-start | bytes 811016 | tf_op jit(solution)/shard_map/ppermute | solution.py:35
  21.1 15.8 %collective-permute-start.16 = (bf16[256,1024]{1,0:T(8,128)(2,1)S(1)}, bf16[256,1024]{1,0:T(8,128)(2,1)S(1)}, u32[]{:S(2)}, u32[]{:S(2)}) collective-permute-start(bf16[256,1024]{1,0:T(8,128)(2,1)S(1)} %collective-permute-done.3), channel_id=1, source_target_pairs={{0,8},{1,9},{2,10},{3,11},{4,12},{5,13},{6,14},{7,15},{8,0},{9,1},... | collective-permute-start | bytes 1572872 | tf_op jit(solution)/shard_map/ppermute | solution.py:35
  33.6 14.7 %collective-permute-start.4 = (bf16[2,528,256]{2,1,0:T(8,128)(2,1)S(1)}, bf16[2,528,256]{2,1,0:T(8,128)(2,1)S(1)}, u32[]{:S(2)}, u32[]{:S(2)}) collective-permute-start(bf16[2,528,256]{2,1,0:T(8,128)(2,1)S(1)} %pad_maximum_fusion.1.refs_4_), channel_id=1, source_target_pairs={{0,8},{1,9},{2,10},{3,11},{4,12},{5,13},{6,14},{7,15},{8,16},{9,17... | collective-permute-start | bytes 1622024 | tf_op jit(solution)/shard_map/ppermute | solution.py:35
  35.2 13.1 %collective-permute-start.5 = (bf16[2,528,256]{2,1,0:T(8,128)(2,1)S(1)}, bf16[2,528,256]{2,1,0:T(8,128)(2,1)S(1)}, u32[]{:S(2)}, u32[]{:S(2)}) collective-permute-start(bf16[2,528,256]{2,1,0:T(8,128)(2,1)S(1)} %pad_maximum_fusion.1.refs_4_), channel_id=1, source_target_pairs={{0,24},{1,25},{2,26},{3,27},{4,28},{5,29},{6,30},{7,31},{8,0},{9,1... | collective-permute-start | bytes 1622024 | tf_op jit(solution)/shard_map/ppermute | solution.py:35
  36.9 13.6 %collective-permute-start.8 = (bf16[2,528,256]{2,1,0:T(8,128)(2,1)S(1)}, bf16[2,528,256]{2,1,0:T(8,128)(2,1)S(1)}, u32[]{:S(2)}, u32[]{:S(2)}) collective-permute-start(bf16[2,528,256]{2,1,0:T(8,128)(2,1)S(1)} %pad_maximum_fusion.1.refs_4_), channel_id=1, source_target_pairs={{0,4},{1,5},{2,6},{3,7},{4,0},{5,1},{6,2},{7,3},{8,12},{9,13},{10,... | collective-permute-start | bytes 1622024 | tf_op jit(solution)/shard_map/ppermute | solution.py:35
  37.0 15.3 %copy-start.1 = (bf16[528,256]{1,0:T(8,128)(2,1)S(1)}, bf16[528,256]{1,0:T(8,128)(2,1)}, u32[]{:S(2)}) copy-start(bf16[528,256]{1,0:T(8,128)(2,1)} %get-tuple-element.43.refs_0_) | copy-start | bytes 811012
  37.0 28.0 %collective-permute-start.17 = (bf16[2,256,1024]{2,1,0:T(8,128)(2,1)S(1)}, bf16[2,256,1024]{2,1,0:T(8,128)(2,1)S(1)}, u32[]{:S(2)}, u32[]{:S(2)}) collective-permute-start(bf16[2,256,1024]{2,1,0:T(8,128)(2,1)S(1)} %pad_maximum_fusion.refs_0_), channel_id=1, source_target_pairs={{0,32},{1,33},{2,34},{3,35},{4,36},{5,37},{6,38},{7,39},{8,40},{9,... | collective-permute-start | bytes 3145736 | tf_op jit(solution)/shard_map/ppermute | solution.py:35
  48.3 4.0 %collective-permute-start.10 = (bf16[2,528,256]{2,1,0:T(8,128)(2,1)S(1)}, bf16[2,528,256]{2,1,0:T(8,128)(2,1)S(1)}, u32[]{:S(2)}, u32[]{:S(2)}) collective-permute-start(bf16[2,528,256]{2,1,0:T(8,128)(2,1)S(1)} %collective-permute-done.5.refs_6_), channel_id=1, source_target_pairs={{0,4},{1,5},{2,6},{3,7},{4,0},{5,1},{6,2},{7,3},{8,12},{9,13},{10,... | collective-permute-start | bytes 1622024 | tf_op jit(solution)/shard_map/ppermute | solution.py:35
  48.3 4.0 %collective-permute-start.9 = (bf16[2,528,256]{2,1,0:T(8,128)(2,1)S(1)}, bf16[2,528,256]{2,1,0:T(8,128)(2,1)S(1)}, u32[]{:S(2)}, u32[]{:S(2)}) collective-permute-start(bf16[2,528,256]{2,1,0:T(8,128)(2,1)S(1)} %collective-permute-done.4.refs_5_), channel_id=1, source_target_pairs={{0,4},{1,5},{2,6},{3,7},{4,0},{5,1},{6,2},{7,3},{8,12},{9,13},{10,... | collective-permute-start | bytes 1622024 | tf_op jit(solution)/shard_map/ppermute | solution.py:35
  48.8 10.7 %collective-permute-start.6 = (bf16[528,256]{1,0:T(8,128)(2,1)S(1)}, bf16[528,256]{1,0:T(8,128)(2,1)S(1)}, u32[]{:S(2)}, u32[]{:S(2)}) collective-permute-start(bf16[528,256]{1,0:T(8,128)(2,1)S(1)} %slice_bitcast_fusion.1), channel_id=1, source_target_pairs={{0,8},{1,9},{2,10},{3,11},{4,12},{5,13},{6,14},{7,15},{8,16},{9,17... | collective-permute-start | bytes 811016 | tf_op jit(solution)/shard_map/ppermute | solution.py:35
  50.5 19.6 %copy-start = (bf16[2048,1024]{1,0:T(8,128)(2,1)S(1)}, bf16[2048,1024]{1,0:T(8,128)(2,1)}, u32[]{:S(2)}) copy-start(bf16[2048,1024]{1,0:T(8,128)(2,1)} %shard_map.57.refs_4_) | copy-start | bytes 12582916
  50.5 9.1 %collective-permute-start.7 = (bf16[528,256]{1,0:T(8,128)(2,1)S(1)}, bf16[528,256]{1,0:T(8,128)(2,1)S(1)}, u32[]{:S(2)}, u32[]{:S(2)}) collective-permute-start(bf16[528,256]{1,0:T(8,128)(2,1)S(1)} %slice_bitcast_fusion), channel_id=1, source_target_pairs={{0,24},{1,25},{2,26},{3,27},{4,28},{5,29},{6,30},{7,31},{8,0},{9,1... | collective-permute-start | bytes 811016 | tf_op jit(solution)/shard_map/ppermute | solution.py:35
  59.6 2.6 %collective-permute-start.11 = (bf16[1,528,256]{2,1,0:T(8,128)(2,1)S(1)}, bf16[1,528,256]{2,1,0:T(8,128)(2,1)S(1)}, u32[]{:S(2)}, u32[]{:S(2)}) collective-permute-start(bf16[1,528,256]{2,1,0:T(8,128)(2,1)S(1)} %bitcast.12), channel_id=1, source_target_pairs={{0,4},{1,5},{2,6},{3,7},{4,0},{5,1},{6,2},{7,3},{8,12},{9,13},{10,... | collective-permute-start | bytes 811016 | tf_op jit(solution)/shard_map/ppermute | solution.py:35
  59.7 2.5 %collective-permute-start.12 = (bf16[1,528,256]{2,1,0:T(8,128)(2,1)S(1)}, bf16[1,528,256]{2,1,0:T(8,128)(2,1)S(1)}, u32[]{:S(2)}, u32[]{:S(2)}) collective-permute-start(bf16[1,528,256]{2,1,0:T(8,128)(2,1)S(1)} %bitcast.14), channel_id=1, source_target_pairs={{0,4},{1,5},{2,6},{3,7},{4,0},{5,1},{6,2},{7,3},{8,12},{9,13},{10,... | collective-permute-start | bytes 811016 | tf_op jit(solution)/shard_map/ppermute | solution.py:35
  60.2 10.0 %collective-permute-start.18 = (bf16[2,256,1024]{2,1,0:T(8,128)(2,1)S(1)}, bf16[2,256,1024]{2,1,0:T(8,128)(2,1)S(1)}, u32[]{:S(2)}, u32[]{:S(2)}) collective-permute-start(bf16[2,256,1024]{2,1,0:T(8,128)(2,1)S(1)} %pad_maximum_fusion.refs_0_), channel_id=1, source_target_pairs={{0,4},{1,5},{2,6},{3,7},{4,0},{5,1},{6,2},{7,3},{8,12},{9,13},{10,... | collective-permute-start | bytes 3145736 | tf_op jit(solution)/shard_map/ppermute | solution.py:35
  65.1 5.1 %collective-permute-start.19 = (bf16[2,256,1024]{2,1,0:T(8,128)(2,1)S(1)}, bf16[2,256,1024]{2,1,0:T(8,128)(2,1)S(1)}, u32[]{:S(2)}, u32[]{:S(2)}) collective-permute-start(bf16[2,256,1024]{2,1,0:T(8,128)(2,1)S(1)} %collective-permute-done.17.refs_1_), channel_id=1, source_target_pairs={{0,4},{1,5},{2,6},{3,7},{4,0},{5,1},{6,2},{7,3},{8,12},{9,13},{10,... | collective-permute-start | bytes 3145736 | tf_op jit(solution)/shard_map/ppermute | solution.py:35
  67.4 9.2 %collective-permute-start.13 = (bf16[512,256]{1,0:T(8,128)(2,1)S(1)}, bf16[512,256]{1,0:T(8,128)(2,1)S(1)}, u32[]{:S(2)}, u32[]{:S(2)}) collective-permute-start(bf16[512,256]{1,0:T(8,128)(2,1)S(1)} %get-tuple-element.61), channel_id=1, source_target_pairs={{0,32},{1,33},{2,34},{3,35},{4,36},{5,37},{6,38},{7,39},{8,40},{9,... | collective-permute-start | bytes 786440 | tf_op jit(solution)/shard_map/ppermute | solution.py:35
  67.5 10.8 %collective-permute-start.14 = (bf16[512,256]{1,0:T(8,128)(2,1)S(1)}, bf16[512,256]{1,0:T(8,128)(2,1)S(1)}, u32[]{:S(2)}, u32[]{:S(2)}) collective-permute-start(bf16[512,256]{1,0:T(8,128)(2,1)S(1)} %get-tuple-element.68.c0), channel_id=1, source_target_pairs={{0,64},{1,65},{2,66},{3,67},{4,68},{5,69},{6,70},{7,71},{8,72},{9,... | collective-permute-start | bytes 786440 | tf_op jit(solution)/shard_map/ppermute | solution.py:35
  70.1 12.9 %collective-permute-start.15 = (bf16[512,256]{1,0:T(8,128)(2,1)S(1)}, bf16[512,256]{1,0:T(8,128)(2,1)S(1)}, u32[]{:S(2)}, u32[]{:S(2)}) collective-permute-start(bf16[512,256]{1,0:T(8,128)(2,1)S(1)} %get-tuple-element.61), channel_id=1, source_target_pairs={{0,96},{1,97},{2,98},{3,99},{4,100},{5,101},{6,102},{7,103},{8,104... | collective-permute-start | bytes 786440 | tf_op jit(solution)/shard_map/ppermute | solution.py:35
  83.8 9.2 %collective-permute-start.20 = (bf16[256,512]{1,0:T(8,128)(2,1)S(1)}, bf16[256,512]{1,0:T(8,128)(2,1)S(1)}, u32[]{:S(2)}, u32[]{:S(2)}) collective-permute-start(bf16[256,512]{1,0:T(8,128)(2,1)S(1)} %get-tuple-element.73), channel_id=1, source_target_pairs={{0,1},{1,2},{2,3},{3,0},{4,5},{5,6},{6,7},{7,4},{8,9},{9,10},{10,1... | collective-permute-start | bytes 786440 | tf_op jit(solution)/shard_map/ppermute | solution.py:35
  84.4 10.1 %collective-permute-start.21 = (bf16[256,512]{1,0:T(8,128)(2,1)S(1)}, bf16[256,512]{1,0:T(8,128)(2,1)S(1)}, u32[]{:S(2)}, u32[]{:S(2)}) collective-permute-start(bf16[256,512]{1,0:T(8,128)(2,1)S(1)} %get-tuple-element.74), channel_id=1, source_target_pairs={{0,3},{1,0},{2,1},{3,2},{4,7},{5,4},{6,5},{7,6},{8,11},{9,8},{10,9... | collective-permute-start | bytes 786440 | tf_op jit(solution)/shard_map/ppermute | solution.py:35
  87.8 10.8 %collective-permute-start.23 = (bf16[256,512]{1,0:T(8,128)(2,1)S(1)}, bf16[256,512]{1,0:T(8,128)(2,1)S(1)}, u32[]{:S(2)}, u32[]{:S(2)}) collective-permute-start(bf16[256,512]{1,0:T(8,128)(2,1)S(1)} %get-tuple-element.76), channel_id=1, source_target_pairs={{0,1},{1,2},{2,3},{3,0},{4,5},{5,6},{6,7},{7,4},{8,9},{9,10},{10,1... | collective-permute-start | bytes 786440 | tf_op jit(solution)/shard_map/ppermute | solution.py:35
  89.6 10.5 %collective-permute-start.24 = (bf16[256,512]{1,0:T(8,128)(2,1)S(1)}, bf16[256,512]{1,0:T(8,128)(2,1)S(1)}, u32[]{:S(2)}, u32[]{:S(2)}) collective-permute-start(bf16[256,512]{1,0:T(8,128)(2,1)S(1)} %get-tuple-element.77), channel_id=1, source_target_pairs={{0,3},{1,0},{2,1},{3,2},{4,7},{5,4},{6,5},{7,6},{8,11},{9,8},{10,9... | collective-permute-start | bytes 786440 | tf_op jit(solution)/shard_map/ppermute | solution.py:35
  94.6 8.8 %collective-permute-start.22 = (bf16[256,512]{1,0:T(8,128)(2,1)S(1)}, bf16[256,512]{1,0:T(8,128)(2,1)S(1)}, u32[]{:S(2)}, u32[]{:S(2)}) collective-permute-start(bf16[256,512]{1,0:T(8,128)(2,1)S(1)} %get-tuple-element.75), channel_id=1, source_target_pairs={{0,1},{1,2},{2,3},{3,0},{4,5},{5,6},{6,7},{7,4},{8,9},{9,10},{10,1... | collective-permute-start | bytes 786440 | tf_op jit(solution)/shard_map/ppermute | solution.py:35
  95.2 9.6 %collective-permute-start.25 = (bf16[256,512]{1,0:T(8,128)(2,1)S(1)}, bf16[256,512]{1,0:T(8,128)(2,1)S(1)}, u32[]{:S(2)}, u32[]{:S(2)}) collective-permute-start(bf16[256,512]{1,0:T(8,128)(2,1)S(1)} %get-tuple-element.78), channel_id=1, source_target_pairs={{0,3},{1,0},{2,1},{3,2},{4,7},{5,4},{6,5},{7,6},{8,11},{9,8},{10,9... | collective-permute-start | bytes 786440 | tf_op jit(solution)/shard_map/ppermute | solution.py:35
